TPU v7x, 32 devices: a whole 2x2x4 slice. The times are simulated.
32 devices in a mesh: sib: 2 (over x), leaf: 16 (over z, y, core).
Axes of the slice: x: 2, y: 2, z: 4, core: 2. Of those that a mesh axis runs over, the one named last changes fastest.
Arguments:
- t_int: float32 [16, 512, 1024], P('leaf', 'sib'), as said below
- t_ext: float32 [16, 512, 512], P('leaf', 'sib'), may hold values from -6 to 6
- iface_map: int32 [16, 512], P('leaf'), may hold values from 0 to 511, each once within a row
Outputs:
- own_map: float32 [16, 512, 512], P('leaf', 'sib')
- cross_map: float32 [16, 512, 512], P('leaf', 'sib')
- solution_op: float32 [16, 512, 512], P('leaf', 'sib')
Inputs may be any that keep to these rules, and one draw needn't show every extreme that they name: For each box, the last 512 columns of t_int form a symmetric matrix equal to the identity plus a positive semidefinite matrix. `iface_map`: each row is a permutation of 0 to 511.
All inputs are finite; a program needn't handle non-finite values.
Results may differ from a plain program's by a relative error of at most 0.0003.
Values sent between devices are 32-bit elements; how exact they have to be, the bound alone decides.
No kernel may reach another device: no remote copies, remote signals or barrier semaphores. Data moves between devices by JAX's collectives and lax.ppermute only.
A program may use at most 64 MiB of HBM per device.

v0:
```python
import functools

import jax
import jax.numpy as jnp
from jax import lax
from jax.experimental import pallas as pl
from jax.experimental.pallas import tpu as pltpu
from jax.sharding import PartitionSpec as P

F32 = jnp.float32
BF16 = jnp.bfloat16
TILE = 128
VMEM_LIMIT = 48 * 2**20


def split3(x):
    high = x.astype(BF16).astype(F32)
    rest = x - high
    middle = rest.astype(BF16).astype(F32)
    return high, middle, rest - middle


def contract(left, right, dims):
    return lax.dot_general(left, right, (dims, ((), ())), preferred_element_type=F32)


def full(left, right, dims=((1,), (0,))):
    return lax.dot_general(
        left, right, (dims, ((), ())), precision=lax.Precision.HIGHEST, preferred_element_type=F32
    )


def three_pass(left, right, dims):
    lh, rh = left.astype(BF16), right.astype(BF16)
    ll, rl = (left - lh.astype(F32)).astype(BF16), (right - rh.astype(F32)).astype(BF16)
    return contract(lh, rh, dims) + (contract(lh, rl, dims) + contract(ll, rh, dims))


def pick_left(onehot, x, dims):
    high, middle, low = (part.astype(BF16) for part in split3(x))
    return contract(onehot, high, dims) + (contract(onehot, middle, dims) + contract(onehot, low, dims))


def pick_right(x, onehot, dims):
    high, middle, low = (part.astype(BF16) for part in split3(x))
    return contract(high, onehot, dims) + (contract(middle, onehot, dims) + contract(low, onehot, dims))


def over_lanes(x, lane):
    return jnp.broadcast_to(x[:, lane : lane + 1], (8, TILE))


def over_rows(x, row):
    return jnp.broadcast_to(x[row : row + 1, :], (8, TILE))


def reciprocal(d):
    r = pltpu.reciprocal(d, approx=True)
    return r * (2.0 - d * r)


def invert_tile(work, slabs=2):
    width = 8 * slabs
    lane = lax.broadcasted_iota(jnp.int32, (8, TILE), 1)
    row = lax.broadcasted_iota(jnp.int32, (8, TILE), 0)
    lane_all = lax.broadcasted_iota(jnp.int32, (TILE, TILE), 1)
    is_row = [row == j for j in range(8)]
    for base in range(0, TILE, width):
        old = [work[base + 8 * s : base + 8 * s + 8, :] for s in range(slabs)]
        columns = [[over_lanes(old[s], base + m) for s in range(slabs)] for m in range(width)]
        inside = (lane >= base) & (lane < base + width)
        new = [
            jnp.where(inside, jnp.where(lane - base - 8 * s == row, 1.0, 0.0).astype(F32), old[s])
            for s in range(slabs)
        ]
        pivot = over_rows(columns[0][0], 0)
        for j in range(width):
            js, jr = divmod(j, 8)
            inverse = reciprocal(pivot)
            here = columns[j]
            scaled = [c * inverse for c in here]
            for m in range(j + 1, width):
                picked = over_rows(columns[m][js], jr)
                if m == j + 1:
                    later = [columns[m][s] - (here[s] * picked) * inverse for s in range(slabs)]
                    pivot = over_rows(later[m // 8], m % 8)
                else:
                    later = [columns[m][s] - scaled[s] * picked for s in range(slabs)]
                later[js] = jnp.where(is_row[jr], picked * inverse, later[js])
                columns[m] = later
            picked = over_rows(new[js], jr)
            later = [new[s] - scaled[s] * picked for s in range(slabs)]
            later[js] = jnp.where(is_row[jr], picked * inverse, later[js])
            new = later
        panel = jnp.concatenate(new, axis=0)
        sign = jnp.where(lane < base, -1.0, jnp.where(inside, 0.0, 1.0)).astype(F32)
        ah, am, al = split3(jnp.concatenate([x * sign for x in old], axis=0))
        bh, bm, bl = split3(panel)
        left = jnp.concatenate([ah, ah, am, am, ah, al], axis=0).astype(BF16)
        right = jnp.concatenate([bh, bm, bh, bm, bl, bh], axis=0).astype(BF16)
        change = contract(left, right, ((0,), (0,)))
        inside_all = (lane_all >= base) & (lane_all < base + width)
        rest = jnp.where(inside_all, 0.0, work) - change
        work = jnp.concatenate(
            [x for x in (rest[:base], panel, rest[base + width :]) if x.shape[0]], axis=0
        )
    return work


def eliminate(a_ref, g_ref, steps):
    size = a_ref.shape[0]
    for k in steps:
        at, after = k * TILE, (k + 1) * TILE
        own = slice(at, after)
        inverse = invert_tile(a_ref[own, own])
        right = full(inverse, g_ref[own, :])
        g_ref[own, :] = right
        if after < size:
            old = a_ref[own, after:]
            panel = full(inverse, old)
            a_ref[own, after:] = panel
        for i in range(k + 1, size // TILE):
            rows = slice(i * TILE, (i + 1) * TILE)
            factor = old[:, (i - k - 1) * TILE : (i - k) * TILE]
            a_ref[rows, i * TILE :] = a_ref[rows, i * TILE :] - full(
                factor, panel[:, (i - k - 1) * TILE :], ((0,), (0,))
            )
            g_ref[rows, :] = g_ref[rows, :] - full(factor, right, ((0,), (0,)))
        for i in range(k):
            rows = slice(i * TILE, (i + 1) * TILE)
            factor = a_ref[rows, own]
            if after < size:
                a_ref[rows, after:] = a_ref[rows, after:] - full(factor, panel)
            g_ref[rows, :] = g_ref[rows, :] - full(factor, right)


def call(body, outs, scratch=(), **cost):
    return pl.pallas_call(
        body,
        out_shape=outs,
        scratch_shapes=list(scratch),
        compiler_params=pltpu.CompilerParams(vmem_limit_bytes=VMEM_LIMIT),
        **cost,
    )


def solve_body(a_ref, r_ref, g_ref, a_work):
    a_work[...] = a_ref[...]
    g_ref[...] = r_ref[...]
    eliminate(a_work, g_ref, range(a_ref.shape[0] // TILE))


def solve(a, r):
    return call(
        solve_body, jax.ShapeDtypeStruct(r.shape, F32), [pltpu.VMEM(a.shape, F32)]
    )(a, r)


def first_body(
    half, t_ref, diag_ref, near_ref, far_ref, other_ref, column_ref, row_ref, first_ref, a_out, g_out, p_out, m_work
):
    n = 2 * half
    q = half // 2
    width = t_ref.shape[1] - n
    mine = first_ref[0]

    def block(i, j):
        return (slice(i * q, (i + 1) * q), slice(j * q, (j + 1) * q))

    def part(ref, i):
        return ref[i * q : (i + 1) * q, :]

    def put(i, j, value):
        m_work[block(i, j)] = value
        if i != j:
            m_work[block(j, i)] = value.T

    for base, ref in ((0, near_ref), (2, far_ref)):
        put(base, base, part(ref, 0))
        put(base, base + 1, part(ref, 1))
        put(base + 1, base + 1, part(ref, 2))
    put(0, 3, part(near_ref, 3))
    put(2, 1, part(far_ref, 3))

    @pl.when(mine == 0)
    def _():
        put(0, 2, part(near_ref, 4))
        put(3, 1, part(far_ref, 4))

    @pl.when(mine != 0)
    def _():
        put(1, 3, part(near_ref, 4))
        put(2, 0, part(far_ref, 4))

    same = column_ref[...] == row_ref[...]
    onehot = jnp.where(same, 1.0, 0.0).astype(BF16)
    p_out[...] = onehot
    moved = pick_right(m_work[...], onehot, ((1,), (1,)))
    here = pl.ds(pl.multiple_of(width + mine * half, half), half)
    there = pl.ds(pl.multiple_of(width + (1 - mine) * half, half), half)
    a_out[0:half, 0:half] = t_ref[:, here]
    a_out[0:half, half:n] = t_ref[:, there]
    a_out[block(2, 2)] = part(diag_ref, 0)
    a_out[block(2, 3)] = part(diag_ref, 1)
    a_out[block(3, 3)] = part(diag_ref, 2)
    for i in range(n // TILE):
        rows, later = slice(i * TILE, (i + 1) * TILE), slice(i * TILE, n)
        a_out[rows, later] = a_out[rows, later] + pick_left(onehot[rows, :], moved[:, later], ((1,), (0,)))
    g_out[0:half, :] = t_ref[:, 0:width]
    g_out[half:n, :] = other_ref[...]
    eliminate(a_out, g_out, range(n // TILE // 2))


def second_body(
    half, a_ref, g_in, p_ref, t_ref, other_ref, ext_ref, row_ref, first_ref, own_ref, sol_ref, h_ref, a_work, g_work
):
    n = 2 * half
    mine = first_ref[0]
    a_work[...] = a_ref[...]
    g_work[...] = g_in[...]
    eliminate(a_work, g_work, range(n // TILE // 2, n // TILE))
    block = pl.ds(pl.multiple_of(mine * half, half), half)
    g = g_work[...]
    h_ref[...] = pick_left(p_ref[...], g_work[:, block], ((0,), (0,)))
    left = jnp.concatenate([t_ref[:, block], other_ref[:, block]], axis=0)
    own_ref[...] = ext_ref[...] - three_pass(left, g, ((0,), (0,)))
    target = lax.broadcasted_iota(jnp.int32, (half, n), 0) + mine * half
    onehot = jnp.where(row_ref[...] == target, 1.0, 0.0).astype(BF16)
    sol_ref[...] = -pick_left(onehot, g, ((1,), (0,)))


def cross_body(h_ref, near_ref, far_ref, out_ref):
    half = near_ref.shape[0]
    out_ref[...] = -(
        three_pass(h_ref[0:half, :], near_ref[...], ((0,), (0,)))
        + three_pass(h_ref[half:, :], far_ref[...], ((0,), (0,)))
    )


def sibling(x):
    size = lax.axis_size("leaf")
    return lax.ppermute(x, "leaf", [(i, i ^ size // 2) for i in range(size)])


def across(x):
    return lax.ppermute(x, "sib", [(0, 1), (1, 0)])


def two_shards(t_int, t_ext, iface_map):
    t_int, t_ext = t_int[0], t_ext[0]
    half, n = t_int.shape[0], iface_map.shape[1]
    q, width = half // 2, t_int.shape[1] - n
    mine = lax.axis_index("sib")
    here, there = width + mine * half, width + (1 - mine) * half
    cut = lambda row, column: lax.dynamic_slice(t_int, (row, column), (q, q))
    diag = jnp.concatenate([cut(0, here), cut(0, here + q), cut(q, here + q)], axis=0)
    packed = jnp.concatenate([diag, cut(0, there + q), cut(mine * q, there + mine * q)], axis=0)
    near = sibling(packed)
    other_map = sibling(iface_map)
    diag_other = across(diag)
    outer = t_int[:, :width]
    outer_other = across(outer)
    far = across(near)
    outer_late, _ = lax.optimization_barrier((outer, near))
    outer_near = sibling(outer_late)
    rolled = lambda m: lax.dynamic_slice(jnp.concatenate([m, m], axis=1), (0, mine * half), (1, n))
    own_row, other_row = rolled(iface_map), rolled(other_map)
    first = mine.astype(jnp.int32).reshape(1)

    f = lambda *shape: jax.ShapeDtypeStruct(shape, F32)
    vmem, smem = pl.BlockSpec(memory_space=pltpu.VMEM), pl.BlockSpec(memory_space=pltpu.SMEM)
    a, g, onehot = pl.pallas_call(
        functools.partial(first_body, half),
        out_shape=(f(n, n), f(n, width), jax.ShapeDtypeStruct((n, n), BF16)),
        in_specs=[vmem] * 7 + [smem],
        scratch_shapes=[pltpu.VMEM((n, n), F32)],
        compiler_params=pltpu.CompilerParams(vmem_limit_bytes=VMEM_LIMIT),
    )(t_int, diag_other, near, far, outer_other, own_row.reshape(n, 1), other_row, first)
    a, g, outer_near = lax.optimization_barrier((a, g, outer_near))
    outer_far = across(outer_near)
    own_map, solution_op, h = pl.pallas_call(
        functools.partial(second_body, half),
        out_shape=(f(half, width), f(half, width), f(n, half)),
        in_specs=[vmem] * 7 + [smem],
        scratch_shapes=[pltpu.VMEM((n, n), F32), pltpu.VMEM((n, width), F32)],
        compiler_params=pltpu.CompilerParams(vmem_limit_bytes=VMEM_LIMIT),
    )(a, g, onehot, t_int, outer_other, t_ext, own_row, first)
    cross_map = call(cross_body, f(half, width))(h, outer_near, outer_far)
    return own_map[None], cross_map[None], solution_op[None]


def common_order(matrix, index_map):
    points = index_map.shape[0]
    inverse = jnp.zeros((points,), jnp.int32).at[index_map].set(jnp.arange(points, dtype=jnp.int32))
    picked = matrix[inverse]
    outer_width = matrix.shape[1] - points
    return (picked[:, :outer_width], picked[:, outer_width + inverse])


def many_shards(t_int, t_ext, iface_map):
    shard_rows = t_ext.shape[1]
    first_row = lax.axis_index("sib") * shard_rows
    near_rows, other_map = sibling((t_int, iface_map))
    own_rows = lax.all_gather(t_int, "sib", axis=1, tiled=True)
    other_rows = lax.all_gather(near_rows, "sib", axis=1, tiled=True)
    own_outer, own_iface = common_order(own_rows[0], iface_map[0])
    other_outer, other_iface = common_order(other_rows[0], other_map[0])
    g = solve(own_iface + other_iface, own_outer)
    product = lambda left, right: full(left, right, ((0,), (0,)))
    left = lax.dynamic_slice_in_dim(own_outer, first_row, shard_rows, 1)
    left_g = lax.dynamic_slice_in_dim(g, first_row, shard_rows, 1)
    own_map = t_ext - product(left, g)[None]
    cross_map = -product(left_g, other_outer)[None]
    solution_op = -lax.dynamic_slice_in_dim(g, first_row, shard_rows, 0)[None]
    return own_map, cross_map, solution_op


def solution(mesh):
    placed = P("leaf", "sib", None)
    return jax.shard_map(
        two_shards if mesh.shape["sib"] == 2 else many_shards,
        mesh=mesh,
        in_specs=(placed, placed, P("leaf", None)),
        out_specs=(placed, placed, placed),
        check_vma=False,
    )
```

profile of v0, /device:TPU:0, one launch (start us, length us, event | category | flops | bytes accessed | tf_op | source)
XLA Modules:
  0.0 75.9 jit_solution(14456950797081264840)
XLA Ops:
  0.6 0.9 %constant_dynamic-update-slice_fusion.2 = (f32[640,128]{1,0:T(8,128)S(1)}, f32[128,128]{1,0:T(8,128)S(1)}) fusion(f32[1,256,1024]{2,1,0:T(8,128)} %param.3, s32[]{:T(128)S(6)} %select_n.20), kind=kLoop, calls=%fused_computation.8 | loop fusion | bytes 196612
  1.5 0.9 %constant_dynamic-update-slice_fusion.1 = (f32[640,128]{1,0:T(8,128)S(1)}, f32[128,128]{1,0:T(8,128)S(1)}) fusion(f32[640,128]{1,0:T(8,128)S(1)} %get-tuple-element.27, f32[1,256,1024]{2,1,0:T(8,128)} %param.3, s32[]{:T(128)S(6)} %select_n.21), kind=kLoop, calls=%fused_computation.7 | loop fusion | bytes 196612
  2.4 0.9 %constant_dynamic-update-slice_fusion = (f32[640,128]{1,0:T(8,128)S(1)}, f32[128,128]{1,0:T(8,128)S(1)}) fusion(f32[640,128]{1,0:T(8,128)S(1)} %get-tuple-element.25, f32[1,256,1024]{2,1,0:T(8,128)} %param.3, s32[]{:T(128)S(6)} %select_n.21), kind=kLoop, calls=%fused_computation.6 | loop fusion | bytes 196612
  3.2 0.0 copy-start
  3.2 0.9 %bitcast_dynamic-update-slice_fusion.1 = f32[640,128]{1,0:T(8,128)S(1)} fusion(f32[640,128]{1,0:T(8,128)S(1)} %get-tuple-element.23, f32[1,256,1024]{2,1,0:T(8,128)} %param.3, s32[]{:T(128)S(6)} %select_n.22), kind=kLoop, calls=%fused_computation.2 | loop fusion | bytes 131076
  4.2 0.8 %bitcast_dynamic-update-slice_fusion = f32[640,128]{1,0:T(8,128)S(1)} fusion(f32[640,128]{1,0:T(8,128)S(1)} %bitcast_dynamic-update-slice_fusion.1, f32[1,256,1024]{2,1,0:T(8,128)} %param.3, s32[]{:T(128)S(6)} %select_n.23, s32[]{:T(128)S(6)} %select_n.24), kind=kLoop, calls=%fused_computation.1 | loop fusion | bytes 131080 | tf_op jit(solution)/shard_map/concatenate | solution.py:257
  5.0 4.0 %collective-permute-start.1 = (f32[640,128]{1,0:T(8,128)S(1)}, f32[640,128]{1,0:T(8,128)S(1)}, u32[]{:S(2)}, u32[]{:S(2)}) collective-permute-start(f32[640,128]{1,0:T(8,128)S(1)} %bitcast_dynamic-update-slice_fusion), channel_id=1, source_target_pairs={{0,8},{1,9},{2,10},{3,11},{4,12},{5,13},{6,14},{7,15},{8,0},{9,1},... | collective-permute-start | bytes 983048 | tf_op jit(solution)/shard_map/ppermute | solution.py:242
  9.1 1.9 %slice.4 = f32[256,512]{1,0:T(8,128)} slice(f32[256,1024]{1,0:T(8,128)} %bitcast.21), slice={[0:256], [0:512]} | slice | bytes 1048576 | tf_op jit(solution)/shard_map/slice | solution.py:261
  10.9 1.5 %collective-permute-start.3 = (f32[256,512]{1,0:T(8,128)}, f32[256,512]{1,0:T(8,128)S(1)}, u32[]{:S(2)}, u32[]{:S(2)}) collective-permute-start(f32[256,512]{1,0:T(8,128)} %slice.4), channel_id=1, source_target_pairs={{0,16},{16,0},{1,17},{17,1},{2,18},{18,2},{3,19},{19,3},{4,20},{20... | collective-permute-start | bytes 1572872 | tf_op jit(solution)/shard_map/ppermute | solution.py:246
  12.4 11.4 %collective-permute-done.1.near_ref = f32[640,128]{1,0:T(8,128)S(1)} collective-permute-done((f32[640,128]{1,0:T(8,128)S(1)}, f32[640,128]{1,0:T(8,128)S(1)}, u32[]{:S(2)}, u32[]{:S(2)}) %collective-permute-start.1) | collective-permute-done | bytes 327712 | tf_op jit(solution)/shard_map/ppermute | solution.py:242
  23.8 0.0 collective-permute-start.5
  23.8 2.9 %collective-permute-start.4 = (s32[1,512]{1,0:T(1,128)S(1)}, s32[1,512]{1,0:T(1,128)S(1)}, u32[]{:S(2)}, u32[]{:S(2)}) collective-permute-start(s32[1,512]{1,0:T(1,128)S(1)} %copy-done.2), channel_id=1, source_target_pairs={{0,8},{1,9},{2,10},{3,11},{4,12},{5,13},{6,14},{7,15},{8,0},{9,1},... | collective-permute-start | bytes 6152 | tf_op jit(solution)/shard_map/ppermute | solution.py:242
  26.7 1.5 %collective-permute-start.2 = (f32[640,128]{1,0:T(8,128)S(1)}, f32[640,128]{1,0:T(8,128)S(1)}, u32[]{:S(2)}, u32[]{:S(2)}) collective-permute-start(f32[640,128]{1,0:T(8,128)S(1)} %collective-permute-done.1.near_ref), channel_id=1, source_target_pairs={{0,16},{16,0},{1,17},{17,1},{2,18},{18,2},{3,19},{19,3},{4,20},{20... | collective-permute-start | bytes 983048 | tf_op jit(solution)/shard_map/ppermute | solution.py:246
  28.3 0.5 collective-permute-start
  28.8 0.1 copy.6.column_ref
  29.0 20.3 %collective-permute-done.4 = s32[1,512]{1,0:T(1,128)S(1)} collective-permute-done((s32[1,512]{1,0:T(1,128)S(1)}, s32[1,512]{1,0:T(1,128)S(1)}, u32[]{:S(2)}, u32[]{:S(2)}) %collective-permute-start.4) | collective-permute-done | bytes 2080 | tf_op jit(solution)/shard_map/ppermute | solution.py:242
  49.3 0.0 collective-permute-done.diag_ref
  49.4 0.0 collective-permute-done.2.far_ref
  49.4 0.0 copy-start.1
  49.4 12.0 %shard_map.58 = (f32[512,512]{1,0:T(8,128)S(1)}, f32[512,512]{1,0:T(8,128)S(1)}, bf16[512,512]{1,0:T(8,128)(2,1)S(1)}) custom-call(f32[256,1024]{1,0:T(8,128)S(1)} %bitcast.22, f32[384,128]{1,0:T(8,128)S(1)} %collective-permute-done.diag_ref, f32[640,128]{1,0:T(8,128)S(1)} %collective-permute-done.1.near_ref, f32[640,128]{1,0:T(8,128)S(1)} %collective-permute-done.2.far_ref, ...), custom_call_target="tpu_custom_call" | custom-call | tf_op jit(solution)/shard_map/pallas_call | solution.py:272
  61.4 0.0 collective-permute-done.5.near_ref
  61.4 1.4 %collective-permute-start.6 = (f32[256,512]{1,0:T(8,128)S(1)}, f32[256,512]{1,0:T(8,128)S(1)}, u32[]{:S(2)}, u32[]{:S(2)}) collective-permute-start(f32[256,512]{1,0:T(8,128)S(1)} %collective-permute-done.5.near_ref), channel_id=1, source_target_pairs={{0,16},{16,0},{1,17},{17,1},{2,18},{18,2},{3,19},{19,3},{4,20},{20... | collective-permute-start | bytes 1572872 | tf_op jit(solution)/shard_map/ppermute | solution.py:246
  62.8 11.7 %shard_map.59 = (f32[256,512]{1,0:T(8,128)}, f32[256,512]{1,0:T(8,128)}, f32[512,256]{1,0:T(8,128)S(1)}) custom-call(f32[512,512]{1,0:T(8,128)S(1)} %get-tuple-element.16.a_ref, f32[512,512]{1,0:T(8,128)S(1)} %get-tuple-element.17.g_in, bf16[512,512]{1,0:T(8,128)(2,1)S(1)} %get-tuple-element.18.p_ref, f32[256,1024]{1,0:T(8,128)S(1)} %bitcast.23, ...), custom_call_target="tpu_custom_call" | custom-call | tf_op jit(solution)/shard_map/pallas_call | solution.py:281
  74.5 1.4 %shard_map.60 = f32[256,512]{1,0:T(8,128)} custom-call(f32[512,256]{1,0:T(8,128)S(1)} %get-tuple-element.20.h_ref, f32[256,512]{1,0:T(8,128)S(1)} %collective-permute-done.5.near_ref, f32[256,512]{1,0:T(8,128)S(1)} %collective-permute-done.6.far_ref), custom_call_target="tpu_custom_call" | custom-call | tf_op jit(solution)/shard_map/pallas_call | solution.py:288
  (10 shorter events, 0.1 us)
Async XLA Ops:
  3.2 46.2 %copy-start = (f32[1,256,1024]{2,1,0:T(8,128)S(1)}, f32[1,256,1024]{2,1,0:T(8,128)}, u32[]{:S(2)}) copy-start(f32[1,256,1024]{2,1,0:T(8,128)} %param.3) | copy-start | bytes 3145732
  5.0 18.8 %collective-permute-start.1 = (f32[640,128]{1,0:T(8,128)S(1)}, f32[640,128]{1,0:T(8,128)S(1)}, u32[]{:S(2)}, u32[]{:S(2)}) collective-permute-start(f32[640,128]{1,0:T(8,128)S(1)} %bitcast_dynamic-update-slice_fusion), channel_id=1, source_target_pairs={{0,8},{1,9},{2,10},{3,11},{4,12},{5,13},{6,14},{7,15},{8,0},{9,1},... | collective-permute-start | bytes 983048 | tf_op jit(solution)/shard_map/ppermute | solution.py:242
  9.1 14.7 %copy-start.2 = (s32[1,512]{1,0:T(1,128)S(1)}, s32[1,512]{1,0:T(1,128)}, u32[]{:S(2)}) copy-start(s32[1,512]{1,0:T(1,128)} %param.5) | copy-start | bytes 6148
  10.9 38.4 %collective-permute-start.3 = (f32[256,512]{1,0:T(8,128)}, f32[256,512]{1,0:T(8,128)S(1)}, u32[]{:S(2)}, u32[]{:S(2)}) collective-permute-start(f32[256,512]{1,0:T(8,128)} %slice.4), channel_id=1, source_target_pairs={{0,16},{16,0},{1,17},{17,1},{2,18},{18,2},{3,19},{19,3},{4,20},{20... | collective-permute-start | bytes 1572872 | tf_op jit(solution)/shard_map/ppermute | solution.py:246
  23.8 37.6 %collective-permute-start.5 = (f32[256,512]{1,0:T(8,128)}, f32[256,512]{1,0:T(8,128)S(1)}, u32[]{:S(2)}, u32[]{:S(2)}) collective-permute-start(f32[256,512]{1,0:T(8,128)} %slice.4), channel_id=1, source_target_pairs={{0,8},{1,9},{2,10},{3,11},{4,12},{5,13},{6,14},{7,15},{8,0},{9,1},... | collective-permute-start | bytes 1572872 | tf_op jit(solution)/shard_map/ppermute | solution.py:242
  23.8 25.5 %collective-permute-start.4 = (s32[1,512]{1,0:T(1,128)S(1)}, s32[1,512]{1,0:T(1,128)S(1)}, u32[]{:S(2)}, u32[]{:S(2)}) collective-permute-start(s32[1,512]{1,0:T(1,128)S(1)} %copy-done.2), channel_id=1, source_target_pairs={{0,8},{1,9},{2,10},{3,11},{4,12},{5,13},{6,14},{7,15},{8,0},{9,1},... | collective-permute-start | bytes 6152 | tf_op jit(solution)/shard_map/ppermute | solution.py:242
  26.7 22.7 %collective-permute-start.2 = (f32[640,128]{1,0:T(8,128)S(1)}, f32[640,128]{1,0:T(8,128)S(1)}, u32[]{:S(2)}, u32[]{:S(2)}) collective-permute-start(f32[640,128]{1,0:T(8,128)S(1)} %collective-permute-done.1.near_ref), channel_id=1, source_target_pairs={{0,16},{16,0},{1,17},{17,1},{2,18},{18,2},{3,19},{19,3},{4,20},{20... | collective-permute-start | bytes 983048 | tf_op jit(solution)/shard_map/ppermute | solution.py:246
  28.3 21.1 %collective-permute-start = (f32[384,128]{1,0:T(8,128)S(1)}, f32[384,128]{1,0:T(8,128)S(1)}, u32[]{:S(2)}, u32[]{:S(2)}) collective-permute-start(f32[384,128]{1,0:T(8,128)S(1)} %pad_maximum_fusion), channel_id=1, source_target_pairs={{0,16},{16,0},{1,17},{17,1},{2,18},{18,2},{3,19},{19,3},{4,20},{20... | collective-permute-start | bytes 589832 | tf_op jit(solution)/shard_map/ppermute | solution.py:246
  49.4 13.4 %copy-start.1 = (f32[1,256,512]{2,1,0:T(8,128)S(1)}, f32[1,256,512]{2,1,0:T(8,128)}, u32[]{:S(2)}) copy-start(f32[1,256,512]{2,1,0:T(8,128)} %param.4) | copy-start | bytes 1572868
  61.4 13.1 %collective-permute-start.6 = (f32[256,512]{1,0:T(8,128)S(1)}, f32[256,512]{1,0:T(8,128)S(1)}, u32[]{:S(2)}, u32[]{:S(2)}) collective-permute-start(f32[256,512]{1,0:T(8,128)S(1)} %collective-permute-done.5.near_ref), channel_id=1, source_target_pairs={{0,16},{16,0},{1,17},{17,1},{2,18},{18,2},{3,19},{19,3},{4,20},{20... | collective-permute-start | bytes 1572872 | tf_op jit(solution)/shard_map/ppermute | solution.py:246
where the time goes:
time: 76.2 us; the launch traced here: 75.9 us
  waiting for transfers between devices  31.7 us (42%)
  Pallas kernels  25.1 us (33%)
  starting transfers between devices  11.9 us (16%)
  local copies, waits for them, and re-layouts  6.39 us (8%)
    ppermute x3, waiting for transfers between devices, sibling(): return lax.ppermute(x, 'leaf', [(i, i ^ size // 2) for i in range(size)])  31.7 us
    pallas_call x1, Pallas kernels, two_shards(): pl.pallas_call(functools.partial(first_body, half), out_shape=(f(n, n), f...  12 us
    pallas_call x1, Pallas kernels, two_shards(): pl.pallas_call(functools.partial(second_body, half), out_shape=(f(half, w...  11.7 us
    ppermute x3, starting transfers between devices, sibling(): return lax.ppermute(x, 'leaf', [(i, i ^ size // 2) for i in range(size)])  6.96 us
    ppermute x4, starting transfers between devices, across(): return lax.ppermute(x, 'sib', [(0, 1), (1, 0)])  4.96 us
    unnamed x10, local copies, waits for them, and re-layouts  3.52 us
    slice x1, local copies, waits for them, and re-layouts, two_shards(): outer = t_int[:, :width]  1.88 us
  transfers between devices with their start and end apart: 7, of which 2 were waited for; matrix products, arithmetic and copies ran while one was open for 3% of the time, Pallas kernels for 31%

commit v1 on v0

--- a/solution.py
+++ b/solution.py
@@ -157,7 +157,7 @@
 
 
 def first_body(
-    half, t_ref, diag_ref, near_ref, far_ref, other_ref, column_ref, row_ref, first_ref, a_out, g_out, p_out, m_work
+    half, steps, t_ref, diag_ref, near_ref, near_side, far_ref, far_side, other_ref, column_ref, row_ref, first_ref, a_out, g_out, p_out, m_work
 ):
     n = 2 * half
     q = half // 2
@@ -179,18 +179,18 @@
         put(base, base, part(ref, 0))
         put(base, base + 1, part(ref, 1))
         put(base + 1, base + 1, part(ref, 2))
-    put(0, 3, part(near_ref, 3))
-    put(2, 1, part(far_ref, 3))
+    put(0, 3, part(near_side, 0))
+    put(2, 1, part(far_side, 0))
 
     @pl.when(mine == 0)
     def _():
-        put(0, 2, part(near_ref, 4))
-        put(3, 1, part(far_ref, 4))
+        put(0, 2, part(near_side, 1))
+        put(3, 1, part(far_side, 1))
 
     @pl.when(mine != 0)
     def _():
-        put(1, 3, part(near_ref, 4))
-        put(2, 0, part(far_ref, 4))
+        put(1, 3, part(near_side, 1))
+        put(2, 0, part(far_side, 1))
 
     same = column_ref[...] == row_ref[...]
     onehot = jnp.where(same, 1.0, 0.0).astype(BF16)
@@ -208,17 +208,23 @@
         a_out[rows, later] = a_out[rows, later] + pick_left(onehot[rows, :], moved[:, later], ((1,), (0,)))
     g_out[0:half, :] = t_ref[:, 0:width]
     g_out[half:n, :] = other_ref[...]
-    eliminate(a_out, g_out, range(n // TILE // 2))
-
-
-def second_body(
-    half, a_ref, g_in, p_ref, t_ref, other_ref, ext_ref, row_ref, first_ref, own_ref, sol_ref, h_ref, a_work, g_work
+    eliminate(a_out, g_out, steps)
+
+
+def middle_body(steps, a_in, g_in, a_out, g_out):
+    a_out[...] = a_in[...]
+    g_out[...] = g_in[...]
+    eliminate(a_out, g_out, steps)
+
+
+def last_body(
+    half, steps, a_ref, g_in, p_ref, t_ref, other_ref, ext_ref, row_ref, first_ref, own_ref, sol_ref, h_ref, a_work, g_work
 ):
     n = 2 * half
     mine = first_ref[0]
     a_work[...] = a_ref[...]
     g_work[...] = g_in[...]
-    eliminate(a_work, g_work, range(n // TILE // 2, n // TILE))
+    eliminate(a_work, g_work, steps)
     block = pl.ds(pl.multiple_of(mine * half, half), half)
     g = g_work[...]
     h_ref[...] = pick_left(p_ref[...], g_work[:, block], ((0,), (0,)))
@@ -229,12 +235,43 @@
     sol_ref[...] = -pick_left(onehot, g, ((1,), (0,)))
 
 
-def cross_body(h_ref, near_ref, far_ref, out_ref):
-    half = near_ref.shape[0]
-    out_ref[...] = -(
-        three_pass(h_ref[0:half, :], near_ref[...], ((0,), (0,)))
-        + three_pass(h_ref[half:, :], far_ref[...], ((0,), (0,)))
-    )
+def cross_body(h_ref, *refs):
+    *parts, out_ref = refs
+    total, at = None, 0
+    for ref in parts:
+        end = at + ref.shape[0]
+        term = three_pass(h_ref[at:end, :], ref[...], ((0,), (0,)))
+        total, at = term if total is None else total + term, end
+    out_ref[...] = -total
+
+
+def pack_body(half, t_ref, first_ref, diag_ref, side_ref, outer_ref, *rest):
+    *chunks, sems = rest
+    q = half // 2
+    width = outer_ref.shape[1]
+    mine = first_ref[0]
+    here, there = width + mine * half, width + (1 - mine) * half
+
+    def cut(row, column):
+        return t_ref.at[pl.ds(pl.multiple_of(row, q), q), pl.ds(pl.multiple_of(column, q), q)]
+
+    moves = [
+        (cut(0, here), diag_ref.at[0:q, :]),
+        (cut(0, here + q), diag_ref.at[q : 2 * q, :]),
+        (cut(q, here + q), diag_ref.at[2 * q : 3 * q, :]),
+        (cut(0, there + q), side_ref.at[0:q, :]),
+        (cut(mine * q, there + mine * q), side_ref.at[q : 2 * q, :]),
+        (t_ref.at[:, 0:width], outer_ref),
+    ]
+    at = 0
+    for chunk in chunks:
+        moves.append((t_ref.at[at : at + chunk.shape[0], 0:width], chunk))
+        at += chunk.shape[0]
+    copies = [pltpu.make_async_copy(x, y, sems.at[i]) for i, (x, y) in enumerate(moves)]
+    for copy in copies:
+        copy.start()
+    for copy in copies:
+        copy.wait()
 
 
 def sibling(x):
@@ -246,46 +283,71 @@
     return lax.ppermute(x, "sib", [(0, 1), (1, 0)])
 
 
+def kernel(body, outs, places, scratch=()):
+    return pl.pallas_call(
+        body,
+        out_shape=outs,
+        in_specs=[pl.BlockSpec(memory_space=place) for place in places],
+        scratch_shapes=list(scratch),
+        compiler_params=pltpu.CompilerParams(vmem_limit_bytes=VMEM_LIMIT),
+    )
+
+
+def pack(t_int, first, half, width, chunk_rows):
+    f = lambda *shape: jax.ShapeDtypeStruct(shape, F32)
+    q = half // 2
+    outs = [f(3 * q, q), f(2 * q, q), f(half, width)] + [f(rows, width) for rows in chunk_rows]
+    return pl.pallas_call(
+        functools.partial(pack_body, half),
+        out_shape=outs,
+        in_specs=[pl.BlockSpec(memory_space=pl.ANY), pl.BlockSpec(memory_space=pltpu.SMEM)],
+        out_specs=[pl.BlockSpec(memory_space=pl.ANY)] * len(outs),
+        scratch_shapes=[pltpu.SemaphoreType.DMA((6 + len(chunk_rows),))],
+    )(t_int, first)
+
+
 def two_shards(t_int, t_ext, iface_map):
     t_int, t_ext = t_int[0], t_ext[0]
     half, n = t_int.shape[0], iface_map.shape[1]
-    q, width = half // 2, t_int.shape[1] - n
-    mine = lax.axis_index("sib")
-    here, there = width + mine * half, width + (1 - mine) * half
-    cut = lambda row, column: lax.dynamic_slice(t_int, (row, column), (q, q))
-    diag = jnp.concatenate([cut(0, here), cut(0, here + q), cut(q, here + q)], axis=0)
-    packed = jnp.concatenate([diag, cut(0, there + q), cut(mine * q, there + mine * q)], axis=0)
-    near = sibling(packed)
+    width = t_int.shape[1] - n
+    tiles = n // TILE
+    mine = lax.axis_index("sib").astype(jnp.int32)
+    first = mine.reshape(1)
+    diag, side, outer, chunk_a, chunk_b = pack(t_int, first, half, width, (half // 2, half // 2))
+    near, near_side = sibling(diag), sibling(side)
     other_map = sibling(iface_map)
-    diag_other = across(diag)
-    outer = t_int[:, :width]
-    outer_other = across(outer)
-    far = across(near)
-    outer_late, _ = lax.optimization_barrier((outer, near))
-    outer_near = sibling(outer_late)
+    diag_other, outer_other = across(diag), across(outer)
+    near_held, diag_other = lax.optimization_barrier((near, diag_other))
+    far = across(near_held)
+    side_held, outer_other = lax.optimization_barrier((near_side, outer_other))
+    far_side = across(side_held)
+    chunk_a, chunk_b, _, _ = lax.optimization_barrier((chunk_a, chunk_b, near_held, near_side))
+    near_a, near_b = sibling(chunk_a), sibling(chunk_b)
     rolled = lambda m: lax.dynamic_slice(jnp.concatenate([m, m], axis=1), (0, mine * half), (1, n))
     own_row, other_row = rolled(iface_map), rolled(other_map)
-    first = mine.astype(jnp.int32).reshape(1)
 
     f = lambda *shape: jax.ShapeDtypeStruct(shape, F32)
-    vmem, smem = pl.BlockSpec(memory_space=pltpu.VMEM), pl.BlockSpec(memory_space=pltpu.SMEM)
-    a, g, onehot = pl.pallas_call(
-        functools.partial(first_body, half),
-        out_shape=(f(n, n), f(n, width), jax.ShapeDtypeStruct((n, n), BF16)),
-        in_specs=[vmem] * 7 + [smem],
-        scratch_shapes=[pltpu.VMEM((n, n), F32)],
-        compiler_params=pltpu.CompilerParams(vmem_limit_bytes=VMEM_LIMIT),
-    )(t_int, diag_other, near, far, outer_other, own_row.reshape(n, 1), other_row, first)
-    a, g, outer_near = lax.optimization_barrier((a, g, outer_near))
-    outer_far = across(outer_near)
-    own_map, solution_op, h = pl.pallas_call(
-        functools.partial(second_body, half),
-        out_shape=(f(half, width), f(half, width), f(n, half)),
-        in_specs=[vmem] * 7 + [smem],
-        scratch_shapes=[pltpu.VMEM((n, n), F32), pltpu.VMEM((n, width), F32)],
-        compiler_params=pltpu.CompilerParams(vmem_limit_bytes=VMEM_LIMIT),
+    vmem, smem = pltpu.VMEM, pltpu.SMEM
+    a, g, onehot = kernel(
+        functools.partial(first_body, half, range(tiles // 2)),
+        (f(n, n), f(n, width), jax.ShapeDtypeStruct((n, n), BF16)),
+        [vmem] * 9 + [smem],
+        [pltpu.VMEM((n, n), F32)],
+    )(t_int, diag_other, near, near_side, far, far_side, outer_other, own_row.reshape(n, 1), other_row, first)
+    a, g, near_a = lax.optimization_barrier((a, g, near_a))
+    far_a = across(near_a)
+    a, g = kernel(
+        functools.partial(middle_body, range(tiles // 2, tiles - 1)), (f(n, n), f(n, width)), [vmem] * 2
+    )(a, g)
+    a, g, near_b, far_a = lax.optimization_barrier((a, g, near_b, far_a))
+    far_b = across(near_b)
+    own_map, solution_op, h = kernel(
+        functools.partial(last_body, half, range(tiles - 1, tiles)),
+        (f(half, width), f(half, width), f(n, half)),
+        [vmem] * 7 + [smem],
+        [pltpu.VMEM((n, n), F32), pltpu.VMEM((n, width), F32)],
     )(a, g, onehot, t_int, outer_other, t_ext, own_row, first)
-    cross_map = call(cross_body, f(half, width))(h, outer_near, outer_far)
+    cross_map = kernel(cross_body, f(half, width), [vmem] * 5)(h, near_a, near_b, far_a, far_b)
     return own_map[None], cross_map[None], solution_op[None]
 
 

time: 76.2 us -> 114 us (1.50)
  the two profiles are of different devices: /device:TPU:0 before, /device:TPU:8 now
where the time goes in v1:
time: 114 us
  Pallas kernels  68.7 us (60%)
  starting transfers between devices  22.6 us (20%)
  waiting for transfers between devices  22.1 us (19%)
    pallas_call x1, Pallas kernels, pack(): pl.pallas_call(functools.partial(pack_body, half), out_shape=outs, in_spe...  42.9 us
    ppermute x5, waiting for transfers between devices, sibling(): return lax.ppermute(x, 'leaf', [(i, i ^ size // 2) for i in range(size)])  18.1 us
    ppermute x6, starting transfers between devices, across(): return lax.ppermute(x, 'sib', [(0, 1), (1, 0)])  13.1 us
    pallas_call x1, Pallas kernels, two_shards(): kernel(functools.partial(first_body, half, range(tiles // 2)), (f(n, n),...  12 us
    ppermute x5, starting transfers between devices, sibling(): return lax.ppermute(x, 'leaf', [(i, i ^ size // 2) for i in range(size)])  9.5 us
    pallas_call x1, Pallas kernels, two_shards(): kernel(functools.partial(last_body, half, range(tiles - 1, tiles)), (f(ha...  7.01 us
    pallas_call x1, Pallas kernels, two_shards(): kernel(functools.partial(middle_body, range(tiles // 2, tiles - 1)), (f(n...  5.03 us
    ppermute x6, waiting for transfers between devices, across(): return lax.ppermute(x, 'sib', [(0, 1), (1, 0)])  3.97 us
  transfers between devices with their start and end apart: 11, of which 4 were waited for; matrix products, arithmetic and copies ran while one was open for 0% of the time, Pallas kernels for 21%

profile of v1, /device:TPU:8, one launch (start us, length us, event | category | flops | bytes accessed | tf_op | source)
XLA Modules:
  0.0 114.3 jit_solution(16858368035168643438)
XLA Ops:
  0.6 42.9 %shard_map.58 = (f32[384,128]{1,0:T(8,128)}, f32[256,128]{1,0:T(8,128)}, f32[256,512]{1,0:T(8,128)}, f32[128,512]{1,0:T(8,128)}, f32[128,512]{1,0:T(8,128)}) custom-call(f32[256,1024]{1,0:T(8,128)} %bitcast.8, s32[1]{0:T(128)} %bitcast.1.first_ref), custom_call_target="tpu_custom_call" | custom-call | tf_op jit(solution)/shard_map/pallas_call | solution.py:300
  43.5 1.6 %collective-permute-start.4 = (f32[256,512]{1,0:T(8,128)}, f32[256,512]{1,0:T(8,128)S(1)}, u32[]{:S(2)}, u32[]{:S(2)}) collective-permute-start(f32[256,512]{1,0:T(8,128)} %get-tuple-element.33), channel_id=1, source_target_pairs={{0,16},{16,0},{1,17},{17,1},{2,18},{18,2},{3,19},{19,3},{4,20},{20... | collective-permute-start | bytes 1572872 | tf_op jit(solution)/shard_map/ppermute | solution.py:283
  45.1 2.6 %collective-permute-start = (f32[384,128]{1,0:T(8,128)}, f32[384,128]{1,0:T(8,128)S(1)}, u32[]{:S(2)}, u32[]{:S(2)}) collective-permute-start(f32[384,128]{1,0:T(8,128)} %get-tuple-element.29), channel_id=1, source_target_pairs={{0,8},{1,9},{2,10},{3,11},{4,12},{5,13},{6,14},{7,15},{8,0},{9,1},... | collective-permute-start | bytes 589832 | tf_op jit(solution)/shard_map/ppermute | solution.py:279
  47.7 0.5 collective-permute-start.1
  48.2 0.3 collective-permute-start.2
  48.5 10.3 %collective-permute-done.near_ref = f32[384,128]{1,0:T(8,128)S(1)} collective-permute-done((f32[384,128]{1,0:T(8,128)}, f32[384,128]{1,0:T(8,128)S(1)}, u32[]{:S(2)}, u32[]{:S(2)}) %collective-permute-start) | collective-permute-done | bytes 196640 | tf_op jit(solution)/shard_map/ppermute | solution.py:279
  58.9 2.8 %collective-permute-done.1.diag_ref = f32[384,128]{1,0:T(8,128)S(1)} collective-permute-done((f32[384,128]{1,0:T(8,128)}, f32[384,128]{1,0:T(8,128)S(1)}, u32[]{:S(2)}, u32[]{:S(2)}) %collective-permute-start.1) | collective-permute-done | bytes 196640 | tf_op jit(solution)/shard_map/ppermute | solution.py:283
  61.7 3.2 %collective-permute-start.7 = (f32[128,512]{1,0:T(8,128)}, f32[128,512]{1,0:T(8,128)S(1)}, u32[]{:S(2)}, u32[]{:S(2)}) collective-permute-start(f32[128,512]{1,0:T(8,128)} %get-tuple-element.40), channel_id=1, source_target_pairs={{0,8},{1,9},{2,10},{3,11},{4,12},{5,13},{6,14},{7,15},{8,0},{9,1},... | collective-permute-start | bytes 786440 | tf_op jit(solution)/shard_map/ppermute | solution.py:279
  64.9 0.0 collective-permute-start.6
  64.9 1.2 %collective-permute-start.3 = (f32[384,128]{1,0:T(8,128)S(1)}, f32[384,128]{1,0:T(8,128)S(1)}, u32[]{:S(2)}, u32[]{:S(2)}) collective-permute-start(f32[384,128]{1,0:T(8,128)S(1)} %collective-permute-done.near_ref), channel_id=1, source_target_pairs={{0,16},{16,0},{1,17},{17,1},{2,18},{18,2},{3,19},{19,3},{4,20},{20... | collective-permute-start | bytes 589832 | tf_op jit(solution)/shard_map/ppermute | solution.py:283
  66.1 0.0 collective-permute-done.4.other_ref
  66.1 0.8 collective-permute-start.5
  66.9 0.1 copy.6.column_ref
  67.1 7.8 %collective-permute-done.6 = s32[1,512]{1,0:T(1,128)S(1)} collective-permute-done((s32[1,512]{1,0:T(1,128)S(1)}, s32[1,512]{1,0:T(1,128)S(1)}, u32[]{:S(2)}, u32[]{:S(2)}) %collective-permute-start.6) | collective-permute-done | bytes 2080 | tf_op jit(solution)/shard_map/ppermute | solution.py:279
  74.9 3.4 %collective-permute-start.8 = (f32[128,512]{1,0:T(8,128)S(1)}, f32[128,512]{1,0:T(8,128)S(1)}, u32[]{:S(2)}, u32[]{:S(2)}) collective-permute-start(f32[128,512]{1,0:T(8,128)S(1)} %copy-done.3), channel_id=1, source_target_pairs={{0,8},{1,9},{2,10},{3,11},{4,12},{5,13},{6,14},{7,15},{8,0},{9,1},... | collective-permute-start | bytes 786440 | tf_op jit(solution)/shard_map/ppermute | solution.py:279
  78.2 0.0 collective-permute-done.3.far_ref
  78.2 12.0 %shard_map.59 = (f32[512,512]{1,0:T(8,128)S(1)}, f32[512,512]{1,0:T(8,128)S(1)}, bf16[512,512]{1,0:T(8,128)(2,1)S(1)}) custom-call(f32[256,1024]{1,0:T(8,128)S(1)} %bitcast.9, f32[384,128]{1,0:T(8,128)S(1)} %collective-permute-done.1.diag_ref, f32[384,128]{1,0:T(8,128)S(1)} %collective-permute-done.near_ref, ...), custom_call_target="tpu_custom_call" | custom-call | tf_op jit(solution)/shard_map/pallas_call | solution.py:331
  90.3 0.0 copy-start.1
  90.3 7.2 %collective-permute-start.9 = (f32[128,512]{1,0:T(8,128)S(1)}, f32[128,512]{1,0:T(8,128)S(1)}, u32[]{:S(2)}, u32[]{:S(2)}) collective-permute-start(f32[128,512]{1,0:T(8,128)S(1)} %collective-permute-done.7.refs_0_), channel_id=1, source_target_pairs={{0,16},{16,0},{1,17},{17,1},{2,18},{18,2},{3,19},{19,3},{4,20},{20... | collective-permute-start | bytes 786440 | tf_op jit(solution)/shard_map/ppermute | solution.py:283
  97.5 5.0 %shard_map.60 = (f32[512,512]{1,0:T(8,128)S(1)}, f32[512,512]{1,0:T(8,128)S(1)}) custom-call(f32[512,512]{1,0:T(8,128)S(1)} %get-tuple-element.41.a_in, f32[512,512]{1,0:T(8,128)S(1)} %get-tuple-element.42.g_in), custom_call_target="tpu_custom_call" | custom-call | tf_op jit(solution)/shard_map/pallas_call | solution.py:339
  102.6 1.2 %collective-permute-done.9.refs_2_ = f32[128,512]{1,0:T(8,128)S(1)} collective-permute-done((f32[128,512]{1,0:T(8,128)S(1)}, f32[128,512]{1,0:T(8,128)S(1)}, u32[]{:S(2)}, u32[]{:S(2)}) %collective-permute-start.9) | collective-permute-done | bytes 262176 | tf_op jit(solution)/shard_map/ppermute | solution.py:283
  103.7 1.7 %collective-permute-start.10 = (f32[128,512]{1,0:T(8,128)S(1)}, f32[128,512]{1,0:T(8,128)S(1)}, u32[]{:S(2)}, u32[]{:S(2)}) collective-permute-start(f32[128,512]{1,0:T(8,128)S(1)} %collective-permute-done.8.refs_1_), channel_id=1, source_target_pairs={{0,16},{16,0},{1,17},{17,1},{2,18},{18,2},{3,19},{19,3},{4,20},{20... | collective-permute-start | bytes 786440 | tf_op jit(solution)/shard_map/ppermute | solution.py:283
  105.5 7.0 %shard_map.61 = (f32[256,512]{1,0:T(8,128)}, f32[256,512]{1,0:T(8,128)}, f32[512,256]{1,0:T(8,128)S(1)}) custom-call(f32[512,512]{1,0:T(8,128)S(1)} %get-tuple-element.47.a_ref, f32[512,512]{1,0:T(8,128)S(1)} %get-tuple-element.48.g_in, bf16[512,512]{1,0:T(8,128)(2,1)S(1)} %get-tuple-element.49.p_ref, f32[256,1024]{1,0:T(8,128)S(1)} %bitcast.10, ...), custom_call_target="tpu_custom_call" | custom-call | tf_op jit(solution)/shard_map/pallas_call | solution.py:344
  112.5 1.8 %shard_map.62 = f32[256,512]{1,0:T(8,128)} custom-call(f32[512,256]{1,0:T(8,128)S(1)} %get-tuple-element.51.h_ref, f32[128,512]{1,0:T(8,128)S(1)} %collective-permute-done.7.refs_0_, f32[128,512]{1,0:T(8,128)S(1)} %collective-permute-done.8.refs_1_, f32[128,512]{1,0:T(8,128)S(1)} %collective-permute-done.9.refs_2_, ...), custom_call_target="tpu_custom_call" | custom-call | tf_op jit(solution)/shard_map/pallas_call | solution.py:350
  (15 shorter events, 0.1 us)
Async XLA Ops:
  0.6 77.6 %copy-start = (f32[1,256,1024]{2,1,0:T(8,128)S(1)}, f32[1,256,1024]{2,1,0:T(8,128)}, u32[]{:S(2)}) copy-start(f32[1,256,1024]{2,1,0:T(8,128)} %param.3) | copy-start | bytes 3145732
  43.5 22.6 %collective-permute-start.4 = (f32[256,512]{1,0:T(8,128)}, f32[256,512]{1,0:T(8,128)S(1)}, u32[]{:S(2)}, u32[]{:S(2)}) collective-permute-start(f32[256,512]{1,0:T(8,128)} %get-tuple-element.33), channel_id=1, source_target_pairs={{0,16},{16,0},{1,17},{17,1},{2,18},{18,2},{3,19},{19,3},{4,20},{20... | collective-permute-start | bytes 1572872 | tf_op jit(solution)/shard_map/ppermute | solution.py:283
  45.1 13.8 %collective-permute-start = (f32[384,128]{1,0:T(8,128)}, f32[384,128]{1,0:T(8,128)S(1)}, u32[]{:S(2)}, u32[]{:S(2)}) collective-permute-start(f32[384,128]{1,0:T(8,128)} %get-tuple-element.29), channel_id=1, source_target_pairs={{0,8},{1,9},{2,10},{3,11},{4,12},{5,13},{6,14},{7,15},{8,0},{9,1},... | collective-permute-start | bytes 589832 | tf_op jit(solution)/shard_map/ppermute | solution.py:279
  47.7 14.0 %collective-permute-start.1 = (f32[384,128]{1,0:T(8,128)}, f32[384,128]{1,0:T(8,128)S(1)}, u32[]{:S(2)}, u32[]{:S(2)}) collective-permute-start(f32[384,128]{1,0:T(8,128)} %get-tuple-element.29), channel_id=1, source_target_pairs={{0,16},{16,0},{1,17},{17,1},{2,18},{18,2},{3,19},{19,3},{4,20},{20... | collective-permute-start | bytes 589832 | tf_op jit(solution)/shard_map/ppermute | solution.py:283
  48.2 16.7 %copy-start.2 = (s32[1,512]{1,0:T(1,128)S(1)}, s32[1,512]{1,0:T(1,128)}, u32[]{:S(2)}) copy-start(s32[1,512]{1,0:T(1,128)} %param.5) | copy-start | bytes 6148
  48.2 26.7 %copy-start.3 = (f32[128,512]{1,0:T(8,128)S(1)}, f32[128,512]{1,0:T(8,128)}, u32[]{:S(2)}) copy-start(f32[128,512]{1,0:T(8,128)} %get-tuple-element.45) | copy-start | bytes 786436
  48.2 13.5 %collective-permute-start.2 = (f32[256,128]{1,0:T(8,128)}, f32[256,128]{1,0:T(8,128)S(1)}, u32[]{:S(2)}, u32[]{:S(2)}) collective-permute-start(f32[256,128]{1,0:T(8,128)} %get-tuple-element.31), channel_id=1, source_target_pairs={{0,8},{1,9},{2,10},{3,11},{4,12},{5,13},{6,14},{7,15},{8,0},{9,1},... | collective-permute-start | bytes 393224 | tf_op jit(solution)/shard_map/ppermute | solution.py:279
  61.7 28.6 %collective-permute-start.7 = (f32[128,512]{1,0:T(8,128)}, f32[128,512]{1,0:T(8,128)S(1)}, u32[]{:S(2)}, u32[]{:S(2)}) collective-permute-start(f32[128,512]{1,0:T(8,128)} %get-tuple-element.40), channel_id=1, source_target_pairs={{0,8},{1,9},{2,10},{3,11},{4,12},{5,13},{6,14},{7,15},{8,0},{9,1},... | collective-permute-start | bytes 786440 | tf_op jit(solution)/shard_map/ppermute | solution.py:279
  64.9 10.0 %collective-permute-start.6 = (s32[1,512]{1,0:T(1,128)S(1)}, s32[1,512]{1,0:T(1,128)S(1)}, u32[]{:S(2)}, u32[]{:S(2)}) collective-permute-start(s32[1,512]{1,0:T(1,128)S(1)} %copy-done.2), channel_id=1, source_target_pairs={{0,8},{1,9},{2,10},{3,11},{4,12},{5,13},{6,14},{7,15},{8,0},{9,1},... | collective-permute-start | bytes 6152 | tf_op jit(solution)/shard_map/ppermute | solution.py:279
  64.9 13.4 %collective-permute-start.3 = (f32[384,128]{1,0:T(8,128)S(1)}, f32[384,128]{1,0:T(8,128)S(1)}, u32[]{:S(2)}, u32[]{:S(2)}) collective-permute-start(f32[384,128]{1,0:T(8,128)S(1)} %collective-permute-done.near_ref), channel_id=1, source_target_pairs={{0,16},{16,0},{1,17},{17,1},{2,18},{18,2},{3,19},{19,3},{4,20},{20... | collective-permute-start | bytes 589832 | tf_op jit(solution)/shard_map/ppermute | solution.py:283
  66.1 12.1 %collective-permute-start.5 = (f32[256,128]{1,0:T(8,128)S(1)}, f32[256,128]{1,0:T(8,128)S(1)}, u32[]{:S(2)}, u32[]{:S(2)}) collective-permute-start(f32[256,128]{1,0:T(8,128)S(1)} %collective-permute-done.2.near_side), channel_id=1, source_target_pairs={{0,16},{16,0},{1,17},{17,1},{2,18},{18,2},{3,19},{19,3},{4,20},{20... | collective-permute-start | bytes 393224 | tf_op jit(solution)/shard_map/ppermute | solution.py:283
  74.9 27.7 %collective-permute-start.8 = (f32[128,512]{1,0:T(8,128)S(1)}, f32[128,512]{1,0:T(8,128)S(1)}, u32[]{:S(2)}, u32[]{:S(2)}) collective-permute-start(f32[128,512]{1,0:T(8,128)S(1)} %copy-done.3), channel_id=1, source_target_pairs={{0,8},{1,9},{2,10},{3,11},{4,12},{5,13},{6,14},{7,15},{8,0},{9,1},... | collective-permute-start | bytes 786440 | tf_op jit(solution)/shard_map/ppermute | solution.py:279
  90.3 15.2 %copy-start.1 = (f32[1,256,512]{2,1,0:T(8,128)S(1)}, f32[1,256,512]{2,1,0:T(8,128)}, u32[]{:S(2)}) copy-start(f32[1,256,512]{2,1,0:T(8,128)} %param.4) | copy-start | bytes 1572868
  90.3 13.4 %collective-permute-start.9 = (f32[128,512]{1,0:T(8,128)S(1)}, f32[128,512]{1,0:T(8,128)S(1)}, u32[]{:S(2)}, u32[]{:S(2)}) collective-permute-start(f32[128,512]{1,0:T(8,128)S(1)} %collective-permute-done.7.refs_0_), channel_id=1, source_target_pairs={{0,16},{16,0},{1,17},{17,1},{2,18},{18,2},{3,19},{19,3},{4,20},{20... | collective-permute-start | bytes 786440 | tf_op jit(solution)/shard_map/ppermute | solution.py:283
  103.7 8.8 %collective-permute-start.10 = (f32[128,512]{1,0:T(8,128)S(1)}, f32[128,512]{1,0:T(8,128)S(1)}, u32[]{:S(2)}, u32[]{:S(2)}) collective-permute-start(f32[128,512]{1,0:T(8,128)S(1)} %collective-permute-done.8.refs_1_), channel_id=1, source_target_pairs={{0,16},{16,0},{1,17},{17,1},{2,18},{18,2},{3,19},{19,3},{4,20},{20... | collective-permute-start | bytes 786440 | tf_op jit(solution)/shard_map/ppermute | solution.py:283

commit v2 on v1

--- a/solution.py
+++ b/solution.py
@@ -246,7 +246,7 @@
 
 
 def pack_body(half, t_ref, first_ref, diag_ref, side_ref, outer_ref, *rest):
-    *chunks, sems = rest
+    chunks = rest
     q = half // 2
     width = outer_ref.shape[1]
     mine = first_ref[0]
@@ -267,11 +267,8 @@
     for chunk in chunks:
         moves.append((t_ref.at[at : at + chunk.shape[0], 0:width], chunk))
         at += chunk.shape[0]
-    copies = [pltpu.make_async_copy(x, y, sems.at[i]) for i, (x, y) in enumerate(moves)]
-    for copy in copies:
-        copy.start()
-    for copy in copies:
-        copy.wait()
+    for source, target in moves:
+        target[...] = source[...]
 
 
 def sibling(x):
@@ -297,13 +294,7 @@
     f = lambda *shape: jax.ShapeDtypeStruct(shape, F32)
     q = half // 2
     outs = [f(3 * q, q), f(2 * q, q), f(half, width)] + [f(rows, width) for rows in chunk_rows]
-    return pl.pallas_call(
-        functools.partial(pack_body, half),
-        out_shape=outs,
-        in_specs=[pl.BlockSpec(memory_space=pl.ANY), pl.BlockSpec(memory_space=pltpu.SMEM)],
-        out_specs=[pl.BlockSpec(memory_space=pl.ANY)] * len(outs),
-        scratch_shapes=[pltpu.SemaphoreType.DMA((6 + len(chunk_rows),))],
-    )(t_int, first)
+    return kernel(functools.partial(pack_body, half), outs, [pltpu.VMEM, pltpu.SMEM])(t_int, first)
 
 
 def two_shards(t_int, t_ext, iface_map):
@@ -321,7 +312,9 @@
     far = across(near_held)
     side_held, outer_other = lax.optimization_barrier((near_side, outer_other))
     far_side = across(side_held)
-    chunk_a, chunk_b, _, _ = lax.optimization_barrier((chunk_a, chunk_b, near_held, near_side))
+    chunk_a, chunk_b, _, _, other_map = lax.optimization_barrier(
+        (chunk_a, chunk_b, near_held, near_side, other_map)
+    )
     near_a, near_b = sibling(chunk_a), sibling(chunk_b)
     rolled = lambda m: lax.dynamic_slice(jnp.concatenate([m, m], axis=1), (0, mine * half), (1, n))
     own_row, other_row = rolled(iface_map), rolled(other_map)

time: 114 us -> 63.1 us (0.55)
  the two profiles are of different devices: /device:TPU:8 before, /device:TPU:0 now
where the time goes in v2:
time: 63.1 us; the launch traced here: 62.9 us
  Pallas kernels  26.6 us (42%)
  starting transfers between devices  17.2 us (27%)
  waiting for transfers between devices  16 us (25%)
  local copies, waits for them, and re-layouts  2.32 us (4%)
  between operations  0.73 us (1%)
    pallas_call x1, Pallas kernels, two_shards(): kernel(functools.partial(first_body, half, range(tiles // 2)), (f(n, n),...  12 us
    ppermute x5, waiting for transfers between devices, sibling(): return lax.ppermute(x, 'leaf', [(i, i ^ size // 2) for i in range(size)])  10.5 us
    ppermute x6, starting transfers between devices, across(): return lax.ppermute(x, 'sib', [(0, 1), (1, 0)])  8.91 us
    ppermute x5, starting transfers between devices, sibling(): return lax.ppermute(x, 'leaf', [(i, i ^ size // 2) for i in range(size)])  8.27 us
    pallas_call x1, Pallas kernels, two_shards(): kernel(functools.partial(last_body, half, range(tiles - 1, tiles)), (f(ha...  7.01 us
    ppermute x6, waiting for transfers between devices, across(): return lax.ppermute(x, 'sib', [(0, 1), (1, 0)])  5.52 us
    pallas_call x1, Pallas kernels, two_shards(): kernel(functools.partial(middle_body, range(tiles // 2, tiles - 1)), (f(n...  5.03 us
    unnamed x12, local copies, waits for them, and re-layouts  2.17 us
  transfers between devices with their start and end apart: 11, of which 5 were waited for; matrix products, arithmetic and copies ran while one was open for 0% of the time, Pallas kernels for 38%

profile of v2, /device:TPU:0, one launch (start us, length us, event | category | flops | bytes accessed | tf_op | source)
XLA Modules:
  0.0 62.9 jit_solution(11290463830863926142)
XLA Ops:
  0.6 1.2 %copy-done = f32[1,256,1024]{2,1,0:T(8,128)S(1)} copy-done((f32[1,256,1024]{2,1,0:T(8,128)S(1)}, f32[1,256,1024]{2,1,0:T(8,128)}, u32[]{:S(2)}) %copy-start) | copy-done | bytes 1048600
  1.9 0.8 %shard_map.58 = (f32[384,128]{1,0:T(8,128)S(1)}, f32[256,128]{1,0:T(8,128)S(1)}, f32[256,512]{1,0:T(8,128)S(1)}, f32[128,512]{1,0:T(8,128)}, f32[128,512]{1,0:T(8,128)S(1)}) custom-call(f32[256,1024]{1,0:T(8,128)S(1)} %bitcast.8, s32[1]{0:T(128)} %bitcast.1.first_ref), custom_call_target="tpu_custom_call" | custom-call | tf_op jit(solution)/shard_map/pallas_call | solution.py:297
  2.7 0.7 %copy-done.3 = f32[128,512]{1,0:T(8,128)} copy-done((f32[128,512]{1,0:T(8,128)}, f32[128,512]{1,0:T(8,128)S(1)}, u32[]{:S(2)}) %copy-start.3) | copy-done | bytes 262168
  3.4 2.9 %collective-permute-start.4 = (f32[256,512]{1,0:T(8,128)S(1)}, f32[256,512]{1,0:T(8,128)S(1)}, u32[]{:S(2)}, u32[]{:S(2)}) collective-permute-start(f32[256,512]{1,0:T(8,128)S(1)} %get-tuple-element.34), channel_id=1, source_target_pairs={{0,16},{16,0},{1,17},{17,1},{2,18},{18,2},{3,19},{19,3},{4,20},{20... | collective-permute-start | bytes 1572872 | tf_op jit(solution)/shard_map/ppermute | solution.py:280
  6.3 2.6 %collective-permute-start = (f32[384,128]{1,0:T(8,128)S(1)}, f32[384,128]{1,0:T(8,128)S(1)}, u32[]{:S(2)}, u32[]{:S(2)}) collective-permute-start(f32[384,128]{1,0:T(8,128)S(1)} %get-tuple-element.30), channel_id=1, source_target_pairs={{0,8},{1,9},{2,10},{3,11},{4,12},{5,13},{6,14},{7,15},{8,0},{9,1},... | collective-permute-start | bytes 589832 | tf_op jit(solution)/shard_map/ppermute | solution.py:276
  8.9 0.5 collective-permute-start.1
  9.4 2.9 %collective-permute-start.6 = (s32[1,512]{1,0:T(1,128)S(1)}, s32[1,512]{1,0:T(1,128)S(1)}, u32[]{:S(2)}, u32[]{:S(2)}) collective-permute-start(s32[1,512]{1,0:T(1,128)S(1)} %copy-done.5), channel_id=1, source_target_pairs={{0,8},{1,9},{2,10},{3,11},{4,12},{5,13},{6,14},{7,15},{8,0},{9,1},... | collective-permute-start | bytes 6152 | tf_op jit(solution)/shard_map/ppermute | solution.py:276
  12.4 9.4 %collective-permute-done.near_ref = f32[384,128]{1,0:T(8,128)S(1)} collective-permute-done((f32[384,128]{1,0:T(8,128)S(1)}, f32[384,128]{1,0:T(8,128)S(1)}, u32[]{:S(2)}, u32[]{:S(2)}) %collective-permute-start) | collective-permute-done | bytes 196640 | tf_op jit(solution)/shard_map/ppermute | solution.py:276
  21.8 0.6 %collective-permute-done.1.diag_ref = f32[384,128]{1,0:T(8,128)S(1)} collective-permute-done((f32[384,128]{1,0:T(8,128)S(1)}, f32[384,128]{1,0:T(8,128)S(1)}, u32[]{:S(2)}, u32[]{:S(2)}) %collective-permute-start.1) | collective-permute-done | bytes 196640 | tf_op jit(solution)/shard_map/ppermute | solution.py:280
  22.4 1.0 %collective-permute-done.6 = s32[1,512]{1,0:T(1,128)S(1)} collective-permute-done((s32[1,512]{1,0:T(1,128)S(1)}, s32[1,512]{1,0:T(1,128)S(1)}, u32[]{:S(2)}, u32[]{:S(2)}) %collective-permute-start.6) | collective-permute-done | bytes 2080 | tf_op jit(solution)/shard_map/ppermute | solution.py:276
  23.5 1.8 %collective-permute-start.7 = (f32[128,512]{1,0:T(8,128)}, f32[128,512]{1,0:T(8,128)S(1)}, u32[]{:S(2)}, u32[]{:S(2)}) collective-permute-start(f32[128,512]{1,0:T(8,128)} %get-tuple-element.42), channel_id=1, source_target_pairs={{0,8},{1,9},{2,10},{3,11},{4,12},{5,13},{6,14},{7,15},{8,0},{9,1},... | collective-permute-start | bytes 786440 | tf_op jit(solution)/shard_map/ppermute | solution.py:276
  25.3 1.5 %collective-permute-start.3 = (f32[384,128]{1,0:T(8,128)S(1)}, f32[384,128]{1,0:T(8,128)S(1)}, u32[]{:S(2)}, u32[]{:S(2)}) collective-permute-start(f32[384,128]{1,0:T(8,128)S(1)} %collective-permute-done.near_ref), channel_id=1, source_target_pairs={{0,16},{16,0},{1,17},{17,1},{2,18},{18,2},{3,19},{19,3},{4,20},{20... | collective-permute-start | bytes 589832 | tf_op jit(solution)/shard_map/ppermute | solution.py:280
  26.8 0.5 collective-permute-start.5
  27.3 0.1 copy.6.column_ref
  27.5 0.2 copy-done.4
  27.7 1.0 %collective-permute-start.8 = (f32[128,512]{1,0:T(8,128)S(1)}, f32[128,512]{1,0:T(8,128)S(1)}, u32[]{:S(2)}, u32[]{:S(2)}) collective-permute-start(f32[128,512]{1,0:T(8,128)S(1)} %copy-done.4), channel_id=1, source_target_pairs={{0,8},{1,9},{2,10},{3,11},{4,12},{5,13},{6,14},{7,15},{8,0},{9,1},... | collective-permute-start | bytes 786440 | tf_op jit(solution)/shard_map/ppermute | solution.py:276
  28.7 3.5 %collective-permute-done.3.far_ref = f32[384,128]{1,0:T(8,128)S(1)} collective-permute-done((f32[384,128]{1,0:T(8,128)S(1)}, f32[384,128]{1,0:T(8,128)S(1)}, u32[]{:S(2)}, u32[]{:S(2)}) %collective-permute-start.3) | collective-permute-done | bytes 196640 | tf_op jit(solution)/shard_map/ppermute | solution.py:280
  32.2 1.4 %collective-permute-done.5.far_side = f32[256,128]{1,0:T(8,128)S(1)} collective-permute-done((f32[256,128]{1,0:T(8,128)S(1)}, f32[256,128]{1,0:T(8,128)S(1)}, u32[]{:S(2)}, u32[]{:S(2)}) %collective-permute-start.5) | collective-permute-done | bytes 131104 | tf_op jit(solution)/shard_map/ppermute | solution.py:280
  33.6 12.0 %shard_map.59 = (f32[512,512]{1,0:T(8,128)S(1)}, f32[512,512]{1,0:T(8,128)S(1)}, bf16[512,512]{1,0:T(8,128)(2,1)S(1)}) custom-call(f32[256,1024]{1,0:T(8,128)S(1)} %bitcast.9, f32[384,128]{1,0:T(8,128)S(1)} %collective-permute-done.1.diag_ref, f32[384,128]{1,0:T(8,128)S(1)} %collective-permute-done.near_ref, ...), custom_call_target="tpu_custom_call" | custom-call | tf_op jit(solution)/shard_map/pallas_call | solution.py:324
  45.6 1.6 %collective-permute-start.9 = (f32[128,512]{1,0:T(8,128)S(1)}, f32[128,512]{1,0:T(8,128)S(1)}, u32[]{:S(2)}, u32[]{:S(2)}) collective-permute-start(f32[128,512]{1,0:T(8,128)S(1)} %collective-permute-done.7.refs_0_), channel_id=1, source_target_pairs={{0,16},{16,0},{1,17},{17,1},{2,18},{18,2},{3,19},{19,3},{4,20},{20... | collective-permute-start | bytes 786440 | tf_op jit(solution)/shard_map/ppermute | solution.py:280
  47.3 5.0 %shard_map.60 = (f32[512,512]{1,0:T(8,128)S(1)}, f32[512,512]{1,0:T(8,128)S(1)}) custom-call(f32[512,512]{1,0:T(8,128)S(1)} %get-tuple-element.43.a_in, f32[512,512]{1,0:T(8,128)S(1)} %get-tuple-element.44.g_in), custom_call_target="tpu_custom_call" | custom-call | tf_op jit(solution)/shard_map/pallas_call | solution.py:332
  52.3 1.8 %collective-permute-start.10 = (f32[128,512]{1,0:T(8,128)S(1)}, f32[128,512]{1,0:T(8,128)S(1)}, u32[]{:S(2)}, u32[]{:S(2)}) collective-permute-start(f32[128,512]{1,0:T(8,128)S(1)} %collective-permute-done.8.refs_1_), channel_id=1, source_target_pairs={{0,16},{16,0},{1,17},{17,1},{2,18},{18,2},{3,19},{19,3},{4,20},{20... | collective-permute-start | bytes 786440 | tf_op jit(solution)/shard_map/ppermute | solution.py:280
  54.1 7.0 %shard_map.61 = (f32[256,512]{1,0:T(8,128)}, f32[256,512]{1,0:T(8,128)}, f32[512,256]{1,0:T(8,128)S(1)}) custom-call(f32[512,512]{1,0:T(8,128)S(1)} %get-tuple-element.49.a_ref, f32[512,512]{1,0:T(8,128)S(1)} %get-tuple-element.50.g_in, bf16[512,512]{1,0:T(8,128)(2,1)S(1)} %get-tuple-element.51.p_ref, f32[256,1024]{1,0:T(8,128)S(1)} %bitcast.10, ...), custom_call_target="tpu_custom_call" | custom-call | tf_op jit(solution)/shard_map/pallas_call | solution.py:337
  61.1 1.8 %shard_map.62 = f32[256,512]{1,0:T(8,128)} custom-call(f32[512,256]{1,0:T(8,128)S(1)} %get-tuple-element.53.h_ref, f32[128,512]{1,0:T(8,128)S(1)} %collective-permute-done.7.refs_0_, f32[128,512]{1,0:T(8,128)S(1)} %collective-permute-done.8.refs_1_, f32[128,512]{1,0:T(8,128)S(1)} %collective-permute-done.9.refs_2_, ...), custom_call_target="tpu_custom_call" | custom-call | tf_op jit(solution)/shard_map/pallas_call | solution.py:343
  (19 shorter events, 0.1 us)
Async XLA Ops:
  0.6 1.2 %copy-start = (f32[1,256,1024]{2,1,0:T(8,128)S(1)}, f32[1,256,1024]{2,1,0:T(8,128)}, u32[]{:S(2)}) copy-start(f32[1,256,1024]{2,1,0:T(8,128)} %param.3) | copy-start | bytes 3145732
  1.9 31.7 %copy-start.1 = (f32[1,256,1024]{2,1,0:T(8,128)S(1)}, f32[1,256,1024]{2,1,0:T(8,128)}, u32[]{:S(2)}) copy-start(f32[1,256,1024]{2,1,0:T(8,128)} %param.3) | copy-start | bytes 3145732
  2.7 0.7 %copy-start.3 = (f32[128,512]{1,0:T(8,128)}, f32[128,512]{1,0:T(8,128)S(1)}, u32[]{:S(2)}) copy-start(f32[128,512]{1,0:T(8,128)S(1)} %get-tuple-element.47) | copy-start | bytes 786436
  3.4 6.1 %copy-start.5 = (s32[1,512]{1,0:T(1,128)S(1)}, s32[1,512]{1,0:T(1,128)}, u32[]{:S(2)}) copy-start(s32[1,512]{1,0:T(1,128)} %param.5) | copy-start | bytes 6148
  3.4 23.4 %collective-permute-start.4 = (f32[256,512]{1,0:T(8,128)S(1)}, f32[256,512]{1,0:T(8,128)S(1)}, u32[]{:S(2)}, u32[]{:S(2)}) collective-permute-start(f32[256,512]{1,0:T(8,128)S(1)} %get-tuple-element.34), channel_id=1, source_target_pairs={{0,16},{16,0},{1,17},{17,1},{2,18},{18,2},{3,19},{19,3},{4,20},{20... | collective-permute-start | bytes 1572872 | tf_op jit(solution)/shard_map/ppermute | solution.py:280
  6.3 15.5 %collective-permute-start = (f32[384,128]{1,0:T(8,128)S(1)}, f32[384,128]{1,0:T(8,128)S(1)}, u32[]{:S(2)}, u32[]{:S(2)}) collective-permute-start(f32[384,128]{1,0:T(8,128)S(1)} %get-tuple-element.30), channel_id=1, source_target_pairs={{0,8},{1,9},{2,10},{3,11},{4,12},{5,13},{6,14},{7,15},{8,0},{9,1},... | collective-permute-start | bytes 589832 | tf_op jit(solution)/shard_map/ppermute | solution.py:276
  8.9 13.5 %collective-permute-start.1 = (f32[384,128]{1,0:T(8,128)S(1)}, f32[384,128]{1,0:T(8,128)S(1)}, u32[]{:S(2)}, u32[]{:S(2)}) collective-permute-start(f32[384,128]{1,0:T(8,128)S(1)} %get-tuple-element.30), channel_id=1, source_target_pairs={{0,16},{16,0},{1,17},{17,1},{2,18},{18,2},{3,19},{19,3},{4,20},{20... | collective-permute-start | bytes 589832 | tf_op jit(solution)/shard_map/ppermute | solution.py:280
  9.4 14.1 %collective-permute-start.2 = (f32[256,128]{1,0:T(8,128)S(1)}, f32[256,128]{1,0:T(8,128)S(1)}, u32[]{:S(2)}, u32[]{:S(2)}) collective-permute-start(f32[256,128]{1,0:T(8,128)S(1)} %get-tuple-element.32), channel_id=1, source_target_pairs={{0,8},{1,9},{2,10},{3,11},{4,12},{5,13},{6,14},{7,15},{8,0},{9,1},... | collective-permute-start | bytes 393224 | tf_op jit(solution)/shard_map/ppermute | solution.py:276
  9.4 14.0 %collective-permute-start.6 = (s32[1,512]{1,0:T(1,128)S(1)}, s32[1,512]{1,0:T(1,128)S(1)}, u32[]{:S(2)}, u32[]{:S(2)}) collective-permute-start(s32[1,512]{1,0:T(1,128)S(1)} %copy-done.5), channel_id=1, source_target_pairs={{0,8},{1,9},{2,10},{3,11},{4,12},{5,13},{6,14},{7,15},{8,0},{9,1},... | collective-permute-start | bytes 6152 | tf_op jit(solution)/shard_map/ppermute | solution.py:276
  23.5 22.1 %collective-permute-start.7 = (f32[128,512]{1,0:T(8,128)}, f32[128,512]{1,0:T(8,128)S(1)}, u32[]{:S(2)}, u32[]{:S(2)}) collective-permute-start(f32[128,512]{1,0:T(8,128)} %get-tuple-element.42), channel_id=1, source_target_pairs={{0,8},{1,9},{2,10},{3,11},{4,12},{5,13},{6,14},{7,15},{8,0},{9,1},... | collective-permute-start | bytes 786440 | tf_op jit(solution)/shard_map/ppermute | solution.py:276
  25.3 6.9 %collective-permute-start.3 = (f32[384,128]{1,0:T(8,128)S(1)}, f32[384,128]{1,0:T(8,128)S(1)}, u32[]{:S(2)}, u32[]{:S(2)}) collective-permute-start(f32[384,128]{1,0:T(8,128)S(1)} %collective-permute-done.near_ref), channel_id=1, source_target_pairs={{0,16},{16,0},{1,17},{17,1},{2,18},{18,2},{3,19},{19,3},{4,20},{20... | collective-permute-start | bytes 589832 | tf_op jit(solution)/shard_map/ppermute | solution.py:280
  26.8 1.0 %copy-start.4 = (f32[128,512]{1,0:T(8,128)S(1)}, f32[128,512]{1,0:T(8,128)}, u32[]{:S(2)}) copy-start(f32[128,512]{1,0:T(8,128)} %copy-done.3) | copy-start | bytes 786436
  26.8 6.8 %collective-permute-start.5 = (f32[256,128]{1,0:T(8,128)S(1)}, f32[256,128]{1,0:T(8,128)S(1)}, u32[]{:S(2)}, u32[]{:S(2)}) collective-permute-start(f32[256,128]{1,0:T(8,128)S(1)} %collective-permute-done.2.near_side), channel_id=1, source_target_pairs={{0,16},{16,0},{1,17},{17,1},{2,18},{18,2},{3,19},{19,3},{4,20},{20... | collective-permute-start | bytes 393224 | tf_op jit(solution)/shard_map/ppermute | solution.py:280
  27.7 24.6 %collective-permute-start.8 = (f32[128,512]{1,0:T(8,128)S(1)}, f32[128,512]{1,0:T(8,128)S(1)}, u32[]{:S(2)}, u32[]{:S(2)}) collective-permute-start(f32[128,512]{1,0:T(8,128)S(1)} %copy-done.4), channel_id=1, source_target_pairs={{0,8},{1,9},{2,10},{3,11},{4,12},{5,13},{6,14},{7,15},{8,0},{9,1},... | collective-permute-start | bytes 786440 | tf_op jit(solution)/shard_map/ppermute | solution.py:276
  45.6 8.5 %copy-start.2 = (f32[1,256,512]{2,1,0:T(8,128)S(1)}, f32[1,256,512]{2,1,0:T(8,128)}, u32[]{:S(2)}) copy-start(f32[1,256,512]{2,1,0:T(8,128)} %param.4) | copy-start | bytes 1572868
  45.6 6.7 %collective-permute-start.9 = (f32[128,512]{1,0:T(8,128)S(1)}, f32[128,512]{1,0:T(8,128)S(1)}, u32[]{:S(2)}, u32[]{:S(2)}) collective-permute-start(f32[128,512]{1,0:T(8,128)S(1)} %collective-permute-done.7.refs_0_), channel_id=1, source_target_pairs={{0,16},{16,0},{1,17},{17,1},{2,18},{18,2},{3,19},{19,3},{4,20},{20... | collective-permute-start | bytes 786440 | tf_op jit(solution)/shard_map/ppermute | solution.py:280
  52.3 8.8 %collective-permute-start.10 = (f32[128,512]{1,0:T(8,128)S(1)}, f32[128,512]{1,0:T(8,128)S(1)}, u32[]{:S(2)}, u32[]{:S(2)}) collective-permute-start(f32[128,512]{1,0:T(8,128)S(1)} %collective-permute-done.8.refs_1_), channel_id=1, source_target_pairs={{0,16},{16,0},{1,17},{17,1},{2,18},{18,2},{3,19},{19,3},{4,20},{20... | collective-permute-start | bytes 786440 | tf_op jit(solution)/shard_map/ppermute | solution.py:280

commit v3 on v2

--- a/solution.py
+++ b/solution.py
@@ -54,44 +54,46 @@
     return jnp.broadcast_to(x[row : row + 1, :], (8, TILE))
 
 
-def reciprocal(d):
-    r = pltpu.reciprocal(d, approx=True)
-    return r * (2.0 - d * r)
-
-
 def invert_tile(work, slabs=2):
     width = 8 * slabs
     lane = lax.broadcasted_iota(jnp.int32, (8, TILE), 1)
     row = lax.broadcasted_iota(jnp.int32, (8, TILE), 0)
     lane_all = lax.broadcasted_iota(jnp.int32, (TILE, TILE), 1)
     is_row = [row == j for j in range(8)]
+
+    def slab_list(x, base):
+        return [x[base + 8 * s : base + 8 * s + 8, :] for s in range(slabs)]
+
+    old = slab_list(work, 0)
     for base in range(0, TILE, width):
-        old = [work[base + 8 * s : base + 8 * s + 8, :] for s in range(slabs)]
-        columns = [[over_lanes(old[s], base + m) for s in range(slabs)] for m in range(width)]
-        inside = (lane >= base) & (lane < base + width)
+        after = base + width
+        columns = [[over_lanes(x, base + m) for x in old] for m in range(width)]
+        following = slab_list(work, after) if after < TILE else []
+        factors = [[over_lanes(x, base + m) for x in following] for m in range(width)]
+        inside = (lane >= base) & (lane < after)
         new = [
             jnp.where(inside, jnp.where(lane - base - 8 * s == row, 1.0, 0.0).astype(F32), old[s])
             for s in range(slabs)
         ]
         pivot = over_rows(columns[0][0], 0)
+        scale = [None] * slabs
         for j in range(width):
             js, jr = divmod(j, 8)
-            inverse = reciprocal(pivot)
-            here = columns[j]
+            inverse = pltpu.reciprocal(pivot, approx=True)
+            scale[js] = inverse if jr == 0 else jnp.where(is_row[jr], inverse, scale[js])
+            here = list(columns[j])
+            here[js] = jnp.where(is_row[jr], 0.0, here[js])
             scaled = [c * inverse for c in here]
             for m in range(j + 1, width):
                 picked = over_rows(columns[m][js], jr)
                 if m == j + 1:
-                    later = [columns[m][s] - (here[s] * picked) * inverse for s in range(slabs)]
-                    pivot = over_rows(later[m // 8], m % 8)
+                    columns[m] = [c - (h * picked) * inverse for c, h in zip(columns[m], here)]
+                    pivot = over_rows(columns[m][m // 8], m % 8)
                 else:
-                    later = [columns[m][s] - scaled[s] * picked for s in range(slabs)]
-                later[js] = jnp.where(is_row[jr], picked * inverse, later[js])
-                columns[m] = later
+                    columns[m] = [c - h * picked for c, h in zip(columns[m], scaled)]
             picked = over_rows(new[js], jr)
-            later = [new[s] - scaled[s] * picked for s in range(slabs)]
-            later[js] = jnp.where(is_row[jr], picked * inverse, later[js])
-            new = later
+            new = [x - h * picked for x, h in zip(new, scaled)]
+        new = [x * y for x, y in zip(new, scale)]
         panel = jnp.concatenate(new, axis=0)
         sign = jnp.where(lane < base, -1.0, jnp.where(inside, 0.0, 1.0)).astype(F32)
         ah, am, al = split3(jnp.concatenate([x * sign for x in old], axis=0))
@@ -99,16 +101,25 @@
         left = jnp.concatenate([ah, ah, am, am, ah, al], axis=0).astype(BF16)
         right = jnp.concatenate([bh, bm, bh, bm, bl, bh], axis=0).astype(BF16)
         change = contract(left, right, ((0,), (0,)))
-        inside_all = (lane_all >= base) & (lane_all < base + width)
+        inside_all = (lane_all >= base) & (lane_all < after)
         rest = jnp.where(inside_all, 0.0, work) - change
-        work = jnp.concatenate(
-            [x for x in (rest[:base], panel, rest[base + width :]) if x.shape[0]], axis=0
-        )
+        parts = [rest[:base], panel, rest[after:]]
+        if following:
+            rows = [over_rows(new[m // 8], m % 8) for m in range(width)]
+            old = []
+            for s in range(slabs):
+                sums = []
+                for q in range(4):
+                    terms = [factors[m][s] * rows[m] for m in range(q, width, 4)]
+                    sums.append(functools.reduce(lambda x, y: x + y, terms))
+                old.append(jnp.where(inside, 0.0, following[s]) - ((sums[0] + sums[1]) + (sums[2] + sums[3])))
+            parts = [rest[:base], panel, *old, rest[after + width :]]
+        work = jnp.concatenate([x for x in parts if x.shape[0]], axis=0)
     return work
 
 
 def eliminate(a_ref, g_ref, steps):
-    size = a_ref.shape[0]
+    size, rows_of_g = a_ref.shape[0], g_ref.shape[0]
     for k in steps:
         at, after = k * TILE, (k + 1) * TILE
         own = slice(at, after)
@@ -125,7 +136,8 @@
             a_ref[rows, i * TILE :] = a_ref[rows, i * TILE :] - full(
                 factor, panel[:, (i - k - 1) * TILE :], ((0,), (0,))
             )
-            g_ref[rows, :] = g_ref[rows, :] - full(factor, right, ((0,), (0,)))
+            if (i + 1) * TILE <= rows_of_g:
+                g_ref[rows, :] = g_ref[rows, :] - full(factor, right, ((0,), (0,)))
         for i in range(k):
             rows = slice(i * TILE, (i + 1) * TILE)
             factor = a_ref[rows, own]
@@ -157,7 +169,7 @@
 
 
 def first_body(
-    half, steps, t_ref, diag_ref, near_ref, near_side, far_ref, far_side, other_ref, column_ref, row_ref, first_ref, a_out, g_out, p_out, m_work
+    half, steps, t_ref, diag_ref, near_ref, near_side, far_ref, far_side, column_ref, row_ref, first_ref, a_out, b_out, p_out, m_work
 ):
     n = 2 * half
     q = half // 2
@@ -206,14 +218,20 @@
     for i in range(n // TILE):
         rows, later = slice(i * TILE, (i + 1) * TILE), slice(i * TILE, n)
         a_out[rows, later] = a_out[rows, later] + pick_left(onehot[rows, :], moved[:, later], ((1,), (0,)))
-    g_out[0:half, :] = t_ref[:, 0:width]
-    g_out[half:n, :] = other_ref[...]
-    eliminate(a_out, g_out, steps)
-
-
-def middle_body(steps, a_in, g_in, a_out, g_out):
+    top = b_out.shape[0]
+    on_diagonal = [lax.broadcasted_iota(jnp.int32, (top, top), axis) for axis in (0, 1)]
+    b_out[...] = jnp.where(on_diagonal[0] == on_diagonal[1], 1.0, 0.0).astype(F32)
+    eliminate(a_out, b_out, steps)
+
+
+def middle_body(steps, a_in, b_ref, upper_ref, lower_ref, a_out, g_out):
+    top, half = b_ref.shape[0], upper_ref.shape[0]
     a_out[...] = a_in[...]
-    g_out[...] = g_in[...]
+    g_out[0:half, :] = upper_ref[...]
+    g_out[half:, :] = lower_ref[...]
+    first = g_out[0:top, :]
+    g_out[top:, :] = g_out[top:, :] - full(a_in[0:top, top:], first, ((0,), (0,)))
+    g_out[0:top, :] = full(b_ref[...], first)
     eliminate(a_out, g_out, steps)
 
 
@@ -245,30 +263,28 @@
     out_ref[...] = -total
 
 
-def pack_body(half, t_ref, first_ref, diag_ref, side_ref, outer_ref, *rest):
-    chunks = rest
+def pack_iface_body(half, width, t_ref, first_ref, diag_ref, side_ref):
     q = half // 2
-    width = outer_ref.shape[1]
     mine = first_ref[0]
     here, there = width + mine * half, width + (1 - mine) * half
 
     def cut(row, column):
-        return t_ref.at[pl.ds(pl.multiple_of(row, q), q), pl.ds(pl.multiple_of(column, q), q)]
-
-    moves = [
-        (cut(0, here), diag_ref.at[0:q, :]),
-        (cut(0, here + q), diag_ref.at[q : 2 * q, :]),
-        (cut(q, here + q), diag_ref.at[2 * q : 3 * q, :]),
-        (cut(0, there + q), side_ref.at[0:q, :]),
-        (cut(mine * q, there + mine * q), side_ref.at[q : 2 * q, :]),
-        (t_ref.at[:, 0:width], outer_ref),
-    ]
+        return t_ref[pl.ds(pl.multiple_of(row, q), q), pl.ds(pl.multiple_of(column, q), q)]
+
+    diag_ref[0:q, :] = cut(0, here)
+    diag_ref[q : 2 * q, :] = cut(0, here + q)
+    diag_ref[2 * q : 3 * q, :] = cut(q, here + q)
+    side_ref[0:q, :] = cut(0, there + q)
+    side_ref[q : 2 * q, :] = cut(mine * q, there + mine * q)
+
+
+def pack_outer_body(t_ref, outer_ref, *chunks):
+    width = outer_ref.shape[1]
+    outer_ref[...] = t_ref[:, 0:width]
     at = 0
     for chunk in chunks:
-        moves.append((t_ref.at[at : at + chunk.shape[0], 0:width], chunk))
+        chunk[...] = t_ref[at : at + chunk.shape[0], 0:width]
         at += chunk.shape[0]
-    for source, target in moves:
-        target[...] = source[...]
 
 
 def sibling(x):
@@ -280,21 +296,15 @@
     return lax.ppermute(x, "sib", [(0, 1), (1, 0)])
 
 
-def kernel(body, outs, places, scratch=()):
+def kernel(body, outs, places, scratch=(), flops=1e8):
     return pl.pallas_call(
         body,
         out_shape=outs,
         in_specs=[pl.BlockSpec(memory_space=place) for place in places],
         scratch_shapes=list(scratch),
         compiler_params=pltpu.CompilerParams(vmem_limit_bytes=VMEM_LIMIT),
+        cost_estimate=pl.CostEstimate(flops=int(flops), bytes_accessed=1 << 20, transcendentals=0),
     )
-
-
-def pack(t_int, first, half, width, chunk_rows):
-    f = lambda *shape: jax.ShapeDtypeStruct(shape, F32)
-    q = half // 2
-    outs = [f(3 * q, q), f(2 * q, q), f(half, width)] + [f(rows, width) for rows in chunk_rows]
-    return kernel(functools.partial(pack_body, half), outs, [pltpu.VMEM, pltpu.SMEM])(t_int, first)
 
 
 def two_shards(t_int, t_ext, iface_map):
@@ -302,36 +312,41 @@
     half, n = t_int.shape[0], iface_map.shape[1]
     width = t_int.shape[1] - n
     tiles = n // TILE
+    q = half // 2
+    f = lambda *shape: jax.ShapeDtypeStruct(shape, F32)
+    vmem, smem = pltpu.VMEM, pltpu.SMEM
     mine = lax.axis_index("sib").astype(jnp.int32)
     first = mine.reshape(1)
-    diag, side, outer, chunk_a, chunk_b = pack(t_int, first, half, width, (half // 2, half // 2))
+    diag, side = kernel(
+        functools.partial(pack_iface_body, half, width), (f(3 * q, q), f(2 * q, q)), [vmem, smem]
+    )(t_int, first)
     near, near_side = sibling(diag), sibling(side)
     other_map = sibling(iface_map)
-    diag_other, outer_other = across(diag), across(outer)
-    near_held, diag_other = lax.optimization_barrier((near, diag_other))
-    far = across(near_held)
-    side_held, outer_other = lax.optimization_barrier((near_side, outer_other))
-    far_side = across(side_held)
-    chunk_a, chunk_b, _, _, other_map = lax.optimization_barrier(
-        (chunk_a, chunk_b, near_held, near_side, other_map)
-    )
+    diag_other = across(diag)
+    far = across(near)
+    near_side, near = lax.optimization_barrier((near_side, near))
+    far_side = across(near_side)
+    outer, chunk_a, chunk_b = kernel(pack_outer_body, (f(half, width), f(q, width), f(q, width)), [vmem])(t_int)
+    outer_late, _ = lax.optimization_barrier((outer, far))
+    outer_other = across(outer_late)
+    chunk_a, chunk_b, _, _, other_map = lax.optimization_barrier((chunk_a, chunk_b, near, near_side, other_map))
     near_a, near_b = sibling(chunk_a), sibling(chunk_b)
     rolled = lambda m: lax.dynamic_slice(jnp.concatenate([m, m], axis=1), (0, mine * half), (1, n))
     own_row, other_row = rolled(iface_map), rolled(other_map)
 
-    f = lambda *shape: jax.ShapeDtypeStruct(shape, F32)
-    vmem, smem = pltpu.VMEM, pltpu.SMEM
-    a, g, onehot = kernel(
+    top = tiles // 2 * TILE
+    a, b, onehot = kernel(
         functools.partial(first_body, half, range(tiles // 2)),
-        (f(n, n), f(n, width), jax.ShapeDtypeStruct((n, n), BF16)),
-        [vmem] * 9 + [smem],
+        (f(n, n), f(top, top), jax.ShapeDtypeStruct((n, n), BF16)),
+        [vmem] * 8 + [smem],
         [pltpu.VMEM((n, n), F32)],
-    )(t_int, diag_other, near, near_side, far, far_side, outer_other, own_row.reshape(n, 1), other_row, first)
-    a, g, near_a = lax.optimization_barrier((a, g, near_a))
+        10e9,
+    )(t_int, diag_other, near, near_side, far, far_side, own_row.reshape(n, 1), other_row, first)
+    a, b, near_a = lax.optimization_barrier((a, b, near_a))
     far_a = across(near_a)
     a, g = kernel(
-        functools.partial(middle_body, range(tiles // 2, tiles - 1)), (f(n, n), f(n, width)), [vmem] * 2
-    )(a, g)
+        functools.partial(middle_body, range(tiles // 2, tiles - 1)), (f(n, n), f(n, width)), [vmem] * 4, (), 5e9
+    )(a, b, outer, outer_other)
     a, g, near_b, far_a = lax.optimization_barrier((a, g, near_b, far_a))
     far_b = across(near_b)
     own_map, solution_op, h = kernel(
@@ -339,6 +354,7 @@
         (f(half, width), f(half, width), f(n, half)),
         [vmem] * 7 + [smem],
         [pltpu.VMEM((n, n), F32), pltpu.VMEM((n, width), F32)],
+        7e9,
     )(a, g, onehot, t_int, outer_other, t_ext, own_row, first)
     cross_map = kernel(cross_body, f(half, width), [vmem] * 5)(h, near_a, near_b, far_a, far_b)
     return own_map[None], cross_map[None], solution_op[None]

time: 63.1 us -> 62.1 us (0.984)
  Pallas kernels: 26.6 us -> 22.4 us
  waiting for transfers between devices: 16 us -> 19.1 us
  starting transfers between devices: 17.2 us -> 18.3 us
  local copies, waits for them, and re-layouts: 2.32 us -> 1.38 us
    ppermute x5, waiting for transfers between devices: 10.5 us -> 14.4 us  [sibling(): return lax.ppermute(x, 'leaf', [(i, i ^ size // 2) for i in range(size)])]
    pallas_call x1, Pallas kernels: 12 us -> 9.07 us  [two_shards(): kernel(functools.partial(first_body, half, range(tiles // 2)), (f(n, n),...]
    ppermute x5, starting transfers between devices: 8.27 us -> 9.75 us  [sibling(): return lax.ppermute(x, 'leaf', [(i, i ^ size // 2) for i in range(size)])]
    unnamed x12 -> x8, local copies, waits for them, and re-layouts: 2.17 us -> 1.23 us
    ppermute x6, waiting for transfers between devices: 5.52 us -> 4.74 us  [across(): return lax.ppermute(x, 'sib', [(0, 1), (1, 0)])]
    pallas_call x1 -> x2, Pallas kernels: 0.8 us -> 0.11 us  [the longest x1 0.07 us: two_shards(): kernel(pack_outer_body, (f(half, width), f(q, width), f(q, width)), [vmem])]
  transfers between devices with their start and end apart: 11 -> 11, of which waited for: 5 -> 4; matrix products, arithmetic and copies ran while one was open for 0% -> 0% of each run, Pallas kernels for 38% -> 33%
where the time goes in v3:
time: 62.1 us; the launch traced here: 62 us
  Pallas kernels  22.4 us (36%)
  waiting for transfers between devices  19.1 us (31%)
  starting transfers between devices  18.3 us (29%)
  local copies, waits for them, and re-layouts  1.38 us (2%)
  between operations  0.74 us (1%)
    ppermute x5, waiting for transfers between devices, sibling(): return lax.ppermute(x, 'leaf', [(i, i ^ size // 2) for i in range(size)])  14.4 us
    ppermute x5, starting transfers between devices, sibling(): return lax.ppermute(x, 'leaf', [(i, i ^ size // 2) for i in range(size)])  9.75 us
    pallas_call x1, Pallas kernels, two_shards(): kernel(functools.partial(first_body, half, range(tiles // 2)), (f(n, n),...  9.07 us
    ppermute x6, starting transfers between devices, across(): return lax.ppermute(x, 'sib', [(0, 1), (1, 0)])  8.52 us
    pallas_call x1, Pallas kernels, two_shards(): kernel(functools.partial(last_body, half, range(tiles - 1, tiles)), (f(ha...  6.42 us
    pallas_call x1, Pallas kernels, two_shards(): kernel(functools.partial(middle_body, range(tiles // 2, tiles - 1)), (f(n...  5.04 us
    ppermute x6, waiting for transfers between devices, across(): return lax.ppermute(x, 'sib', [(0, 1), (1, 0)])  4.74 us
    pallas_call x1, Pallas kernels, two_shards(): kernel(cross_body, f(half, width), [vmem] * 5)  1.8 us
  transfers between devices with their start and end apart: 11, of which 4 were waited for; matrix products, arithmetic and copies ran while one was open for 0% of the time, Pallas kernels for 33%

profile of v3, /device:TPU:0, one launch (start us, length us, event | category | flops | bytes accessed | tf_op | source)
XLA Modules:
  0.0 62.0 jit_solution(5687064815688220143)
XLA Ops:
  0.6 1.2 %copy-done = f32[1,256,1024]{2,1,0:T(8,128)S(1)} copy-done((f32[1,256,1024]{2,1,0:T(8,128)S(1)}, f32[1,256,1024]{2,1,0:T(8,128)}, u32[]{:S(2)}) %copy-start) | copy-done | bytes 1048600
  1.9 0.0 copy-start.3
  1.9 4.1 %collective-permute-start.2 = (f32[384,128]{1,0:T(8,128)S(1)}, f32[384,128]{1,0:T(8,128)S(1)}, u32[]{:S(2)}, u32[]{:S(2)}) collective-permute-start(f32[384,128]{1,0:T(8,128)S(1)} %get-tuple-element.29), channel_id=1, source_target_pairs={{0,8},{1,9},{2,10},{3,11},{4,12},{5,13},{6,14},{7,15},{8,0},{9,1},... | collective-permute-start | bytes 589832 | tf_op jit(solution)/shard_map/ppermute | solution.py:292
  6.0 0.1 collective-permute-start.1
  6.1 1.7 %collective-permute-start = (f32[384,128]{1,0:T(8,128)S(1)}, f32[384,128]{1,0:T(8,128)S(1)}, u32[]{:S(2)}, u32[]{:S(2)}) collective-permute-start(f32[384,128]{1,0:T(8,128)S(1)} %get-tuple-element.29), channel_id=1, source_target_pairs={{0,16},{16,0},{1,17},{17,1},{2,18},{18,2},{3,19},{19,3},{4,20},{20... | collective-permute-start | bytes 589832 | tf_op jit(solution)/shard_map/ppermute | solution.py:296
  7.9 2.6 %collective-permute-start.5 = (s32[1,512]{1,0:T(1,128)S(1)}, s32[1,512]{1,0:T(1,128)S(1)}, u32[]{:S(2)}, u32[]{:S(2)}) collective-permute-start(s32[1,512]{1,0:T(1,128)S(1)} %copy-done.3), channel_id=1, source_target_pairs={{0,8},{1,9},{2,10},{3,11},{4,12},{5,13},{6,14},{7,15},{8,0},{9,1},... | collective-permute-start | bytes 6152 | tf_op jit(solution)/shard_map/ppermute | solution.py:292
  10.5 10.4 %collective-permute-done.1.near_side = f32[256,128]{1,0:T(8,128)S(1)} collective-permute-done((f32[256,128]{1,0:T(8,128)S(1)}, f32[256,128]{1,0:T(8,128)S(1)}, u32[]{:S(2)}, u32[]{:S(2)}) %collective-permute-start.1) | collective-permute-done | bytes 131104 | tf_op jit(solution)/shard_map/ppermute | solution.py:292
  20.8 0.0 collective-permute-done.2.near_ref
  20.8 1.5 %collective-permute-start.4 = (f32[256,128]{1,0:T(8,128)S(1)}, f32[256,128]{1,0:T(8,128)S(1)}, u32[]{:S(2)}, u32[]{:S(2)}) collective-permute-start(f32[256,128]{1,0:T(8,128)S(1)} %collective-permute-done.1.near_side), channel_id=1, source_target_pairs={{0,16},{16,0},{1,17},{17,1},{2,18},{18,2},{3,19},{19,3},{4,20},{20... | collective-permute-start | bytes 393224 | tf_op jit(solution)/shard_map/ppermute | solution.py:296
  22.4 0.5 collective-permute-start.3
  22.9 0.1 shard_map.59
  23.0 0.1 copy.6.column_ref
  23.1 0.1 collective-permute-start.6
  23.2 2.9 %collective-permute-start.8 = (f32[128,512]{1,0:T(8,128)S(1)}, f32[128,512]{1,0:T(8,128)S(1)}, u32[]{:S(2)}, u32[]{:S(2)}) collective-permute-start(f32[128,512]{1,0:T(8,128)S(1)} %get-tuple-element.45), channel_id=1, source_target_pairs={{0,8},{1,9},{2,10},{3,11},{4,12},{5,13},{6,14},{7,15},{8,0},{9,1},... | collective-permute-start | bytes 786440 | tf_op jit(solution)/shard_map/ppermute | solution.py:292
  26.1 3.6 %collective-permute-done.3.far_ref = f32[384,128]{1,0:T(8,128)S(1)} collective-permute-done((f32[384,128]{1,0:T(8,128)S(1)}, f32[384,128]{1,0:T(8,128)S(1)}, u32[]{:S(2)}, u32[]{:S(2)}) %collective-permute-start.3) | collective-permute-done | bytes 196640 | tf_op jit(solution)/shard_map/ppermute | solution.py:296
  29.7 1.2 %collective-permute-start.7 = (f32[256,512]{1,0:T(8,128)S(1)}, f32[256,512]{1,0:T(8,128)S(1)}, u32[]{:S(2)}, u32[]{:S(2)}) collective-permute-start(f32[256,512]{1,0:T(8,128)S(1)} %get-tuple-element.42.upper_ref), channel_id=1, source_target_pairs={{0,16},{16,0},{1,17},{17,1},{2,18},{18,2},{3,19},{19,3},{4,20},{20... | collective-permute-start | bytes 1572872 | tf_op jit(solution)/shard_map/ppermute | solution.py:296
  31.0 9.1 %shard_map.60 = (f32[512,512]{1,0:T(8,128)S(1)}, f32[256,256]{1,0:T(8,128)S(1)}, bf16[512,512]{1,0:T(8,128)(2,1)S(1)}) custom-call(f32[256,1024]{1,0:T(8,128)S(1)} %bitcast.10, f32[384,128]{1,0:T(8,128)S(1)} %collective-permute-done.diag_ref, f32[384,128]{1,0:T(8,128)S(1)} %collective-permute-done.2.near_ref, ...), custom_call_target="tpu_custom_call" | custom-call | flops 10000000000 | bytes 1048576 | tf_op jit(solution)/shard_map/pallas_call | solution.py:338
  40.0 4.0 %collective-permute-done.6.refs_0_ = f32[128,512]{1,0:T(8,128)S(1)} collective-permute-done((f32[128,512]{1,0:T(8,128)S(1)}, f32[128,512]{1,0:T(8,128)S(1)}, u32[]{:S(2)}, u32[]{:S(2)}) %collective-permute-start.6) | collective-permute-done | bytes 262176 | tf_op jit(solution)/shard_map/ppermute | solution.py:292
  44.0 1.5 %collective-permute-start.9 = (f32[128,512]{1,0:T(8,128)S(1)}, f32[128,512]{1,0:T(8,128)S(1)}, u32[]{:S(2)}, u32[]{:S(2)}) collective-permute-start(f32[128,512]{1,0:T(8,128)S(1)} %collective-permute-done.6.refs_0_), channel_id=1, source_target_pairs={{0,16},{16,0},{1,17},{17,1},{2,18},{18,2},{3,19},{19,3},{4,20},{20... | collective-permute-start | bytes 786440 | tf_op jit(solution)/shard_map/ppermute | solution.py:296
  45.5 5.0 %shard_map.61 = (f32[512,512]{1,0:T(8,128)S(1)}, f32[512,512]{1,0:T(8,128)S(1)}) custom-call(f32[512,512]{1,0:T(8,128)S(1)} %get-tuple-element.39.a_in, f32[256,256]{1,0:T(8,128)S(1)} %get-tuple-element.40.b_ref, f32[256,512]{1,0:T(8,128)S(1)} %get-tuple-element.42.upper_ref, f32[256,512]{1,0:T(8,128)S(1)} %collective-permute-done.7.lower_ref.other_ref), custom_call_target="tpu_custom_call" | custom-call | flops 5000000000 | bytes 1048576 | tf_op jit(solution)/shard_map/pallas_call | solution.py:347
  50.6 1.2 %collective-permute-done.9.refs_2_ = f32[128,512]{1,0:T(8,128)S(1)} collective-permute-done((f32[128,512]{1,0:T(8,128)S(1)}, f32[128,512]{1,0:T(8,128)S(1)}, u32[]{:S(2)}, u32[]{:S(2)}) %collective-permute-start.9) | collective-permute-done | bytes 262176 | tf_op jit(solution)/shard_map/ppermute | solution.py:296
  51.8 2.0 %collective-permute-start.10 = (f32[128,512]{1,0:T(8,128)S(1)}, f32[128,512]{1,0:T(8,128)S(1)}, u32[]{:S(2)}, u32[]{:S(2)}) collective-permute-start(f32[128,512]{1,0:T(8,128)S(1)} %collective-permute-done.8.refs_1_), channel_id=1, source_target_pairs={{0,16},{16,0},{1,17},{17,1},{2,18},{18,2},{3,19},{19,3},{4,20},{20... | collective-permute-start | bytes 786440 | tf_op jit(solution)/shard_map/ppermute | solution.py:296
  53.8 6.4 %shard_map.62 = (f32[256,512]{1,0:T(8,128)}, f32[256,512]{1,0:T(8,128)}, f32[512,256]{1,0:T(8,128)S(1)}) custom-call(f32[512,512]{1,0:T(8,128)S(1)} %get-tuple-element.47.a_ref, f32[512,512]{1,0:T(8,128)S(1)} %get-tuple-element.48.g_in, bf16[512,512]{1,0:T(8,128)(2,1)S(1)} %get-tuple-element.49.p_ref, f32[256,1024]{1,0:T(8,128)S(1)} %bitcast.11, ...), custom_call_target="tpu_custom_call" | custom-call | flops 7000000000 | bytes 1048576 | tf_op jit(solution)/shard_map/pallas_call | solution.py:352
  60.2 1.8 %shard_map.63 = f32[256,512]{1,0:T(8,128)} custom-call(f32[512,256]{1,0:T(8,128)S(1)} %get-tuple-element.51.h_ref, f32[128,512]{1,0:T(8,128)S(1)} %collective-permute-done.6.refs_0_, f32[128,512]{1,0:T(8,128)S(1)} %collective-permute-done.8.refs_1_, f32[128,512]{1,0:T(8,128)S(1)} %collective-permute-done.9.refs_2_, ...), custom_call_target="tpu_custom_call" | custom-call | flops 100000000 | bytes 1048576 | tf_op jit(solution)/shard_map/pallas_call | solution.py:359
  (16 shorter events, 0.1 us)
Async XLA Ops:
  0.6 1.2 %copy-start = (f32[1,256,1024]{2,1,0:T(8,128)S(1)}, f32[1,256,1024]{2,1,0:T(8,128)}, u32[]{:S(2)}) copy-start(f32[1,256,1024]{2,1,0:T(8,128)} %param.3) | copy-start | bytes 3145732
  1.9 21.0 %copy-start.1 = (f32[1,256,1024]{2,1,0:T(8,128)S(1)}, f32[1,256,1024]{2,1,0:T(8,128)}, u32[]{:S(2)}) copy-start(f32[1,256,1024]{2,1,0:T(8,128)} %param.3) | copy-start | bytes 3145732
  1.9 5.9 %copy-start.3 = (s32[1,512]{1,0:T(1,128)S(1)}, s32[1,512]{1,0:T(1,128)}, u32[]{:S(2)}) copy-start(s32[1,512]{1,0:T(1,128)} %param.5) | copy-start | bytes 6148
  1.9 18.9 %collective-permute-start.2 = (f32[384,128]{1,0:T(8,128)S(1)}, f32[384,128]{1,0:T(8,128)S(1)}, u32[]{:S(2)}, u32[]{:S(2)}) collective-permute-start(f32[384,128]{1,0:T(8,128)S(1)} %get-tuple-element.29), channel_id=1, source_target_pairs={{0,8},{1,9},{2,10},{3,11},{4,12},{5,13},{6,14},{7,15},{8,0},{9,1},... | collective-permute-start | bytes 589832 | tf_op jit(solution)/shard_map/ppermute | solution.py:292
  6.0 14.8 %collective-permute-start.1 = (f32[256,128]{1,0:T(8,128)S(1)}, f32[256,128]{1,0:T(8,128)S(1)}, u32[]{:S(2)}, u32[]{:S(2)}) collective-permute-start(f32[256,128]{1,0:T(8,128)S(1)} %get-tuple-element.30), channel_id=1, source_target_pairs={{0,8},{1,9},{2,10},{3,11},{4,12},{5,13},{6,14},{7,15},{8,0},{9,1},... | collective-permute-start | bytes 393224 | tf_op jit(solution)/shard_map/ppermute | solution.py:292
  6.1 24.8 %collective-permute-start = (f32[384,128]{1,0:T(8,128)S(1)}, f32[384,128]{1,0:T(8,128)S(1)}, u32[]{:S(2)}, u32[]{:S(2)}) collective-permute-start(f32[384,128]{1,0:T(8,128)S(1)} %get-tuple-element.29), channel_id=1, source_target_pairs={{0,16},{16,0},{1,17},{17,1},{2,18},{18,2},{3,19},{19,3},{4,20},{20... | collective-permute-start | bytes 589832 | tf_op jit(solution)/shard_map/ppermute | solution.py:296
  7.9 15.3 %collective-permute-start.5 = (s32[1,512]{1,0:T(1,128)S(1)}, s32[1,512]{1,0:T(1,128)S(1)}, u32[]{:S(2)}, u32[]{:S(2)}) collective-permute-start(s32[1,512]{1,0:T(1,128)S(1)} %copy-done.3), channel_id=1, source_target_pairs={{0,8},{1,9},{2,10},{3,11},{4,12},{5,13},{6,14},{7,15},{8,0},{9,1},... | collective-permute-start | bytes 6152 | tf_op jit(solution)/shard_map/ppermute | solution.py:292
  20.8 10.1 %collective-permute-start.4 = (f32[256,128]{1,0:T(8,128)S(1)}, f32[256,128]{1,0:T(8,128)S(1)}, u32[]{:S(2)}, u32[]{:S(2)}) collective-permute-start(f32[256,128]{1,0:T(8,128)S(1)} %collective-permute-done.1.near_side), channel_id=1, source_target_pairs={{0,16},{16,0},{1,17},{17,1},{2,18},{18,2},{3,19},{19,3},{4,20},{20... | collective-permute-start | bytes 393224 | tf_op jit(solution)/shard_map/ppermute | solution.py:296
  22.4 7.3 %collective-permute-start.3 = (f32[384,128]{1,0:T(8,128)S(1)}, f32[384,128]{1,0:T(8,128)S(1)}, u32[]{:S(2)}, u32[]{:S(2)}) collective-permute-start(f32[384,128]{1,0:T(8,128)S(1)} %collective-permute-done.2.near_ref), channel_id=1, source_target_pairs={{0,16},{16,0},{1,17},{17,1},{2,18},{18,2},{3,19},{19,3},{4,20},{20... | collective-permute-start | bytes 589832 | tf_op jit(solution)/shard_map/ppermute | solution.py:296
  23.1 20.9 %collective-permute-start.6 = (f32[128,512]{1,0:T(8,128)S(1)}, f32[128,512]{1,0:T(8,128)S(1)}, u32[]{:S(2)}, u32[]{:S(2)}) collective-permute-start(f32[128,512]{1,0:T(8,128)S(1)} %get-tuple-element.38), channel_id=1, source_target_pairs={{0,8},{1,9},{2,10},{3,11},{4,12},{5,13},{6,14},{7,15},{8,0},{9,1},... | collective-permute-start | bytes 786440 | tf_op jit(solution)/shard_map/ppermute | solution.py:292
  23.2 27.4 %collective-permute-start.8 = (f32[128,512]{1,0:T(8,128)S(1)}, f32[128,512]{1,0:T(8,128)S(1)}, u32[]{:S(2)}, u32[]{:S(2)}) collective-permute-start(f32[128,512]{1,0:T(8,128)S(1)} %get-tuple-element.45), channel_id=1, source_target_pairs={{0,8},{1,9},{2,10},{3,11},{4,12},{5,13},{6,14},{7,15},{8,0},{9,1},... | collective-permute-start | bytes 786440 | tf_op jit(solution)/shard_map/ppermute | solution.py:292
  29.7 15.8 %collective-permute-start.7 = (f32[256,512]{1,0:T(8,128)S(1)}, f32[256,512]{1,0:T(8,128)S(1)}, u32[]{:S(2)}, u32[]{:S(2)}) collective-permute-start(f32[256,512]{1,0:T(8,128)S(1)} %get-tuple-element.42.upper_ref), channel_id=1, source_target_pairs={{0,16},{16,0},{1,17},{17,1},{2,18},{18,2},{3,19},{19,3},{4,20},{20... | collective-permute-start | bytes 1572872 | tf_op jit(solution)/shard_map/ppermute | solution.py:296
  44.0 9.7 %copy-start.2 = (f32[1,256,512]{2,1,0:T(8,128)S(1)}, f32[1,256,512]{2,1,0:T(8,128)}, u32[]{:S(2)}) copy-start(f32[1,256,512]{2,1,0:T(8,128)} %param.4) | copy-start | bytes 1572868
  44.0 7.7 %collective-permute-start.9 = (f32[128,512]{1,0:T(8,128)S(1)}, f32[128,512]{1,0:T(8,128)S(1)}, u32[]{:S(2)}, u32[]{:S(2)}) collective-permute-start(f32[128,512]{1,0:T(8,128)S(1)} %collective-permute-done.6.refs_0_), channel_id=1, source_target_pairs={{0,16},{16,0},{1,17},{17,1},{2,18},{18,2},{3,19},{19,3},{4,20},{20... | collective-permute-start | bytes 786440 | tf_op jit(solution)/shard_map/ppermute | solution.py:296
  51.8 8.4 %collective-permute-start.10 = (f32[128,512]{1,0:T(8,128)S(1)}, f32[128,512]{1,0:T(8,128)S(1)}, u32[]{:S(2)}, u32[]{:S(2)}) collective-permute-start(f32[128,512]{1,0:T(8,128)S(1)} %collective-permute-done.8.refs_1_), channel_id=1, source_target_pairs={{0,16},{16,0},{1,17},{17,1},{2,18},{18,2},{3,19},{19,3},{4,20},{20... | collective-permute-start | bytes 786440 | tf_op jit(solution)/shard_map/ppermute | solution.py:296

commit v4 on v3

--- a/solution.py
+++ b/solution.py
@@ -10,6 +10,7 @@
 F32 = jnp.float32
 BF16 = jnp.bfloat16
 TILE = 128
+CHUNKS = 4
 VMEM_LIMIT = 48 * 2**20
 
 
@@ -169,7 +170,7 @@
 
 
 def first_body(
-    half, steps, t_ref, diag_ref, near_ref, near_side, far_ref, far_side, column_ref, row_ref, first_ref, a_out, b_out, p_out, m_work
+    half, steps, t_ref, diag_ref, near_ref, far_ref, column_ref, row_ref, first_ref, a_out, b_out, p_out, m_work
 ):
     n = 2 * half
     q = half // 2
@@ -191,18 +192,18 @@
         put(base, base, part(ref, 0))
         put(base, base + 1, part(ref, 1))
         put(base + 1, base + 1, part(ref, 2))
-    put(0, 3, part(near_side, 0))
-    put(2, 1, part(far_side, 0))
+    put(0, 3, part(near_ref, 3))
+    put(2, 1, part(far_ref, 3))
 
     @pl.when(mine == 0)
     def _():
-        put(0, 2, part(near_side, 1))
-        put(3, 1, part(far_side, 1))
+        put(0, 2, part(near_ref, 4))
+        put(3, 1, part(far_ref, 4))
 
     @pl.when(mine != 0)
     def _():
-        put(1, 3, part(near_side, 1))
-        put(2, 0, part(far_side, 1))
+        put(1, 3, part(near_ref, 4))
+        put(2, 0, part(far_ref, 4))
 
     same = column_ref[...] == row_ref[...]
     onehot = jnp.where(same, 1.0, 0.0).astype(BF16)
@@ -224,46 +225,60 @@
     eliminate(a_out, b_out, steps)
 
 
-def middle_body(steps, a_in, b_ref, upper_ref, lower_ref, a_out, g_out):
-    top, half = b_ref.shape[0], upper_ref.shape[0]
+def middle_body(steps, a_in, b_ref, t_ref, early_ref, late_ref, a_out, g_out, other_out):
+    top, half, q = b_ref.shape[0], t_ref.shape[0], early_ref.shape[1]
+    width = g_out.shape[1]
     a_out[...] = a_in[...]
-    g_out[0:half, :] = upper_ref[...]
-    g_out[half:, :] = lower_ref[...]
+    for at, rows, columns in early_blocks(3 * q, early_ref.shape[0], q, width):
+        other_out[0:rows, columns] = early_ref[at : at + rows, :]
+    other_out[half - late_ref.shape[0] :, :] = late_ref[...]
+    g_out[0:half, :] = t_ref[:, 0:width]
+    g_out[half:, :] = other_out[...]
     first = g_out[0:top, :]
     g_out[top:, :] = g_out[top:, :] - full(a_in[0:top, top:], first, ((0,), (0,)))
     g_out[0:top, :] = full(b_ref[...], first)
     eliminate(a_out, g_out, steps)
 
 
-def last_body(
-    half, steps, a_ref, g_in, p_ref, t_ref, other_ref, ext_ref, row_ref, first_ref, own_ref, sol_ref, h_ref, a_work, g_work
+def last_body(steps, a_ref, g_in, g_out, a_work):
+    a_work[...] = a_ref[...]
+    g_out[...] = g_in[...]
+    eliminate(a_work, g_out, steps)
+
+
+def cross_terms(h_ref, at, parts):
+    total = None
+    for ref in parts:
+        term = three_pass(h_ref[at : at + ref.shape[0], :], ref[...], ((0,), (0,)))
+        total = term if total is None else total + term
+        at += ref.shape[0]
+    return total
+
+
+def output_body(
+    half, g_ref, p_ref, t_ref, other_ref, ext_ref, row_ref, first_ref, *refs
 ):
+    *parts, own_ref, sol_ref, h_ref, cross_ref = refs
     n = 2 * half
     mine = first_ref[0]
-    a_work[...] = a_ref[...]
-    g_work[...] = g_in[...]
-    eliminate(a_work, g_work, steps)
     block = pl.ds(pl.multiple_of(mine * half, half), half)
-    g = g_work[...]
-    h_ref[...] = pick_left(p_ref[...], g_work[:, block], ((0,), (0,)))
+    g = g_ref[...]
+    h_ref[...] = pick_left(p_ref[...], g_ref[:, block], ((0,), (0,)))
     left = jnp.concatenate([t_ref[:, block], other_ref[:, block]], axis=0)
     own_ref[...] = ext_ref[...] - three_pass(left, g, ((0,), (0,)))
     target = lax.broadcasted_iota(jnp.int32, (half, n), 0) + mine * half
     onehot = jnp.where(row_ref[...] == target, 1.0, 0.0).astype(BF16)
     sol_ref[...] = -pick_left(onehot, g, ((1,), (0,)))
-
-
-def cross_body(h_ref, *refs):
+    cross_ref[...] = cross_terms(h_ref, 0, parts)
+
+
+def cross_body(h_ref, partial_ref, *refs):
     *parts, out_ref = refs
-    total, at = None, 0
-    for ref in parts:
-        end = at + ref.shape[0]
-        term = three_pass(h_ref[at:end, :], ref[...], ((0,), (0,)))
-        total, at = term if total is None else total + term, end
-    out_ref[...] = -total
-
-
-def pack_iface_body(half, width, t_ref, first_ref, diag_ref, side_ref):
+    at = h_ref.shape[0] - sum(ref.shape[0] for ref in parts)
+    out_ref[...] = -(partial_ref[...] + cross_terms(h_ref, at, parts))
+
+
+def pack_iface_body(half, width, t_ref, first_ref, pack_ref, early_ref):
     q = half // 2
     mine = first_ref[0]
     here, there = width + mine * half, width + (1 - mine) * half
@@ -271,16 +286,24 @@
     def cut(row, column):
         return t_ref[pl.ds(pl.multiple_of(row, q), q), pl.ds(pl.multiple_of(column, q), q)]
 
-    diag_ref[0:q, :] = cut(0, here)
-    diag_ref[q : 2 * q, :] = cut(0, here + q)
-    diag_ref[2 * q : 3 * q, :] = cut(q, here + q)
-    side_ref[0:q, :] = cut(0, there + q)
-    side_ref[q : 2 * q, :] = cut(mine * q, there + mine * q)
-
-
-def pack_outer_body(t_ref, outer_ref, *chunks):
-    width = outer_ref.shape[1]
-    outer_ref[...] = t_ref[:, 0:width]
+    for ref in (pack_ref, early_ref):
+        ref[0:q, :] = cut(0, here)
+        ref[q : 2 * q, :] = cut(0, here + q)
+        ref[2 * q : 3 * q, :] = cut(q, here + q)
+    pack_ref[3 * q : 4 * q, :] = cut(0, there + q)
+    pack_ref[4 * q : 5 * q, :] = cut(mine * q, there + mine * q)
+    for at, rows, columns in early_blocks(3 * q, early_ref.shape[0], q, width):
+        early_ref[at : at + rows, :] = t_ref[0:rows, columns]
+
+
+def early_blocks(start, end, q, width):
+    rows = (end - start) * q // width
+    return [(start + i * rows, rows, slice(i * q, (i + 1) * q)) for i in range(width // q)]
+
+
+def pack_outer_body(t_ref, late_ref, *chunks):
+    half, width = t_ref.shape[0], late_ref.shape[1]
+    late_ref[...] = t_ref[half - late_ref.shape[0] :, 0:width]
     at = 0
     for chunk in chunks:
         chunk[...] = t_ref[at : at + chunk.shape[0], 0:width]
@@ -317,20 +340,23 @@
     vmem, smem = pltpu.VMEM, pltpu.SMEM
     mine = lax.axis_index("sib").astype(jnp.int32)
     first = mine.reshape(1)
-    diag, side = kernel(
-        functools.partial(pack_iface_body, half, width), (f(3 * q, q), f(2 * q, q)), [vmem, smem]
+    other_map = sibling(iface_map)
+    early_rows = half * 5 // 8
+    packed, early = kernel(
+        functools.partial(pack_iface_body, half, width),
+        (f(5 * q, q), f(3 * q + early_rows * width // q, q)),
+        [vmem, smem],
     )(t_int, first)
-    near, near_side = sibling(diag), sibling(side)
-    other_map = sibling(iface_map)
-    diag_other = across(diag)
+    near = sibling(packed)
+    early_other = across(early)
     far = across(near)
-    near_side, near = lax.optimization_barrier((near_side, near))
-    far_side = across(near_side)
-    outer, chunk_a, chunk_b = kernel(pack_outer_body, (f(half, width), f(q, width), f(q, width)), [vmem])(t_int)
-    outer_late, _ = lax.optimization_barrier((outer, far))
-    outer_other = across(outer_late)
-    chunk_a, chunk_b, _, _, other_map = lax.optimization_barrier((chunk_a, chunk_b, near, near_side, other_map))
-    near_a, near_b = sibling(chunk_a), sibling(chunk_b)
+    late, *chunks = kernel(
+        pack_outer_body, [f(half - early_rows, width)] + [f(half // CHUNKS, width)] * CHUNKS, [vmem]
+    )(t_int)
+    late, _ = lax.optimization_barrier((late, far))
+    late_other = across(late)
+    *chunks, _, other_map = lax.optimization_barrier((*chunks, near, other_map))
+    near_r = [sibling(chunk) for chunk in chunks]
     rolled = lambda m: lax.dynamic_slice(jnp.concatenate([m, m], axis=1), (0, mine * half), (1, n))
     own_row, other_row = rolled(iface_map), rolled(other_map)
 
@@ -338,25 +364,35 @@
     a, b, onehot = kernel(
         functools.partial(first_body, half, range(tiles // 2)),
         (f(n, n), f(top, top), jax.ShapeDtypeStruct((n, n), BF16)),
-        [vmem] * 8 + [smem],
+        [vmem] * 6 + [smem],
         [pltpu.VMEM((n, n), F32)],
         10e9,
-    )(t_int, diag_other, near, near_side, far, far_side, own_row.reshape(n, 1), other_row, first)
-    a, b, near_a = lax.optimization_barrier((a, b, near_a))
-    far_a = across(near_a)
-    a, g = kernel(
-        functools.partial(middle_body, range(tiles // 2, tiles - 1)), (f(n, n), f(n, width)), [vmem] * 4, (), 5e9
-    )(a, b, outer, outer_other)
-    a, g, near_b, far_a = lax.optimization_barrier((a, g, near_b, far_a))
-    far_b = across(near_b)
-    own_map, solution_op, h = kernel(
-        functools.partial(last_body, half, range(tiles - 1, tiles)),
-        (f(half, width), f(half, width), f(n, half)),
-        [vmem] * 7 + [smem],
-        [pltpu.VMEM((n, n), F32), pltpu.VMEM((n, width), F32)],
-        7e9,
-    )(a, g, onehot, t_int, outer_other, t_ext, own_row, first)
-    cross_map = kernel(cross_body, f(half, width), [vmem] * 5)(h, near_a, near_b, far_a, far_b)
+    )(t_int, early_other, near, far, own_row.reshape(n, 1), other_row, first)
+    a, b, near_r[0] = lax.optimization_barrier((a, b, near_r[0]))
+    far_r = [across(near_r[0])]
+    a, g, other = kernel(
+        functools.partial(middle_body, range(tiles // 2, tiles - 1)),
+        (f(n, n), f(n, width), f(half, width)),
+        [vmem] * 5,
+        (),
+        5e9,
+    )(a, b, t_int, early_other, late_other)
+    a, g, near_r[1] = lax.optimization_barrier((a, g, near_r[1]))
+    far_r.append(across(near_r[1]))
+    g = kernel(
+        functools.partial(last_body, range(tiles - 1, tiles)), f(n, width), [vmem] * 2, [pltpu.VMEM((n, n), F32)], 5e9
+    )(a, g)
+    g, *near_r[2:] = lax.optimization_barrier((g, *near_r[2:]))
+    far_r += [across(x) for x in near_r[2:]]
+    parts = [*near_r, *far_r[:2]]
+    own_map, solution_op, h, partial = kernel(
+        functools.partial(output_body, half),
+        (f(half, width), f(half, width), f(n, half), f(half, width)),
+        [vmem] * 6 + [smem] + [vmem] * len(parts),
+        (),
+        4e9,
+    )(g, onehot, t_int, other, t_ext, own_row, first, *parts)
+    cross_map = kernel(cross_body, f(half, width), [vmem] * (CHUNKS))(h, partial, *far_r[2:])
     return own_map[None], cross_map[None], solution_op[None]
 
 

time: 62.1 us -> 61.8 us (level)
  starting transfers between devices: 18.3 us -> 15.9 us
  local copies, waits for them, and re-layouts: 1.38 us -> 2.68 us
    ppermute x5 -> x6, starting transfers between devices: 9.75 us -> 7.76 us  [sibling(): return lax.ppermute(x, 'leaf', [(i, i ^ size // 2) for i in range(size)])]
    unnamed x8 -> x12, local copies, waits for them, and re-layouts: 1.23 us -> 2.54 us
    ppermute x5 -> x6, waiting for transfers between devices: 14.4 us -> 15.5 us  [sibling(): return lax.ppermute(x, 'leaf', [(i, i ^ size // 2) for i in range(size)])]
    ppermute x6 -> x7, waiting for transfers between devices: 4.74 us -> 4.23 us  [across(): return lax.ppermute(x, 'sib', [(0, 1), (1, 0)])]
    ppermute x6 -> x7, starting transfers between devices: 8.52 us -> 8.17 us  [across(): return lax.ppermute(x, 'sib', [(0, 1), (1, 0)])]
    pallas_call x4 -> x5, Pallas kernels: 8.33 us -> 8.41 us  [the longest x1 4.14 us: two_shards(): kernel(functools.partial(last_body, range(tiles - 1, tiles)), f(n, width)...]
  transfers between devices with their start and end apart: 11 -> 13, of which waited for: 4 -> 5; matrix products, arithmetic and copies ran while one was open for 0% -> 0% of each run, Pallas kernels for 33% -> 34%
where the time goes in v4:
time: 61.8 us; the launch traced here: 61.7 us
  Pallas kernels  22.5 us (36%)
  waiting for transfers between devices  19.7 us (32%)
  starting transfers between devices  15.9 us (26%)
  local copies, waits for them, and re-layouts  2.68 us (4%)
  between operations  0.8 us (1%)
    ppermute x6, waiting for transfers between devices, sibling(): return lax.ppermute(x, 'leaf', [(i, i ^ size // 2) for i in range(size)])  15.5 us
    pallas_call x1, Pallas kernels, two_shards(): kernel(functools.partial(first_body, half, range(tiles // 2)), (f(n, n),...  9.07 us
    ppermute x7, starting transfers between devices, across(): return lax.ppermute(x, 'sib', [(0, 1), (1, 0)])  8.17 us
    ppermute x6, starting transfers between devices, sibling(): return lax.ppermute(x, 'leaf', [(i, i ^ size // 2) for i in range(size)])  7.76 us
    pallas_call x1, Pallas kernels, two_shards(): kernel(functools.partial(middle_body, range(tiles // 2, tiles - 1)), (f(n...  5.05 us
    ppermute x7, waiting for transfers between devices, across(): return lax.ppermute(x, 'sib', [(0, 1), (1, 0)])  4.23 us
    pallas_call x1, Pallas kernels, two_shards(): kernel(functools.partial(last_body, range(tiles - 1, tiles)), f(n, width)...  4.14 us
    pallas_call x1, Pallas kernels, two_shards(): kernel(functools.partial(output_body, half), (f(half, width), f(half, wid...  2.76 us
  transfers between devices with their start and end apart: 13, of which 5 were waited for; matrix products, arithmetic and copies ran while one was open for 0% of the time, Pallas kernels for 34%

profile of v4, /device:TPU:0, one launch (start us, length us, event | category | flops | bytes accessed | tf_op | source)
XLA Modules:
  0.0 61.7 jit_solution(1856569484415062118)
XLA Ops:
  0.6 1.2 %copy-done = f32[1,256,1024]{2,1,0:T(8,128)S(1)} copy-done((f32[1,256,1024]{2,1,0:T(8,128)S(1)}, f32[1,256,1024]{2,1,0:T(8,128)}, u32[]{:S(2)}) %copy-start) | copy-done | bytes 1048600
  2.0 4.1 %collective-permute-start.1 = (f32[640,128]{1,0:T(8,128)S(1)}, f32[640,128]{1,0:T(8,128)S(1)}, u32[]{:S(2)}, u32[]{:S(2)}) collective-permute-start(f32[640,128]{1,0:T(8,128)S(1)} %get-tuple-element.36), channel_id=1, source_target_pairs={{0,8},{1,9},{2,10},{3,11},{4,12},{5,13},{6,14},{7,15},{8,0},{9,1},... | collective-permute-start | bytes 983048 | tf_op jit(solution)/shard_map/ppermute | solution.py:315
  6.1 1.5 %collective-permute-start = (f32[1024,128]{1,0:T(8,128)S(1)}, f32[1024,128]{1,0:T(8,128)S(1)}, u32[]{:S(2)}, u32[]{:S(2)}) collective-permute-start(f32[1024,128]{1,0:T(8,128)S(1)} %get-tuple-element.35), channel_id=1, source_target_pairs={{0,16},{16,0},{1,17},{17,1},{2,18},{18,2},{3,19},{19,3},{4,20},{20... | collective-permute-start | bytes 1572872 | tf_op jit(solution)/shard_map/ppermute | solution.py:319
  7.5 0.3 collective-permute-start.3
  7.9 13.0 %collective-permute-done.1.near_ref = f32[640,128]{1,0:T(8,128)S(1)} collective-permute-done((f32[640,128]{1,0:T(8,128)S(1)}, f32[640,128]{1,0:T(8,128)S(1)}, u32[]{:S(2)}, u32[]{:S(2)}) %collective-permute-start.1) | collective-permute-done | bytes 327712 | tf_op jit(solution)/shard_map/ppermute | solution.py:315
  20.9 1.5 %collective-permute-start.2 = (f32[640,128]{1,0:T(8,128)S(1)}, f32[640,128]{1,0:T(8,128)S(1)}, u32[]{:S(2)}, u32[]{:S(2)}) collective-permute-start(f32[640,128]{1,0:T(8,128)S(1)} %collective-permute-done.1.near_ref), channel_id=1, source_target_pairs={{0,16},{16,0},{1,17},{17,1},{2,18},{18,2},{3,19},{19,3},{4,20},{20... | collective-permute-start | bytes 983048 | tf_op jit(solution)/shard_map/ppermute | solution.py:319
  22.5 0.6 %copy-done.3 = f32[64,512]{1,0:T(8,128)} copy-done((f32[64,512]{1,0:T(8,128)}, f32[64,512]{1,0:T(8,128)S(1)}, u32[]{:S(2)}) %copy-start.3) | copy-done | bytes 131096
  23.2 0.7 %copy-done.4 = f32[64,512]{1,0:T(8,128)} copy-done((f32[64,512]{1,0:T(8,128)}, f32[64,512]{1,0:T(8,128)S(1)}, u32[]{:S(2)}) %copy-start.4) | copy-done | bytes 131096
  24.1 2.9 %collective-permute-start.6 = (f32[64,512]{1,0:T(8,128)}, f32[64,512]{1,0:T(8,128)S(1)}, u32[]{:S(2)}, u32[]{:S(2)}) collective-permute-start(f32[64,512]{1,0:T(8,128)} %copy-done.3), channel_id=1, source_target_pairs={{0,8},{1,9},{2,10},{3,11},{4,12},{5,13},{6,14},{7,15},{8,0},{9,1},... | collective-permute-start | bytes 393224 | tf_op jit(solution)/shard_map/ppermute | solution.py:315
  27.1 2.7 %collective-permute-done.2.far_ref = f32[640,128]{1,0:T(8,128)S(1)} collective-permute-done((f32[640,128]{1,0:T(8,128)S(1)}, f32[640,128]{1,0:T(8,128)S(1)}, u32[]{:S(2)}, u32[]{:S(2)}) %collective-permute-start.2) | collective-permute-done | bytes 327712 | tf_op jit(solution)/shard_map/ppermute | solution.py:319
  29.7 0.3 collective-permute-start.8
  30.0 1.0 %collective-permute-start.5 = (f32[96,512]{1,0:T(8,128)S(1)}, f32[96,512]{1,0:T(8,128)S(1)}, u32[]{:S(2)}, u32[]{:S(2)}) collective-permute-start(f32[96,512]{1,0:T(8,128)S(1)} %get-tuple-element.48), channel_id=1, source_target_pairs={{0,16},{16,0},{1,17},{17,1},{2,18},{18,2},{3,19},{19,3},{4,20},{20... | collective-permute-start | bytes 589832 | tf_op jit(solution)/shard_map/ppermute | solution.py:319
  31.0 9.1 %shard_map.60 = (f32[512,512]{1,0:T(8,128)S(1)}, f32[256,256]{1,0:T(8,128)S(1)}, bf16[512,512]{1,0:T(8,128)(2,1)S(1)}) custom-call(f32[256,1024]{1,0:T(8,128)S(1)} %bitcast.10, f32[1024,128]{1,0:T(8,128)S(1)} %collective-permute-done.diag_ref.early_ref, f32[640,128]{1,0:T(8,128)S(1)} %collective-permute-done.1.near_ref, ...), custom_call_target="tpu_custom_call" | custom-call | flops 10000000000 | bytes 1048576 | tf_op jit(solution)/shard_map/pallas_call | solution.py:364
  40.0 2.5 %collective-permute-done.4.refs_0_ = f32[64,512]{1,0:T(8,128)S(1)} collective-permute-done((f32[64,512]{1,0:T(8,128)}, f32[64,512]{1,0:T(8,128)S(1)}, u32[]{:S(2)}, u32[]{:S(2)}) %collective-permute-start.4) | collective-permute-done | bytes 131104 | tf_op jit(solution)/shard_map/ppermute | solution.py:315
  42.5 0.5 collective-permute-start.9
  43.1 5.1 %shard_map.61 = (f32[512,512]{1,0:T(8,128)S(1)}, f32[512,512]{1,0:T(8,128)S(1)}, f32[256,512]{1,0:T(8,128)S(1)}) custom-call(f32[512,512]{1,0:T(8,128)S(1)} %get-tuple-element.45.a_in, f32[256,256]{1,0:T(8,128)S(1)} %get-tuple-element.46.b_ref, f32[256,1024]{1,0:T(8,128)S(1)} %bitcast.11, f32[1024,128]{1,0:T(8,128)S(1)} %collective-permute-done.diag_ref.early_ref, ...), custom_call_target="tpu_custom_call" | custom-call | flops 5000000000 | bytes 1048576 | tf_op jit(solution)/shard_map/pallas_call | solution.py:373
  48.1 1.5 %collective-permute-start.10 = (f32[64,512]{1,0:T(8,128)S(1)}, f32[64,512]{1,0:T(8,128)S(1)}, u32[]{:S(2)}, u32[]{:S(2)}) collective-permute-start(f32[64,512]{1,0:T(8,128)S(1)} %collective-permute-done.6.refs_1_), channel_id=1, source_target_pairs={{0,16},{16,0},{1,17},{17,1},{2,18},{18,2},{3,19},{19,3},{4,20},{20... | collective-permute-start | bytes 393224 | tf_op jit(solution)/shard_map/ppermute | solution.py:319
  49.7 4.1 %shard_map.62.g_ref = f32[512,512]{1,0:T(8,128)S(1)} custom-call(f32[512,512]{1,0:T(8,128)S(1)} %get-tuple-element.52.a_ref, f32[512,512]{1,0:T(8,128)S(1)} %get-tuple-element.53.g_in), custom_call_target="tpu_custom_call" | custom-call | flops 5000000000 | bytes 1048576 | tf_op jit(solution)/shard_map/pallas_call | solution.py:382
  53.9 0.6 collective-permute-start.11
  54.5 1.5 %collective-permute-start.12 = (f32[64,512]{1,0:T(8,128)S(1)}, f32[64,512]{1,0:T(8,128)S(1)}, u32[]{:S(2)}, u32[]{:S(2)}) collective-permute-start(f32[64,512]{1,0:T(8,128)S(1)} %collective-permute-done.8.refs_3_), channel_id=1, source_target_pairs={{0,16},{16,0},{1,17},{17,1},{2,18},{18,2},{3,19},{19,3},{4,20},{20... | collective-permute-start | bytes 393224 | tf_op jit(solution)/shard_map/ppermute | solution.py:319
  56.0 2.8 %shard_map.63 = (f32[256,512]{1,0:T(8,128)}, f32[256,512]{1,0:T(8,128)}, f32[512,256]{1,0:T(8,128)S(1)}, f32[256,512]{1,0:T(8,128)S(1)}) custom-call(f32[512,512]{1,0:T(8,128)S(1)} %shard_map.62.g_ref, bf16[512,512]{1,0:T(8,128)(2,1)S(1)} %get-tuple-element.57.p_ref, f32[256,1024]{1,0:T(8,128)S(1)} %bitcast.12, f32[256,512]{1,0:T(8,128)S(1)} %get-tuple-element.58.other_ref, ...), custom_call_target="tpu_custom_call" | custom-call | flops 4000000000 | bytes 1048576 | tf_op jit(solution)/shard_map/pallas_call | solution.py:388
  58.7 0.2 collective-permute-done.11.refs_0_
  58.9 1.4 %collective-permute-done.12.refs_1_ = f32[64,512]{1,0:T(8,128)S(1)} collective-permute-done((f32[64,512]{1,0:T(8,128)S(1)}, f32[64,512]{1,0:T(8,128)S(1)}, u32[]{:S(2)}, u32[]{:S(2)}) %collective-permute-start.12) | collective-permute-done | bytes 131104 | tf_op jit(solution)/shard_map/ppermute | solution.py:319
  60.3 1.4 %shard_map.64 = f32[256,512]{1,0:T(8,128)} custom-call(f32[512,256]{1,0:T(8,128)S(1)} %get-tuple-element.64.h_ref, f32[256,512]{1,0:T(8,128)S(1)} %get-tuple-element.65.partial_ref, f32[64,512]{1,0:T(8,128)S(1)} %collective-permute-done.11.refs_0_, f32[64,512]{1,0:T(8,128)S(1)} %collective-permute-done.12.refs_1_), custom_call_target="tpu_custom_call" | custom-call | flops 100000000 | bytes 1048576 | tf_op jit(solution)/shard_map/pallas_call | solution.py:395
  (25 shorter events, 0.5 us)
Async XLA Ops:
  0.6 1.2 %copy-start = (f32[1,256,1024]{2,1,0:T(8,128)S(1)}, f32[1,256,1024]{2,1,0:T(8,128)}, u32[]{:S(2)}) copy-start(f32[1,256,1024]{2,1,0:T(8,128)} %param.3) | copy-start | bytes 3145732
  1.9 20.6 %copy-start.1 = (f32[1,256,1024]{2,1,0:T(8,128)S(1)}, f32[1,256,1024]{2,1,0:T(8,128)}, u32[]{:S(2)}) copy-start(f32[1,256,1024]{2,1,0:T(8,128)} %param.3) | copy-start | bytes 3145732
  1.9 5.6 %copy-start.5 = (s32[1,512]{1,0:T(1,128)S(1)}, s32[1,512]{1,0:T(1,128)}, u32[]{:S(2)}) copy-start(s32[1,512]{1,0:T(1,128)} %param.5) | copy-start | bytes 6148
  2.0 18.9 %collective-permute-start.1 = (f32[640,128]{1,0:T(8,128)S(1)}, f32[640,128]{1,0:T(8,128)S(1)}, u32[]{:S(2)}, u32[]{:S(2)}) collective-permute-start(f32[640,128]{1,0:T(8,128)S(1)} %get-tuple-element.36), channel_id=1, source_target_pairs={{0,8},{1,9},{2,10},{3,11},{4,12},{5,13},{6,14},{7,15},{8,0},{9,1},... | collective-permute-start | bytes 983048 | tf_op jit(solution)/shard_map/ppermute | solution.py:315
  6.1 23.9 %collective-permute-start = (f32[1024,128]{1,0:T(8,128)S(1)}, f32[1024,128]{1,0:T(8,128)S(1)}, u32[]{:S(2)}, u32[]{:S(2)}) collective-permute-start(f32[1024,128]{1,0:T(8,128)S(1)} %get-tuple-element.35), channel_id=1, source_target_pairs={{0,16},{16,0},{1,17},{17,1},{2,18},{18,2},{3,19},{19,3},{4,20},{20... | collective-permute-start | bytes 1572872 | tf_op jit(solution)/shard_map/ppermute | solution.py:319
  7.5 16.4 %collective-permute-start.3 = (s32[1,512]{1,0:T(1,128)S(1)}, s32[1,512]{1,0:T(1,128)S(1)}, u32[]{:S(2)}, u32[]{:S(2)}) collective-permute-start(s32[1,512]{1,0:T(1,128)S(1)} %copy-done.5), channel_id=1, source_target_pairs={{0,8},{1,9},{2,10},{3,11},{4,12},{5,13},{6,14},{7,15},{8,0},{9,1},... | collective-permute-start | bytes 6152 | tf_op jit(solution)/shard_map/ppermute | solution.py:315
  20.9 8.9 %collective-permute-start.2 = (f32[640,128]{1,0:T(8,128)S(1)}, f32[640,128]{1,0:T(8,128)S(1)}, u32[]{:S(2)}, u32[]{:S(2)}) collective-permute-start(f32[640,128]{1,0:T(8,128)S(1)} %collective-permute-done.1.near_ref), channel_id=1, source_target_pairs={{0,16},{16,0},{1,17},{17,1},{2,18},{18,2},{3,19},{19,3},{4,20},{20... | collective-permute-start | bytes 983048 | tf_op jit(solution)/shard_map/ppermute | solution.py:319
  22.5 0.7 %copy-start.3 = (f32[64,512]{1,0:T(8,128)}, f32[64,512]{1,0:T(8,128)S(1)}, u32[]{:S(2)}) copy-start(f32[64,512]{1,0:T(8,128)S(1)} %get-tuple-element.51) | copy-start | bytes 393220
  23.2 0.7 %copy-start.4 = (f32[64,512]{1,0:T(8,128)}, f32[64,512]{1,0:T(8,128)S(1)}, u32[]{:S(2)}) copy-start(f32[64,512]{1,0:T(8,128)S(1)} %get-tuple-element.44) | copy-start | bytes 393220
  24.0 18.5 %collective-permute-start.4 = (f32[64,512]{1,0:T(8,128)}, f32[64,512]{1,0:T(8,128)S(1)}, u32[]{:S(2)}, u32[]{:S(2)}) collective-permute-start(f32[64,512]{1,0:T(8,128)} %copy-done.4), channel_id=1, source_target_pairs={{0,8},{1,9},{2,10},{3,11},{4,12},{5,13},{6,14},{7,15},{8,0},{9,1},... | collective-permute-start | bytes 393224 | tf_op jit(solution)/shard_map/ppermute | solution.py:315
  24.1 24.1 %collective-permute-start.6 = (f32[64,512]{1,0:T(8,128)}, f32[64,512]{1,0:T(8,128)S(1)}, u32[]{:S(2)}, u32[]{:S(2)}) collective-permute-start(f32[64,512]{1,0:T(8,128)} %copy-done.3), channel_id=1, source_target_pairs={{0,8},{1,9},{2,10},{3,11},{4,12},{5,13},{6,14},{7,15},{8,0},{9,1},... | collective-permute-start | bytes 393224 | tf_op jit(solution)/shard_map/ppermute | solution.py:315
  27.0 26.9 %collective-permute-start.7 = (f32[64,512]{1,0:T(8,128)S(1)}, f32[64,512]{1,0:T(8,128)S(1)}, u32[]{:S(2)}, u32[]{:S(2)}) collective-permute-start(f32[64,512]{1,0:T(8,128)S(1)} %get-tuple-element.54), channel_id=1, source_target_pairs={{0,8},{1,9},{2,10},{3,11},{4,12},{5,13},{6,14},{7,15},{8,0},{9,1},... | collective-permute-start | bytes 393224 | tf_op jit(solution)/shard_map/ppermute | solution.py:315
  29.7 24.1 %collective-permute-start.8 = (f32[64,512]{1,0:T(8,128)S(1)}, f32[64,512]{1,0:T(8,128)S(1)}, u32[]{:S(2)}, u32[]{:S(2)}) collective-permute-start(f32[64,512]{1,0:T(8,128)S(1)} %get-tuple-element.55), channel_id=1, source_target_pairs={{0,8},{1,9},{2,10},{3,11},{4,12},{5,13},{6,14},{7,15},{8,0},{9,1},... | collective-permute-start | bytes 393224 | tf_op jit(solution)/shard_map/ppermute | solution.py:315
  30.0 13.1 %collective-permute-start.5 = (f32[96,512]{1,0:T(8,128)S(1)}, f32[96,512]{1,0:T(8,128)S(1)}, u32[]{:S(2)}, u32[]{:S(2)}) collective-permute-start(f32[96,512]{1,0:T(8,128)S(1)} %get-tuple-element.48), channel_id=1, source_target_pairs={{0,16},{16,0},{1,17},{17,1},{2,18},{18,2},{3,19},{19,3},{4,20},{20... | collective-permute-start | bytes 589832 | tf_op jit(solution)/shard_map/ppermute | solution.py:319
  42.5 13.4 %collective-permute-start.9 = (f32[64,512]{1,0:T(8,128)S(1)}, f32[64,512]{1,0:T(8,128)S(1)}, u32[]{:S(2)}, u32[]{:S(2)}) collective-permute-start(f32[64,512]{1,0:T(8,128)S(1)} %collective-permute-done.4.refs_0_), channel_id=1, source_target_pairs={{0,16},{16,0},{1,17},{17,1},{2,18},{18,2},{3,19},{19,3},{4,20},{20... | collective-permute-start | bytes 393224 | tf_op jit(solution)/shard_map/ppermute | solution.py:319
  48.1 7.8 %copy-start.2 = (f32[1,256,512]{2,1,0:T(8,128)S(1)}, f32[1,256,512]{2,1,0:T(8,128)}, u32[]{:S(2)}) copy-start(f32[1,256,512]{2,1,0:T(8,128)} %param.4) | copy-start | bytes 1572868
  48.1 7.8 %collective-permute-start.10 = (f32[64,512]{1,0:T(8,128)S(1)}, f32[64,512]{1,0:T(8,128)S(1)}, u32[]{:S(2)}, u32[]{:S(2)}) collective-permute-start(f32[64,512]{1,0:T(8,128)S(1)} %collective-permute-done.6.refs_1_), channel_id=1, source_target_pairs={{0,16},{16,0},{1,17},{17,1},{2,18},{18,2},{3,19},{19,3},{4,20},{20... | collective-permute-start | bytes 393224 | tf_op jit(solution)/shard_map/ppermute | solution.py:319
  53.9 5.0 %collective-permute-start.11 = (f32[64,512]{1,0:T(8,128)S(1)}, f32[64,512]{1,0:T(8,128)S(1)}, u32[]{:S(2)}, u32[]{:S(2)}) collective-permute-start(f32[64,512]{1,0:T(8,128)S(1)} %collective-permute-done.7.refs_2_), channel_id=1, source_target_pairs={{0,16},{16,0},{1,17},{17,1},{2,18},{18,2},{3,19},{19,3},{4,20},{20... | collective-permute-start | bytes 393224 | tf_op jit(solution)/shard_map/ppermute | solution.py:319
  54.5 5.8 %collective-permute-start.12 = (f32[64,512]{1,0:T(8,128)S(1)}, f32[64,512]{1,0:T(8,128)S(1)}, u32[]{:S(2)}, u32[]{:S(2)}) collective-permute-start(f32[64,512]{1,0:T(8,128)S(1)} %collective-permute-done.8.refs_3_), channel_id=1, source_target_pairs={{0,16},{16,0},{1,17},{17,1},{2,18},{18,2},{3,19},{19,3},{4,20},{20... | collective-permute-start | bytes 393224 | tf_op jit(solution)/shard_map/ppermute | solution.py:319

commit v5 on v4

--- a/solution.py
+++ b/solution.py
@@ -10,7 +10,7 @@
 F32 = jnp.float32
 BF16 = jnp.bfloat16
 TILE = 128
-CHUNKS = 4
+PARTS = (4, 8, 4)
 VMEM_LIMIT = 48 * 2**20
 
 
@@ -169,56 +169,59 @@
     )(a, r)
 
 
-def first_body(
-    half, steps, t_ref, diag_ref, near_ref, far_ref, column_ref, row_ref, first_ref, a_out, b_out, p_out, m_work
-):
-    n = 2 * half
-    q = half // 2
+def tile_block(q, i, j):
+    return (slice(i * q, (i + 1) * q), slice(j * q, (j + 1) * q))
+
+
+def put_sibling(m_ref, ref, base, mine):
+    q = ref.shape[1]
+    other = 2 - base
+
+    def put(i, j, at):
+        value = ref[at * q : (at + 1) * q, :]
+        m_ref[tile_block(q, i, j)] = value
+        if i != j:
+            m_ref[tile_block(q, j, i)] = value.T
+
+    put(base, base, 0)
+    put(base, base + 1, 1)
+    put(base + 1, base + 1, 2)
+    put(base, other + 1, 3)
+    sender = mine if base == 0 else 1 - mine
+
+    @pl.when(sender == 0)
+    def _():
+        put(base, other, 4)
+
+    @pl.when(sender != 0)
+    def _():
+        put(base + 1, other + 1, 4)
+
+
+def prepare_body(half, t_ref, early_ref, near_ref, column_ref, first_ref, a_out, m_out, p_out):
+    n, q = 2 * half, half // 2
     width = t_ref.shape[1] - n
     mine = first_ref[0]
-
-    def block(i, j):
-        return (slice(i * q, (i + 1) * q), slice(j * q, (j + 1) * q))
-
-    def part(ref, i):
-        return ref[i * q : (i + 1) * q, :]
-
-    def put(i, j, value):
-        m_work[block(i, j)] = value
-        if i != j:
-            m_work[block(j, i)] = value.T
-
-    for base, ref in ((0, near_ref), (2, far_ref)):
-        put(base, base, part(ref, 0))
-        put(base, base + 1, part(ref, 1))
-        put(base + 1, base + 1, part(ref, 2))
-    put(0, 3, part(near_ref, 3))
-    put(2, 1, part(far_ref, 3))
-
-    @pl.when(mine == 0)
-    def _():
-        put(0, 2, part(near_ref, 4))
-        put(3, 1, part(far_ref, 4))
-
-    @pl.when(mine != 0)
-    def _():
-        put(1, 3, part(near_ref, 4))
-        put(2, 0, part(far_ref, 4))
-
-    same = column_ref[...] == row_ref[...]
-    onehot = jnp.where(same, 1.0, 0.0).astype(BF16)
-    p_out[...] = onehot
-    moved = pick_right(m_work[...], onehot, ((1,), (1,)))
+    put_sibling(m_out, near_ref, 0, mine)
+    row = jnp.concatenate([near_ref[5 * q + i : 5 * q + i + 1, :] for i in range(n // q)], axis=1)
+    p_out[...] = jnp.where(column_ref[...] == row, 1.0, 0.0).astype(BF16)
     here = pl.ds(pl.multiple_of(width + mine * half, half), half)
     there = pl.ds(pl.multiple_of(width + (1 - mine) * half, half), half)
     a_out[0:half, 0:half] = t_ref[:, here]
     a_out[0:half, half:n] = t_ref[:, there]
-    a_out[block(2, 2)] = part(diag_ref, 0)
-    a_out[block(2, 3)] = part(diag_ref, 1)
-    a_out[block(3, 3)] = part(diag_ref, 2)
+    a_out[tile_block(q, 2, 2)] = early_ref[0:q, :]
+    a_out[tile_block(q, 2, 3)] = early_ref[q : 2 * q, :]
+    a_out[tile_block(q, 3, 3)] = early_ref[2 * q : 3 * q, :]
+
+
+def first_body(steps, a_in, m_in, p_ref, far_ref, first_ref, a_out, b_out, m_work):
+    n = a_in.shape[0]
+    m_work[...] = m_in[...]
+    put_sibling(m_work, far_ref, 2, first_ref[0])
+    moved = pick_right(m_work[...], p_ref[...], ((1,), (1,)))
     for i in range(n // TILE):
         rows, later = slice(i * TILE, (i + 1) * TILE), slice(i * TILE, n)
-        a_out[rows, later] = a_out[rows, later] + pick_left(onehot[rows, :], moved[:, later], ((1,), (0,)))
+        a_out[rows, later] = a_in[rows, later] + pick_left(p_ref[rows, :], moved[:, later], ((1,), (0,)))
     top = b_out.shape[0]
     on_diagonal = [lax.broadcasted_iota(jnp.int32, (top, top), axis) for axis in (0, 1)]
     b_out[...] = jnp.where(on_diagonal[0] == on_diagonal[1], 1.0, 0.0).astype(F32)
@@ -267,7 +270,7 @@
     left = jnp.concatenate([t_ref[:, block], other_ref[:, block]], axis=0)
     own_ref[...] = ext_ref[...] - three_pass(left, g, ((0,), (0,)))
     target = lax.broadcasted_iota(jnp.int32, (half, n), 0) + mine * half
-    onehot = jnp.where(row_ref[...] == target, 1.0, 0.0).astype(BF16)
+    onehot = jnp.where(row_ref[...].astype(jnp.int32) == target, 1.0, 0.0).astype(BF16)
     sol_ref[...] = -pick_left(onehot, g, ((1,), (0,)))
     cross_ref[...] = cross_terms(h_ref, 0, parts)
 
@@ -278,22 +281,27 @@
     out_ref[...] = -(partial_ref[...] + cross_terms(h_ref, at, parts))
 
 
-def pack_iface_body(half, width, t_ref, first_ref, pack_ref, early_ref):
-    q = half // 2
+def pack_iface_body(half, width, t_ref, map_ref, first_ref, pack_ref, early_ref, row_ref, column_ref):
+    q, n = half // 2, 2 * half
     mine = first_ref[0]
     here, there = width + mine * half, width + (1 - mine) * half
 
     def cut(row, column):
         return t_ref[pl.ds(pl.multiple_of(row, q), q), pl.ds(pl.multiple_of(column, q), q)]
 
-    for ref in (pack_ref, early_ref):
-        ref[0:q, :] = cut(0, here)
-        ref[q : 2 * q, :] = cut(0, here + q)
-        ref[2 * q : 3 * q, :] = cut(q, here + q)
-    pack_ref[3 * q : 4 * q, :] = cut(0, there + q)
-    pack_ref[4 * q : 5 * q, :] = cut(mine * q, there + mine * q)
+    diagonal = [cut(0, here), cut(0, here + q), cut(q, here + q)]
+    for i, block in enumerate([*diagonal, cut(0, there + q), cut(mine * q, there + mine * q)]):
+        pack_ref[i * q : (i + 1) * q, :] = block
+    for i, block in enumerate(diagonal):
+        early_ref[i * q : (i + 1) * q, :] = block
     for at, rows, columns in early_blocks(3 * q, early_ref.shape[0], q, width):
         early_ref[at : at + rows, :] = t_ref[0:rows, columns]
+    spans = [pl.ds(pl.multiple_of(x * half, half), half) for x in (mine, 1 - mine)]
+    row = jnp.concatenate([map_ref[:, span] for span in spans], axis=1).astype(F32)
+    row_ref[...] = row
+    column_ref[...] = jnp.broadcast_to(row, (8, n)).T[:, 0:1]
+    parts = [row[:, i * q : (i + 1) * q] for i in range(n // q)]
+    pack_ref[5 * q :, :] = jnp.concatenate(parts + parts, axis=0)[0:8, :]
 
 
 def early_blocks(start, end, q, width):
@@ -340,34 +348,35 @@
     vmem, smem = pltpu.VMEM, pltpu.SMEM
     mine = lax.axis_index("sib").astype(jnp.int32)
     first = mine.reshape(1)
-    other_map = sibling(iface_map)
     early_rows = half * 5 // 8
-    packed, early = kernel(
+    packed, early, own_row, column = kernel(
         functools.partial(pack_iface_body, half, width),
-        (f(5 * q, q), f(3 * q + early_rows * width // q, q)),
-        [vmem, smem],
-    )(t_int, first)
+        (f(5 * q + 8, q), f(3 * q + early_rows * width // q, q), f(1, n), f(n, 1)),
+        [vmem, vmem, smem],
+    )(t_int, iface_map, first)
     near = sibling(packed)
     early_other = across(early)
     far = across(near)
     late, *chunks = kernel(
-        pack_outer_body, [f(half - early_rows, width)] + [f(half // CHUNKS, width)] * CHUNKS, [vmem]
+        pack_outer_body, [f(half - early_rows, width)] + [f(half * part // 16, width) for part in PARTS], [vmem]
     )(t_int)
     late, _ = lax.optimization_barrier((late, far))
     late_other = across(late)
-    *chunks, _, other_map = lax.optimization_barrier((*chunks, near, other_map))
+    *chunks, _ = lax.optimization_barrier((*chunks, near))
     near_r = [sibling(chunk) for chunk in chunks]
-    rolled = lambda m: lax.dynamic_slice(jnp.concatenate([m, m], axis=1), (0, mine * half), (1, n))
-    own_row, other_row = rolled(iface_map), rolled(other_map)
-
+    a, m, onehot = kernel(
+        functools.partial(prepare_body, half),
+        (f(n, n), f(n, n), jax.ShapeDtypeStruct((n, n), BF16)),
+        [vmem] * 4 + [smem],
+    )(t_int, early_other, near, column, first)
     top = tiles // 2 * TILE
-    a, b, onehot = kernel(
-        functools.partial(first_body, half, range(tiles // 2)),
-        (f(n, n), f(top, top), jax.ShapeDtypeStruct((n, n), BF16)),
-        [vmem] * 6 + [smem],
+    a, b = kernel(
+        functools.partial(first_body, range(tiles // 2)),
+        (f(n, n), f(top, top)),
+        [vmem] * 4 + [smem],
         [pltpu.VMEM((n, n), F32)],
         10e9,
-    )(t_int, early_other, near, far, own_row.reshape(n, 1), other_row, first)
+    )(a, m, onehot, far, first)
     a, b, near_r[0] = lax.optimization_barrier((a, b, near_r[0]))
     far_r = [across(near_r[0])]
     a, g, other = kernel(
@@ -382,8 +391,8 @@
     g = kernel(
         functools.partial(last_body, range(tiles - 1, tiles)), f(n, width), [vmem] * 2, [pltpu.VMEM((n, n), F32)], 5e9
     )(a, g)
-    g, *near_r[2:] = lax.optimization_barrier((g, *near_r[2:]))
-    far_r += [across(x) for x in near_r[2:]]
+    g, near_r[2] = lax.optimization_barrier((g, near_r[2]))
+    far_r.append(across(near_r[2]))
     parts = [*near_r, *far_r[:2]]
     own_map, solution_op, h, partial = kernel(
         functools.partial(output_body, half),
@@ -392,7 +401,7 @@
         (),
         4e9,
     )(g, onehot, t_int, other, t_ext, own_row, first, *parts)
-    cross_map = kernel(cross_body, f(half, width), [vmem] * (CHUNKS))(h, partial, *far_r[2:])
+    cross_map = kernel(cross_body, f(half, width), [vmem] * 3)(h, partial, far_r[2])
     return own_map[None], cross_map[None], solution_op[None]
 
 

time: 61.8 us -> 59.4 us (0.961)
  starting transfers between devices: 15.9 us -> 14.1 us
  local copies, waits for them, and re-layouts: 2.68 us -> 1.91 us
    ppermute x7 -> x6, waiting for transfers between devices: 4.23 us -> 5.88 us  [across(): return lax.ppermute(x, 'sib', [(0, 1), (1, 0)])]
    ppermute x7 -> x6, starting transfers between devices: 8.17 us -> 6.97 us  [across(): return lax.ppermute(x, 'sib', [(0, 1), (1, 0)])]
    ppermute x6 -> x4, waiting for transfers between devices: 15.5 us -> 14.3 us  [sibling(): return lax.ppermute(x, 'leaf', [(i, i ^ size // 2) for i in range(size)])]
    unnamed x12 -> x8, local copies, waits for them, and re-layouts: 2.54 us -> 1.91 us
    ppermute x6 -> x4, starting transfers between devices: 7.76 us -> 7.16 us  [sibling(): return lax.ppermute(x, 'leaf', [(i, i ^ size // 2) for i in range(size)])]
    pallas_call x4 -> x5, Pallas kernels: 10.6 us -> 10.6 us  [the longest x1 8.85 us: two_shards(): kernel(functools.partial(first_body, range(tiles // 2)), (f(n, n), f(top,...]
  transfers between devices with their start and end apart: 13 -> 10, of which waited for: 5 -> 5; matrix products, arithmetic and copies ran while one was open for 0% -> 0% of each run, Pallas kernels for 34% -> 35%
where the time goes in v5:
time: 59.4 us; the launch traced here: 59.2 us
  Pallas kernels  22.3 us (38%)
  waiting for transfers between devices  20.1 us (34%)
  starting transfers between devices  14.1 us (24%)
  local copies, waits for them, and re-layouts  1.91 us (3%)
  between operations  0.73 us (1%)
    ppermute x4, waiting for transfers between devices, sibling(): return lax.ppermute(x, 'leaf', [(i, i ^ size // 2) for i in range(size)])  14.3 us
    pallas_call x1, Pallas kernels, two_shards(): kernel(functools.partial(first_body, range(tiles // 2)), (f(n, n), f(top,...  8.85 us
    ppermute x4, starting transfers between devices, sibling(): return lax.ppermute(x, 'leaf', [(i, i ^ size // 2) for i in range(size)])  7.16 us
    ppermute x6, starting transfers between devices, across(): return lax.ppermute(x, 'sib', [(0, 1), (1, 0)])  6.97 us
    ppermute x6, waiting for transfers between devices, across(): return lax.ppermute(x, 'sib', [(0, 1), (1, 0)])  5.88 us
    pallas_call x1, Pallas kernels, two_shards(): kernel(functools.partial(middle_body, range(tiles // 2, tiles - 1)), (f(n...  5.04 us
    pallas_call x1, Pallas kernels, two_shards(): kernel(functools.partial(last_body, range(tiles - 1, tiles)), f(n, width)...  4.13 us
    pallas_call x1, Pallas kernels, two_shards(): kernel(functools.partial(output_body, half), (f(half, width), f(half, wid...  2.54 us
  transfers between devices with their start and end apart: 10, of which 5 were waited for; matrix products, arithmetic and copies ran while one was open for 0% of the time, Pallas kernels for 35%

profile of v5, /device:TPU:0, one launch (start us, length us, event | category | flops | bytes accessed | tf_op | source)
XLA Modules:
  0.0 59.2 jit_solution(9081592958040299345)
XLA Ops:
  0.6 0.7 %copy-done.2 = s32[1,512]{1,0:T(1,128)S(1)} copy-done((s32[1,512]{1,0:T(1,128)S(1)}, s32[1,512]{1,0:T(1,128)}, u32[]{:S(2)}) %copy-start.2) | copy-done | bytes 2072
  1.3 1.2 %copy-done = f32[1,256,1024]{2,1,0:T(8,128)S(1)} copy-done((f32[1,256,1024]{2,1,0:T(8,128)S(1)}, f32[1,256,1024]{2,1,0:T(8,128)}, u32[]{:S(2)}) %copy-start) | copy-done | bytes 1048600
  2.5 0.2 shard_map.58
  2.7 4.1 %collective-permute-start.1 = (f32[648,128]{1,0:T(8,128)S(1)}, f32[648,128]{1,0:T(8,128)S(1)}, u32[]{:S(2)}, u32[]{:S(2)}) collective-permute-start(f32[648,128]{1,0:T(8,128)S(1)} %get-tuple-element.36), channel_id=1, source_target_pairs={{0,8},{1,9},{2,10},{3,11},{4,12},{5,13},{6,14},{7,15},{8,0},{9,1},... | collective-permute-start | bytes 995336 | tf_op jit(solution)/shard_map/ppermute | solution.py:323
  6.8 1.5 %collective-permute-start = (f32[1024,128]{1,0:T(8,128)S(1)}, f32[1024,128]{1,0:T(8,128)S(1)}, u32[]{:S(2)}, u32[]{:S(2)}) collective-permute-start(f32[1024,128]{1,0:T(8,128)S(1)} %get-tuple-element.35), channel_id=1, source_target_pairs={{0,16},{16,0},{1,17},{17,1},{2,18},{18,2},{3,19},{19,3},{4,20},{20... | collective-permute-start | bytes 1572872 | tf_op jit(solution)/shard_map/ppermute | solution.py:327
  8.3 13.4 %collective-permute-done.1.near_ref = f32[648,128]{1,0:T(8,128)S(1)} collective-permute-done((f32[648,128]{1,0:T(8,128)S(1)}, f32[648,128]{1,0:T(8,128)S(1)}, u32[]{:S(2)}, u32[]{:S(2)}) %collective-permute-start.1) | collective-permute-done | bytes 331808 | tf_op jit(solution)/shard_map/ppermute | solution.py:323
  21.7 1.5 %collective-permute-start.2 = (f32[648,128]{1,0:T(8,128)S(1)}, f32[648,128]{1,0:T(8,128)S(1)}, u32[]{:S(2)}, u32[]{:S(2)}) collective-permute-start(f32[648,128]{1,0:T(8,128)S(1)} %collective-permute-done.1.near_ref), channel_id=1, source_target_pairs={{0,16},{16,0},{1,17},{17,1},{2,18},{18,2},{3,19},{19,3},{4,20},{20... | collective-permute-start | bytes 995336 | tf_op jit(solution)/shard_map/ppermute | solution.py:327
  23.3 0.1 collective-permute-start.3
  23.4 2.9 %collective-permute-start.5 = (f32[128,512]{1,0:T(8,128)S(1)}, f32[128,512]{1,0:T(8,128)S(1)}, u32[]{:S(2)}, u32[]{:S(2)}) collective-permute-start(f32[128,512]{1,0:T(8,128)S(1)} %get-tuple-element.53), channel_id=1, source_target_pairs={{0,8},{1,9},{2,10},{3,11},{4,12},{5,13},{6,14},{7,15},{8,0},{9,1},... | collective-permute-start | bytes 786440 | tf_op jit(solution)/shard_map/ppermute | solution.py:323
  26.3 0.1 collective-permute-start.6
  26.4 0.3 shard_map.59
  26.7 4.0 %collective-permute-done.2.far_ref = f32[648,128]{1,0:T(8,128)S(1)} collective-permute-done((f32[648,128]{1,0:T(8,128)S(1)}, f32[648,128]{1,0:T(8,128)S(1)}, u32[]{:S(2)}, u32[]{:S(2)}) %collective-permute-start.2) | collective-permute-done | bytes 331808 | tf_op jit(solution)/shard_map/ppermute | solution.py:327
  30.7 1.2 %collective-permute-start.4 = (f32[96,512]{1,0:T(8,128)S(1)}, f32[96,512]{1,0:T(8,128)S(1)}, u32[]{:S(2)}, u32[]{:S(2)}) collective-permute-start(f32[96,512]{1,0:T(8,128)S(1)} %get-tuple-element.50), channel_id=1, source_target_pairs={{0,16},{16,0},{1,17},{17,1},{2,18},{18,2},{3,19},{19,3},{4,20},{20... | collective-permute-start | bytes 589832 | tf_op jit(solution)/shard_map/ppermute | solution.py:327
  32.0 8.8 %shard_map.60 = (f32[512,512]{1,0:T(8,128)S(1)}, f32[256,256]{1,0:T(8,128)S(1)}) custom-call(f32[512,512]{1,0:T(8,128)S(1)} %get-tuple-element.38.a_in, f32[512,512]{1,0:T(8,128)S(1)} %get-tuple-element.39.m_in, bf16[512,512]{1,0:T(8,128)(2,1)S(1)} %get-tuple-element.40.p_ref, f32[648,128]{1,0:T(8,128)S(1)} %collective-permute-done.2.far_ref, s32[1]{0:T(128)} %bitcast.1.first_ref), custom_call_target="tpu_custom_call" | custom-call | flops 10000000000 | bytes 1048576 | tf_op jit(solution)/shard_map/pallas_call | solution.py:373
  40.8 0.8 %collective-permute-done.3.refs_0_ = f32[64,512]{1,0:T(8,128)S(1)} collective-permute-done((f32[64,512]{1,0:T(8,128)S(1)}, f32[64,512]{1,0:T(8,128)S(1)}, u32[]{:S(2)}, u32[]{:S(2)}) %collective-permute-start.3) | collective-permute-done | bytes 131104 | tf_op jit(solution)/shard_map/ppermute | solution.py:323
  41.7 0.5 collective-permute-start.7
  42.2 5.0 %shard_map.62 = (f32[512,512]{1,0:T(8,128)S(1)}, f32[512,512]{1,0:T(8,128)S(1)}, f32[256,512]{1,0:T(8,128)S(1)}) custom-call(f32[512,512]{1,0:T(8,128)S(1)} %get-tuple-element.47.a_in, f32[256,256]{1,0:T(8,128)S(1)} %get-tuple-element.48.b_ref, f32[256,1024]{1,0:T(8,128)S(1)} %bitcast.9, f32[1024,128]{1,0:T(8,128)S(1)} %collective-permute-done.early_ref, ...), custom_call_target="tpu_custom_call" | custom-call | flops 5000000000 | bytes 1048576 | tf_op jit(solution)/shard_map/pallas_call | solution.py:382
  47.3 1.6 %collective-permute-start.8 = (f32[128,512]{1,0:T(8,128)S(1)}, f32[128,512]{1,0:T(8,128)S(1)}, u32[]{:S(2)}, u32[]{:S(2)}) collective-permute-start(f32[128,512]{1,0:T(8,128)S(1)} %collective-permute-done.5.refs_1_), channel_id=1, source_target_pairs={{0,16},{16,0},{1,17},{17,1},{2,18},{18,2},{3,19},{19,3},{4,20},{20... | collective-permute-start | bytes 786440 | tf_op jit(solution)/shard_map/ppermute | solution.py:327
  48.8 4.1 %shard_map.63.g_ref = f32[512,512]{1,0:T(8,128)S(1)} custom-call(f32[512,512]{1,0:T(8,128)S(1)} %get-tuple-element.54.a_ref, f32[512,512]{1,0:T(8,128)S(1)} %get-tuple-element.55.g_in), custom_call_target="tpu_custom_call" | custom-call | flops 5000000000 | bytes 1048576 | tf_op jit(solution)/shard_map/pallas_call | solution.py:391
  53.0 0.6 %collective-permute-start.9 = (f32[64,512]{1,0:T(8,128)S(1)}, f32[64,512]{1,0:T(8,128)S(1)}, u32[]{:S(2)}, u32[]{:S(2)}) collective-permute-start(f32[64,512]{1,0:T(8,128)S(1)} %collective-permute-done.6.refs_2_), channel_id=1, source_target_pairs={{0,16},{16,0},{1,17},{17,1},{2,18},{18,2},{3,19},{19,3},{4,20},{20... | collective-permute-start | bytes 393224 | tf_op jit(solution)/shard_map/ppermute | solution.py:327
  53.6 1.5 %collective-permute-done.8.refs_4_ = f32[128,512]{1,0:T(8,128)S(1)} collective-permute-done((f32[128,512]{1,0:T(8,128)S(1)}, f32[128,512]{1,0:T(8,128)S(1)}, u32[]{:S(2)}, u32[]{:S(2)}) %collective-permute-start.8) | collective-permute-done | bytes 262176 | tf_op jit(solution)/shard_map/ppermute | solution.py:327
  55.1 2.5 %shard_map.64 = (f32[256,512]{1,0:T(8,128)}, f32[256,512]{1,0:T(8,128)}, f32[512,256]{1,0:T(8,128)S(1)}, f32[256,512]{1,0:T(8,128)S(1)}) custom-call(f32[512,512]{1,0:T(8,128)S(1)} %shard_map.63.g_ref, bf16[512,512]{1,0:T(8,128)(2,1)S(1)} %get-tuple-element.40.p_ref, f32[256,1024]{1,0:T(8,128)S(1)} %bitcast.10, f32[256,512]{1,0:T(8,128)S(1)} %get-tuple-element.58.other_ref, ...), custom_call_target="tpu_custom_call" | custom-call | flops 4000000000 | bytes 1048576 | tf_op jit(solution)/shard_map/pallas_call | solution.py:397
  57.7 0.4 collective-permute-done.9.refs_0_
  58.0 1.2 %shard_map.65 = f32[256,512]{1,0:T(8,128)} custom-call(f32[512,256]{1,0:T(8,128)S(1)} %get-tuple-element.64.h_ref, f32[256,512]{1,0:T(8,128)S(1)} %get-tuple-element.65.partial_ref, f32[64,512]{1,0:T(8,128)S(1)} %collective-permute-done.9.refs_0_), custom_call_target="tpu_custom_call" | custom-call | flops 100000000 | bytes 1048576 | tf_op jit(solution)/shard_map/pallas_call | solution.py:404
  (12 shorter events, 0.1 us)
Async XLA Ops:
  0.6 0.7 %copy-start.2 = (s32[1,512]{1,0:T(1,128)S(1)}, s32[1,512]{1,0:T(1,128)}, u32[]{:S(2)}) copy-start(s32[1,512]{1,0:T(1,128)} %map_ref.1) | copy-start | bytes 6148
  1.3 1.2 %copy-start = (f32[1,256,1024]{2,1,0:T(8,128)S(1)}, f32[1,256,1024]{2,1,0:T(8,128)}, u32[]{:S(2)}) copy-start(f32[1,256,1024]{2,1,0:T(8,128)} %param.3) | copy-start | bytes 3145732
  2.7 19.0 %collective-permute-start.1 = (f32[648,128]{1,0:T(8,128)S(1)}, f32[648,128]{1,0:T(8,128)S(1)}, u32[]{:S(2)}, u32[]{:S(2)}) collective-permute-start(f32[648,128]{1,0:T(8,128)S(1)} %get-tuple-element.36), channel_id=1, source_target_pairs={{0,8},{1,9},{2,10},{3,11},{4,12},{5,13},{6,14},{7,15},{8,0},{9,1},... | collective-permute-start | bytes 995336 | tf_op jit(solution)/shard_map/ppermute | solution.py:323
  6.8 19.6 %collective-permute-start = (f32[1024,128]{1,0:T(8,128)S(1)}, f32[1024,128]{1,0:T(8,128)S(1)}, u32[]{:S(2)}, u32[]{:S(2)}) collective-permute-start(f32[1024,128]{1,0:T(8,128)S(1)} %get-tuple-element.35), channel_id=1, source_target_pairs={{0,16},{16,0},{1,17},{17,1},{2,18},{18,2},{3,19},{19,3},{4,20},{20... | collective-permute-start | bytes 1572872 | tf_op jit(solution)/shard_map/ppermute | solution.py:327
  21.7 9.0 %collective-permute-start.2 = (f32[648,128]{1,0:T(8,128)S(1)}, f32[648,128]{1,0:T(8,128)S(1)}, u32[]{:S(2)}, u32[]{:S(2)}) collective-permute-start(f32[648,128]{1,0:T(8,128)S(1)} %collective-permute-done.1.near_ref), channel_id=1, source_target_pairs={{0,16},{16,0},{1,17},{17,1},{2,18},{18,2},{3,19},{19,3},{4,20},{20... | collective-permute-start | bytes 995336 | tf_op jit(solution)/shard_map/ppermute | solution.py:327
  23.3 18.3 %collective-permute-start.3 = (f32[64,512]{1,0:T(8,128)S(1)}, f32[64,512]{1,0:T(8,128)S(1)}, u32[]{:S(2)}, u32[]{:S(2)}) collective-permute-start(f32[64,512]{1,0:T(8,128)S(1)} %get-tuple-element.46), channel_id=1, source_target_pairs={{0,8},{1,9},{2,10},{3,11},{4,12},{5,13},{6,14},{7,15},{8,0},{9,1},... | collective-permute-start | bytes 393224 | tf_op jit(solution)/shard_map/ppermute | solution.py:323
  23.4 23.9 %collective-permute-start.5 = (f32[128,512]{1,0:T(8,128)S(1)}, f32[128,512]{1,0:T(8,128)S(1)}, u32[]{:S(2)}, u32[]{:S(2)}) collective-permute-start(f32[128,512]{1,0:T(8,128)S(1)} %get-tuple-element.53), channel_id=1, source_target_pairs={{0,8},{1,9},{2,10},{3,11},{4,12},{5,13},{6,14},{7,15},{8,0},{9,1},... | collective-permute-start | bytes 786440 | tf_op jit(solution)/shard_map/ppermute | solution.py:323
  26.3 26.7 %collective-permute-start.6 = (f32[64,512]{1,0:T(8,128)S(1)}, f32[64,512]{1,0:T(8,128)S(1)}, u32[]{:S(2)}, u32[]{:S(2)}) collective-permute-start(f32[64,512]{1,0:T(8,128)S(1)} %get-tuple-element.56), channel_id=1, source_target_pairs={{0,8},{1,9},{2,10},{3,11},{4,12},{5,13},{6,14},{7,15},{8,0},{9,1},... | collective-permute-start | bytes 393224 | tf_op jit(solution)/shard_map/ppermute | solution.py:323
  30.7 11.5 %collective-permute-start.4 = (f32[96,512]{1,0:T(8,128)S(1)}, f32[96,512]{1,0:T(8,128)S(1)}, u32[]{:S(2)}, u32[]{:S(2)}) collective-permute-start(f32[96,512]{1,0:T(8,128)S(1)} %get-tuple-element.50), channel_id=1, source_target_pairs={{0,16},{16,0},{1,17},{17,1},{2,18},{18,2},{3,19},{19,3},{4,20},{20... | collective-permute-start | bytes 589832 | tf_op jit(solution)/shard_map/ppermute | solution.py:327
  32.0 10.2 %copy-start.1 = (f32[1,256,1024]{2,1,0:T(8,128)S(1)}, f32[1,256,1024]{2,1,0:T(8,128)}, u32[]{:S(2)}) copy-start(f32[1,256,1024]{2,1,0:T(8,128)} %param.3) | copy-start | bytes 3145732
  41.7 11.9 %collective-permute-start.7 = (f32[64,512]{1,0:T(8,128)S(1)}, f32[64,512]{1,0:T(8,128)S(1)}, u32[]{:S(2)}, u32[]{:S(2)}) collective-permute-start(f32[64,512]{1,0:T(8,128)S(1)} %collective-permute-done.3.refs_0_), channel_id=1, source_target_pairs={{0,16},{16,0},{1,17},{17,1},{2,18},{18,2},{3,19},{19,3},{4,20},{20... | collective-permute-start | bytes 393224 | tf_op jit(solution)/shard_map/ppermute | solution.py:327
  47.3 7.9 %copy-start.3 = (f32[1,256,512]{2,1,0:T(8,128)S(1)}, f32[1,256,512]{2,1,0:T(8,128)}, u32[]{:S(2)}) copy-start(f32[1,256,512]{2,1,0:T(8,128)} %param.4) | copy-start | bytes 1572868
  47.3 7.8 %collective-permute-start.8 = (f32[128,512]{1,0:T(8,128)S(1)}, f32[128,512]{1,0:T(8,128)S(1)}, u32[]{:S(2)}, u32[]{:S(2)}) collective-permute-start(f32[128,512]{1,0:T(8,128)S(1)} %collective-permute-done.5.refs_1_), channel_id=1, source_target_pairs={{0,16},{16,0},{1,17},{17,1},{2,18},{18,2},{3,19},{19,3},{4,20},{20... | collective-permute-start | bytes 786440 | tf_op jit(solution)/shard_map/ppermute | solution.py:327
  53.0 5.0 %collective-permute-start.9 = (f32[64,512]{1,0:T(8,128)S(1)}, f32[64,512]{1,0:T(8,128)S(1)}, u32[]{:S(2)}, u32[]{:S(2)}) collective-permute-start(f32[64,512]{1,0:T(8,128)S(1)} %collective-permute-done.6.refs_2_), channel_id=1, source_target_pairs={{0,16},{16,0},{1,17},{17,1},{2,18},{18,2},{3,19},{19,3},{4,20},{20... | collective-permute-start | bytes 393224 | tf_op jit(solution)/shard_map/ppermute | solution.py:327

commit v6 on v5

--- a/solution.py
+++ b/solution.py
@@ -173,51 +173,70 @@
     return (slice(i * q, (i + 1) * q), slice(j * q, (j + 1) * q))
 
 
-def put_sibling(m_ref, ref, base, mine):
-    q = ref.shape[1]
+def put_sibling(m_ref, diag_ref, side_ref, base, mine):
+    q = side_ref.shape[1]
     other = 2 - base
 
-    def put(i, j, at):
-        value = ref[at * q : (at + 1) * q, :]
+    def put(i, j, value):
         m_ref[tile_block(q, i, j)] = value
         if i != j:
             m_ref[tile_block(q, j, i)] = value.T
 
-    put(base, base, 0)
-    put(base, base + 1, 1)
-    put(base + 1, base + 1, 2)
-    put(base, other + 1, 3)
+    first, cross, second = unpack_diagonal(diag_ref)
+    put(base, base, first)
+    put(base, base + 1, cross)
+    put(base + 1, base + 1, second)
+    put(base, other + 1, side_ref[0:q, :])
     sender = mine if base == 0 else 1 - mine
 
     @pl.when(sender == 0)
     def _():
-        put(base, other, 4)
+        put(base, other, side_ref[q : 2 * q, :])
 
     @pl.when(sender != 0)
     def _():
-        put(base + 1, other + 1, 4)
-
-
-def prepare_body(half, t_ref, early_ref, near_ref, column_ref, first_ref, a_out, m_out, p_out):
+        put(base + 1, other + 1, side_ref[q : 2 * q, :])
+
+
+def pack_diagonal(first, cross, second):
+    q = first.shape[0]
+    e = q // 2
+    lane = lax.broadcasted_iota(jnp.int32, (e, q), 1)
+    corners = jnp.where(lane < e, second[0:e, :], first[e:, :])
+    return [cross, first[0:e, :], second[e:, :], corners]
+
+
+def unpack_diagonal(ref):
+    q = ref.shape[1]
+    e = q // 2
+    upper, lower, corners = ref[q : q + e, :], ref[q + e : 2 * q, :], ref[2 * q : 2 * q + e, :]
+    first = jnp.concatenate([upper, jnp.concatenate([upper.T[e:, :], corners[:, e:]], axis=1)], axis=0)
+    second = jnp.concatenate([jnp.concatenate([corners[:, 0:e], lower.T[0:e, :]], axis=1), lower], axis=0)
+    return first, ref[0:q, :], second
+
+
+def prepare_body(half, t_ref, early_ref, near_ref, side_ref, column_ref, first_ref, a_out, m_out, p_out):
     n, q = 2 * half, half // 2
     width = t_ref.shape[1] - n
     mine = first_ref[0]
-    put_sibling(m_out, near_ref, 0, mine)
-    row = jnp.concatenate([near_ref[5 * q + i : 5 * q + i + 1, :] for i in range(n // q)], axis=1)
+    put_sibling(m_out, near_ref, side_ref, 0, mine)
+    at = 5 * q // 2
+    row = jnp.concatenate([near_ref[at + i : at + i + 1, :] for i in range(n // q)], axis=1)
     p_out[...] = jnp.where(column_ref[...] == row, 1.0, 0.0).astype(BF16)
     here = pl.ds(pl.multiple_of(width + mine * half, half), half)
     there = pl.ds(pl.multiple_of(width + (1 - mine) * half, half), half)
     a_out[0:half, 0:half] = t_ref[:, here]
     a_out[0:half, half:n] = t_ref[:, there]
-    a_out[tile_block(q, 2, 2)] = early_ref[0:q, :]
-    a_out[tile_block(q, 2, 3)] = early_ref[q : 2 * q, :]
-    a_out[tile_block(q, 3, 3)] = early_ref[2 * q : 3 * q, :]
-
-
-def first_body(steps, a_in, m_in, p_ref, far_ref, first_ref, a_out, b_out, m_work):
+    first, cross, second = unpack_diagonal(early_ref)
+    a_out[tile_block(q, 2, 2)] = first
+    a_out[tile_block(q, 2, 3)] = cross
+    a_out[tile_block(q, 3, 3)] = second
+
+
+def first_body(steps, a_in, m_in, p_ref, far_ref, side_ref, first_ref, a_out, b_out, m_work):
     n = a_in.shape[0]
     m_work[...] = m_in[...]
-    put_sibling(m_work, far_ref, 2, first_ref[0])
+    put_sibling(m_work, far_ref, side_ref, 2, first_ref[0])
     moved = pick_right(m_work[...], p_ref[...], ((1,), (1,)))
     for i in range(n // TILE):
         rows, later = slice(i * TILE, (i + 1) * TILE), slice(i * TILE, n)
@@ -228,15 +247,11 @@
     eliminate(a_out, b_out, steps)
 
 
-def middle_body(steps, a_in, b_ref, t_ref, early_ref, late_ref, a_out, g_out, other_out):
-    top, half, q = b_ref.shape[0], t_ref.shape[0], early_ref.shape[1]
-    width = g_out.shape[1]
+def middle_body(steps, a_in, b_ref, t_ref, other_ref, a_out, g_out):
+    top, half = b_ref.shape[0], t_ref.shape[0]
     a_out[...] = a_in[...]
-    for at, rows, columns in early_blocks(3 * q, early_ref.shape[0], q, width):
-        other_out[0:rows, columns] = early_ref[at : at + rows, :]
-    other_out[half - late_ref.shape[0] :, :] = late_ref[...]
-    g_out[0:half, :] = t_ref[:, 0:width]
-    g_out[half:, :] = other_out[...]
+    g_out[0:half, :] = t_ref[:, 0 : g_out.shape[1]]
+    g_out[half:, :] = other_ref[...]
     first = g_out[0:top, :]
     g_out[top:, :] = g_out[top:, :] - full(a_in[0:top, top:], first, ((0,), (0,)))
     g_out[0:top, :] = full(b_ref[...], first)
@@ -281,7 +296,7 @@
     out_ref[...] = -(partial_ref[...] + cross_terms(h_ref, at, parts))
 
 
-def pack_iface_body(half, width, t_ref, map_ref, first_ref, pack_ref, early_ref, row_ref, column_ref):
+def pack_iface_body(half, width, t_ref, map_ref, first_ref, diag_ref, side_ref, row_ref, column_ref):
     q, n = half // 2, 2 * half
     mine = first_ref[0]
     here, there = width + mine * half, width + (1 - mine) * half
@@ -289,32 +304,25 @@
     def cut(row, column):
         return t_ref[pl.ds(pl.multiple_of(row, q), q), pl.ds(pl.multiple_of(column, q), q)]
 
-    diagonal = [cut(0, here), cut(0, here + q), cut(q, here + q)]
-    for i, block in enumerate([*diagonal, cut(0, there + q), cut(mine * q, there + mine * q)]):
-        pack_ref[i * q : (i + 1) * q, :] = block
-    for i, block in enumerate(diagonal):
-        early_ref[i * q : (i + 1) * q, :] = block
-    for at, rows, columns in early_blocks(3 * q, early_ref.shape[0], q, width):
-        early_ref[at : at + rows, :] = t_ref[0:rows, columns]
+    at = 0
+    for block in pack_diagonal(cut(0, here), cut(0, here + q), cut(q, here + q)):
+        diag_ref[at : at + block.shape[0], :] = block
+        at += block.shape[0]
+    side_ref[0:q, :] = cut(0, there + q)
+    side_ref[q : 2 * q, :] = cut(mine * q, there + mine * q)
     spans = [pl.ds(pl.multiple_of(x * half, half), half) for x in (mine, 1 - mine)]
     row = jnp.concatenate([map_ref[:, span] for span in spans], axis=1).astype(F32)
     row_ref[...] = row
     column_ref[...] = jnp.broadcast_to(row, (8, n)).T[:, 0:1]
     parts = [row[:, i * q : (i + 1) * q] for i in range(n // q)]
-    pack_ref[5 * q :, :] = jnp.concatenate(parts + parts, axis=0)[0:8, :]
-
-
-def early_blocks(start, end, q, width):
-    rows = (end - start) * q // width
-    return [(start + i * rows, rows, slice(i * q, (i + 1) * q)) for i in range(width // q)]
-
-
-def pack_outer_body(t_ref, late_ref, *chunks):
-    half, width = t_ref.shape[0], late_ref.shape[1]
-    late_ref[...] = t_ref[half - late_ref.shape[0] :, 0:width]
+    diag_ref[at:, :] = jnp.concatenate(parts + parts, axis=0)[0:8, :]
+
+
+def pack_outer_body(t_ref, outer_ref, *chunks):
+    outer_ref[...] = t_ref[:, 0 : outer_ref.shape[1]]
     at = 0
     for chunk in chunks:
-        chunk[...] = t_ref[at : at + chunk.shape[0], 0:width]
+        chunk[...] = t_ref[at : at + chunk.shape[0], 0 : chunk.shape[1]]
         at += chunk.shape[0]
 
 
@@ -348,44 +356,43 @@
     vmem, smem = pltpu.VMEM, pltpu.SMEM
     mine = lax.axis_index("sib").astype(jnp.int32)
     first = mine.reshape(1)
-    early_rows = half * 5 // 8
-    packed, early, own_row, column = kernel(
+    diag, side, own_row, column = kernel(
         functools.partial(pack_iface_body, half, width),
-        (f(5 * q + 8, q), f(3 * q + early_rows * width // q, q), f(1, n), f(n, 1)),
+        (f(5 * q // 2 + 8, q), f(2 * q, q), f(1, n), f(n, 1)),
         [vmem, vmem, smem],
     )(t_int, iface_map, first)
-    near = sibling(packed)
-    early_other = across(early)
+    near = sibling(diag)
+    diag_other = across(diag)
     far = across(near)
-    late, *chunks = kernel(
-        pack_outer_body, [f(half - early_rows, width)] + [f(half * part // 16, width) for part in PARTS], [vmem]
+    side, diag_other = lax.optimization_barrier((side, diag_other))
+    near_side = sibling(side)
+    near, near_side = lax.optimization_barrier((near, near_side))
+    far_side = across(near_side)
+    outer, *chunks = kernel(
+        pack_outer_body, [f(half, width)] + [f(half * part // 16, width) for part in PARTS], [vmem]
     )(t_int)
-    late, _ = lax.optimization_barrier((late, far))
-    late_other = across(late)
-    *chunks, _ = lax.optimization_barrier((*chunks, near))
-    near_r = [sibling(chunk) for chunk in chunks]
+    other = across(outer)
+    leading, _ = lax.optimization_barrier((chunks[0], near_side))
+    *following, _ = lax.optimization_barrier((*chunks[1:], far))
+    near_r = [sibling(chunk) for chunk in (leading, *following)]
     a, m, onehot = kernel(
         functools.partial(prepare_body, half),
         (f(n, n), f(n, n), jax.ShapeDtypeStruct((n, n), BF16)),
-        [vmem] * 4 + [smem],
-    )(t_int, early_other, near, column, first)
+        [vmem] * 5 + [smem],
+    )(t_int, diag_other, near, near_side, column, first)
     top = tiles // 2 * TILE
     a, b = kernel(
         functools.partial(first_body, range(tiles // 2)),
         (f(n, n), f(top, top)),
-        [vmem] * 4 + [smem],
+        [vmem] * 5 + [smem],
         [pltpu.VMEM((n, n), F32)],
         10e9,
-    )(a, m, onehot, far, first)
+    )(a, m, onehot, far, far_side, first)
     a, b, near_r[0] = lax.optimization_barrier((a, b, near_r[0]))
     far_r = [across(near_r[0])]
-    a, g, other = kernel(
-        functools.partial(middle_body, range(tiles // 2, tiles - 1)),
-        (f(n, n), f(n, width), f(half, width)),
-        [vmem] * 5,
-        (),
-        5e9,
-    )(a, b, t_int, early_other, late_other)
+    a, g = kernel(
+        functools.partial(middle_body, range(tiles // 2, tiles - 1)), (f(n, n), f(n, width)), [vmem] * 4, (), 5e9
+    )(a, b, t_int, other)
     a, g, near_r[1] = lax.optimization_barrier((a, g, near_r[1]))
     far_r.append(across(near_r[1]))
     g = kernel(

time: 59.4 us -> 59.5 us (level)
  waiting for transfers between devices: 20.1 us -> 17.4 us
  starting transfers between devices: 14.1 us -> 16.6 us
    ppermute x4 -> x5, waiting for transfers between devices: 14.3 us -> 11.1 us  [sibling(): return lax.ppermute(x, 'leaf', [(i, i ^ size // 2) for i in range(size)])]
    ppermute x6 -> x7, starting transfers between devices: 6.97 us -> 8.26 us  [across(): return lax.ppermute(x, 'sib', [(0, 1), (1, 0)])]
    ppermute x4 -> x5, starting transfers between devices: 7.16 us -> 8.35 us  [sibling(): return lax.ppermute(x, 'leaf', [(i, i ^ size // 2) for i in range(size)])]
    ppermute x6 -> x7, waiting for transfers between devices: 5.88 us -> 6.31 us  [across(): return lax.ppermute(x, 'sib', [(0, 1), (1, 0)])]
  transfers between devices with their start and end apart: 10 -> 12, of which waited for: 5 -> 7; matrix products, arithmetic and copies ran while one was open for 0% -> 0% of each run, Pallas kernels for 35% -> 36%
where the time goes in v6:
time: 59.5 us; the launch traced here: 59.3 us
  Pallas kernels  22.6 us (38%)
  waiting for transfers between devices  17.4 us (29%)
  starting transfers between devices  16.6 us (28%)
  local copies, waits for them, and re-layouts  1.91 us (3%)
  between operations  0.72 us (1%)
    ppermute x5, waiting for transfers between devices, sibling(): return lax.ppermute(x, 'leaf', [(i, i ^ size // 2) for i in range(size)])  11.1 us
    pallas_call x1, Pallas kernels, two_shards(): kernel(functools.partial(first_body, range(tiles // 2)), (f(n, n), f(top,...  9 us
    ppermute x5, starting transfers between devices, sibling(): return lax.ppermute(x, 'leaf', [(i, i ^ size // 2) for i in range(size)])  8.35 us
    ppermute x7, starting transfers between devices, across(): return lax.ppermute(x, 'sib', [(0, 1), (1, 0)])  8.26 us
    ppermute x7, waiting for transfers between devices, across(): return lax.ppermute(x, 'sib', [(0, 1), (1, 0)])  6.31 us
    pallas_call x1, Pallas kernels, two_shards(): kernel(functools.partial(middle_body, range(tiles // 2, tiles - 1)), (f(n...  5.04 us
    pallas_call x1, Pallas kernels, two_shards(): kernel(functools.partial(last_body, range(tiles - 1, tiles)), f(n, width)...  4.13 us
    pallas_call x1, Pallas kernels, two_shards(): kernel(functools.partial(output_body, half), (f(half, width), f(half, wid...  2.54 us
  transfers between devices with their start and end apart: 12, of which 7 were waited for; matrix products, arithmetic and copies ran while one was open for 0% of the time, Pallas kernels for 36%

profile of v6, /device:TPU:0, one launch (start us, length us, event | category | flops | bytes accessed | tf_op | source)
XLA Modules:
  0.0 59.3 jit_solution(13408443585407436661)
XLA Ops:
  0.6 0.7 %copy-done.2 = s32[1,512]{1,0:T(1,128)S(1)} copy-done((s32[1,512]{1,0:T(1,128)S(1)}, s32[1,512]{1,0:T(1,128)}, u32[]{:S(2)}) %copy-start.2) | copy-done | bytes 2072
  1.3 1.2 %copy-done = f32[1,256,1024]{2,1,0:T(8,128)S(1)} copy-done((f32[1,256,1024]{2,1,0:T(8,128)S(1)}, f32[1,256,1024]{2,1,0:T(8,128)}, u32[]{:S(2)}) %copy-start) | copy-done | bytes 1048600
  2.7 3.0 %collective-permute-start = (f32[328,128]{1,0:T(8,128)S(1)}, f32[328,128]{1,0:T(8,128)S(1)}, u32[]{:S(2)}, u32[]{:S(2)}) collective-permute-start(f32[328,128]{1,0:T(8,128)S(1)} %get-tuple-element.38), channel_id=1, source_target_pairs={{0,16},{16,0},{1,17},{17,1},{2,18},{18,2},{3,19},{19,3},{4,20},{20... | collective-permute-start | bytes 503816 | tf_op jit(solution)/shard_map/ppermute | solution.py:335
  5.7 2.6 %collective-permute-start.1 = (f32[328,128]{1,0:T(8,128)S(1)}, f32[328,128]{1,0:T(8,128)S(1)}, u32[]{:S(2)}, u32[]{:S(2)}) collective-permute-start(f32[328,128]{1,0:T(8,128)S(1)} %get-tuple-element.38), channel_id=1, source_target_pairs={{0,8},{1,9},{2,10},{3,11},{4,12},{5,13},{6,14},{7,15},{8,0},{9,1},... | collective-permute-start | bytes 503816 | tf_op jit(solution)/shard_map/ppermute | solution.py:331
  8.3 1.7 %collective-permute-done.early_ref = f32[328,128]{1,0:T(8,128)S(1)} collective-permute-done((f32[328,128]{1,0:T(8,128)S(1)}, f32[328,128]{1,0:T(8,128)S(1)}, u32[]{:S(2)}, u32[]{:S(2)}) %collective-permute-start) | collective-permute-done | bytes 167968 | tf_op jit(solution)/shard_map/ppermute | solution.py:335
  10.0 2.8 %collective-permute-start.2 = (f32[256,128]{1,0:T(8,128)S(1)}, f32[256,128]{1,0:T(8,128)S(1)}, u32[]{:S(2)}, u32[]{:S(2)}) collective-permute-start(f32[256,128]{1,0:T(8,128)S(1)} %get-tuple-element.40), channel_id=1, source_target_pairs={{0,8},{1,9},{2,10},{3,11},{4,12},{5,13},{6,14},{7,15},{8,0},{9,1},... | collective-permute-start | bytes 393224 | tf_op jit(solution)/shard_map/ppermute | solution.py:331
  12.8 7.1 %collective-permute-done.1.near_ref = f32[328,128]{1,0:T(8,128)S(1)} collective-permute-done((f32[328,128]{1,0:T(8,128)S(1)}, f32[328,128]{1,0:T(8,128)S(1)}, u32[]{:S(2)}, u32[]{:S(2)}) %collective-permute-start.1) | collective-permute-done | bytes 167968 | tf_op jit(solution)/shard_map/ppermute | solution.py:331
  20.4 1.2 %collective-permute-done.2.side_ref = f32[256,128]{1,0:T(8,128)S(1)} collective-permute-done((f32[256,128]{1,0:T(8,128)S(1)}, f32[256,128]{1,0:T(8,128)S(1)}, u32[]{:S(2)}, u32[]{:S(2)}) %collective-permute-start.2) | collective-permute-done | bytes 131104 | tf_op jit(solution)/shard_map/ppermute | solution.py:331
  21.6 0.5 collective-permute-start.4
  22.1 1.6 %collective-permute-start.6 = (f32[256,512]{1,0:T(8,128)S(1)}, f32[256,512]{1,0:T(8,128)S(1)}, u32[]{:S(2)}, u32[]{:S(2)}) collective-permute-start(f32[256,512]{1,0:T(8,128)S(1)} %get-tuple-element.53), channel_id=1, source_target_pairs={{0,16},{16,0},{1,17},{17,1},{2,18},{18,2},{3,19},{19,3},{4,20},{20... | collective-permute-start | bytes 1572872 | tf_op jit(solution)/shard_map/ppermute | solution.py:335
  23.7 0.5 shard_map.59
  24.2 2.7 %collective-permute-done.3.far_ref = f32[328,128]{1,0:T(8,128)S(1)} collective-permute-done((f32[328,128]{1,0:T(8,128)S(1)}, f32[328,128]{1,0:T(8,128)S(1)}, u32[]{:S(2)}, u32[]{:S(2)}) %collective-permute-start.3) | collective-permute-done | bytes 167968 | tf_op jit(solution)/shard_map/ppermute | solution.py:335
  27.2 2.7 %collective-permute-start.8 = (f32[64,512]{1,0:T(8,128)S(1)}, f32[64,512]{1,0:T(8,128)S(1)}, u32[]{:S(2)}, u32[]{:S(2)}) collective-permute-start(f32[64,512]{1,0:T(8,128)S(1)} %get-tuple-element.61), channel_id=1, source_target_pairs={{0,8},{1,9},{2,10},{3,11},{4,12},{5,13},{6,14},{7,15},{8,0},{9,1},... | collective-permute-start | bytes 393224 | tf_op jit(solution)/shard_map/ppermute | solution.py:331
  29.9 9.0 %shard_map.60 = (f32[512,512]{1,0:T(8,128)S(1)}, f32[256,256]{1,0:T(8,128)S(1)}) custom-call(f32[512,512]{1,0:T(8,128)S(1)} %get-tuple-element.44.a_in, f32[512,512]{1,0:T(8,128)S(1)} %get-tuple-element.45.m_in, bf16[512,512]{1,0:T(8,128)(2,1)S(1)} %get-tuple-element.46.p_ref, f32[328,128]{1,0:T(8,128)S(1)} %collective-permute-done.3.far_ref, ...), custom_call_target="tpu_custom_call" | custom-call | flops 10000000000 | bytes 1048576 | tf_op jit(solution)/shard_map/pallas_call | solution.py:384
  38.9 2.8 %collective-permute-done.5.refs_0_ = f32[64,512]{1,0:T(8,128)S(1)} collective-permute-done((f32[64,512]{1,0:T(8,128)S(1)}, f32[64,512]{1,0:T(8,128)S(1)}, u32[]{:S(2)}, u32[]{:S(2)}) %collective-permute-start.5) | collective-permute-done | bytes 131104 | tf_op jit(solution)/shard_map/ppermute | solution.py:331
  41.7 0.6 collective-permute-start.9
  42.3 5.0 %shard_map.62 = (f32[512,512]{1,0:T(8,128)S(1)}, f32[512,512]{1,0:T(8,128)S(1)}) custom-call(f32[512,512]{1,0:T(8,128)S(1)} %get-tuple-element.51.a_in, f32[256,256]{1,0:T(8,128)S(1)} %get-tuple-element.52.b_ref, f32[256,1024]{1,0:T(8,128)S(1)} %bitcast.9, f32[256,512]{1,0:T(8,128)S(1)} %collective-permute-done.6.other_ref), custom_call_target="tpu_custom_call" | custom-call | flops 5000000000 | bytes 1048576 | tf_op jit(solution)/shard_map/pallas_call | solution.py:393
  47.4 1.6 %collective-permute-start.10 = (f32[128,512]{1,0:T(8,128)S(1)}, f32[128,512]{1,0:T(8,128)S(1)}, u32[]{:S(2)}, u32[]{:S(2)}) collective-permute-start(f32[128,512]{1,0:T(8,128)S(1)} %collective-permute-done.7.refs_1_), channel_id=1, source_target_pairs={{0,16},{16,0},{1,17},{17,1},{2,18},{18,2},{3,19},{19,3},{4,20},{20... | collective-permute-start | bytes 786440 | tf_op jit(solution)/shard_map/ppermute | solution.py:335
  48.9 4.1 %shard_map.63.g_ref = f32[512,512]{1,0:T(8,128)S(1)} custom-call(f32[512,512]{1,0:T(8,128)S(1)} %get-tuple-element.59.a_ref, f32[512,512]{1,0:T(8,128)S(1)} %get-tuple-element.60.g_in), custom_call_target="tpu_custom_call" | custom-call | flops 5000000000 | bytes 1048576 | tf_op jit(solution)/shard_map/pallas_call | solution.py:398
  53.1 0.6 %collective-permute-start.11 = (f32[64,512]{1,0:T(8,128)S(1)}, f32[64,512]{1,0:T(8,128)S(1)}, u32[]{:S(2)}, u32[]{:S(2)}) collective-permute-start(f32[64,512]{1,0:T(8,128)S(1)} %collective-permute-done.8.refs_2_), channel_id=1, source_target_pairs={{0,16},{16,0},{1,17},{17,1},{2,18},{18,2},{3,19},{19,3},{4,20},{20... | collective-permute-start | bytes 393224 | tf_op jit(solution)/shard_map/ppermute | solution.py:335
  53.7 0.8 %collective-permute-done.10.refs_4_ = f32[128,512]{1,0:T(8,128)S(1)} collective-permute-done((f32[128,512]{1,0:T(8,128)S(1)}, f32[128,512]{1,0:T(8,128)S(1)}, u32[]{:S(2)}, u32[]{:S(2)}) %collective-permute-start.10) | collective-permute-done | bytes 262176 | tf_op jit(solution)/shard_map/ppermute | solution.py:335
  54.5 2.5 %shard_map.64 = (f32[256,512]{1,0:T(8,128)}, f32[256,512]{1,0:T(8,128)}, f32[512,256]{1,0:T(8,128)S(1)}, f32[256,512]{1,0:T(8,128)S(1)}) custom-call(f32[512,512]{1,0:T(8,128)S(1)} %shard_map.63.g_ref, bf16[512,512]{1,0:T(8,128)(2,1)S(1)} %get-tuple-element.46.p_ref, f32[256,1024]{1,0:T(8,128)S(1)} %bitcast.10, ...), custom_call_target="tpu_custom_call" | custom-call | flops 4000000000 | bytes 1048576 | tf_op jit(solution)/shard_map/pallas_call | solution.py:404
  57.1 1.0 %collective-permute-done.11.refs_0_ = f32[64,512]{1,0:T(8,128)S(1)} collective-permute-done((f32[64,512]{1,0:T(8,128)S(1)}, f32[64,512]{1,0:T(8,128)S(1)}, u32[]{:S(2)}, u32[]{:S(2)}) %collective-permute-start.11) | collective-permute-done | bytes 131104 | tf_op jit(solution)/shard_map/ppermute | solution.py:335
  58.1 1.2 %shard_map.65 = f32[256,512]{1,0:T(8,128)} custom-call(f32[512,256]{1,0:T(8,128)S(1)} %get-tuple-element.68.h_ref, f32[256,512]{1,0:T(8,128)S(1)} %get-tuple-element.69.partial_ref, f32[64,512]{1,0:T(8,128)S(1)} %collective-permute-done.11.refs_0_), custom_call_target="tpu_custom_call" | custom-call | flops 100000000 | bytes 1048576 | tf_op jit(solution)/shard_map/pallas_call | solution.py:411
  (16 shorter events, 1.0 us)
Async XLA Ops:
  0.6 0.7 %copy-start.2 = (s32[1,512]{1,0:T(1,128)S(1)}, s32[1,512]{1,0:T(1,128)}, u32[]{:S(2)}) copy-start(s32[1,512]{1,0:T(1,128)} %map_ref.1) | copy-start | bytes 6148
  1.3 1.2 %copy-start = (f32[1,256,1024]{2,1,0:T(8,128)S(1)}, f32[1,256,1024]{2,1,0:T(8,128)}, u32[]{:S(2)}) copy-start(f32[1,256,1024]{2,1,0:T(8,128)} %param.3) | copy-start | bytes 3145732
  2.7 7.3 %collective-permute-start = (f32[328,128]{1,0:T(8,128)S(1)}, f32[328,128]{1,0:T(8,128)S(1)}, u32[]{:S(2)}, u32[]{:S(2)}) collective-permute-start(f32[328,128]{1,0:T(8,128)S(1)} %get-tuple-element.38), channel_id=1, source_target_pairs={{0,16},{16,0},{1,17},{17,1},{2,18},{18,2},{3,19},{19,3},{4,20},{20... | collective-permute-start | bytes 503816 | tf_op jit(solution)/shard_map/ppermute | solution.py:335
  5.7 14.2 %collective-permute-start.1 = (f32[328,128]{1,0:T(8,128)S(1)}, f32[328,128]{1,0:T(8,128)S(1)}, u32[]{:S(2)}, u32[]{:S(2)}) collective-permute-start(f32[328,128]{1,0:T(8,128)S(1)} %get-tuple-element.38), channel_id=1, source_target_pairs={{0,8},{1,9},{2,10},{3,11},{4,12},{5,13},{6,14},{7,15},{8,0},{9,1},... | collective-permute-start | bytes 503816 | tf_op jit(solution)/shard_map/ppermute | solution.py:331
  10.0 11.6 %collective-permute-start.2 = (f32[256,128]{1,0:T(8,128)S(1)}, f32[256,128]{1,0:T(8,128)S(1)}, u32[]{:S(2)}, u32[]{:S(2)}) collective-permute-start(f32[256,128]{1,0:T(8,128)S(1)} %get-tuple-element.40), channel_id=1, source_target_pairs={{0,8},{1,9},{2,10},{3,11},{4,12},{5,13},{6,14},{7,15},{8,0},{9,1},... | collective-permute-start | bytes 393224 | tf_op jit(solution)/shard_map/ppermute | solution.py:331
  19.9 7.1 %collective-permute-start.3 = (f32[328,128]{1,0:T(8,128)S(1)}, f32[328,128]{1,0:T(8,128)S(1)}, u32[]{:S(2)}, u32[]{:S(2)}) collective-permute-start(f32[328,128]{1,0:T(8,128)S(1)} %collective-permute-done.1.near_ref), channel_id=1, source_target_pairs={{0,16},{16,0},{1,17},{17,1},{2,18},{18,2},{3,19},{19,3},{4,20},{20... | collective-permute-start | bytes 503816 | tf_op jit(solution)/shard_map/ppermute | solution.py:335
  21.6 8.4 %collective-permute-start.4 = (f32[256,128]{1,0:T(8,128)S(1)}, f32[256,128]{1,0:T(8,128)S(1)}, u32[]{:S(2)}, u32[]{:S(2)}) collective-permute-start(f32[256,128]{1,0:T(8,128)S(1)} %collective-permute-done.2.side_ref), channel_id=1, source_target_pairs={{0,16},{16,0},{1,17},{17,1},{2,18},{18,2},{3,19},{19,3},{4,20},{20... | collective-permute-start | bytes 393224 | tf_op jit(solution)/shard_map/ppermute | solution.py:335
  22.1 20.2 %collective-permute-start.6 = (f32[256,512]{1,0:T(8,128)S(1)}, f32[256,512]{1,0:T(8,128)S(1)}, u32[]{:S(2)}, u32[]{:S(2)}) collective-permute-start(f32[256,512]{1,0:T(8,128)S(1)} %get-tuple-element.53), channel_id=1, source_target_pairs={{0,16},{16,0},{1,17},{17,1},{2,18},{18,2},{3,19},{19,3},{4,20},{20... | collective-permute-start | bytes 1572872 | tf_op jit(solution)/shard_map/ppermute | solution.py:335
  23.7 18.0 %collective-permute-start.5 = (f32[64,512]{1,0:T(8,128)S(1)}, f32[64,512]{1,0:T(8,128)S(1)}, u32[]{:S(2)}, u32[]{:S(2)}) collective-permute-start(f32[64,512]{1,0:T(8,128)S(1)} %get-tuple-element.50), channel_id=1, source_target_pairs={{0,8},{1,9},{2,10},{3,11},{4,12},{5,13},{6,14},{7,15},{8,0},{9,1},... | collective-permute-start | bytes 393224 | tf_op jit(solution)/shard_map/ppermute | solution.py:331
  27.0 20.4 %collective-permute-start.7 = (f32[128,512]{1,0:T(8,128)S(1)}, f32[128,512]{1,0:T(8,128)S(1)}, u32[]{:S(2)}, u32[]{:S(2)}) collective-permute-start(f32[128,512]{1,0:T(8,128)S(1)} %get-tuple-element.58), channel_id=1, source_target_pairs={{0,8},{1,9},{2,10},{3,11},{4,12},{5,13},{6,14},{7,15},{8,0},{9,1},... | collective-permute-start | bytes 786440 | tf_op jit(solution)/shard_map/ppermute | solution.py:331
  27.2 25.8 %collective-permute-start.8 = (f32[64,512]{1,0:T(8,128)S(1)}, f32[64,512]{1,0:T(8,128)S(1)}, u32[]{:S(2)}, u32[]{:S(2)}) collective-permute-start(f32[64,512]{1,0:T(8,128)S(1)} %get-tuple-element.61), channel_id=1, source_target_pairs={{0,8},{1,9},{2,10},{3,11},{4,12},{5,13},{6,14},{7,15},{8,0},{9,1},... | collective-permute-start | bytes 393224 | tf_op jit(solution)/shard_map/ppermute | solution.py:331
  29.9 12.4 %copy-start.1 = (f32[1,256,1024]{2,1,0:T(8,128)S(1)}, f32[1,256,1024]{2,1,0:T(8,128)}, u32[]{:S(2)}) copy-start(f32[1,256,1024]{2,1,0:T(8,128)} %param.3) | copy-start | bytes 3145732
  41.7 11.9 %collective-permute-start.9 = (f32[64,512]{1,0:T(8,128)S(1)}, f32[64,512]{1,0:T(8,128)S(1)}, u32[]{:S(2)}, u32[]{:S(2)}) collective-permute-start(f32[64,512]{1,0:T(8,128)S(1)} %collective-permute-done.5.refs_0_), channel_id=1, source_target_pairs={{0,16},{16,0},{1,17},{17,1},{2,18},{18,2},{3,19},{19,3},{4,20},{20... | collective-permute-start | bytes 393224 | tf_op jit(solution)/shard_map/ppermute | solution.py:335
  47.3 7.2 %copy-start.3 = (f32[1,256,512]{2,1,0:T(8,128)S(1)}, f32[1,256,512]{2,1,0:T(8,128)}, u32[]{:S(2)}) copy-start(f32[1,256,512]{2,1,0:T(8,128)} %param.4) | copy-start | bytes 1572868
  47.4 7.1 %collective-permute-start.10 = (f32[128,512]{1,0:T(8,128)S(1)}, f32[128,512]{1,0:T(8,128)S(1)}, u32[]{:S(2)}, u32[]{:S(2)}) collective-permute-start(f32[128,512]{1,0:T(8,128)S(1)} %collective-permute-done.7.refs_1_), channel_id=1, source_target_pairs={{0,16},{16,0},{1,17},{17,1},{2,18},{18,2},{3,19},{19,3},{4,20},{20... | collective-permute-start | bytes 786440 | tf_op jit(solution)/shard_map/ppermute | solution.py:335
  53.1 5.0 %collective-permute-start.11 = (f32[64,512]{1,0:T(8,128)S(1)}, f32[64,512]{1,0:T(8,128)S(1)}, u32[]{:S(2)}, u32[]{:S(2)}) collective-permute-start(f32[64,512]{1,0:T(8,128)S(1)} %collective-permute-done.8.refs_2_), channel_id=1, source_target_pairs={{0,16},{16,0},{1,17},{17,1},{2,18},{18,2},{3,19},{19,3},{4,20},{20... | collective-permute-start | bytes 393224 | tf_op jit(solution)/shard_map/ppermute | solution.py:335

commit v7 on v6

--- a/solution.py
+++ b/solution.py
@@ -10,7 +10,6 @@
 F32 = jnp.float32
 BF16 = jnp.bfloat16
 TILE = 128
-PARTS = (4, 8, 4)
 VMEM_LIMIT = 48 * 2**20
 
 
@@ -215,7 +214,7 @@
     return first, ref[0:q, :], second
 
 
-def prepare_body(half, t_ref, early_ref, near_ref, side_ref, column_ref, first_ref, a_out, m_out, p_out):
+def prepare_body(half, t_ref, early_ref, near_ref, side_ref, column_ref, first_ref, a_out, m_out, p_out, outer_out):
     n, q = 2 * half, half // 2
     width = t_ref.shape[1] - n
     mine = first_ref[0]
@@ -231,6 +230,7 @@
     a_out[tile_block(q, 2, 2)] = first
     a_out[tile_block(q, 2, 3)] = cross
     a_out[tile_block(q, 3, 3)] = second
+    outer_out[...] = t_ref[:, column_blocks(half, mine)[0]]
 
 
 def first_body(steps, a_in, m_in, p_ref, far_ref, side_ref, first_ref, a_out, b_out, m_work):
@@ -247,56 +247,67 @@
     eliminate(a_out, b_out, steps)
 
 
-def middle_body(steps, a_in, b_ref, t_ref, other_ref, a_out, g_out):
+def middle_body(steps, a_in, b_ref, t_ref, mine_ref, others_ref, first_ref, a_out, g_out):
     top, half = b_ref.shape[0], t_ref.shape[0]
+    here, there = column_blocks(half, first_ref[0])
     a_out[...] = a_in[...]
     g_out[0:half, :] = t_ref[:, 0 : g_out.shape[1]]
-    g_out[half:, :] = other_ref[...]
+    g_out[half:, here] = mine_ref[...]
+    g_out[half:, there] = others_ref[...]
     first = g_out[0:top, :]
     g_out[top:, :] = g_out[top:, :] - full(a_in[0:top, top:], first, ((0,), (0,)))
     g_out[0:top, :] = full(b_ref[...], first)
     eliminate(a_out, g_out, steps)
 
 
+def column_blocks(half, mine):
+    return [pl.ds(pl.multiple_of(x * half, half), half) for x in (mine, 1 - mine)]
+
+
 def last_body(steps, a_ref, g_in, g_out, a_work):
     a_work[...] = a_ref[...]
     g_out[...] = g_in[...]
     eliminate(a_work, g_out, steps)
 
 
-def cross_terms(h_ref, at, parts):
-    total = None
-    for ref in parts:
-        term = three_pass(h_ref[at : at + ref.shape[0], :], ref[...], ((0,), (0,)))
-        total = term if total is None else total + term
-        at += ref.shape[0]
-    return total
+def send_body(half, g_ref, p_ref, chunk_ref, first_ref, h_out, send_out):
+    _, there = column_blocks(half, first_ref[0])
+    h = pick_left(p_ref[...], g_ref[:, there], ((0,), (0,)))
+    h_out[...] = h
+    send_out[...] = -three_pass(h, chunk_ref[...], ((0,), (0,)))
+
+
+def send_more_body(h_ref, chunk_ref, send_out):
+    send_out[...] = -three_pass(h_ref[...], chunk_ref[...], ((0,), (0,)))
 
 
 def output_body(
-    half, g_ref, p_ref, t_ref, other_ref, ext_ref, row_ref, first_ref, *refs
+    half, g_ref, p_ref, t_ref, mine_ref, others_ref, ext_ref, row_ref, first_ref, chunk_a, chunk_b, own_ref, sol_ref, keep_ref
 ):
-    *parts, own_ref, sol_ref, h_ref, cross_ref = refs
-    n = 2 * half
+    n, q = 2 * half, half // 2
     mine = first_ref[0]
-    block = pl.ds(pl.multiple_of(mine * half, half), half)
+    here, there = column_blocks(half, mine)
     g = g_ref[...]
-    h_ref[...] = pick_left(p_ref[...], g_ref[:, block], ((0,), (0,)))
-    left = jnp.concatenate([t_ref[:, block], other_ref[:, block]], axis=0)
+    left = jnp.concatenate([t_ref[:, here], mine_ref[...]], axis=0)
     own_ref[...] = ext_ref[...] - three_pass(left, g, ((0,), (0,)))
     target = lax.broadcasted_iota(jnp.int32, (half, n), 0) + mine * half
     onehot = jnp.where(row_ref[...].astype(jnp.int32) == target, 1.0, 0.0).astype(BF16)
     sol_ref[...] = -pick_left(onehot, g, ((1,), (0,)))
-    cross_ref[...] = cross_terms(h_ref, 0, parts)
-
-
-def cross_body(h_ref, partial_ref, *refs):
-    *parts, out_ref = refs
-    at = h_ref.shape[0] - sum(ref.shape[0] for ref in parts)
-    out_ref[...] = -(partial_ref[...] + cross_terms(h_ref, at, parts))
-
-
-def pack_iface_body(half, width, t_ref, map_ref, first_ref, diag_ref, side_ref, row_ref, column_ref):
+    h = pick_left(p_ref[...], g_ref[:, here], ((0,), (0,)))
+    for i, chunk in enumerate((chunk_a, chunk_b)):
+        keep_ref[:, i * q : (i + 1) * q] = -three_pass(h, chunk[...], ((0,), (0,)))
+
+
+def cross_body(keep_ref, first_part, second_part, first_ref, out_ref):
+    half, q = keep_ref.shape[0], first_part.shape[1]
+    mine = first_ref[0]
+    here, _ = column_blocks(half, mine)
+    out_ref[:, here] = keep_ref[...]
+    for i, part in enumerate((first_part, second_part)):
+        out_ref[:, pl.ds(pl.multiple_of((1 - mine) * half + i * q, q), q)] = part[...]
+
+
+def pack_iface_body(half, width, t_ref, map_ref, first_ref, diag_ref, side_ref, outer_ref, row_ref, column_ref):
     q, n = half // 2, 2 * half
     mine = first_ref[0]
     here, there = width + mine * half, width + (1 - mine) * half
@@ -310,7 +321,8 @@
         at += block.shape[0]
     side_ref[0:q, :] = cut(0, there + q)
     side_ref[q : 2 * q, :] = cut(mine * q, there + mine * q)
-    spans = [pl.ds(pl.multiple_of(x * half, half), half) for x in (mine, 1 - mine)]
+    spans = column_blocks(half, mine)
+    outer_ref[...] = t_ref[:, spans[1]]
     row = jnp.concatenate([map_ref[:, span] for span in spans], axis=1).astype(F32)
     row_ref[...] = row
     column_ref[...] = jnp.broadcast_to(row, (8, n)).T[:, 0:1]
@@ -318,12 +330,13 @@
     diag_ref[at:, :] = jnp.concatenate(parts + parts, axis=0)[0:8, :]
 
 
-def pack_outer_body(t_ref, outer_ref, *chunks):
-    outer_ref[...] = t_ref[:, 0 : outer_ref.shape[1]]
-    at = 0
-    for chunk in chunks:
-        chunk[...] = t_ref[at : at + chunk.shape[0], 0 : chunk.shape[1]]
-        at += chunk.shape[0]
+def pack_outer_body(t_ref, mine_ref, first_ref, *chunks):
+    half = t_ref.shape[0]
+    mine = first_ref[0]
+    for i, chunk in enumerate(chunks):
+        width = chunk.shape[1]
+        chunk[0:half, :] = t_ref[:, pl.ds(pl.multiple_of(mine * half + i * width, width), width)]
+        chunk[half:, :] = mine_ref[:, i * width : (i + 1) * width]
 
 
 def sibling(x):
@@ -356,30 +369,29 @@
     vmem, smem = pltpu.VMEM, pltpu.SMEM
     mine = lax.axis_index("sib").astype(jnp.int32)
     first = mine.reshape(1)
-    diag, side, own_row, column = kernel(
+    diag, side, outer, own_row, column = kernel(
         functools.partial(pack_iface_body, half, width),
-        (f(5 * q // 2 + 8, q), f(2 * q, q), f(1, n), f(n, 1)),
+        (f(5 * q // 2 + 8, q), f(2 * q, q), f(half, half), f(1, n), f(n, 1)),
         [vmem, vmem, smem],
     )(t_int, iface_map, first)
     near = sibling(diag)
     diag_other = across(diag)
     far = across(near)
-    side, diag_other = lax.optimization_barrier((side, diag_other))
+    side, outer, diag_other = lax.optimization_barrier((side, outer, diag_other))
     near_side = sibling(side)
+    outer_mine = across(outer)
     near, near_side = lax.optimization_barrier((near, near_side))
     far_side = across(near_side)
-    outer, *chunks = kernel(
-        pack_outer_body, [f(half, width)] + [f(half * part // 16, width) for part in PARTS], [vmem]
-    )(t_int)
-    other = across(outer)
-    leading, _ = lax.optimization_barrier((chunks[0], near_side))
-    *following, _ = lax.optimization_barrier((*chunks[1:], far))
-    near_r = [sibling(chunk) for chunk in (leading, *following)]
-    a, m, onehot = kernel(
+    chunks = kernel(pack_outer_body, [f(n, q)] * 2, [vmem, vmem, smem])(t_int, outer_mine, first)
+    *chunks, _ = lax.optimization_barrier((*chunks, near_side))
+    near_r = [sibling(chunk) for chunk in chunks]
+    first_late, *_ = lax.optimization_barrier((first, *chunks))
+    a, m, onehot, outer = kernel(
         functools.partial(prepare_body, half),
-        (f(n, n), f(n, n), jax.ShapeDtypeStruct((n, n), BF16)),
+        (f(n, n), f(n, n), jax.ShapeDtypeStruct((n, n), BF16), f(half, half)),
         [vmem] * 5 + [smem],
-    )(t_int, diag_other, near, near_side, column, first)
+    )(t_int, diag_other, near, near_side, column, first_late)
+    outer_others = across(outer)
     top = tiles // 2 * TILE
     a, b = kernel(
         functools.partial(first_body, range(tiles // 2)),
@@ -388,27 +400,29 @@
         [pltpu.VMEM((n, n), F32)],
         10e9,
     )(a, m, onehot, far, far_side, first)
-    a, b, near_r[0] = lax.optimization_barrier((a, b, near_r[0]))
-    far_r = [across(near_r[0])]
     a, g = kernel(
-        functools.partial(middle_body, range(tiles // 2, tiles - 1)), (f(n, n), f(n, width)), [vmem] * 4, (), 5e9
-    )(a, b, t_int, other)
-    a, g, near_r[1] = lax.optimization_barrier((a, g, near_r[1]))
-    far_r.append(across(near_r[1]))
+        functools.partial(middle_body, range(tiles // 2, tiles - 1)),
+        (f(n, n), f(n, width)),
+        [vmem] * 5 + [smem],
+        (),
+        5e9,
+    )(a, b, t_int, outer_mine, outer_others, first)
     g = kernel(
         functools.partial(last_body, range(tiles - 1, tiles)), f(n, width), [vmem] * 2, [pltpu.VMEM((n, n), F32)], 5e9
     )(a, g)
-    g, near_r[2] = lax.optimization_barrier((g, near_r[2]))
-    far_r.append(across(near_r[2]))
-    parts = [*near_r, *far_r[:2]]
-    own_map, solution_op, h, partial = kernel(
+    h, send = kernel(
+        functools.partial(send_body, half), (f(n, half), f(half, q)), [vmem] * 3 + [smem], (), 1e9
+    )(g, onehot, near_r[0], first)
+    cross_a = across(send)
+    cross_b = across(kernel(send_more_body, f(half, q), [vmem] * 2, (), 5e9)(h, near_r[1]))
+    own_map, solution_op, keep = kernel(
         functools.partial(output_body, half),
-        (f(half, width), f(half, width), f(n, half), f(half, width)),
-        [vmem] * 6 + [smem] + [vmem] * len(parts),
+        (f(half, width), f(half, width), f(half, half)),
+        [vmem] * 7 + [smem] + [vmem] * 2,
         (),
-        4e9,
-    )(g, onehot, t_int, other, t_ext, own_row, first, *parts)
-    cross_map = kernel(cross_body, f(half, width), [vmem] * 3)(h, partial, far_r[2])
+        1e6,
+    )(g, onehot, t_int, outer_mine, outer_others, t_ext, own_row, first, *near_r)
+    cross_map = kernel(cross_body, f(half, width), [vmem] * 3 + [smem])(keep, cross_a, cross_b, first)
     return own_map[None], cross_map[None], solution_op[None]
 
 

time: 59.5 us -> 56.1 us (0.943)
  waiting for transfers between devices: 17.4 us -> 10.8 us
  Pallas kernels: 22.6 us -> 24.8 us
  starting transfers between devices: 16.6 us -> 17.6 us
    ppermute x5 -> x4, waiting for transfers between devices: 11.1 us -> 6.8 us  [sibling(): return lax.ppermute(x, 'leaf', [(i, i ^ size // 2) for i in range(size)])]
    ppermute x7, waiting for transfers between devices: 6.31 us -> 4.01 us  [across(): return lax.ppermute(x, 'sib', [(0, 1), (1, 0)])]
    pallas_call x2 -> x4, Pallas kernels: 1.25 us -> 2.62 us  [the longest x1 1.31 us: two_shards(): kernel(functools.partial(send_body, half), (f(n, half), f(half, q)), [vme...]
    ppermute x7, starting transfers between devices: 8.26 us -> 9.46 us  [across(): return lax.ppermute(x, 'sib', [(0, 1), (1, 0)])]
    pallas_call x1, Pallas kernels: 2.54 us -> 3.22 us  [two_shards(): kernel(functools.partial(output_body, half), (f(half, width), f(half, wid...]
    ppermute x5 -> x4, starting transfers between devices: 8.35 us -> 8.16 us  [sibling(): return lax.ppermute(x, 'leaf', [(i, i ^ size // 2) for i in range(size)])]
  transfers between devices with their start and end apart: 12 -> 11, of which waited for: 7 -> 5; matrix products, arithmetic and copies ran while one was open for 0% -> 0% of each run, Pallas kernels for 36% -> 43%
where the time goes in v7:
time: 56.1 us; the launch traced here: 55.9 us
  Pallas kernels  24.8 us (44%)
  starting transfers between devices  17.6 us (31%)
  waiting for transfers between devices  10.8 us (19%)
  local copies, waits for them, and re-layouts  1.91 us (3%)
  between operations  0.76 us (1%)
    ppermute x7, starting transfers between devices, across(): return lax.ppermute(x, 'sib', [(0, 1), (1, 0)])  9.46 us
    pallas_call x1, Pallas kernels, two_shards(): kernel(functools.partial(first_body, range(tiles // 2)), (f(n, n), f(top,...  9.05 us
    ppermute x4, starting transfers between devices, sibling(): return lax.ppermute(x, 'leaf', [(i, i ^ size // 2) for i in range(size)])  8.16 us
    ppermute x4, waiting for transfers between devices, sibling(): return lax.ppermute(x, 'leaf', [(i, i ^ size // 2) for i in range(size)])  6.8 us
    pallas_call x1, Pallas kernels, two_shards(): kernel(functools.partial(middle_body, range(tiles // 2, tiles - 1)), (f(n...  5.08 us
    pallas_call x1, Pallas kernels, two_shards(): kernel(functools.partial(last_body, range(tiles - 1, tiles)), f(n, width)...  4.13 us
    ppermute x7, waiting for transfers between devices, across(): return lax.ppermute(x, 'sib', [(0, 1), (1, 0)])  4.01 us
    pallas_call x1, Pallas kernels, two_shards(): kernel(functools.partial(output_body, half), (f(half, width), f(half, wid...  3.22 us
  transfers between devices with their start and end apart: 11, of which 5 were waited for; matrix products, arithmetic and copies ran while one was open for 0% of the time, Pallas kernels for 43%

profile of v7, /device:TPU:0, one launch (start us, length us, event | category | flops | bytes accessed | tf_op | source)
XLA Modules:
  0.0 55.9 jit_solution(13380108395026335003)
XLA Ops:
  0.6 0.7 %copy-done.3 = s32[1,512]{1,0:T(1,128)S(1)} copy-done((s32[1,512]{1,0:T(1,128)S(1)}, s32[1,512]{1,0:T(1,128)}, u32[]{:S(2)}) %copy-start.3) | copy-done | bytes 2072
  1.3 1.2 %copy-done = f32[1,256,1024]{2,1,0:T(8,128)S(1)} copy-done((f32[1,256,1024]{2,1,0:T(8,128)S(1)}, f32[1,256,1024]{2,1,0:T(8,128)}, u32[]{:S(2)}) %copy-start) | copy-done | bytes 1048600
  2.7 3.0 %collective-permute-start = (f32[328,128]{1,0:T(8,128)S(1)}, f32[328,128]{1,0:T(8,128)S(1)}, u32[]{:S(2)}, u32[]{:S(2)}) collective-permute-start(f32[328,128]{1,0:T(8,128)S(1)} %get-tuple-element.33), channel_id=1, source_target_pairs={{0,16},{16,0},{1,17},{17,1},{2,18},{18,2},{3,19},{19,3},{4,20},{20... | collective-permute-start | bytes 503816 | tf_op jit(solution)/shard_map/ppermute | solution.py:348
  5.7 2.6 %collective-permute-start.1 = (f32[328,128]{1,0:T(8,128)S(1)}, f32[328,128]{1,0:T(8,128)S(1)}, u32[]{:S(2)}, u32[]{:S(2)}) collective-permute-start(f32[328,128]{1,0:T(8,128)S(1)} %get-tuple-element.33), channel_id=1, source_target_pairs={{0,8},{1,9},{2,10},{3,11},{4,12},{5,13},{6,14},{7,15},{8,0},{9,1},... | collective-permute-start | bytes 503816 | tf_op jit(solution)/shard_map/ppermute | solution.py:344
  8.3 1.7 %collective-permute-done.early_ref = f32[328,128]{1,0:T(8,128)S(1)} collective-permute-done((f32[328,128]{1,0:T(8,128)S(1)}, f32[328,128]{1,0:T(8,128)S(1)}, u32[]{:S(2)}, u32[]{:S(2)}) %collective-permute-start) | collective-permute-done | bytes 167968 | tf_op jit(solution)/shard_map/ppermute | solution.py:348
  10.0 1.7 %collective-permute-start.3 = (f32[256,256]{1,0:T(8,128)S(1)}, f32[256,256]{1,0:T(8,128)S(1)}, u32[]{:S(2)}, u32[]{:S(2)}) collective-permute-start(f32[256,256]{1,0:T(8,128)S(1)} %get-tuple-element.39), channel_id=1, source_target_pairs={{0,16},{16,0},{1,17},{17,1},{2,18},{18,2},{3,19},{19,3},{4,20},{20... | collective-permute-start | bytes 786440 | tf_op jit(solution)/shard_map/ppermute | solution.py:348
  11.8 2.6 %collective-permute-start.2 = (f32[256,128]{1,0:T(8,128)S(1)}, f32[256,128]{1,0:T(8,128)S(1)}, u32[]{:S(2)}, u32[]{:S(2)}) collective-permute-start(f32[256,128]{1,0:T(8,128)S(1)} %get-tuple-element.35), channel_id=1, source_target_pairs={{0,8},{1,9},{2,10},{3,11},{4,12},{5,13},{6,14},{7,15},{8,0},{9,1},... | collective-permute-start | bytes 393224 | tf_op jit(solution)/shard_map/ppermute | solution.py:344
  14.4 5.6 %collective-permute-done.1.near_ref = f32[328,128]{1,0:T(8,128)S(1)} collective-permute-done((f32[328,128]{1,0:T(8,128)S(1)}, f32[328,128]{1,0:T(8,128)S(1)}, u32[]{:S(2)}, u32[]{:S(2)}) %collective-permute-start.1) | collective-permute-done | bytes 167968 | tf_op jit(solution)/shard_map/ppermute | solution.py:344
  20.0 0.4 collective-permute-start.4
  20.4 1.2 %collective-permute-done.2.side_ref = f32[256,128]{1,0:T(8,128)S(1)} collective-permute-done((f32[256,128]{1,0:T(8,128)S(1)}, f32[256,128]{1,0:T(8,128)S(1)}, u32[]{:S(2)}, u32[]{:S(2)}) %collective-permute-start.2) | collective-permute-done | bytes 131104 | tf_op jit(solution)/shard_map/ppermute | solution.py:344
  21.6 0.5 collective-permute-start.5
  22.2 2.9 %collective-permute-start.8 = (f32[512,128]{1,0:T(8,128)S(1)}, f32[512,128]{1,0:T(8,128)S(1)}, u32[]{:S(2)}, u32[]{:S(2)}) collective-permute-start(f32[512,128]{1,0:T(8,128)S(1)} %get-tuple-element.43), channel_id=1, source_target_pairs={{0,8},{1,9},{2,10},{3,11},{4,12},{5,13},{6,14},{7,15},{8,0},{9,1},... | collective-permute-start | bytes 786440 | tf_op jit(solution)/shard_map/ppermute | solution.py:344
  25.1 0.5 shard_map.60
  25.6 1.7 %collective-permute-start.6 = (f32[256,256]{1,0:T(8,128)S(1)}, f32[256,256]{1,0:T(8,128)S(1)}, u32[]{:S(2)}, u32[]{:S(2)}) collective-permute-start(f32[256,256]{1,0:T(8,128)S(1)} %get-tuple-element.50), channel_id=1, source_target_pairs={{0,16},{16,0},{1,17},{17,1},{2,18},{18,2},{3,19},{19,3},{4,20},{20... | collective-permute-start | bytes 786440 | tf_op jit(solution)/shard_map/ppermute | solution.py:348
  27.3 1.7 %collective-permute-done.5.side_ref = f32[256,128]{1,0:T(8,128)S(1)} collective-permute-done((f32[256,128]{1,0:T(8,128)S(1)}, f32[256,128]{1,0:T(8,128)S(1)}, u32[]{:S(2)}, u32[]{:S(2)}) %collective-permute-start.5) | collective-permute-done | bytes 131104 | tf_op jit(solution)/shard_map/ppermute | solution.py:348
  29.0 9.1 %shard_map.61 = (f32[512,512]{1,0:T(8,128)S(1)}, f32[256,256]{1,0:T(8,128)S(1)}) custom-call(f32[512,512]{1,0:T(8,128)S(1)} %get-tuple-element.45.a_in, f32[512,512]{1,0:T(8,128)S(1)} %get-tuple-element.46.m_in, bf16[512,512]{1,0:T(8,128)(2,1)S(1)} %get-tuple-element.47.p_ref, f32[328,128]{1,0:T(8,128)S(1)} %collective-permute-done.4.far_ref, ...), custom_call_target="tpu_custom_call" | custom-call | flops 10000000000 | bytes 1048576 | tf_op jit(solution)/shard_map/pallas_call | solution.py:396
  38.1 5.1 %shard_map.62 = (f32[512,512]{1,0:T(8,128)S(1)}, f32[512,512]{1,0:T(8,128)S(1)}) custom-call(f32[512,512]{1,0:T(8,128)S(1)} %get-tuple-element.48.a_in, f32[256,256]{1,0:T(8,128)S(1)} %get-tuple-element.49.b_ref, f32[256,1024]{1,0:T(8,128)S(1)} %bitcast.9, f32[256,256]{1,0:T(8,128)S(1)} %collective-permute-done.3.mine_ref, ...), custom_call_target="tpu_custom_call" | custom-call | flops 5000000000 | bytes 1048576 | tf_op jit(solution)/shard_map/pallas_call | solution.py:403
  43.2 4.1 %shard_map.63.g_ref = f32[512,512]{1,0:T(8,128)S(1)} custom-call(f32[512,512]{1,0:T(8,128)S(1)} %get-tuple-element.51.a_ref, f32[512,512]{1,0:T(8,128)S(1)} %get-tuple-element.52.g_in), custom_call_target="tpu_custom_call" | custom-call | flops 5000000000 | bytes 1048576 | tf_op jit(solution)/shard_map/pallas_call | solution.py:410
  47.3 1.3 %shard_map.65 = (f32[512,256]{1,0:T(8,128)S(1)}, f32[256,128]{1,0:T(8,128)S(1)}) custom-call(f32[512,512]{1,0:T(8,128)S(1)} %shard_map.63.g_ref, bf16[512,512]{1,0:T(8,128)(2,1)S(1)} %get-tuple-element.47.p_ref, f32[512,128]{1,0:T(8,128)S(1)} %collective-permute-done.7.chunk_a.chunk_ref, s32[1]{0:T(128)} %bitcast.1.first_ref), custom_call_target="tpu_custom_call" | custom-call | flops 1000000000 | bytes 1048576 | tf_op jit(solution)/shard_map/pallas_call | solution.py:413
  48.7 0.4 shard_map.66
  49.1 2.1 %collective-permute-start.10 = (f32[256,128]{1,0:T(8,128)S(1)}, f32[256,128]{1,0:T(8,128)S(1)}, u32[]{:S(2)}, u32[]{:S(2)}) collective-permute-start(f32[256,128]{1,0:T(8,128)S(1)} %shard_map.66), channel_id=1, source_target_pairs={{0,16},{16,0},{1,17},{17,1},{2,18},{18,2},{3,19},{19,3},{4,20},{20... | collective-permute-start | bytes 393224 | tf_op jit(solution)/shard_map/ppermute | solution.py:348
  51.2 3.2 %shard_map.64 = (f32[256,512]{1,0:T(8,128)}, f32[256,512]{1,0:T(8,128)}, f32[256,256]{1,0:T(8,128)S(1)}) custom-call(f32[512,512]{1,0:T(8,128)S(1)} %shard_map.63.g_ref, bf16[512,512]{1,0:T(8,128)(2,1)S(1)} %get-tuple-element.47.p_ref, f32[256,1024]{1,0:T(8,128)S(1)} %bitcast.10, f32[256,256]{1,0:T(8,128)S(1)} %collective-permute-done.3.mine_ref, ...), custom_call_target="tpu_custom_call" | custom-call | flops 1000000 | bytes 1048576 | tf_op jit(solution)/shard_map/pallas_call | solution.py:418
  54.4 0.6 %collective-permute-done.10.second_part = f32[256,128]{1,0:T(8,128)S(1)} collective-permute-done((f32[256,128]{1,0:T(8,128)S(1)}, f32[256,128]{1,0:T(8,128)S(1)}, u32[]{:S(2)}, u32[]{:S(2)}) %collective-permute-start.10) | collective-permute-done | bytes 131104 | tf_op jit(solution)/shard_map/ppermute | solution.py:348
  55.0 0.8 %shard_map.67 = f32[256,512]{1,0:T(8,128)} custom-call(f32[256,256]{1,0:T(8,128)S(1)} %get-tuple-element.55.keep_ref, f32[256,128]{1,0:T(8,128)S(1)} %collective-permute-done.9.first_part, f32[256,128]{1,0:T(8,128)S(1)} %collective-permute-done.10.second_part, s32[1]{0:T(128)} %bitcast.1.first_ref), custom_call_target="tpu_custom_call" | custom-call | flops 100000000 | bytes 1048576 | tf_op jit(solution)/shard_map/pallas_call | solution.py:425
  (16 shorter events, 0.4 us)
Async XLA Ops:
  0.6 0.7 %copy-start.3 = (s32[1,512]{1,0:T(1,128)S(1)}, s32[1,512]{1,0:T(1,128)}, u32[]{:S(2)}) copy-start(s32[1,512]{1,0:T(1,128)} %map_ref.1) | copy-start | bytes 6148
  1.3 1.2 %copy-start = (f32[1,256,1024]{2,1,0:T(8,128)S(1)}, f32[1,256,1024]{2,1,0:T(8,128)}, u32[]{:S(2)}) copy-start(f32[1,256,1024]{2,1,0:T(8,128)} %param.3) | copy-start | bytes 3145732
  2.7 7.3 %collective-permute-start = (f32[328,128]{1,0:T(8,128)S(1)}, f32[328,128]{1,0:T(8,128)S(1)}, u32[]{:S(2)}, u32[]{:S(2)}) collective-permute-start(f32[328,128]{1,0:T(8,128)S(1)} %get-tuple-element.33), channel_id=1, source_target_pairs={{0,16},{16,0},{1,17},{17,1},{2,18},{18,2},{3,19},{19,3},{4,20},{20... | collective-permute-start | bytes 503816 | tf_op jit(solution)/shard_map/ppermute | solution.py:348
  5.7 14.2 %collective-permute-start.1 = (f32[328,128]{1,0:T(8,128)S(1)}, f32[328,128]{1,0:T(8,128)S(1)}, u32[]{:S(2)}, u32[]{:S(2)}) collective-permute-start(f32[328,128]{1,0:T(8,128)S(1)} %get-tuple-element.33), channel_id=1, source_target_pairs={{0,8},{1,9},{2,10},{3,11},{4,12},{5,13},{6,14},{7,15},{8,0},{9,1},... | collective-permute-start | bytes 503816 | tf_op jit(solution)/shard_map/ppermute | solution.py:344
  10.0 12.1 %collective-permute-start.3 = (f32[256,256]{1,0:T(8,128)S(1)}, f32[256,256]{1,0:T(8,128)S(1)}, u32[]{:S(2)}, u32[]{:S(2)}) collective-permute-start(f32[256,256]{1,0:T(8,128)S(1)} %get-tuple-element.39), channel_id=1, source_target_pairs={{0,16},{16,0},{1,17},{17,1},{2,18},{18,2},{3,19},{19,3},{4,20},{20... | collective-permute-start | bytes 786440 | tf_op jit(solution)/shard_map/ppermute | solution.py:348
  11.8 9.8 %collective-permute-start.2 = (f32[256,128]{1,0:T(8,128)S(1)}, f32[256,128]{1,0:T(8,128)S(1)}, u32[]{:S(2)}, u32[]{:S(2)}) collective-permute-start(f32[256,128]{1,0:T(8,128)S(1)} %get-tuple-element.35), channel_id=1, source_target_pairs={{0,8},{1,9},{2,10},{3,11},{4,12},{5,13},{6,14},{7,15},{8,0},{9,1},... | collective-permute-start | bytes 393224 | tf_op jit(solution)/shard_map/ppermute | solution.py:344
  20.0 7.4 %collective-permute-start.4 = (f32[328,128]{1,0:T(8,128)S(1)}, f32[328,128]{1,0:T(8,128)S(1)}, u32[]{:S(2)}, u32[]{:S(2)}) collective-permute-start(f32[328,128]{1,0:T(8,128)S(1)} %collective-permute-done.1.near_ref), channel_id=1, source_target_pairs={{0,16},{16,0},{1,17},{17,1},{2,18},{18,2},{3,19},{19,3},{4,20},{20... | collective-permute-start | bytes 503816 | tf_op jit(solution)/shard_map/ppermute | solution.py:348
  21.6 7.4 %collective-permute-start.5 = (f32[256,128]{1,0:T(8,128)S(1)}, f32[256,128]{1,0:T(8,128)S(1)}, u32[]{:S(2)}, u32[]{:S(2)}) collective-permute-start(f32[256,128]{1,0:T(8,128)S(1)} %collective-permute-done.2.side_ref), channel_id=1, source_target_pairs={{0,16},{16,0},{1,17},{17,1},{2,18},{18,2},{3,19},{19,3},{4,20},{20... | collective-permute-start | bytes 393224 | tf_op jit(solution)/shard_map/ppermute | solution.py:348
  22.1 25.2 %collective-permute-start.7 = (f32[512,128]{1,0:T(8,128)S(1)}, f32[512,128]{1,0:T(8,128)S(1)}, u32[]{:S(2)}, u32[]{:S(2)}) collective-permute-start(f32[512,128]{1,0:T(8,128)S(1)} %get-tuple-element.42), channel_id=1, source_target_pairs={{0,8},{1,9},{2,10},{3,11},{4,12},{5,13},{6,14},{7,15},{8,0},{9,1},... | collective-permute-start | bytes 786440 | tf_op jit(solution)/shard_map/ppermute | solution.py:344
  22.2 26.5 %collective-permute-start.8 = (f32[512,128]{1,0:T(8,128)S(1)}, f32[512,128]{1,0:T(8,128)S(1)}, u32[]{:S(2)}, u32[]{:S(2)}) collective-permute-start(f32[512,128]{1,0:T(8,128)S(1)} %get-tuple-element.43), channel_id=1, source_target_pairs={{0,8},{1,9},{2,10},{3,11},{4,12},{5,13},{6,14},{7,15},{8,0},{9,1},... | collective-permute-start | bytes 786440 | tf_op jit(solution)/shard_map/ppermute | solution.py:344
  25.6 12.4 %collective-permute-start.6 = (f32[256,256]{1,0:T(8,128)S(1)}, f32[256,256]{1,0:T(8,128)S(1)}, u32[]{:S(2)}, u32[]{:S(2)}) collective-permute-start(f32[256,256]{1,0:T(8,128)S(1)} %get-tuple-element.50), channel_id=1, source_target_pairs={{0,16},{16,0},{1,17},{17,1},{2,18},{18,2},{3,19},{19,3},{4,20},{20... | collective-permute-start | bytes 786440 | tf_op jit(solution)/shard_map/ppermute | solution.py:348
  29.0 9.1 %copy-start.1 = (f32[1,256,1024]{2,1,0:T(8,128)S(1)}, f32[1,256,1024]{2,1,0:T(8,128)}, u32[]{:S(2)}) copy-start(f32[1,256,1024]{2,1,0:T(8,128)} %param.3) | copy-start | bytes 3145732
  48.6 5.8 %collective-permute-start.9 = (f32[256,128]{1,0:T(8,128)S(1)}, f32[256,128]{1,0:T(8,128)S(1)}, u32[]{:S(2)}, u32[]{:S(2)}) collective-permute-start(f32[256,128]{1,0:T(8,128)S(1)} %get-tuple-element.56), channel_id=1, source_target_pairs={{0,16},{16,0},{1,17},{17,1},{2,18},{18,2},{3,19},{19,3},{4,20},{20... | collective-permute-start | bytes 393224 | tf_op jit(solution)/shard_map/ppermute | solution.py:348
  48.7 2.5 %copy-start.2 = (f32[1,256,512]{2,1,0:T(8,128)S(1)}, f32[1,256,512]{2,1,0:T(8,128)}, u32[]{:S(2)}) copy-start(f32[1,256,512]{2,1,0:T(8,128)} %param.4) | copy-start | bytes 1572868
  49.1 5.9 %collective-permute-start.10 = (f32[256,128]{1,0:T(8,128)S(1)}, f32[256,128]{1,0:T(8,128)S(1)}, u32[]{:S(2)}, u32[]{:S(2)}) collective-permute-start(f32[256,128]{1,0:T(8,128)S(1)} %shard_map.66), channel_id=1, source_target_pairs={{0,16},{16,0},{1,17},{17,1},{2,18},{18,2},{3,19},{19,3},{4,20},{20... | collective-permute-start | bytes 393224 | tf_op jit(solution)/shard_map/ppermute | solution.py:348

commit v8 on v7

--- a/solution.py
+++ b/solution.py
@@ -214,14 +214,12 @@
     return first, ref[0:q, :], second
 
 
-def prepare_body(half, t_ref, early_ref, near_ref, side_ref, column_ref, first_ref, a_out, m_out, p_out, outer_out):
+def prepare_body(half, t_ref, early_ref, near_ref, side_ref, column_ref, row_ref, first_ref, a_out, m_out, p_out, outer_out):
     n, q = 2 * half, half // 2
     width = t_ref.shape[1] - n
     mine = first_ref[0]
     put_sibling(m_out, near_ref, side_ref, 0, mine)
-    at = 5 * q // 2
-    row = jnp.concatenate([near_ref[at + i : at + i + 1, :] for i in range(n // q)], axis=1)
-    p_out[...] = jnp.where(column_ref[...] == row, 1.0, 0.0).astype(BF16)
+    p_out[...] = jnp.where(column_ref[...] == row_ref[...], 1.0, 0.0).astype(BF16)
     here = pl.ds(pl.multiple_of(width + mine * half, half), half)
     there = pl.ds(pl.multiple_of(width + (1 - mine) * half, half), half)
     a_out[0:half, 0:half] = t_ref[:, here]
@@ -307,8 +305,8 @@
         out_ref[:, pl.ds(pl.multiple_of((1 - mine) * half + i * q, q), q)] = part[...]
 
 
-def pack_iface_body(half, width, t_ref, map_ref, first_ref, diag_ref, side_ref, outer_ref, row_ref, column_ref):
-    q, n = half // 2, 2 * half
+def pack_iface_body(half, width, t_ref, first_ref, diag_ref, side_ref, outer_ref):
+    q = half // 2
     mine = first_ref[0]
     here, there = width + mine * half, width + (1 - mine) * half
 
@@ -321,13 +319,13 @@
         at += block.shape[0]
     side_ref[0:q, :] = cut(0, there + q)
     side_ref[q : 2 * q, :] = cut(mine * q, there + mine * q)
-    spans = column_blocks(half, mine)
-    outer_ref[...] = t_ref[:, spans[1]]
-    row = jnp.concatenate([map_ref[:, span] for span in spans], axis=1).astype(F32)
+    outer_ref[...] = t_ref[:, column_blocks(half, mine)[1]]
+
+
+def map_body(half, map_ref, first_ref, row_ref, column_ref):
+    row = jnp.concatenate([map_ref[:, block] for block in column_blocks(half, first_ref[0])], axis=1).astype(F32)
     row_ref[...] = row
-    column_ref[...] = jnp.broadcast_to(row, (8, n)).T[:, 0:1]
-    parts = [row[:, i * q : (i + 1) * q] for i in range(n // q)]
-    diag_ref[at:, :] = jnp.concatenate(parts + parts, axis=0)[0:8, :]
+    column_ref[...] = jnp.broadcast_to(row, (8, 2 * half)).T[:, 0:1]
 
 
 def pack_outer_body(t_ref, mine_ref, first_ref, *chunks):
@@ -369,28 +367,29 @@
     vmem, smem = pltpu.VMEM, pltpu.SMEM
     mine = lax.axis_index("sib").astype(jnp.int32)
     first = mine.reshape(1)
-    diag, side, outer, own_row, column = kernel(
+    diag, side, outer = kernel(
         functools.partial(pack_iface_body, half, width),
-        (f(5 * q // 2 + 8, q), f(2 * q, q), f(half, half), f(1, n), f(n, 1)),
-        [vmem, vmem, smem],
-    )(t_int, iface_map, first)
-    near = sibling(diag)
+        (f(5 * q // 2, q), f(2 * q, q), f(half, half)),
+        [vmem, smem],
+    )(t_int, first)
+    near, near_side = sibling(diag), sibling(side)
     diag_other = across(diag)
     far = across(near)
-    side, outer, diag_other = lax.optimization_barrier((side, outer, diag_other))
-    near_side = sibling(side)
+    outer, diag_other = lax.optimization_barrier((outer, diag_other))
     outer_mine = across(outer)
+    own_row, column = kernel(functools.partial(map_body, half), (f(1, n), f(n, 1)), [vmem, smem])(iface_map, first)
+    other_row = sibling(own_row)
     near, near_side = lax.optimization_barrier((near, near_side))
     far_side = across(near_side)
     chunks = kernel(pack_outer_body, [f(n, q)] * 2, [vmem, vmem, smem])(t_int, outer_mine, first)
-    *chunks, _ = lax.optimization_barrier((*chunks, near_side))
+    *chunks, _, other_row = lax.optimization_barrier((*chunks, near_side, other_row))
     near_r = [sibling(chunk) for chunk in chunks]
     first_late, *_ = lax.optimization_barrier((first, *chunks))
     a, m, onehot, outer = kernel(
         functools.partial(prepare_body, half),
         (f(n, n), f(n, n), jax.ShapeDtypeStruct((n, n), BF16), f(half, half)),
-        [vmem] * 5 + [smem],
-    )(t_int, diag_other, near, near_side, column, first_late)
+        [vmem] * 6 + [smem],
+    )(t_int, diag_other, near, near_side, column, other_row, first_late)
     outer_others = across(outer)
     top = tiles // 2 * TILE
     a, b = kernel(

time: 56.1 us -> 58 us (1.034)
  waiting for transfers between devices: 10.8 us -> 13.4 us
  local copies, waits for them, and re-layouts: 1.91 us -> 1.23 us
    ppermute x4 -> x5, waiting for transfers between devices: 6.8 us -> 11.1 us  [sibling(): return lax.ppermute(x, 'leaf', [(i, i ^ size // 2) for i in range(size)])]
    ppermute x7, waiting for transfers between devices: 4.01 us -> 2.25 us  [across(): return lax.ppermute(x, 'sib', [(0, 1), (1, 0)])]
    unnamed x8, local copies, waits for them, and re-layouts: 1.91 us -> 1.23 us
    ppermute x4 -> x5, starting transfers between devices: 8.16 us -> 8.17 us  [sibling(): return lax.ppermute(x, 'leaf', [(i, i ^ size // 2) for i in range(size)])]
  transfers between devices with their start and end apart: 11 -> 12, of which waited for: 5 -> 5; matrix products, arithmetic and copies ran while one was open for 0% -> 0% of each run, Pallas kernels for 43% -> 41%
where the time goes in v8:
time: 58 us; the launch traced here: 57.9 us
  Pallas kernels  24.8 us (43%)
  starting transfers between devices  17.7 us (31%)
  waiting for transfers between devices  13.4 us (23%)
  local copies, waits for them, and re-layouts  1.23 us (2%)
  between operations  0.76 us (1%)
    ppermute x5, waiting for transfers between devices, sibling(): return lax.ppermute(x, 'leaf', [(i, i ^ size // 2) for i in range(size)])  11.1 us
    ppermute x7, starting transfers between devices, across(): return lax.ppermute(x, 'sib', [(0, 1), (1, 0)])  9.49 us
    pallas_call x1, Pallas kernels, two_shards(): kernel(functools.partial(first_body, range(tiles // 2)), (f(n, n), f(top,...  9.07 us
    ppermute x5, starting transfers between devices, sibling(): return lax.ppermute(x, 'leaf', [(i, i ^ size // 2) for i in range(size)])  8.17 us
    pallas_call x1, Pallas kernels, two_shards(): kernel(functools.partial(middle_body, range(tiles // 2, tiles - 1)), (f(n...  5.09 us
    pallas_call x1, Pallas kernels, two_shards(): kernel(functools.partial(last_body, range(tiles - 1, tiles)), f(n, width)...  4.12 us
    pallas_call x1, Pallas kernels, two_shards(): kernel(functools.partial(output_body, half), (f(half, width), f(half, wid...  3.22 us
    ppermute x7, waiting for transfers between devices, across(): return lax.ppermute(x, 'sib', [(0, 1), (1, 0)])  2.25 us
  transfers between devices with their start and end apart: 12, of which 5 were waited for; matrix products, arithmetic and copies ran while one was open for 0% of the time, Pallas kernels for 41%

profile of v8, /device:TPU:0, one launch (start us, length us, event | category | flops | bytes accessed | tf_op | source)
XLA Modules:
  0.0 57.9 jit_solution(11702483008043719220)
XLA Ops:
  0.6 1.2 %copy-done = f32[1,256,1024]{2,1,0:T(8,128)S(1)} copy-done((f32[1,256,1024]{2,1,0:T(8,128)S(1)}, f32[1,256,1024]{2,1,0:T(8,128)}, u32[]{:S(2)}) %copy-start) | copy-done | bytes 1048600
  1.9 3.0 %collective-permute-start = (f32[320,128]{1,0:T(8,128)S(1)}, f32[320,128]{1,0:T(8,128)S(1)}, u32[]{:S(2)}, u32[]{:S(2)}) collective-permute-start(f32[320,128]{1,0:T(8,128)S(1)} %get-tuple-element.32), channel_id=1, source_target_pairs={{0,16},{16,0},{1,17},{17,1},{2,18},{18,2},{3,19},{19,3},{4,20},{20... | collective-permute-start | bytes 491528 | tf_op jit(solution)/shard_map/ppermute | solution.py:346
  5.0 2.6 %collective-permute-start.1 = (f32[320,128]{1,0:T(8,128)S(1)}, f32[320,128]{1,0:T(8,128)S(1)}, u32[]{:S(2)}, u32[]{:S(2)}) collective-permute-start(f32[320,128]{1,0:T(8,128)S(1)} %get-tuple-element.32), channel_id=1, source_target_pairs={{0,8},{1,9},{2,10},{3,11},{4,12},{5,13},{6,14},{7,15},{8,0},{9,1},... | collective-permute-start | bytes 491528 | tf_op jit(solution)/shard_map/ppermute | solution.py:342
  7.5 1.6 %collective-permute-done.early_ref = f32[320,128]{1,0:T(8,128)S(1)} collective-permute-done((f32[320,128]{1,0:T(8,128)S(1)}, f32[320,128]{1,0:T(8,128)S(1)}, u32[]{:S(2)}, u32[]{:S(2)}) %collective-permute-start) | collective-permute-done | bytes 163872 | tf_op jit(solution)/shard_map/ppermute | solution.py:346
  9.2 1.7 %collective-permute-start.3 = (f32[256,256]{1,0:T(8,128)S(1)}, f32[256,256]{1,0:T(8,128)S(1)}, u32[]{:S(2)}, u32[]{:S(2)}) collective-permute-start(f32[256,256]{1,0:T(8,128)S(1)} %get-tuple-element.38), channel_id=1, source_target_pairs={{0,16},{16,0},{1,17},{17,1},{2,18},{18,2},{3,19},{19,3},{4,20},{20... | collective-permute-start | bytes 786440 | tf_op jit(solution)/shard_map/ppermute | solution.py:346
  10.9 2.6 %collective-permute-start.2 = (f32[256,128]{1,0:T(8,128)S(1)}, f32[256,128]{1,0:T(8,128)S(1)}, u32[]{:S(2)}, u32[]{:S(2)}) collective-permute-start(f32[256,128]{1,0:T(8,128)S(1)} %get-tuple-element.34), channel_id=1, source_target_pairs={{0,8},{1,9},{2,10},{3,11},{4,12},{5,13},{6,14},{7,15},{8,0},{9,1},... | collective-permute-start | bytes 393224 | tf_op jit(solution)/shard_map/ppermute | solution.py:342
  13.5 5.5 %collective-permute-done.1.near_ref = f32[320,128]{1,0:T(8,128)S(1)} collective-permute-done((f32[320,128]{1,0:T(8,128)S(1)}, f32[320,128]{1,0:T(8,128)S(1)}, u32[]{:S(2)}, u32[]{:S(2)}) %collective-permute-start.1) | collective-permute-done | bytes 163872 | tf_op jit(solution)/shard_map/ppermute | solution.py:342
  19.0 0.5 collective-permute-start.5
  19.4 1.2 %collective-permute-done.2.side_ref = f32[256,128]{1,0:T(8,128)S(1)} collective-permute-done((f32[256,128]{1,0:T(8,128)S(1)}, f32[256,128]{1,0:T(8,128)S(1)}, u32[]{:S(2)}, u32[]{:S(2)}) %collective-permute-start.2) | collective-permute-done | bytes 131104 | tf_op jit(solution)/shard_map/ppermute | solution.py:342
  20.6 0.5 collective-permute-start.6
  21.4 4.4 %collective-permute-done.4.row_ref = f32[1,512]{1,0:T(1,128)S(1)} collective-permute-done((f32[1,512]{1,0:T(1,128)S(1)}, f32[1,512]{1,0:T(1,128)S(1)}, u32[]{:S(2)}, u32[]{:S(2)}) %collective-permute-start.4) | collective-permute-done | bytes 2080 | tf_op jit(solution)/shard_map/ppermute | solution.py:342
  25.8 2.9 %collective-permute-start.9 = (f32[512,128]{1,0:T(8,128)S(1)}, f32[512,128]{1,0:T(8,128)S(1)}, u32[]{:S(2)}, u32[]{:S(2)}) collective-permute-start(f32[512,128]{1,0:T(8,128)S(1)} %get-tuple-element.44), channel_id=1, source_target_pairs={{0,8},{1,9},{2,10},{3,11},{4,12},{5,13},{6,14},{7,15},{8,0},{9,1},... | collective-permute-start | bytes 786440 | tf_op jit(solution)/shard_map/ppermute | solution.py:342
  28.7 0.5 shard_map.61
  29.3 1.7 %collective-permute-start.7 = (f32[256,256]{1,0:T(8,128)S(1)}, f32[256,256]{1,0:T(8,128)S(1)}, u32[]{:S(2)}, u32[]{:S(2)}) collective-permute-start(f32[256,256]{1,0:T(8,128)S(1)} %get-tuple-element.51), channel_id=1, source_target_pairs={{0,16},{16,0},{1,17},{17,1},{2,18},{18,2},{3,19},{19,3},{4,20},{20... | collective-permute-start | bytes 786440 | tf_op jit(solution)/shard_map/ppermute | solution.py:346
  30.9 9.1 %shard_map.62 = (f32[512,512]{1,0:T(8,128)S(1)}, f32[256,256]{1,0:T(8,128)S(1)}) custom-call(f32[512,512]{1,0:T(8,128)S(1)} %get-tuple-element.46.a_in, f32[512,512]{1,0:T(8,128)S(1)} %get-tuple-element.47.m_in, bf16[512,512]{1,0:T(8,128)(2,1)S(1)} %get-tuple-element.48.p_ref, f32[320,128]{1,0:T(8,128)S(1)} %collective-permute-done.5.far_ref, ...), custom_call_target="tpu_custom_call" | custom-call | flops 10000000000 | bytes 1048576 | tf_op jit(solution)/shard_map/pallas_call | solution.py:395
  40.0 5.1 %shard_map.63 = (f32[512,512]{1,0:T(8,128)S(1)}, f32[512,512]{1,0:T(8,128)S(1)}) custom-call(f32[512,512]{1,0:T(8,128)S(1)} %get-tuple-element.49.a_in, f32[256,256]{1,0:T(8,128)S(1)} %get-tuple-element.50.b_ref, f32[256,1024]{1,0:T(8,128)S(1)} %bitcast.9, f32[256,256]{1,0:T(8,128)S(1)} %collective-permute-done.3.mine_ref, ...), custom_call_target="tpu_custom_call" | custom-call | flops 5000000000 | bytes 1048576 | tf_op jit(solution)/shard_map/pallas_call | solution.py:402
  45.1 4.1 %shard_map.64.g_ref = f32[512,512]{1,0:T(8,128)S(1)} custom-call(f32[512,512]{1,0:T(8,128)S(1)} %get-tuple-element.52.a_ref, f32[512,512]{1,0:T(8,128)S(1)} %get-tuple-element.53.g_in), custom_call_target="tpu_custom_call" | custom-call | flops 5000000000 | bytes 1048576 | tf_op jit(solution)/shard_map/pallas_call | solution.py:409
  49.3 1.3 %shard_map.66 = (f32[512,256]{1,0:T(8,128)S(1)}, f32[256,128]{1,0:T(8,128)S(1)}) custom-call(f32[512,512]{1,0:T(8,128)S(1)} %shard_map.64.g_ref, bf16[512,512]{1,0:T(8,128)(2,1)S(1)} %get-tuple-element.48.p_ref, f32[512,128]{1,0:T(8,128)S(1)} %collective-permute-done.8.chunk_a.chunk_ref, s32[1]{0:T(128)} %bitcast.1.first_ref), custom_call_target="tpu_custom_call" | custom-call | flops 1000000000 | bytes 1048576 | tf_op jit(solution)/shard_map/pallas_call | solution.py:412
  50.6 0.4 collective-permute-start.10
  51.0 0.4 shard_map.67
  51.4 1.7 %collective-permute-start.11 = (f32[256,128]{1,0:T(8,128)S(1)}, f32[256,128]{1,0:T(8,128)S(1)}, u32[]{:S(2)}, u32[]{:S(2)}) collective-permute-start(f32[256,128]{1,0:T(8,128)S(1)} %shard_map.67), channel_id=1, source_target_pairs={{0,16},{16,0},{1,17},{17,1},{2,18},{18,2},{3,19},{19,3},{4,20},{20... | collective-permute-start | bytes 393224 | tf_op jit(solution)/shard_map/ppermute | solution.py:346
  53.2 3.2 %shard_map.65 = (f32[256,512]{1,0:T(8,128)}, f32[256,512]{1,0:T(8,128)}, f32[256,256]{1,0:T(8,128)S(1)}) custom-call(f32[512,512]{1,0:T(8,128)S(1)} %shard_map.64.g_ref, bf16[512,512]{1,0:T(8,128)(2,1)S(1)} %get-tuple-element.48.p_ref, f32[256,1024]{1,0:T(8,128)S(1)} %bitcast.10, f32[256,256]{1,0:T(8,128)S(1)} %collective-permute-done.3.mine_ref, ...), custom_call_target="tpu_custom_call" | custom-call | flops 1000000 | bytes 1048576 | tf_op jit(solution)/shard_map/pallas_call | solution.py:417
  56.4 0.6 %collective-permute-done.11.second_part = f32[256,128]{1,0:T(8,128)S(1)} collective-permute-done((f32[256,128]{1,0:T(8,128)S(1)}, f32[256,128]{1,0:T(8,128)S(1)}, u32[]{:S(2)}, u32[]{:S(2)}) %collective-permute-start.11) | collective-permute-done | bytes 131104 | tf_op jit(solution)/shard_map/ppermute | solution.py:346
  57.0 0.8 %shard_map.68 = f32[256,512]{1,0:T(8,128)} custom-call(f32[256,256]{1,0:T(8,128)S(1)} %get-tuple-element.55.keep_ref, f32[256,128]{1,0:T(8,128)S(1)} %collective-permute-done.10.first_part, f32[256,128]{1,0:T(8,128)S(1)} %collective-permute-done.11.second_part, s32[1]{0:T(128)} %bitcast.1.first_ref), custom_call_target="tpu_custom_call" | custom-call | flops 100000000 | bytes 1048576 | tf_op jit(solution)/shard_map/pallas_call | solution.py:424
  (19 shorter events, 0.4 us)
Async XLA Ops:
  0.6 1.2 %copy-start = (f32[1,256,1024]{2,1,0:T(8,128)S(1)}, f32[1,256,1024]{2,1,0:T(8,128)}, u32[]{:S(2)}) copy-start(f32[1,256,1024]{2,1,0:T(8,128)} %param.3) | copy-start | bytes 3145732
  1.9 19.5 %copy-start.1 = (f32[1,256,1024]{2,1,0:T(8,128)S(1)}, f32[1,256,1024]{2,1,0:T(8,128)}, u32[]{:S(2)}) copy-start(f32[1,256,1024]{2,1,0:T(8,128)} %param.3) | copy-start | bytes 3145732
  1.9 19.2 %copy-start.3 = (s32[1,512]{1,0:T(1,128)S(1)}, s32[1,512]{1,0:T(1,128)}, u32[]{:S(2)}) copy-start(s32[1,512]{1,0:T(1,128)} %map_ref.1) | copy-start | bytes 6148
  1.9 7.2 %collective-permute-start = (f32[320,128]{1,0:T(8,128)S(1)}, f32[320,128]{1,0:T(8,128)S(1)}, u32[]{:S(2)}, u32[]{:S(2)}) collective-permute-start(f32[320,128]{1,0:T(8,128)S(1)} %get-tuple-element.32), channel_id=1, source_target_pairs={{0,16},{16,0},{1,17},{17,1},{2,18},{18,2},{3,19},{19,3},{4,20},{20... | collective-permute-start | bytes 491528 | tf_op jit(solution)/shard_map/ppermute | solution.py:346
  5.0 14.0 %collective-permute-start.1 = (f32[320,128]{1,0:T(8,128)S(1)}, f32[320,128]{1,0:T(8,128)S(1)}, u32[]{:S(2)}, u32[]{:S(2)}) collective-permute-start(f32[320,128]{1,0:T(8,128)S(1)} %get-tuple-element.32), channel_id=1, source_target_pairs={{0,8},{1,9},{2,10},{3,11},{4,12},{5,13},{6,14},{7,15},{8,0},{9,1},... | collective-permute-start | bytes 491528 | tf_op jit(solution)/shard_map/ppermute | solution.py:342
  9.2 12.2 %collective-permute-start.3 = (f32[256,256]{1,0:T(8,128)S(1)}, f32[256,256]{1,0:T(8,128)S(1)}, u32[]{:S(2)}, u32[]{:S(2)}) collective-permute-start(f32[256,256]{1,0:T(8,128)S(1)} %get-tuple-element.38), channel_id=1, source_target_pairs={{0,16},{16,0},{1,17},{17,1},{2,18},{18,2},{3,19},{19,3},{4,20},{20... | collective-permute-start | bytes 786440 | tf_op jit(solution)/shard_map/ppermute | solution.py:346
  10.9 9.7 %collective-permute-start.2 = (f32[256,128]{1,0:T(8,128)S(1)}, f32[256,128]{1,0:T(8,128)S(1)}, u32[]{:S(2)}, u32[]{:S(2)}) collective-permute-start(f32[256,128]{1,0:T(8,128)S(1)} %get-tuple-element.34), channel_id=1, source_target_pairs={{0,8},{1,9},{2,10},{3,11},{4,12},{5,13},{6,14},{7,15},{8,0},{9,1},... | collective-permute-start | bytes 393224 | tf_op jit(solution)/shard_map/ppermute | solution.py:342
  19.0 11.9 %collective-permute-start.5 = (f32[320,128]{1,0:T(8,128)S(1)}, f32[320,128]{1,0:T(8,128)S(1)}, u32[]{:S(2)}, u32[]{:S(2)}) collective-permute-start(f32[320,128]{1,0:T(8,128)S(1)} %collective-permute-done.1.near_ref), channel_id=1, source_target_pairs={{0,16},{16,0},{1,17},{17,1},{2,18},{18,2},{3,19},{19,3},{4,20},{20... | collective-permute-start | bytes 491528 | tf_op jit(solution)/shard_map/ppermute | solution.py:346
  20.6 10.3 %collective-permute-start.6 = (f32[256,128]{1,0:T(8,128)S(1)}, f32[256,128]{1,0:T(8,128)S(1)}, u32[]{:S(2)}, u32[]{:S(2)}) collective-permute-start(f32[256,128]{1,0:T(8,128)S(1)} %collective-permute-done.2.side_ref), channel_id=1, source_target_pairs={{0,16},{16,0},{1,17},{17,1},{2,18},{18,2},{3,19},{19,3},{4,20},{20... | collective-permute-start | bytes 393224 | tf_op jit(solution)/shard_map/ppermute | solution.py:346
  21.3 4.5 %collective-permute-start.4 = (f32[1,512]{1,0:T(1,128)S(1)}, f32[1,512]{1,0:T(1,128)S(1)}, u32[]{:S(2)}, u32[]{:S(2)}) collective-permute-start(f32[1,512]{1,0:T(1,128)S(1)} %get-tuple-element.41.row_ref), channel_id=1, source_target_pairs={{0,8},{1,9},{2,10},{3,11},{4,12},{5,13},{6,14},{7,15},{8,0},{9,1},... | collective-permute-start | bytes 6152 | tf_op jit(solution)/shard_map/ppermute | solution.py:342
  25.8 23.4 %collective-permute-start.8 = (f32[512,128]{1,0:T(8,128)S(1)}, f32[512,128]{1,0:T(8,128)S(1)}, u32[]{:S(2)}, u32[]{:S(2)}) collective-permute-start(f32[512,128]{1,0:T(8,128)S(1)} %get-tuple-element.43), channel_id=1, source_target_pairs={{0,8},{1,9},{2,10},{3,11},{4,12},{5,13},{6,14},{7,15},{8,0},{9,1},... | collective-permute-start | bytes 786440 | tf_op jit(solution)/shard_map/ppermute | solution.py:342
  25.8 25.2 %collective-permute-start.9 = (f32[512,128]{1,0:T(8,128)S(1)}, f32[512,128]{1,0:T(8,128)S(1)}, u32[]{:S(2)}, u32[]{:S(2)}) collective-permute-start(f32[512,128]{1,0:T(8,128)S(1)} %get-tuple-element.44), channel_id=1, source_target_pairs={{0,8},{1,9},{2,10},{3,11},{4,12},{5,13},{6,14},{7,15},{8,0},{9,1},... | collective-permute-start | bytes 786440 | tf_op jit(solution)/shard_map/ppermute | solution.py:342
  29.3 10.7 %collective-permute-start.7 = (f32[256,256]{1,0:T(8,128)S(1)}, f32[256,256]{1,0:T(8,128)S(1)}, u32[]{:S(2)}, u32[]{:S(2)}) collective-permute-start(f32[256,256]{1,0:T(8,128)S(1)} %get-tuple-element.51), channel_id=1, source_target_pairs={{0,16},{16,0},{1,17},{17,1},{2,18},{18,2},{3,19},{19,3},{4,20},{20... | collective-permute-start | bytes 786440 | tf_op jit(solution)/shard_map/ppermute | solution.py:346
  50.6 5.8 %collective-permute-start.10 = (f32[256,128]{1,0:T(8,128)S(1)}, f32[256,128]{1,0:T(8,128)S(1)}, u32[]{:S(2)}, u32[]{:S(2)}) collective-permute-start(f32[256,128]{1,0:T(8,128)S(1)} %get-tuple-element.56), channel_id=1, source_target_pairs={{0,16},{16,0},{1,17},{17,1},{2,18},{18,2},{3,19},{19,3},{4,20},{20... | collective-permute-start | bytes 393224 | tf_op jit(solution)/shard_map/ppermute | solution.py:346
  51.0 2.1 %copy-start.2 = (f32[1,256,512]{2,1,0:T(8,128)S(1)}, f32[1,256,512]{2,1,0:T(8,128)}, u32[]{:S(2)}) copy-start(f32[1,256,512]{2,1,0:T(8,128)} %param.4) | copy-start | bytes 1572868
  51.4 5.6 %collective-permute-start.11 = (f32[256,128]{1,0:T(8,128)S(1)}, f32[256,128]{1,0:T(8,128)S(1)}, u32[]{:S(2)}, u32[]{:S(2)}) collective-permute-start(f32[256,128]{1,0:T(8,128)S(1)} %shard_map.67), channel_id=1, source_target_pairs={{0,16},{16,0},{1,17},{17,1},{2,18},{18,2},{3,19},{19,3},{4,20},{20... | collective-permute-start | bytes 393224 | tf_op jit(solution)/shard_map/ppermute | solution.py:346

commit v9 on v7

--- a/solution.py
+++ b/solution.py
@@ -377,7 +377,6 @@
     near = sibling(diag)
     diag_other = across(diag)
     far = across(near)
-    side, outer, diag_other = lax.optimization_barrier((side, outer, diag_other))
     near_side = sibling(side)
     outer_mine = across(outer)
     near, near_side = lax.optimization_barrier((near, near_side))

time: 56.1 us -> 55.2 us (0.984)
  starting transfers between devices: 17.6 us -> 15.6 us
  waiting for transfers between devices: 10.8 us -> 11.4 us
    ppermute x4, waiting for transfers between devices: 6.8 us -> 9.56 us  [sibling(): return lax.ppermute(x, 'leaf', [(i, i ^ size // 2) for i in range(size)])]
    ppermute x7, waiting for transfers between devices: 4.01 us -> 1.87 us  [across(): return lax.ppermute(x, 'sib', [(0, 1), (1, 0)])]
    ppermute x7, starting transfers between devices: 9.46 us -> 8.14 us  [across(): return lax.ppermute(x, 'sib', [(0, 1), (1, 0)])]
    ppermute x4, starting transfers between devices: 8.16 us -> 7.42 us  [sibling(): return lax.ppermute(x, 'leaf', [(i, i ^ size // 2) for i in range(size)])]
  transfers between devices with their start and end apart: 11 -> 11, of which waited for: 5 -> 4; matrix products, arithmetic and copies ran while one was open for 0% -> 0% of each run, Pallas kernels for 43% -> 43%
where the time goes in v9:
time: 55.2 us; the launch traced here: 55 us
  Pallas kernels  24.8 us (45%)
  starting transfers between devices  15.6 us (28%)
  waiting for transfers between devices  11.4 us (21%)
  local copies, waits for them, and re-layouts  2.43 us (4%)
  between operations  0.74 us (1%)
    ppermute x4, waiting for transfers between devices, sibling(): return lax.ppermute(x, 'leaf', [(i, i ^ size // 2) for i in range(size)])  9.56 us
    pallas_call x1, Pallas kernels, two_shards(): kernel(functools.partial(first_body, range(tiles // 2)), (f(n, n), f(top,...  9.05 us
    ppermute x7, starting transfers between devices, across(): return lax.ppermute(x, 'sib', [(0, 1), (1, 0)])  8.14 us
    ppermute x4, starting transfers between devices, sibling(): return lax.ppermute(x, 'leaf', [(i, i ^ size // 2) for i in range(size)])  7.42 us
    pallas_call x1, Pallas kernels, two_shards(): kernel(functools.partial(middle_body, range(tiles // 2, tiles - 1)), (f(n...  5.08 us
    pallas_call x1, Pallas kernels, two_shards(): kernel(functools.partial(last_body, range(tiles - 1, tiles)), f(n, width)...  4.13 us
    pallas_call x1, Pallas kernels, two_shards(): kernel(functools.partial(output_body, half), (f(half, width), f(half, wid...  3.22 us
    unnamed x8, local copies, waits for them, and re-layouts  2.43 us
  transfers between devices with their start and end apart: 11, of which 4 were waited for; matrix products, arithmetic and copies ran while one was open for 0% of the time, Pallas kernels for 43%

profile of v9, /device:TPU:0, one launch (start us, length us, event | category | flops | bytes accessed | tf_op | source)
XLA Modules:
  0.0 55.0 jit_solution(17911477839605392757)
XLA Ops:
  0.6 0.7 %copy-done.3 = s32[1,512]{1,0:T(1,128)S(1)} copy-done((s32[1,512]{1,0:T(1,128)S(1)}, s32[1,512]{1,0:T(1,128)}, u32[]{:S(2)}) %copy-start.3) | copy-done | bytes 2072
  1.3 1.2 %copy-done = f32[1,256,1024]{2,1,0:T(8,128)S(1)} copy-done((f32[1,256,1024]{2,1,0:T(8,128)S(1)}, f32[1,256,1024]{2,1,0:T(8,128)}, u32[]{:S(2)}) %copy-start) | copy-done | bytes 1048600
  2.5 0.2 shard_map.58
  2.7 4.1 %collective-permute-start.1 = (f32[328,128]{1,0:T(8,128)S(1)}, f32[328,128]{1,0:T(8,128)S(1)}, u32[]{:S(2)}, u32[]{:S(2)}) collective-permute-start(f32[328,128]{1,0:T(8,128)S(1)} %get-tuple-element.28), channel_id=1, source_target_pairs={{0,8},{1,9},{2,10},{3,11},{4,12},{5,13},{6,14},{7,15},{8,0},{9,1},... | collective-permute-start | bytes 503816 | tf_op jit(solution)/shard_map/ppermute | solution.py:344
  6.8 1.5 %collective-permute-start.3 = (f32[256,256]{1,0:T(8,128)S(1)}, f32[256,256]{1,0:T(8,128)S(1)}, u32[]{:S(2)}, u32[]{:S(2)}) collective-permute-start(f32[256,256]{1,0:T(8,128)S(1)} %get-tuple-element.33), channel_id=1, source_target_pairs={{0,16},{16,0},{1,17},{17,1},{2,18},{18,2},{3,19},{19,3},{4,20},{20... | collective-permute-start | bytes 786440 | tf_op jit(solution)/shard_map/ppermute | solution.py:348
  8.3 0.3 collective-permute-start.2
  8.7 0.3 collective-permute-start
  8.9 9.4 %collective-permute-done.1.near_ref = f32[328,128]{1,0:T(8,128)S(1)} collective-permute-done((f32[328,128]{1,0:T(8,128)S(1)}, f32[328,128]{1,0:T(8,128)S(1)}, u32[]{:S(2)}, u32[]{:S(2)}) %collective-permute-start.1) | collective-permute-done | bytes 167968 | tf_op jit(solution)/shard_map/ppermute | solution.py:344
  18.3 1.8 %collective-permute-start.4 = (f32[328,128]{1,0:T(8,128)S(1)}, f32[328,128]{1,0:T(8,128)S(1)}, u32[]{:S(2)}, u32[]{:S(2)}) collective-permute-start(f32[328,128]{1,0:T(8,128)S(1)} %collective-permute-done.1.near_ref), channel_id=1, source_target_pairs={{0,16},{16,0},{1,17},{17,1},{2,18},{18,2},{3,19},{19,3},{4,20},{20... | collective-permute-start | bytes 503816 | tf_op jit(solution)/shard_map/ppermute | solution.py:348
  20.3 1.5 %collective-permute-start.5 = (f32[256,128]{1,0:T(8,128)S(1)}, f32[256,128]{1,0:T(8,128)S(1)}, u32[]{:S(2)}, u32[]{:S(2)}) collective-permute-start(f32[256,128]{1,0:T(8,128)S(1)} %collective-permute-done.2.side_ref), channel_id=1, source_target_pairs={{0,16},{16,0},{1,17},{17,1},{2,18},{18,2},{3,19},{19,3},{4,20},{20... | collective-permute-start | bytes 393224 | tf_op jit(solution)/shard_map/ppermute | solution.py:348
  22.0 2.9 %collective-permute-start.8 = (f32[512,128]{1,0:T(8,128)S(1)}, f32[512,128]{1,0:T(8,128)S(1)}, u32[]{:S(2)}, u32[]{:S(2)}) collective-permute-start(f32[512,128]{1,0:T(8,128)S(1)} %get-tuple-element.37), channel_id=1, source_target_pairs={{0,8},{1,9},{2,10},{3,11},{4,12},{5,13},{6,14},{7,15},{8,0},{9,1},... | collective-permute-start | bytes 786440 | tf_op jit(solution)/shard_map/ppermute | solution.py:344
  24.9 0.5 shard_map.60
  25.5 0.6 %collective-permute-start.6 = (f32[256,256]{1,0:T(8,128)S(1)}, f32[256,256]{1,0:T(8,128)S(1)}, u32[]{:S(2)}, u32[]{:S(2)}) collective-permute-start(f32[256,256]{1,0:T(8,128)S(1)} %get-tuple-element.44), channel_id=1, source_target_pairs={{0,16},{16,0},{1,17},{17,1},{2,18},{18,2},{3,19},{19,3},{4,20},{20... | collective-permute-start | bytes 786440 | tf_op jit(solution)/shard_map/ppermute | solution.py:348
  26.0 0.7 %collective-permute-done.5.side_ref = f32[256,128]{1,0:T(8,128)S(1)} collective-permute-done((f32[256,128]{1,0:T(8,128)S(1)}, f32[256,128]{1,0:T(8,128)S(1)}, u32[]{:S(2)}, u32[]{:S(2)}) %collective-permute-start.5) | collective-permute-done | bytes 131104 | tf_op jit(solution)/shard_map/ppermute | solution.py:348
  26.7 9.1 %shard_map.61 = (f32[512,512]{1,0:T(8,128)S(1)}, f32[256,256]{1,0:T(8,128)S(1)}) custom-call(f32[512,512]{1,0:T(8,128)S(1)} %get-tuple-element.39.a_in, f32[512,512]{1,0:T(8,128)S(1)} %get-tuple-element.40.m_in, bf16[512,512]{1,0:T(8,128)(2,1)S(1)} %get-tuple-element.41.p_ref, f32[328,128]{1,0:T(8,128)S(1)} %collective-permute-done.4.far_ref, ...), custom_call_target="tpu_custom_call" | custom-call | flops 10000000000 | bytes 1048576 | tf_op jit(solution)/shard_map/pallas_call | solution.py:395
  35.8 5.1 %shard_map.62 = (f32[512,512]{1,0:T(8,128)S(1)}, f32[512,512]{1,0:T(8,128)S(1)}) custom-call(f32[512,512]{1,0:T(8,128)S(1)} %get-tuple-element.42.a_in, f32[256,256]{1,0:T(8,128)S(1)} %get-tuple-element.43.b_ref, f32[256,1024]{1,0:T(8,128)S(1)} %bitcast.9, f32[256,256]{1,0:T(8,128)S(1)} %collective-permute-done.3.mine_ref, ...), custom_call_target="tpu_custom_call" | custom-call | flops 5000000000 | bytes 1048576 | tf_op jit(solution)/shard_map/pallas_call | solution.py:402
  40.9 4.1 %shard_map.63.g_ref = f32[512,512]{1,0:T(8,128)S(1)} custom-call(f32[512,512]{1,0:T(8,128)S(1)} %get-tuple-element.45.a_ref, f32[512,512]{1,0:T(8,128)S(1)} %get-tuple-element.46.g_in), custom_call_target="tpu_custom_call" | custom-call | flops 5000000000 | bytes 1048576 | tf_op jit(solution)/shard_map/pallas_call | solution.py:409
  45.0 1.3 %shard_map.65 = (f32[512,256]{1,0:T(8,128)S(1)}, f32[256,128]{1,0:T(8,128)S(1)}) custom-call(f32[512,512]{1,0:T(8,128)S(1)} %shard_map.63.g_ref, bf16[512,512]{1,0:T(8,128)(2,1)S(1)} %get-tuple-element.41.p_ref, f32[512,128]{1,0:T(8,128)S(1)} %collective-permute-done.7.chunk_a.chunk_ref, s32[1]{0:T(128)} %bitcast.1.first_ref), custom_call_target="tpu_custom_call" | custom-call | flops 1000000000 | bytes 1048576 | tf_op jit(solution)/shard_map/pallas_call | solution.py:412
  46.3 2.3 %collective-permute-start.9 = (f32[256,128]{1,0:T(8,128)S(1)}, f32[256,128]{1,0:T(8,128)S(1)}, u32[]{:S(2)}, u32[]{:S(2)}) collective-permute-start(f32[256,128]{1,0:T(8,128)S(1)} %get-tuple-element.50), channel_id=1, source_target_pairs={{0,16},{16,0},{1,17},{17,1},{2,18},{18,2},{3,19},{19,3},{4,20},{20... | collective-permute-start | bytes 393224 | tf_op jit(solution)/shard_map/ppermute | solution.py:348
  48.7 0.4 shard_map.66
  49.2 0.5 copy-done.2
  49.7 3.2 %shard_map.64 = (f32[256,512]{1,0:T(8,128)}, f32[256,512]{1,0:T(8,128)}, f32[256,256]{1,0:T(8,128)S(1)}) custom-call(f32[512,512]{1,0:T(8,128)S(1)} %shard_map.63.g_ref, bf16[512,512]{1,0:T(8,128)(2,1)S(1)} %get-tuple-element.41.p_ref, f32[256,1024]{1,0:T(8,128)S(1)} %bitcast.10, f32[256,256]{1,0:T(8,128)S(1)} %collective-permute-done.3.mine_ref, ...), custom_call_target="tpu_custom_call" | custom-call | flops 1000000 | bytes 1048576 | tf_op jit(solution)/shard_map/pallas_call | solution.py:417
  52.9 1.2 %collective-permute-done.10.second_part = f32[256,128]{1,0:T(8,128)S(1)} collective-permute-done((f32[256,128]{1,0:T(8,128)S(1)}, f32[256,128]{1,0:T(8,128)S(1)}, u32[]{:S(2)}, u32[]{:S(2)}) %collective-permute-start.10) | collective-permute-done | bytes 131104 | tf_op jit(solution)/shard_map/ppermute | solution.py:348
  54.1 0.8 %shard_map.67 = f32[256,512]{1,0:T(8,128)} custom-call(f32[256,256]{1,0:T(8,128)S(1)} %get-tuple-element.49.keep_ref, f32[256,128]{1,0:T(8,128)S(1)} %collective-permute-done.9.first_part, f32[256,128]{1,0:T(8,128)S(1)} %collective-permute-done.10.second_part, s32[1]{0:T(128)} %bitcast.1.first_ref), custom_call_target="tpu_custom_call" | custom-call | flops 100000000 | bytes 1048576 | tf_op jit(solution)/shard_map/pallas_call | solution.py:424
  (16 shorter events, 0.4 us)
Async XLA Ops:
  0.6 0.7 %copy-start.3 = (s32[1,512]{1,0:T(1,128)S(1)}, s32[1,512]{1,0:T(1,128)}, u32[]{:S(2)}) copy-start(s32[1,512]{1,0:T(1,128)} %map_ref.1) | copy-start | bytes 6148
  1.3 1.2 %copy-start = (f32[1,256,1024]{2,1,0:T(8,128)S(1)}, f32[1,256,1024]{2,1,0:T(8,128)}, u32[]{:S(2)}) copy-start(f32[1,256,1024]{2,1,0:T(8,128)} %param.3) | copy-start | bytes 3145732
  2.7 15.6 %collective-permute-start.1 = (f32[328,128]{1,0:T(8,128)S(1)}, f32[328,128]{1,0:T(8,128)S(1)}, u32[]{:S(2)}, u32[]{:S(2)}) collective-permute-start(f32[328,128]{1,0:T(8,128)S(1)} %get-tuple-element.28), channel_id=1, source_target_pairs={{0,8},{1,9},{2,10},{3,11},{4,12},{5,13},{6,14},{7,15},{8,0},{9,1},... | collective-permute-start | bytes 503816 | tf_op jit(solution)/shard_map/ppermute | solution.py:344
  6.8 15.1 %collective-permute-start.3 = (f32[256,256]{1,0:T(8,128)S(1)}, f32[256,256]{1,0:T(8,128)S(1)}, u32[]{:S(2)}, u32[]{:S(2)}) collective-permute-start(f32[256,256]{1,0:T(8,128)S(1)} %get-tuple-element.33), channel_id=1, source_target_pairs={{0,16},{16,0},{1,17},{17,1},{2,18},{18,2},{3,19},{19,3},{4,20},{20... | collective-permute-start | bytes 786440 | tf_op jit(solution)/shard_map/ppermute | solution.py:348
  8.3 12.0 %collective-permute-start.2 = (f32[256,128]{1,0:T(8,128)S(1)}, f32[256,128]{1,0:T(8,128)S(1)}, u32[]{:S(2)}, u32[]{:S(2)}) collective-permute-start(f32[256,128]{1,0:T(8,128)S(1)} %get-tuple-element.29), channel_id=1, source_target_pairs={{0,8},{1,9},{2,10},{3,11},{4,12},{5,13},{6,14},{7,15},{8,0},{9,1},... | collective-permute-start | bytes 393224 | tf_op jit(solution)/shard_map/ppermute | solution.py:344
  8.7 16.3 %collective-permute-start = (f32[328,128]{1,0:T(8,128)S(1)}, f32[328,128]{1,0:T(8,128)S(1)}, u32[]{:S(2)}, u32[]{:S(2)}) collective-permute-start(f32[328,128]{1,0:T(8,128)S(1)} %get-tuple-element.28), channel_id=1, source_target_pairs={{0,16},{16,0},{1,17},{17,1},{2,18},{18,2},{3,19},{19,3},{4,20},{20... | collective-permute-start | bytes 503816 | tf_op jit(solution)/shard_map/ppermute | solution.py:348
  18.3 8.4 %collective-permute-start.4 = (f32[328,128]{1,0:T(8,128)S(1)}, f32[328,128]{1,0:T(8,128)S(1)}, u32[]{:S(2)}, u32[]{:S(2)}) collective-permute-start(f32[328,128]{1,0:T(8,128)S(1)} %collective-permute-done.1.near_ref), channel_id=1, source_target_pairs={{0,16},{16,0},{1,17},{17,1},{2,18},{18,2},{3,19},{19,3},{4,20},{20... | collective-permute-start | bytes 503816 | tf_op jit(solution)/shard_map/ppermute | solution.py:348
  20.3 6.4 %collective-permute-start.5 = (f32[256,128]{1,0:T(8,128)S(1)}, f32[256,128]{1,0:T(8,128)S(1)}, u32[]{:S(2)}, u32[]{:S(2)}) collective-permute-start(f32[256,128]{1,0:T(8,128)S(1)} %collective-permute-done.2.side_ref), channel_id=1, source_target_pairs={{0,16},{16,0},{1,17},{17,1},{2,18},{18,2},{3,19},{19,3},{4,20},{20... | collective-permute-start | bytes 393224 | tf_op jit(solution)/shard_map/ppermute | solution.py:348
  21.9 23.1 %collective-permute-start.7 = (f32[512,128]{1,0:T(8,128)S(1)}, f32[512,128]{1,0:T(8,128)S(1)}, u32[]{:S(2)}, u32[]{:S(2)}) collective-permute-start(f32[512,128]{1,0:T(8,128)S(1)} %get-tuple-element.36), channel_id=1, source_target_pairs={{0,8},{1,9},{2,10},{3,11},{4,12},{5,13},{6,14},{7,15},{8,0},{9,1},... | collective-permute-start | bytes 786440 | tf_op jit(solution)/shard_map/ppermute | solution.py:344
  22.0 26.6 %collective-permute-start.8 = (f32[512,128]{1,0:T(8,128)S(1)}, f32[512,128]{1,0:T(8,128)S(1)}, u32[]{:S(2)}, u32[]{:S(2)}) collective-permute-start(f32[512,128]{1,0:T(8,128)S(1)} %get-tuple-element.37), channel_id=1, source_target_pairs={{0,8},{1,9},{2,10},{3,11},{4,12},{5,13},{6,14},{7,15},{8,0},{9,1},... | collective-permute-start | bytes 786440 | tf_op jit(solution)/shard_map/ppermute | solution.py:344
  25.5 10.3 %collective-permute-start.6 = (f32[256,256]{1,0:T(8,128)S(1)}, f32[256,256]{1,0:T(8,128)S(1)}, u32[]{:S(2)}, u32[]{:S(2)}) collective-permute-start(f32[256,256]{1,0:T(8,128)S(1)} %get-tuple-element.44), channel_id=1, source_target_pairs={{0,16},{16,0},{1,17},{17,1},{2,18},{18,2},{3,19},{19,3},{4,20},{20... | collective-permute-start | bytes 786440 | tf_op jit(solution)/shard_map/ppermute | solution.py:348
  26.7 9.1 %copy-start.1 = (f32[1,256,1024]{2,1,0:T(8,128)S(1)}, f32[1,256,1024]{2,1,0:T(8,128)}, u32[]{:S(2)}) copy-start(f32[1,256,1024]{2,1,0:T(8,128)} %param.3) | copy-start | bytes 3145732
  46.3 6.6 %collective-permute-start.9 = (f32[256,128]{1,0:T(8,128)S(1)}, f32[256,128]{1,0:T(8,128)S(1)}, u32[]{:S(2)}, u32[]{:S(2)}) collective-permute-start(f32[256,128]{1,0:T(8,128)S(1)} %get-tuple-element.50), channel_id=1, source_target_pairs={{0,16},{16,0},{1,17},{17,1},{2,18},{18,2},{3,19},{19,3},{4,20},{20... | collective-permute-start | bytes 393224 | tf_op jit(solution)/shard_map/ppermute | solution.py:348
  48.7 1.0 %copy-start.2 = (f32[1,256,512]{2,1,0:T(8,128)S(1)}, f32[1,256,512]{2,1,0:T(8,128)}, u32[]{:S(2)}) copy-start(f32[1,256,512]{2,1,0:T(8,128)} %param.4) | copy-start | bytes 1572868
  49.1 5.0 %collective-permute-start.10 = (f32[256,128]{1,0:T(8,128)S(1)}, f32[256,128]{1,0:T(8,128)S(1)}, u32[]{:S(2)}, u32[]{:S(2)}) collective-permute-start(f32[256,128]{1,0:T(8,128)S(1)} %shard_map.66), channel_id=1, source_target_pairs={{0,16},{16,0},{1,17},{17,1},{2,18},{18,2},{3,19},{19,3},{4,20},{20... | collective-permute-start | bytes 393224 | tf_op jit(solution)/shard_map/ppermute | solution.py:348

commit v10 on v9

--- a/solution.py
+++ b/solution.py
@@ -75,22 +75,30 @@
             jnp.where(inside, jnp.where(lane - base - 8 * s == row, 1.0, 0.0).astype(F32), old[s])
             for s in range(slabs)
         ]
-        pivot = over_rows(columns[0][0], 0)
+        corner = [over_rows(columns[0][0], 0), over_rows(columns[1][0], 0), over_rows(columns[1][0], 1)]
         scale = [None] * slabs
         for j in range(width):
             js, jr = divmod(j, 8)
-            inverse = pltpu.reciprocal(pivot, approx=True)
+            if j % 2 == 0:
+                a, b, c = corner
+                inverse = pltpu.reciprocal(a, approx=True)
+                inverse_next = a * pltpu.reciprocal(a * c - b * b, approx=True)
+            else:
+                inverse = inverse_next
             scale[js] = inverse if jr == 0 else jnp.where(is_row[jr], inverse, scale[js])
             here = list(columns[j])
             here[js] = jnp.where(is_row[jr], 0.0, here[js])
             scaled = [c * inverse for c in here]
             for m in range(j + 1, width):
                 picked = over_rows(columns[m][js], jr)
-                if m == j + 1:
-                    columns[m] = [c - (h * picked) * inverse for c, h in zip(columns[m], here)]
-                    pivot = over_rows(columns[m][m // 8], m % 8)
+                if j % 2 == 1 and m <= j + 2:
+                    columns[m] = [x - (h * picked) * inverse for x, h in zip(columns[m], here)]
                 else:
-                    columns[m] = [c - h * picked for c, h in zip(columns[m], scaled)]
+                    columns[m] = [x - h * picked for x, h in zip(columns[m], scaled)]
+            if j % 2 == 1 and j + 1 < width:
+                ms, mr = divmod(j + 1, 8)
+                left, right = columns[j + 1][ms], columns[j + 2][ms]
+                corner = [over_rows(left, mr), over_rows(right, mr), over_rows(right, mr + 1)]
             picked = over_rows(new[js], jr)
             new = [x - h * picked for x, h in zip(new, scaled)]
         new = [x * y for x, y in zip(new, scale)]
@@ -233,41 +241,58 @@
     outer_out[...] = t_ref[:, column_blocks(half, mine)[0]]
 
 
-def first_body(steps, a_in, m_in, p_ref, far_ref, side_ref, first_ref, a_out, b_out, m_work):
+def first_body(steps, a_in, m_in, p_ref, far_ref, side_ref, first_ref, a_out, b_out, scale_out, m_work):
     n = a_in.shape[0]
     m_work[...] = m_in[...]
     put_sibling(m_work, far_ref, side_ref, 2, first_ref[0])
     moved = pick_right(m_work[...], p_ref[...], ((1,), (1,)))
-    for i in range(n // TILE):
-        rows, later = slice(i * TILE, (i + 1) * TILE), slice(i * TILE, n)
-        a_out[rows, later] = a_in[rows, later] + pick_left(p_ref[rows, :], moved[:, later], ((1,), (0,)))
+    tiles = [slice(i * TILE, (i + 1) * TILE) for i in range(n // TILE)]
+    largest = [functools.reduce(jnp.maximum, [ref[tile, tile] for tile in tiles]) for ref in (a_in, m_work)]
+    scale = lax.rsqrt(sum(jnp.max(x, axis=(0, 1), keepdims=True) for x in largest))
+    scale_out[...] = jnp.broadcast_to(scale, scale_out.shape)
+    for i, rows in enumerate(tiles):
+        later = slice(i * TILE, n)
+        both = a_in[rows, later] + pick_left(p_ref[rows, :], moved[:, later], ((1,), (0,)))
+        a_out[rows, later] = both * scale
     top = b_out.shape[0]
     on_diagonal = [lax.broadcasted_iota(jnp.int32, (top, top), axis) for axis in (0, 1)]
     b_out[...] = jnp.where(on_diagonal[0] == on_diagonal[1], 1.0, 0.0).astype(F32)
     eliminate(a_out, b_out, steps)
 
 
-def middle_body(steps, a_in, b_ref, t_ref, mine_ref, others_ref, first_ref, a_out, g_out):
-    top, half = b_ref.shape[0], t_ref.shape[0]
+def middle_body(k, a_ref, b_ref, t_ref, mine_ref, others_ref, scale_ref, first_ref, a_out, g_out):
+    top, half, n, width = b_ref.shape[0], t_ref.shape[0], a_ref.shape[0], g_out.shape[1]
+    own, last = slice(k * TILE, (k + 1) * TILE), slice((k + 1) * TILE, n)
+    inverse = invert_tile(a_ref[own, own])
     here, there = column_blocks(half, first_ref[0])
-    a_out[...] = a_in[...]
-    g_out[0:half, :] = t_ref[:, 0 : g_out.shape[1]]
-    g_out[half:, here] = mine_ref[...]
-    g_out[half:, there] = others_ref[...]
+    scale = scale_ref[0:1, 0:1]
+    g_out[0:half, :] = t_ref[:, 0:width] * scale
+    g_out[half:, here] = mine_ref[...] * scale
+    g_out[half:, there] = others_ref[...] * scale
     first = g_out[0:top, :]
-    g_out[top:, :] = g_out[top:, :] - full(a_in[0:top, top:], first, ((0,), (0,)))
-    g_out[0:top, :] = full(b_ref[...], first)
-    eliminate(a_out, g_out, steps)
+    rest = g_out[top:, :] - full(a_ref[0:top, top:], first, ((0,), (0,)))
+    first = full(b_ref[...], first)
+    old = a_ref[own, last]
+    panel = full(inverse, old)
+    a_out[last, last] = a_ref[last, last] - full(old, panel, ((0,), (0,)))
+    right = full(inverse, rest[0:TILE, :])
+    g_out[own, :] = right
+    g_out[last, :] = rest[TILE:, :] - full(old, right, ((0,), (0,)))
+    factor = a_ref[0:top, own]
+    a_out[0:top, last] = a_ref[0:top, last] - full(factor, panel)
+    a_out[own, last] = panel
+    g_out[0:top, :] = first - full(factor, right)
 
 
 def column_blocks(half, mine):
     return [pl.ds(pl.multiple_of(x * half, half), half) for x in (mine, 1 - mine)]
 
 
-def last_body(steps, a_ref, g_in, g_out, a_work):
-    a_work[...] = a_ref[...]
-    g_out[...] = g_in[...]
-    eliminate(a_work, g_out, steps)
+def last_body(k, a_ref, g_ref, g_out):
+    own, before = slice(k * TILE, (k + 1) * TILE), slice(0, k * TILE)
+    right = full(invert_tile(a_ref[own, own]), g_ref[own, :])
+    g_out[own, :] = right
+    g_out[before, :] = g_ref[before, :] - full(a_ref[before, own], right)
 
 
 def send_body(half, g_ref, p_ref, chunk_ref, first_ref, h_out, send_out):
@@ -391,24 +416,18 @@
         [vmem] * 5 + [smem],
     )(t_int, diag_other, near, near_side, column, first_late)
     outer_others = across(outer)
-    top = tiles // 2 * TILE
-    a, b = kernel(
-        functools.partial(first_body, range(tiles // 2)),
-        (f(n, n), f(top, top)),
+    top = (tiles - 2) * TILE
+    a, b, scale = kernel(
+        functools.partial(first_body, range(tiles - 2)),
+        (f(n, n), f(top, top), f(8, TILE)),
         [vmem] * 5 + [smem],
         [pltpu.VMEM((n, n), F32)],
         10e9,
     )(a, m, onehot, far, far_side, first)
     a, g = kernel(
-        functools.partial(middle_body, range(tiles // 2, tiles - 1)),
-        (f(n, n), f(n, width)),
-        [vmem] * 5 + [smem],
-        (),
-        5e9,
-    )(a, b, t_int, outer_mine, outer_others, first)
-    g = kernel(
-        functools.partial(last_body, range(tiles - 1, tiles)), f(n, width), [vmem] * 2, [pltpu.VMEM((n, n), F32)], 5e9
-    )(a, g)
+        functools.partial(middle_body, tiles - 2), (f(n, n), f(n, width)), [vmem] * 6 + [smem], (), 5e9
+    )(a, b, t_int, outer_mine, outer_others, scale, first)
+    g = kernel(functools.partial(last_body, tiles - 1), f(n, width), [vmem] * 2, (), 5e9)(a, g)
     h, send = kernel(
         functools.partial(send_body, half), (f(n, half), f(half, q)), [vmem] * 3 + [smem], (), 1e9
     )(g, onehot, near_r[0], first)

time: 55.2 us -> 54.1 us (0.980)
  Pallas kernels: 24.8 us -> 23.7 us
    pallas_call x3, Pallas kernels: 18.3 us -> 17.2 us  [the longest x1 8.52 us: two_shards(): kernel(functools.partial(first_body, range(tiles - 2)), (f(n, n), f(top,...]
  transfers between devices with their start and end apart: 11 -> 11, of which waited for: 4 -> 4; matrix products, arithmetic and copies ran while one was open for 0% -> 0% of each run, Pallas kernels for 43% -> 42%
where the time goes in v10:
time: 54.1 us; the launch traced here: 53.9 us
  Pallas kernels  23.7 us (44%)
  starting transfers between devices  15.6 us (29%)
  waiting for transfers between devices  11.4 us (21%)
  local copies, waits for them, and re-layouts  2.42 us (4%)
  between operations  0.74 us (1%)
    ppermute x4, waiting for transfers between devices, sibling(): return lax.ppermute(x, 'leaf', [(i, i ^ size // 2) for i in range(size)])  9.56 us
    pallas_call x1, Pallas kernels, two_shards(): kernel(functools.partial(first_body, range(tiles - 2)), (f(n, n), f(top,...  8.52 us
    ppermute x7, starting transfers between devices, across(): return lax.ppermute(x, 'sib', [(0, 1), (1, 0)])  8.13 us
    ppermute x4, starting transfers between devices, sibling(): return lax.ppermute(x, 'leaf', [(i, i ^ size // 2) for i in range(size)])  7.42 us
    pallas_call x1, Pallas kernels, two_shards(): kernel(functools.partial(middle_body, tiles - 2), (f(n, n), f(n, width)),...  4.8 us
    pallas_call x1, Pallas kernels, two_shards(): kernel(functools.partial(last_body, tiles - 1), f(n, width), [vmem] * 2,...  3.88 us
    pallas_call x1, Pallas kernels, two_shards(): kernel(functools.partial(output_body, half), (f(half, width), f(half, wid...  3.2 us
    unnamed x8, local copies, waits for them, and re-layouts  2.42 us
  transfers between devices with their start and end apart: 11, of which 4 were waited for; matrix products, arithmetic and copies ran while one was open for 0% of the time, Pallas kernels for 42%

profile of v10, /device:TPU:0, one launch (start us, length us, event | category | flops | bytes accessed | tf_op | source)
XLA Modules:
  0.0 53.9 jit_solution(12099345191331666940)
XLA Ops:
  0.6 0.7 %copy-done.3 = s32[1,512]{1,0:T(1,128)S(1)} copy-done((s32[1,512]{1,0:T(1,128)S(1)}, s32[1,512]{1,0:T(1,128)}, u32[]{:S(2)}) %copy-start.3) | copy-done | bytes 2072
  1.3 1.2 %copy-done = f32[1,256,1024]{2,1,0:T(8,128)S(1)} copy-done((f32[1,256,1024]{2,1,0:T(8,128)S(1)}, f32[1,256,1024]{2,1,0:T(8,128)}, u32[]{:S(2)}) %copy-start) | copy-done | bytes 1048600
  2.5 0.2 shard_map.58
  2.7 4.1 %collective-permute-start.1 = (f32[328,128]{1,0:T(8,128)S(1)}, f32[328,128]{1,0:T(8,128)S(1)}, u32[]{:S(2)}, u32[]{:S(2)}) collective-permute-start(f32[328,128]{1,0:T(8,128)S(1)} %get-tuple-element.29), channel_id=1, source_target_pairs={{0,8},{1,9},{2,10},{3,11},{4,12},{5,13},{6,14},{7,15},{8,0},{9,1},... | collective-permute-start | bytes 503816 | tf_op jit(solution)/shard_map/ppermute | solution.py:369
  6.8 1.5 %collective-permute-start.3 = (f32[256,256]{1,0:T(8,128)S(1)}, f32[256,256]{1,0:T(8,128)S(1)}, u32[]{:S(2)}, u32[]{:S(2)}) collective-permute-start(f32[256,256]{1,0:T(8,128)S(1)} %get-tuple-element.34), channel_id=1, source_target_pairs={{0,16},{16,0},{1,17},{17,1},{2,18},{18,2},{3,19},{19,3},{4,20},{20... | collective-permute-start | bytes 786440 | tf_op jit(solution)/shard_map/ppermute | solution.py:373
  8.3 0.3 collective-permute-start.2
  8.7 0.3 collective-permute-start
  8.9 9.4 %collective-permute-done.1.near_ref = f32[328,128]{1,0:T(8,128)S(1)} collective-permute-done((f32[328,128]{1,0:T(8,128)S(1)}, f32[328,128]{1,0:T(8,128)S(1)}, u32[]{:S(2)}, u32[]{:S(2)}) %collective-permute-start.1) | collective-permute-done | bytes 167968 | tf_op jit(solution)/shard_map/ppermute | solution.py:369
  18.3 1.8 %collective-permute-start.4 = (f32[328,128]{1,0:T(8,128)S(1)}, f32[328,128]{1,0:T(8,128)S(1)}, u32[]{:S(2)}, u32[]{:S(2)}) collective-permute-start(f32[328,128]{1,0:T(8,128)S(1)} %collective-permute-done.1.near_ref), channel_id=1, source_target_pairs={{0,16},{16,0},{1,17},{17,1},{2,18},{18,2},{3,19},{19,3},{4,20},{20... | collective-permute-start | bytes 503816 | tf_op jit(solution)/shard_map/ppermute | solution.py:373
  20.3 1.5 %collective-permute-start.5 = (f32[256,128]{1,0:T(8,128)S(1)}, f32[256,128]{1,0:T(8,128)S(1)}, u32[]{:S(2)}, u32[]{:S(2)}) collective-permute-start(f32[256,128]{1,0:T(8,128)S(1)} %collective-permute-done.2.side_ref), channel_id=1, source_target_pairs={{0,16},{16,0},{1,17},{17,1},{2,18},{18,2},{3,19},{19,3},{4,20},{20... | collective-permute-start | bytes 393224 | tf_op jit(solution)/shard_map/ppermute | solution.py:373
  22.0 2.9 %collective-permute-start.8 = (f32[512,128]{1,0:T(8,128)S(1)}, f32[512,128]{1,0:T(8,128)S(1)}, u32[]{:S(2)}, u32[]{:S(2)}) collective-permute-start(f32[512,128]{1,0:T(8,128)S(1)} %get-tuple-element.38), channel_id=1, source_target_pairs={{0,8},{1,9},{2,10},{3,11},{4,12},{5,13},{6,14},{7,15},{8,0},{9,1},... | collective-permute-start | bytes 786440 | tf_op jit(solution)/shard_map/ppermute | solution.py:369
  24.9 0.5 shard_map.60
  25.5 0.6 %collective-permute-start.6 = (f32[256,256]{1,0:T(8,128)S(1)}, f32[256,256]{1,0:T(8,128)S(1)}, u32[]{:S(2)}, u32[]{:S(2)}) collective-permute-start(f32[256,256]{1,0:T(8,128)S(1)} %get-tuple-element.45), channel_id=1, source_target_pairs={{0,16},{16,0},{1,17},{17,1},{2,18},{18,2},{3,19},{19,3},{4,20},{20... | collective-permute-start | bytes 786440 | tf_op jit(solution)/shard_map/ppermute | solution.py:373
  26.1 0.7 %collective-permute-done.5.side_ref = f32[256,128]{1,0:T(8,128)S(1)} collective-permute-done((f32[256,128]{1,0:T(8,128)S(1)}, f32[256,128]{1,0:T(8,128)S(1)}, u32[]{:S(2)}, u32[]{:S(2)}) %collective-permute-start.5) | collective-permute-done | bytes 131104 | tf_op jit(solution)/shard_map/ppermute | solution.py:373
  26.7 8.5 %shard_map.61 = (f32[512,512]{1,0:T(8,128)S(1)}, f32[256,256]{1,0:T(8,128)S(1)}, f32[8,128]{1,0:T(8,128)S(1)}) custom-call(f32[512,512]{1,0:T(8,128)S(1)} %get-tuple-element.40.a_in, f32[512,512]{1,0:T(8,128)S(1)} %get-tuple-element.41.m_in, bf16[512,512]{1,0:T(8,128)(2,1)S(1)} %get-tuple-element.42.p_ref, f32[328,128]{1,0:T(8,128)S(1)} %collective-permute-done.4.far_ref, ...), custom_call_target="tpu_custom_call" | custom-call | flops 10000000000 | bytes 1048576 | tf_op jit(solution)/shard_map/pallas_call | solution.py:420
  35.3 4.8 %shard_map.62 = (f32[512,512]{1,0:T(8,128)S(1)}, f32[512,512]{1,0:T(8,128)S(1)}) custom-call(f32[512,512]{1,0:T(8,128)S(1)} %get-tuple-element.43.a_ref, f32[256,256]{1,0:T(8,128)S(1)} %get-tuple-element.44.b_ref, f32[256,1024]{1,0:T(8,128)S(1)} %bitcast.9, f32[256,256]{1,0:T(8,128)S(1)} %collective-permute-done.3.mine_ref, ...), custom_call_target="tpu_custom_call" | custom-call | flops 5000000000 | bytes 1048576 | tf_op jit(solution)/shard_map/pallas_call | solution.py:427
  40.1 3.9 %shard_map.63.g_ref = f32[512,512]{1,0:T(8,128)S(1)} custom-call(f32[512,512]{1,0:T(8,128)S(1)} %get-tuple-element.47.a_ref, f32[512,512]{1,0:T(8,128)S(1)} %get-tuple-element.48.g_ref), custom_call_target="tpu_custom_call" | custom-call | flops 5000000000 | bytes 1048576 | tf_op jit(solution)/shard_map/pallas_call | solution.py:430
  44.0 1.3 %shard_map.65 = (f32[512,256]{1,0:T(8,128)S(1)}, f32[256,128]{1,0:T(8,128)S(1)}) custom-call(f32[512,512]{1,0:T(8,128)S(1)} %shard_map.63.g_ref, bf16[512,512]{1,0:T(8,128)(2,1)S(1)} %get-tuple-element.42.p_ref, f32[512,128]{1,0:T(8,128)S(1)} %collective-permute-done.7.chunk_a.chunk_ref, s32[1]{0:T(128)} %bitcast.1.first_ref), custom_call_target="tpu_custom_call" | custom-call | flops 1000000000 | bytes 1048576 | tf_op jit(solution)/shard_map/pallas_call | solution.py:431
  45.3 2.3 %collective-permute-start.9 = (f32[256,128]{1,0:T(8,128)S(1)}, f32[256,128]{1,0:T(8,128)S(1)}, u32[]{:S(2)}, u32[]{:S(2)}) collective-permute-start(f32[256,128]{1,0:T(8,128)S(1)} %get-tuple-element.52), channel_id=1, source_target_pairs={{0,16},{16,0},{1,17},{17,1},{2,18},{18,2},{3,19},{19,3},{4,20},{20... | collective-permute-start | bytes 393224 | tf_op jit(solution)/shard_map/ppermute | solution.py:373
  47.6 0.4 shard_map.66
  48.1 0.5 copy-done.2
  48.6 3.2 %shard_map.64 = (f32[256,512]{1,0:T(8,128)}, f32[256,512]{1,0:T(8,128)}, f32[256,256]{1,0:T(8,128)S(1)}) custom-call(f32[512,512]{1,0:T(8,128)S(1)} %shard_map.63.g_ref, bf16[512,512]{1,0:T(8,128)(2,1)S(1)} %get-tuple-element.42.p_ref, f32[256,1024]{1,0:T(8,128)S(1)} %bitcast.10, f32[256,256]{1,0:T(8,128)S(1)} %collective-permute-done.3.mine_ref, ...), custom_call_target="tpu_custom_call" | custom-call | flops 1000000 | bytes 1048576 | tf_op jit(solution)/shard_map/pallas_call | solution.py:436
  51.8 1.2 %collective-permute-done.10.second_part = f32[256,128]{1,0:T(8,128)S(1)} collective-permute-done((f32[256,128]{1,0:T(8,128)S(1)}, f32[256,128]{1,0:T(8,128)S(1)}, u32[]{:S(2)}, u32[]{:S(2)}) %collective-permute-start.10) | collective-permute-done | bytes 131104 | tf_op jit(solution)/shard_map/ppermute | solution.py:373
  53.0 0.8 %shard_map.67 = f32[256,512]{1,0:T(8,128)} custom-call(f32[256,256]{1,0:T(8,128)S(1)} %get-tuple-element.51.keep_ref, f32[256,128]{1,0:T(8,128)S(1)} %collective-permute-done.9.first_part, f32[256,128]{1,0:T(8,128)S(1)} %collective-permute-done.10.second_part, s32[1]{0:T(128)} %bitcast.1.first_ref), custom_call_target="tpu_custom_call" | custom-call | flops 100000000 | bytes 1048576 | tf_op jit(solution)/shard_map/pallas_call | solution.py:443
  (16 shorter events, 0.4 us)
Async XLA Ops:
  0.6 0.7 %copy-start.3 = (s32[1,512]{1,0:T(1,128)S(1)}, s32[1,512]{1,0:T(1,128)}, u32[]{:S(2)}) copy-start(s32[1,512]{1,0:T(1,128)} %map_ref.1) | copy-start | bytes 6148
  1.3 1.2 %copy-start = (f32[1,256,1024]{2,1,0:T(8,128)S(1)}, f32[1,256,1024]{2,1,0:T(8,128)}, u32[]{:S(2)}) copy-start(f32[1,256,1024]{2,1,0:T(8,128)} %param.3) | copy-start | bytes 3145732
  2.7 15.6 %collective-permute-start.1 = (f32[328,128]{1,0:T(8,128)S(1)}, f32[328,128]{1,0:T(8,128)S(1)}, u32[]{:S(2)}, u32[]{:S(2)}) collective-permute-start(f32[328,128]{1,0:T(8,128)S(1)} %get-tuple-element.29), channel_id=1, source_target_pairs={{0,8},{1,9},{2,10},{3,11},{4,12},{5,13},{6,14},{7,15},{8,0},{9,1},... | collective-permute-start | bytes 503816 | tf_op jit(solution)/shard_map/ppermute | solution.py:369
  6.8 15.1 %collective-permute-start.3 = (f32[256,256]{1,0:T(8,128)S(1)}, f32[256,256]{1,0:T(8,128)S(1)}, u32[]{:S(2)}, u32[]{:S(2)}) collective-permute-start(f32[256,256]{1,0:T(8,128)S(1)} %get-tuple-element.34), channel_id=1, source_target_pairs={{0,16},{16,0},{1,17},{17,1},{2,18},{18,2},{3,19},{19,3},{4,20},{20... | collective-permute-start | bytes 786440 | tf_op jit(solution)/shard_map/ppermute | solution.py:373
  8.3 12.0 %collective-permute-start.2 = (f32[256,128]{1,0:T(8,128)S(1)}, f32[256,128]{1,0:T(8,128)S(1)}, u32[]{:S(2)}, u32[]{:S(2)}) collective-permute-start(f32[256,128]{1,0:T(8,128)S(1)} %get-tuple-element.30), channel_id=1, source_target_pairs={{0,8},{1,9},{2,10},{3,11},{4,12},{5,13},{6,14},{7,15},{8,0},{9,1},... | collective-permute-start | bytes 393224 | tf_op jit(solution)/shard_map/ppermute | solution.py:369
  8.7 16.3 %collective-permute-start = (f32[328,128]{1,0:T(8,128)S(1)}, f32[328,128]{1,0:T(8,128)S(1)}, u32[]{:S(2)}, u32[]{:S(2)}) collective-permute-start(f32[328,128]{1,0:T(8,128)S(1)} %get-tuple-element.29), channel_id=1, source_target_pairs={{0,16},{16,0},{1,17},{17,1},{2,18},{18,2},{3,19},{19,3},{4,20},{20... | collective-permute-start | bytes 503816 | tf_op jit(solution)/shard_map/ppermute | solution.py:373
  18.3 8.4 %collective-permute-start.4 = (f32[328,128]{1,0:T(8,128)S(1)}, f32[328,128]{1,0:T(8,128)S(1)}, u32[]{:S(2)}, u32[]{:S(2)}) collective-permute-start(f32[328,128]{1,0:T(8,128)S(1)} %collective-permute-done.1.near_ref), channel_id=1, source_target_pairs={{0,16},{16,0},{1,17},{17,1},{2,18},{18,2},{3,19},{19,3},{4,20},{20... | collective-permute-start | bytes 503816 | tf_op jit(solution)/shard_map/ppermute | solution.py:373
  20.3 6.4 %collective-permute-start.5 = (f32[256,128]{1,0:T(8,128)S(1)}, f32[256,128]{1,0:T(8,128)S(1)}, u32[]{:S(2)}, u32[]{:S(2)}) collective-permute-start(f32[256,128]{1,0:T(8,128)S(1)} %collective-permute-done.2.side_ref), channel_id=1, source_target_pairs={{0,16},{16,0},{1,17},{17,1},{2,18},{18,2},{3,19},{19,3},{4,20},{20... | collective-permute-start | bytes 393224 | tf_op jit(solution)/shard_map/ppermute | solution.py:373
  21.9 22.0 %collective-permute-start.7 = (f32[512,128]{1,0:T(8,128)S(1)}, f32[512,128]{1,0:T(8,128)S(1)}, u32[]{:S(2)}, u32[]{:S(2)}) collective-permute-start(f32[512,128]{1,0:T(8,128)S(1)} %get-tuple-element.37), channel_id=1, source_target_pairs={{0,8},{1,9},{2,10},{3,11},{4,12},{5,13},{6,14},{7,15},{8,0},{9,1},... | collective-permute-start | bytes 786440 | tf_op jit(solution)/shard_map/ppermute | solution.py:369
  22.0 25.6 %collective-permute-start.8 = (f32[512,128]{1,0:T(8,128)S(1)}, f32[512,128]{1,0:T(8,128)S(1)}, u32[]{:S(2)}, u32[]{:S(2)}) collective-permute-start(f32[512,128]{1,0:T(8,128)S(1)} %get-tuple-element.38), channel_id=1, source_target_pairs={{0,8},{1,9},{2,10},{3,11},{4,12},{5,13},{6,14},{7,15},{8,0},{9,1},... | collective-permute-start | bytes 786440 | tf_op jit(solution)/shard_map/ppermute | solution.py:369
  25.5 9.8 %collective-permute-start.6 = (f32[256,256]{1,0:T(8,128)S(1)}, f32[256,256]{1,0:T(8,128)S(1)}, u32[]{:S(2)}, u32[]{:S(2)}) collective-permute-start(f32[256,256]{1,0:T(8,128)S(1)} %get-tuple-element.45), channel_id=1, source_target_pairs={{0,16},{16,0},{1,17},{17,1},{2,18},{18,2},{3,19},{19,3},{4,20},{20... | collective-permute-start | bytes 786440 | tf_op jit(solution)/shard_map/ppermute | solution.py:373
  26.7 8.5 %copy-start.1 = (f32[1,256,1024]{2,1,0:T(8,128)S(1)}, f32[1,256,1024]{2,1,0:T(8,128)}, u32[]{:S(2)}) copy-start(f32[1,256,1024]{2,1,0:T(8,128)} %param.3) | copy-start | bytes 3145732
  45.3 6.5 %collective-permute-start.9 = (f32[256,128]{1,0:T(8,128)S(1)}, f32[256,128]{1,0:T(8,128)S(1)}, u32[]{:S(2)}, u32[]{:S(2)}) collective-permute-start(f32[256,128]{1,0:T(8,128)S(1)} %get-tuple-element.52), channel_id=1, source_target_pairs={{0,16},{16,0},{1,17},{17,1},{2,18},{18,2},{3,19},{19,3},{4,20},{20... | collective-permute-start | bytes 393224 | tf_op jit(solution)/shard_map/ppermute | solution.py:373
  47.6 1.0 %copy-start.2 = (f32[1,256,512]{2,1,0:T(8,128)S(1)}, f32[1,256,512]{2,1,0:T(8,128)}, u32[]{:S(2)}) copy-start(f32[1,256,512]{2,1,0:T(8,128)} %param.4) | copy-start | bytes 1572868
  48.0 5.0 %collective-permute-start.10 = (f32[256,128]{1,0:T(8,128)S(1)}, f32[256,128]{1,0:T(8,128)S(1)}, u32[]{:S(2)}, u32[]{:S(2)}) collective-permute-start(f32[256,128]{1,0:T(8,128)S(1)} %shard_map.66), channel_id=1, source_target_pairs={{0,16},{16,0},{1,17},{17,1},{2,18},{18,2},{3,19},{19,3},{4,20},{20... | collective-permute-start | bytes 393224 | tf_op jit(solution)/shard_map/ppermute | solution.py:373

commit v11 on v10

--- a/solution.py
+++ b/solution.py
@@ -260,49 +260,41 @@
     eliminate(a_out, b_out, steps)
 
 
-def middle_body(k, a_ref, b_ref, t_ref, mine_ref, others_ref, scale_ref, first_ref, a_out, g_out):
+def rest_body(k, a_ref, b_ref, t_ref, mine_ref, others_ref, p_ref, scale_ref, first_ref, g_out, h_out):
     top, half, n, width = b_ref.shape[0], t_ref.shape[0], a_ref.shape[0], g_out.shape[1]
-    own, last = slice(k * TILE, (k + 1) * TILE), slice((k + 1) * TILE, n)
+    own, last, before = slice(k * TILE, (k + 1) * TILE), slice((k + 1) * TILE, n), slice(0, (k + 1) * TILE)
+    here, there = column_blocks(half, first_ref[0])
     inverse = invert_tile(a_ref[own, own])
-    here, there = column_blocks(half, first_ref[0])
+    old = a_ref[own, last]
+    panel = full(inverse, old)
+    inverse_last = invert_tile(a_ref[last, last] - full(old, panel, ((0,), (0,))))
     scale = scale_ref[0:1, 0:1]
     g_out[0:half, :] = t_ref[:, 0:width] * scale
     g_out[half:, here] = mine_ref[...] * scale
     g_out[half:, there] = others_ref[...] * scale
     first = g_out[0:top, :]
     rest = g_out[top:, :] - full(a_ref[0:top, top:], first, ((0,), (0,)))
-    first = full(b_ref[...], first)
-    old = a_ref[own, last]
-    panel = full(inverse, old)
-    a_out[last, last] = a_ref[last, last] - full(old, panel, ((0,), (0,)))
     right = full(inverse, rest[0:TILE, :])
+    bottom = rest[TILE:, :] - full(old, right, ((0,), (0,)))
+    factor = a_ref[0:top, own]
+    g_out[0:top, :] = full(b_ref[...], first) - full(factor, right)
     g_out[own, :] = right
-    g_out[last, :] = rest[TILE:, :] - full(old, right, ((0,), (0,)))
-    factor = a_ref[0:top, own]
-    a_out[0:top, last] = a_ref[0:top, last] - full(factor, panel)
-    a_out[own, last] = panel
-    g_out[0:top, :] = first - full(factor, right)
+    factors = jnp.concatenate([a_ref[0:top, last] - full(factor, panel), panel], axis=0)
+    h = pick_left(p_ref[before, :], g_out[before, there], ((0,), (0,)))
+    diagonal = [lax.broadcasted_iota(jnp.int32, (TILE, TILE), axis) for axis in (0, 1)]
+    identity = jnp.where(diagonal[0] == diagonal[1], 1.0, 0.0).astype(BF16)
+    change = contract(p_ref[last, :], identity, ((0,), (0,))) - pick_left(p_ref[before, :], factors, ((0,), (0,)))
+    solved = full(inverse_last, bottom)
+    g_out[last, :] = solved
+    h_out[...] = h + full(change, g_out[last, there])
+    g_out[before, :] = g_out[before, :] - full(factors, solved)
 
 
 def column_blocks(half, mine):
     return [pl.ds(pl.multiple_of(x * half, half), half) for x in (mine, 1 - mine)]
 
 
-def last_body(k, a_ref, g_ref, g_out):
-    own, before = slice(k * TILE, (k + 1) * TILE), slice(0, k * TILE)
-    right = full(invert_tile(a_ref[own, own]), g_ref[own, :])
-    g_out[own, :] = right
-    g_out[before, :] = g_ref[before, :] - full(a_ref[before, own], right)
-
-
-def send_body(half, g_ref, p_ref, chunk_ref, first_ref, h_out, send_out):
-    _, there = column_blocks(half, first_ref[0])
-    h = pick_left(p_ref[...], g_ref[:, there], ((0,), (0,)))
-    h_out[...] = h
-    send_out[...] = -three_pass(h, chunk_ref[...], ((0,), (0,)))
-
-
-def send_more_body(h_ref, chunk_ref, send_out):
+def send_body(h_ref, chunk_ref, send_out):
     send_out[...] = -three_pass(h_ref[...], chunk_ref[...], ((0,), (0,)))
 
 
@@ -424,15 +416,12 @@
         [pltpu.VMEM((n, n), F32)],
         10e9,
     )(a, m, onehot, far, far_side, first)
-    a, g = kernel(
-        functools.partial(middle_body, tiles - 2), (f(n, n), f(n, width)), [vmem] * 6 + [smem], (), 5e9
-    )(a, b, t_int, outer_mine, outer_others, scale, first)
-    g = kernel(functools.partial(last_body, tiles - 1), f(n, width), [vmem] * 2, (), 5e9)(a, g)
-    h, send = kernel(
-        functools.partial(send_body, half), (f(n, half), f(half, q)), [vmem] * 3 + [smem], (), 1e9
-    )(g, onehot, near_r[0], first)
-    cross_a = across(send)
-    cross_b = across(kernel(send_more_body, f(half, q), [vmem] * 2, (), 5e9)(h, near_r[1]))
+    g, h = kernel(
+        functools.partial(rest_body, tiles - 2), (f(n, width), f(n, half)), [vmem] * 7 + [smem], (), 10e9
+    )(a, b, t_int, outer_mine, outer_others, onehot, scale, first)
+    cross_a, cross_b = [
+        across(kernel(send_body, f(half, q), [vmem] * 2, (), 5e9)(h, chunk)) for chunk in near_r
+    ]
     own_map, solution_op, keep = kernel(
         functools.partial(output_body, half),
         (f(half, width), f(half, width), f(half, half)),

time: 54.1 us -> 55.2 us (1.020)
  Pallas kernels: 23.7 us -> 24.9 us
  waiting for transfers between devices: 11.4 us -> 12 us
    pallas_call x4 -> x3, Pallas kernels: 10.4 us -> 11.6 us  [the longest x1 10.7 us: two_shards(): kernel(functools.partial(rest_body, tiles - 2), (f(n, width), f(n, half))...]
  transfers between devices with their start and end apart: 11 -> 11, of which waited for: 4 -> 4; matrix products, arithmetic and copies ran while one was open for 0% -> 0% of each run, Pallas kernels for 42% -> 43%
where the time goes in v11:
time: 55.2 us; the launch traced here: 55 us
  Pallas kernels  24.9 us (45%)
  starting transfers between devices  15.5 us (28%)
  waiting for transfers between devices  12 us (22%)
  local copies, waits for them, and re-layouts  1.91 us (3%)
  between operations  0.74 us (1%)
    pallas_call x1, Pallas kernels, two_shards(): kernel(functools.partial(rest_body, tiles - 2), (f(n, width), f(n, half))...  10.7 us
    ppermute x4, waiting for transfers between devices, sibling(): return lax.ppermute(x, 'leaf', [(i, i ^ size // 2) for i in range(size)])  9.56 us
    pallas_call x1, Pallas kernels, two_shards(): kernel(functools.partial(first_body, range(tiles - 2)), (f(n, n), f(top,...  8.52 us
    ppermute x7, starting transfers between devices, across(): return lax.ppermute(x, 'sib', [(0, 1), (1, 0)])  8.11 us
    ppermute x4, starting transfers between devices, sibling(): return lax.ppermute(x, 'leaf', [(i, i ^ size // 2) for i in range(size)])  7.42 us
    pallas_call x1, Pallas kernels, two_shards(): kernel(functools.partial(output_body, half), (f(half, width), f(half, wid...  3.21 us
    ppermute x7, waiting for transfers between devices, across(): return lax.ppermute(x, 'sib', [(0, 1), (1, 0)])  2.41 us
    unnamed x8, local copies, waits for them, and re-layouts  1.91 us
  transfers between devices with their start and end apart: 11, of which 4 were waited for; matrix products, arithmetic and copies ran while one was open for 0% of the time, Pallas kernels for 43%

profile of v11, /device:TPU:0, one launch (start us, length us, event | category | flops | bytes accessed | tf_op | source)
XLA Modules:
  0.0 55.0 jit_solution(6100399370728151226)
XLA Ops:
  0.6 0.7 %copy-done.3 = s32[1,512]{1,0:T(1,128)S(1)} copy-done((s32[1,512]{1,0:T(1,128)S(1)}, s32[1,512]{1,0:T(1,128)}, u32[]{:S(2)}) %copy-start.3) | copy-done | bytes 2072
  1.3 1.2 %copy-done = f32[1,256,1024]{2,1,0:T(8,128)S(1)} copy-done((f32[1,256,1024]{2,1,0:T(8,128)S(1)}, f32[1,256,1024]{2,1,0:T(8,128)}, u32[]{:S(2)}) %copy-start) | copy-done | bytes 1048600
  2.5 0.2 shard_map.58
  2.7 4.1 %collective-permute-start.1 = (f32[328,128]{1,0:T(8,128)S(1)}, f32[328,128]{1,0:T(8,128)S(1)}, u32[]{:S(2)}, u32[]{:S(2)}) collective-permute-start(f32[328,128]{1,0:T(8,128)S(1)} %get-tuple-element.27), channel_id=1, source_target_pairs={{0,8},{1,9},{2,10},{3,11},{4,12},{5,13},{6,14},{7,15},{8,0},{9,1},... | collective-permute-start | bytes 503816 | tf_op jit(solution)/shard_map/ppermute | solution.py:361
  6.8 1.5 %collective-permute-start.3 = (f32[256,256]{1,0:T(8,128)S(1)}, f32[256,256]{1,0:T(8,128)S(1)}, u32[]{:S(2)}, u32[]{:S(2)}) collective-permute-start(f32[256,256]{1,0:T(8,128)S(1)} %get-tuple-element.32), channel_id=1, source_target_pairs={{0,16},{16,0},{1,17},{17,1},{2,18},{18,2},{3,19},{19,3},{4,20},{20... | collective-permute-start | bytes 786440 | tf_op jit(solution)/shard_map/ppermute | solution.py:365
  8.3 0.3 collective-permute-start.2
  8.7 0.3 collective-permute-start
  8.9 9.4 %collective-permute-done.1.near_ref = f32[328,128]{1,0:T(8,128)S(1)} collective-permute-done((f32[328,128]{1,0:T(8,128)S(1)}, f32[328,128]{1,0:T(8,128)S(1)}, u32[]{:S(2)}, u32[]{:S(2)}) %collective-permute-start.1) | collective-permute-done | bytes 167968 | tf_op jit(solution)/shard_map/ppermute | solution.py:361
  18.3 1.8 %collective-permute-start.4 = (f32[328,128]{1,0:T(8,128)S(1)}, f32[328,128]{1,0:T(8,128)S(1)}, u32[]{:S(2)}, u32[]{:S(2)}) collective-permute-start(f32[328,128]{1,0:T(8,128)S(1)} %collective-permute-done.1.near_ref), channel_id=1, source_target_pairs={{0,16},{16,0},{1,17},{17,1},{2,18},{18,2},{3,19},{19,3},{4,20},{20... | collective-permute-start | bytes 503816 | tf_op jit(solution)/shard_map/ppermute | solution.py:365
  20.2 0.1 collective-permute-done.2.side_ref
  20.3 1.5 %collective-permute-start.5 = (f32[256,128]{1,0:T(8,128)S(1)}, f32[256,128]{1,0:T(8,128)S(1)}, u32[]{:S(2)}, u32[]{:S(2)}) collective-permute-start(f32[256,128]{1,0:T(8,128)S(1)} %collective-permute-done.2.side_ref), channel_id=1, source_target_pairs={{0,16},{16,0},{1,17},{17,1},{2,18},{18,2},{3,19},{19,3},{4,20},{20... | collective-permute-start | bytes 393224 | tf_op jit(solution)/shard_map/ppermute | solution.py:365
  22.0 2.9 %collective-permute-start.8 = (f32[512,128]{1,0:T(8,128)S(1)}, f32[512,128]{1,0:T(8,128)S(1)}, u32[]{:S(2)}, u32[]{:S(2)}) collective-permute-start(f32[512,128]{1,0:T(8,128)S(1)} %get-tuple-element.36), channel_id=1, source_target_pairs={{0,8},{1,9},{2,10},{3,11},{4,12},{5,13},{6,14},{7,15},{8,0},{9,1},... | collective-permute-start | bytes 786440 | tf_op jit(solution)/shard_map/ppermute | solution.py:361
  24.9 0.5 shard_map.60
  25.5 0.6 %collective-permute-start.6 = (f32[256,256]{1,0:T(8,128)S(1)}, f32[256,256]{1,0:T(8,128)S(1)}, u32[]{:S(2)}, u32[]{:S(2)}) collective-permute-start(f32[256,256]{1,0:T(8,128)S(1)} %get-tuple-element.43), channel_id=1, source_target_pairs={{0,16},{16,0},{1,17},{17,1},{2,18},{18,2},{3,19},{19,3},{4,20},{20... | collective-permute-start | bytes 786440 | tf_op jit(solution)/shard_map/ppermute | solution.py:365
  26.0 0.7 %collective-permute-done.5.side_ref = f32[256,128]{1,0:T(8,128)S(1)} collective-permute-done((f32[256,128]{1,0:T(8,128)S(1)}, f32[256,128]{1,0:T(8,128)S(1)}, u32[]{:S(2)}, u32[]{:S(2)}) %collective-permute-start.5) | collective-permute-done | bytes 131104 | tf_op jit(solution)/shard_map/ppermute | solution.py:365
  26.7 8.5 %shard_map.61 = (f32[512,512]{1,0:T(8,128)S(1)}, f32[256,256]{1,0:T(8,128)S(1)}, f32[8,128]{1,0:T(8,128)S(1)}) custom-call(f32[512,512]{1,0:T(8,128)S(1)} %get-tuple-element.38.a_in, f32[512,512]{1,0:T(8,128)S(1)} %get-tuple-element.39.m_in, bf16[512,512]{1,0:T(8,128)(2,1)S(1)} %get-tuple-element.40.p_ref, f32[328,128]{1,0:T(8,128)S(1)} %collective-permute-done.4.far_ref, ...), custom_call_target="tpu_custom_call" | custom-call | flops 10000000000 | bytes 1048576 | tf_op jit(solution)/shard_map/pallas_call | solution.py:412
  35.3 10.7 %shard_map.62 = (f32[512,512]{1,0:T(8,128)S(1)}, f32[512,256]{1,0:T(8,128)S(1)}) custom-call(f32[512,512]{1,0:T(8,128)S(1)} %get-tuple-element.41.a_ref, f32[256,256]{1,0:T(8,128)S(1)} %get-tuple-element.42.b_ref, f32[256,1024]{1,0:T(8,128)S(1)} %bitcast.9, f32[256,256]{1,0:T(8,128)S(1)} %collective-permute-done.3.mine_ref, ...), custom_call_target="tpu_custom_call" | custom-call | flops 10000000000 | bytes 1048576 | tf_op jit(solution)/shard_map/pallas_call | solution.py:419
  46.0 0.4 shard_map.64
  46.4 2.3 %collective-permute-start.9 = (f32[256,128]{1,0:T(8,128)S(1)}, f32[256,128]{1,0:T(8,128)S(1)}, u32[]{:S(2)}, u32[]{:S(2)}) collective-permute-start(f32[256,128]{1,0:T(8,128)S(1)} %shard_map.64), channel_id=1, source_target_pairs={{0,16},{16,0},{1,17},{17,1},{2,18},{18,2},{3,19},{19,3},{4,20},{20... | collective-permute-start | bytes 393224 | tf_op jit(solution)/shard_map/ppermute | solution.py:365
  48.7 0.4 shard_map.65
  49.2 0.1 collective-permute-start.10
  49.2 3.2 %shard_map.63 = (f32[256,512]{1,0:T(8,128)}, f32[256,512]{1,0:T(8,128)}, f32[256,256]{1,0:T(8,128)S(1)}) custom-call(f32[512,512]{1,0:T(8,128)S(1)} %get-tuple-element.45.g_ref, bf16[512,512]{1,0:T(8,128)(2,1)S(1)} %get-tuple-element.40.p_ref, f32[256,1024]{1,0:T(8,128)S(1)} %bitcast.10, f32[256,256]{1,0:T(8,128)S(1)} %collective-permute-done.3.mine_ref, ...), custom_call_target="tpu_custom_call" | custom-call | flops 1000000 | bytes 1048576 | tf_op jit(solution)/shard_map/pallas_call | solution.py:425
  52.5 1.7 %collective-permute-done.10.second_part = f32[256,128]{1,0:T(8,128)S(1)} collective-permute-done((f32[256,128]{1,0:T(8,128)S(1)}, f32[256,128]{1,0:T(8,128)S(1)}, u32[]{:S(2)}, u32[]{:S(2)}) %collective-permute-start.10) | collective-permute-done | bytes 131104 | tf_op jit(solution)/shard_map/ppermute | solution.py:365
  54.2 0.8 %shard_map.66 = f32[256,512]{1,0:T(8,128)} custom-call(f32[256,256]{1,0:T(8,128)S(1)} %get-tuple-element.48.keep_ref, f32[256,128]{1,0:T(8,128)S(1)} %collective-permute-done.9.first_part, f32[256,128]{1,0:T(8,128)S(1)} %collective-permute-done.10.second_part, s32[1]{0:T(128)} %bitcast.1.first_ref), custom_call_target="tpu_custom_call" | custom-call | flops 100000000 | bytes 1048576 | tf_op jit(solution)/shard_map/pallas_call | solution.py:432
  (15 shorter events, 0.2 us)
Async XLA Ops:
  0.6 0.7 %copy-start.3 = (s32[1,512]{1,0:T(1,128)S(1)}, s32[1,512]{1,0:T(1,128)}, u32[]{:S(2)}) copy-start(s32[1,512]{1,0:T(1,128)} %map_ref.1) | copy-start | bytes 6148
  1.3 1.2 %copy-start = (f32[1,256,1024]{2,1,0:T(8,128)S(1)}, f32[1,256,1024]{2,1,0:T(8,128)}, u32[]{:S(2)}) copy-start(f32[1,256,1024]{2,1,0:T(8,128)} %param.3) | copy-start | bytes 3145732
  2.7 15.6 %collective-permute-start.1 = (f32[328,128]{1,0:T(8,128)S(1)}, f32[328,128]{1,0:T(8,128)S(1)}, u32[]{:S(2)}, u32[]{:S(2)}) collective-permute-start(f32[328,128]{1,0:T(8,128)S(1)} %get-tuple-element.27), channel_id=1, source_target_pairs={{0,8},{1,9},{2,10},{3,11},{4,12},{5,13},{6,14},{7,15},{8,0},{9,1},... | collective-permute-start | bytes 503816 | tf_op jit(solution)/shard_map/ppermute | solution.py:361
  6.8 15.1 %collective-permute-start.3 = (f32[256,256]{1,0:T(8,128)S(1)}, f32[256,256]{1,0:T(8,128)S(1)}, u32[]{:S(2)}, u32[]{:S(2)}) collective-permute-start(f32[256,256]{1,0:T(8,128)S(1)} %get-tuple-element.32), channel_id=1, source_target_pairs={{0,16},{16,0},{1,17},{17,1},{2,18},{18,2},{3,19},{19,3},{4,20},{20... | collective-permute-start | bytes 786440 | tf_op jit(solution)/shard_map/ppermute | solution.py:365
  8.3 12.0 %collective-permute-start.2 = (f32[256,128]{1,0:T(8,128)S(1)}, f32[256,128]{1,0:T(8,128)S(1)}, u32[]{:S(2)}, u32[]{:S(2)}) collective-permute-start(f32[256,128]{1,0:T(8,128)S(1)} %get-tuple-element.28), channel_id=1, source_target_pairs={{0,8},{1,9},{2,10},{3,11},{4,12},{5,13},{6,14},{7,15},{8,0},{9,1},... | collective-permute-start | bytes 393224 | tf_op jit(solution)/shard_map/ppermute | solution.py:361
  8.7 16.3 %collective-permute-start = (f32[328,128]{1,0:T(8,128)S(1)}, f32[328,128]{1,0:T(8,128)S(1)}, u32[]{:S(2)}, u32[]{:S(2)}) collective-permute-start(f32[328,128]{1,0:T(8,128)S(1)} %get-tuple-element.27), channel_id=1, source_target_pairs={{0,16},{16,0},{1,17},{17,1},{2,18},{18,2},{3,19},{19,3},{4,20},{20... | collective-permute-start | bytes 503816 | tf_op jit(solution)/shard_map/ppermute | solution.py:365
  18.3 8.4 %collective-permute-start.4 = (f32[328,128]{1,0:T(8,128)S(1)}, f32[328,128]{1,0:T(8,128)S(1)}, u32[]{:S(2)}, u32[]{:S(2)}) collective-permute-start(f32[328,128]{1,0:T(8,128)S(1)} %collective-permute-done.1.near_ref), channel_id=1, source_target_pairs={{0,16},{16,0},{1,17},{17,1},{2,18},{18,2},{3,19},{19,3},{4,20},{20... | collective-permute-start | bytes 503816 | tf_op jit(solution)/shard_map/ppermute | solution.py:365
  20.3 6.4 %collective-permute-start.5 = (f32[256,128]{1,0:T(8,128)S(1)}, f32[256,128]{1,0:T(8,128)S(1)}, u32[]{:S(2)}, u32[]{:S(2)}) collective-permute-start(f32[256,128]{1,0:T(8,128)S(1)} %collective-permute-done.2.side_ref), channel_id=1, source_target_pairs={{0,16},{16,0},{1,17},{17,1},{2,18},{18,2},{3,19},{19,3},{4,20},{20... | collective-permute-start | bytes 393224 | tf_op jit(solution)/shard_map/ppermute | solution.py:365
  21.9 24.1 %collective-permute-start.7 = (f32[512,128]{1,0:T(8,128)S(1)}, f32[512,128]{1,0:T(8,128)S(1)}, u32[]{:S(2)}, u32[]{:S(2)}) collective-permute-start(f32[512,128]{1,0:T(8,128)S(1)} %get-tuple-element.35), channel_id=1, source_target_pairs={{0,8},{1,9},{2,10},{3,11},{4,12},{5,13},{6,14},{7,15},{8,0},{9,1},... | collective-permute-start | bytes 786440 | tf_op jit(solution)/shard_map/ppermute | solution.py:361
  22.0 26.7 %collective-permute-start.8 = (f32[512,128]{1,0:T(8,128)S(1)}, f32[512,128]{1,0:T(8,128)S(1)}, u32[]{:S(2)}, u32[]{:S(2)}) collective-permute-start(f32[512,128]{1,0:T(8,128)S(1)} %get-tuple-element.36), channel_id=1, source_target_pairs={{0,8},{1,9},{2,10},{3,11},{4,12},{5,13},{6,14},{7,15},{8,0},{9,1},... | collective-permute-start | bytes 786440 | tf_op jit(solution)/shard_map/ppermute | solution.py:361
  25.5 9.8 %collective-permute-start.6 = (f32[256,256]{1,0:T(8,128)S(1)}, f32[256,256]{1,0:T(8,128)S(1)}, u32[]{:S(2)}, u32[]{:S(2)}) collective-permute-start(f32[256,256]{1,0:T(8,128)S(1)} %get-tuple-element.43), channel_id=1, source_target_pairs={{0,16},{16,0},{1,17},{17,1},{2,18},{18,2},{3,19},{19,3},{4,20},{20... | collective-permute-start | bytes 786440 | tf_op jit(solution)/shard_map/ppermute | solution.py:365
  26.7 8.5 %copy-start.1 = (f32[1,256,1024]{2,1,0:T(8,128)S(1)}, f32[1,256,1024]{2,1,0:T(8,128)}, u32[]{:S(2)}) copy-start(f32[1,256,1024]{2,1,0:T(8,128)} %param.3) | copy-start | bytes 3145732
  46.4 2.8 %copy-start.2 = (f32[1,256,512]{2,1,0:T(8,128)S(1)}, f32[1,256,512]{2,1,0:T(8,128)}, u32[]{:S(2)}) copy-start(f32[1,256,512]{2,1,0:T(8,128)} %param.4) | copy-start | bytes 1572868
  46.4 6.0 %collective-permute-start.9 = (f32[256,128]{1,0:T(8,128)S(1)}, f32[256,128]{1,0:T(8,128)S(1)}, u32[]{:S(2)}, u32[]{:S(2)}) collective-permute-start(f32[256,128]{1,0:T(8,128)S(1)} %shard_map.64), channel_id=1, source_target_pairs={{0,16},{16,0},{1,17},{17,1},{2,18},{18,2},{3,19},{19,3},{4,20},{20... | collective-permute-start | bytes 393224 | tf_op jit(solution)/shard_map/ppermute | solution.py:365
  49.2 5.0 %collective-permute-start.10 = (f32[256,128]{1,0:T(8,128)S(1)}, f32[256,128]{1,0:T(8,128)S(1)}, u32[]{:S(2)}, u32[]{:S(2)}) collective-permute-start(f32[256,128]{1,0:T(8,128)S(1)} %shard_map.65), channel_id=1, source_target_pairs={{0,16},{16,0},{1,17},{17,1},{2,18},{18,2},{3,19},{19,3},{4,20},{20... | collective-permute-start | bytes 393224 | tf_op jit(solution)/shard_map/ppermute | solution.py:365

commit v12 on v10

--- a/solution.py
+++ b/solution.py
@@ -25,8 +25,13 @@
 
 
 def full(left, right, dims=((1,), (0,))):
-    return lax.dot_general(
-        left, right, (dims, ((), ())), precision=lax.Precision.HIGHEST, preferred_element_type=F32
+    (left_dim,), (right_dim,) = dims
+    ah, am, al = (part.astype(BF16) for part in split3(left))
+    bh, bm, bl = (part.astype(BF16) for part in split3(right))
+    return contract(
+        jnp.concatenate([ah, ah, am, am, ah, al], axis=left_dim),
+        jnp.concatenate([bh, bm, bh, bm, bl, bh], axis=right_dim),
+        dims,
     )
 
 
@@ -227,8 +232,8 @@
     width = t_ref.shape[1] - n
     mine = first_ref[0]
     put_sibling(m_out, near_ref, side_ref, 0, mine)
-    at = 5 * q // 2
-    row = jnp.concatenate([near_ref[at + i : at + i + 1, :] for i in range(n // q)], axis=1)
+    at = 2 * q
+    row = jnp.concatenate([side_ref[at + i : at + i + 1, :] for i in range(n // q)], axis=1)
     p_out[...] = jnp.where(column_ref[...] == row, 1.0, 0.0).astype(BF16)
     here = pl.ds(pl.multiple_of(width + mine * half, half), half)
     there = pl.ds(pl.multiple_of(width + (1 - mine) * half, half), half)
@@ -332,27 +337,32 @@
         out_ref[:, pl.ds(pl.multiple_of((1 - mine) * half + i * q, q), q)] = part[...]
 
 
-def pack_iface_body(half, width, t_ref, map_ref, first_ref, diag_ref, side_ref, outer_ref, row_ref, column_ref):
+def cut(t_ref, q, row, column):
+    return t_ref[pl.ds(pl.multiple_of(row, q), q), pl.ds(pl.multiple_of(column, q), q)]
+
+
+def pack_diagonal_body(half, width, t_ref, first_ref, diag_ref):
+    q = half // 2
+    here = width + first_ref[0] * half
+    at = 0
+    for block in pack_diagonal(cut(t_ref, q, 0, here), cut(t_ref, q, 0, here + q), cut(t_ref, q, q, here + q)):
+        diag_ref[at : at + block.shape[0], :] = block
+        at += block.shape[0]
+
+
+def pack_side_body(half, width, t_ref, map_ref, first_ref, side_ref, outer_ref, row_ref, column_ref):
     q, n = half // 2, 2 * half
     mine = first_ref[0]
-    here, there = width + mine * half, width + (1 - mine) * half
-
-    def cut(row, column):
-        return t_ref[pl.ds(pl.multiple_of(row, q), q), pl.ds(pl.multiple_of(column, q), q)]
-
-    at = 0
-    for block in pack_diagonal(cut(0, here), cut(0, here + q), cut(q, here + q)):
-        diag_ref[at : at + block.shape[0], :] = block
-        at += block.shape[0]
-    side_ref[0:q, :] = cut(0, there + q)
-    side_ref[q : 2 * q, :] = cut(mine * q, there + mine * q)
+    there = width + (1 - mine) * half
+    side_ref[0:q, :] = cut(t_ref, q, 0, there + q)
+    side_ref[q : 2 * q, :] = cut(t_ref, q, mine * q, there + mine * q)
     spans = column_blocks(half, mine)
     outer_ref[...] = t_ref[:, spans[1]]
     row = jnp.concatenate([map_ref[:, span] for span in spans], axis=1).astype(F32)
     row_ref[...] = row
     column_ref[...] = jnp.broadcast_to(row, (8, n)).T[:, 0:1]
     parts = [row[:, i * q : (i + 1) * q] for i in range(n // q)]
-    diag_ref[at:, :] = jnp.concatenate(parts + parts, axis=0)[0:8, :]
+    side_ref[2 * q :, :] = jnp.concatenate(parts + parts, axis=0)[0:8, :]
 
 
 def pack_outer_body(t_ref, mine_ref, first_ref, *chunks):
@@ -394,9 +404,10 @@
     vmem, smem = pltpu.VMEM, pltpu.SMEM
     mine = lax.axis_index("sib").astype(jnp.int32)
     first = mine.reshape(1)
-    diag, side, outer, own_row, column = kernel(
-        functools.partial(pack_iface_body, half, width),
-        (f(5 * q // 2 + 8, q), f(2 * q, q), f(half, half), f(1, n), f(n, 1)),
+    diag = kernel(functools.partial(pack_diagonal_body, half, width), f(5 * q // 2, q), [vmem, smem])(t_int, first)
+    side, outer, own_row, column = kernel(
+        functools.partial(pack_side_body, half, width),
+        (f(2 * q + 8, q), f(half, half), f(1, n), f(n, 1)),
         [vmem, vmem, smem],
     )(t_int, iface_map, first)
     near = sibling(diag)
@@ -461,7 +472,9 @@
     own_outer, own_iface = common_order(own_rows[0], iface_map[0])
     other_outer, other_iface = common_order(other_rows[0], other_map[0])
     g = solve(own_iface + other_iface, own_outer)
-    product = lambda left, right: full(left, right, ((0,), (0,)))
+    product = lambda left, right: lax.dot_general(
+        left, right, (((0,), (0,)), ((), ())), precision=lax.Precision.HIGHEST, preferred_element_type=F32
+    )
     left = lax.dynamic_slice_in_dim(own_outer, first_row, shard_rows, 1)
     left_g = lax.dynamic_slice_in_dim(g, first_row, shard_rows, 1)
     own_map = t_ext - product(left, g)[None]

time: 54.1 us -> 52.3 us (0.967)
  starting transfers between devices: 15.6 us -> 16.8 us
  local copies, waits for them, and re-layouts: 2.42 us -> 1.23 us
  Pallas kernels: 23.7 us -> 22.7 us
  waiting for transfers between devices: 11.4 us -> 10.7 us
    unnamed x8, local copies, waits for them, and re-layouts: 2.42 us -> 1.23 us
    ppermute x7, starting transfers between devices: 8.13 us -> 9.15 us  [across(): return lax.ppermute(x, 'sib', [(0, 1), (1, 0)])]
  transfers between devices with their start and end apart: 11 -> 11, of which waited for: 4 -> 6; matrix products, arithmetic and copies ran while one was open for 0% -> 0% of each run, Pallas kernels for 42% -> 42%
where the time goes in v12:
time: 52.3 us; the launch traced here: 52.1 us
  Pallas kernels  22.7 us (43%)
  starting transfers between devices  16.8 us (32%)
  waiting for transfers between devices  10.7 us (20%)
  local copies, waits for them, and re-layouts  1.23 us (2%)
  between operations  0.73 us (1%)
    ppermute x7, starting transfers between devices, across(): return lax.ppermute(x, 'sib', [(0, 1), (1, 0)])  9.15 us
    ppermute x4, waiting for transfers between devices, sibling(): return lax.ppermute(x, 'leaf', [(i, i ^ size // 2) for i in range(size)])  9.09 us
    pallas_call x1, Pallas kernels, two_shards(): kernel(functools.partial(first_body, range(tiles - 2)), (f(n, n), f(top,...  8.17 us
    ppermute x4, starting transfers between devices, sibling(): return lax.ppermute(x, 'leaf', [(i, i ^ size // 2) for i in range(size)])  7.64 us
    pallas_call x1, Pallas kernels, two_shards(): kernel(functools.partial(middle_body, tiles - 2), (f(n, n), f(n, width)),...  4.52 us
    pallas_call x1, Pallas kernels, two_shards(): kernel(functools.partial(last_body, tiles - 1), f(n, width), [vmem] * 2,...  3.5 us
    pallas_call x1, Pallas kernels, two_shards(): kernel(functools.partial(output_body, half), (f(half, width), f(half, wid...  3.2 us
    ppermute x7, waiting for transfers between devices, across(): return lax.ppermute(x, 'sib', [(0, 1), (1, 0)])  1.58 us
  transfers between devices with their start and end apart: 11, of which 6 were waited for; matrix products, arithmetic and copies ran while one was open for 0% of the time, Pallas kernels for 42%

profile of v12, /device:TPU:0, one launch (start us, length us, event | category | flops | bytes accessed | tf_op | source)
XLA Modules:
  0.0 52.1 jit_solution(5348476919537617917)
XLA Ops:
  0.6 1.2 %copy-done = f32[1,256,1024]{2,1,0:T(8,128)S(1)} copy-done((f32[1,256,1024]{2,1,0:T(8,128)S(1)}, f32[1,256,1024]{2,1,0:T(8,128)}, u32[]{:S(2)}) %copy-start) | copy-done | bytes 1048600
  1.9 4.1 %collective-permute-start.1 = (f32[320,128]{1,0:T(8,128)S(1)}, f32[320,128]{1,0:T(8,128)S(1)}, u32[]{:S(2)}, u32[]{:S(2)}) collective-permute-start(f32[320,128]{1,0:T(8,128)S(1)} %shard_map.58), channel_id=1, source_target_pairs={{0,8},{1,9},{2,10},{3,11},{4,12},{5,13},{6,14},{7,15},{8,0},{9,1},... | collective-permute-start | bytes 491528 | tf_op jit(solution)/shard_map/ppermute | solution.py:379
  6.2 1.6 %collective-permute-start.3 = (f32[256,256]{1,0:T(8,128)S(1)}, f32[256,256]{1,0:T(8,128)S(1)}, u32[]{:S(2)}, u32[]{:S(2)}) collective-permute-start(f32[256,256]{1,0:T(8,128)S(1)} %get-tuple-element.32), channel_id=1, source_target_pairs={{0,16},{16,0},{1,17},{17,1},{2,18},{18,2},{3,19},{19,3},{4,20},{20... | collective-permute-start | bytes 786440 | tf_op jit(solution)/shard_map/ppermute | solution.py:383
  7.8 0.6 %collective-permute-start.2 = (f32[264,128]{1,0:T(8,128)S(1)}, f32[264,128]{1,0:T(8,128)S(1)}, u32[]{:S(2)}, u32[]{:S(2)}) collective-permute-start(f32[264,128]{1,0:T(8,128)S(1)} %get-tuple-element.28), channel_id=1, source_target_pairs={{0,8},{1,9},{2,10},{3,11},{4,12},{5,13},{6,14},{7,15},{8,0},{9,1},... | collective-permute-start | bytes 405512 | tf_op jit(solution)/shard_map/ppermute | solution.py:379
  8.3 0.5 %collective-permute-start = (f32[320,128]{1,0:T(8,128)S(1)}, f32[320,128]{1,0:T(8,128)S(1)}, u32[]{:S(2)}, u32[]{:S(2)}) collective-permute-start(f32[320,128]{1,0:T(8,128)S(1)} %shard_map.58), channel_id=1, source_target_pairs={{0,16},{16,0},{1,17},{17,1},{2,18},{18,2},{3,19},{19,3},{4,20},{20... | collective-permute-start | bytes 491528 | tf_op jit(solution)/shard_map/ppermute | solution.py:383
  8.8 8.6 %collective-permute-done.1.near_ref = f32[320,128]{1,0:T(8,128)S(1)} collective-permute-done((f32[320,128]{1,0:T(8,128)S(1)}, f32[320,128]{1,0:T(8,128)S(1)}, u32[]{:S(2)}, u32[]{:S(2)}) %collective-permute-start.1) | collective-permute-done | bytes 163872 | tf_op jit(solution)/shard_map/ppermute | solution.py:379
  17.4 1.8 %collective-permute-start.4 = (f32[320,128]{1,0:T(8,128)S(1)}, f32[320,128]{1,0:T(8,128)S(1)}, u32[]{:S(2)}, u32[]{:S(2)}) collective-permute-start(f32[320,128]{1,0:T(8,128)S(1)} %collective-permute-done.1.near_ref), channel_id=1, source_target_pairs={{0,16},{16,0},{1,17},{17,1},{2,18},{18,2},{3,19},{19,3},{4,20},{20... | collective-permute-start | bytes 491528 | tf_op jit(solution)/shard_map/ppermute | solution.py:383
  19.3 0.2 collective-permute-done.2.side_ref
  19.5 1.5 %collective-permute-start.5 = (f32[264,128]{1,0:T(8,128)S(1)}, f32[264,128]{1,0:T(8,128)S(1)}, u32[]{:S(2)}, u32[]{:S(2)}) collective-permute-start(f32[264,128]{1,0:T(8,128)S(1)} %collective-permute-done.2.side_ref), channel_id=1, source_target_pairs={{0,16},{16,0},{1,17},{17,1},{2,18},{18,2},{3,19},{19,3},{4,20},{20... | collective-permute-start | bytes 405512 | tf_op jit(solution)/shard_map/ppermute | solution.py:383
  21.2 2.9 %collective-permute-start.8 = (f32[512,128]{1,0:T(8,128)S(1)}, f32[512,128]{1,0:T(8,128)S(1)}, u32[]{:S(2)}, u32[]{:S(2)}) collective-permute-start(f32[512,128]{1,0:T(8,128)S(1)} %get-tuple-element.36), channel_id=1, source_target_pairs={{0,8},{1,9},{2,10},{3,11},{4,12},{5,13},{6,14},{7,15},{8,0},{9,1},... | collective-permute-start | bytes 786440 | tf_op jit(solution)/shard_map/ppermute | solution.py:379
  24.1 0.5 shard_map.61
  24.6 0.6 %collective-permute-start.6 = (f32[256,256]{1,0:T(8,128)S(1)}, f32[256,256]{1,0:T(8,128)S(1)}, u32[]{:S(2)}, u32[]{:S(2)}) collective-permute-start(f32[256,256]{1,0:T(8,128)S(1)} %get-tuple-element.43), channel_id=1, source_target_pairs={{0,16},{16,0},{1,17},{17,1},{2,18},{18,2},{3,19},{19,3},{4,20},{20... | collective-permute-start | bytes 786440 | tf_op jit(solution)/shard_map/ppermute | solution.py:383
  25.2 0.6 %collective-permute-done.5.side_ref = f32[264,128]{1,0:T(8,128)S(1)} collective-permute-done((f32[264,128]{1,0:T(8,128)S(1)}, f32[264,128]{1,0:T(8,128)S(1)}, u32[]{:S(2)}, u32[]{:S(2)}) %collective-permute-start.5) | collective-permute-done | bytes 135200 | tf_op jit(solution)/shard_map/ppermute | solution.py:383
  25.8 8.2 %shard_map.62 = (f32[512,512]{1,0:T(8,128)S(1)}, f32[256,256]{1,0:T(8,128)S(1)}, f32[8,128]{1,0:T(8,128)S(1)}) custom-call(f32[512,512]{1,0:T(8,128)S(1)} %get-tuple-element.38.a_in, f32[512,512]{1,0:T(8,128)S(1)} %get-tuple-element.39.m_in, bf16[512,512]{1,0:T(8,128)(2,1)S(1)} %get-tuple-element.40.p_ref, f32[320,128]{1,0:T(8,128)S(1)} %collective-permute-done.4.far_ref, ...), custom_call_target="tpu_custom_call" | custom-call | flops 10000000000 | bytes 1048576 | tf_op jit(solution)/shard_map/pallas_call | solution.py:431
  34.0 4.5 %shard_map.63 = (f32[512,512]{1,0:T(8,128)S(1)}, f32[512,512]{1,0:T(8,128)S(1)}) custom-call(f32[512,512]{1,0:T(8,128)S(1)} %get-tuple-element.41.a_ref, f32[256,256]{1,0:T(8,128)S(1)} %get-tuple-element.42.b_ref, f32[256,1024]{1,0:T(8,128)S(1)} %bitcast.10, f32[256,256]{1,0:T(8,128)S(1)} %collective-permute-done.3.mine_ref, ...), custom_call_target="tpu_custom_call" | custom-call | flops 5000000000 | bytes 1048576 | tf_op jit(solution)/shard_map/pallas_call | solution.py:438
  38.5 3.5 %shard_map.64.g_ref = f32[512,512]{1,0:T(8,128)S(1)} custom-call(f32[512,512]{1,0:T(8,128)S(1)} %get-tuple-element.45.a_ref, f32[512,512]{1,0:T(8,128)S(1)} %get-tuple-element.46.g_ref), custom_call_target="tpu_custom_call" | custom-call | flops 5000000000 | bytes 1048576 | tf_op jit(solution)/shard_map/pallas_call | solution.py:441
  42.0 0.2 collective-permute-done.7.chunk_a.chunk_ref
  42.3 1.3 %shard_map.66 = (f32[512,256]{1,0:T(8,128)S(1)}, f32[256,128]{1,0:T(8,128)S(1)}) custom-call(f32[512,512]{1,0:T(8,128)S(1)} %shard_map.64.g_ref, bf16[512,512]{1,0:T(8,128)(2,1)S(1)} %get-tuple-element.40.p_ref, f32[512,128]{1,0:T(8,128)S(1)} %collective-permute-done.7.chunk_a.chunk_ref, s32[1]{0:T(128)} %bitcast.1.first_ref), custom_call_target="tpu_custom_call" | custom-call | flops 1000000000 | bytes 1048576 | tf_op jit(solution)/shard_map/pallas_call | solution.py:442
  43.6 2.2 %collective-permute-start.9 = (f32[256,128]{1,0:T(8,128)S(1)}, f32[256,128]{1,0:T(8,128)S(1)}, u32[]{:S(2)}, u32[]{:S(2)}) collective-permute-start(f32[256,128]{1,0:T(8,128)S(1)} %get-tuple-element.50), channel_id=1, source_target_pairs={{0,16},{16,0},{1,17},{17,1},{2,18},{18,2},{3,19},{19,3},{4,20},{20... | collective-permute-start | bytes 393224 | tf_op jit(solution)/shard_map/ppermute | solution.py:383
  45.8 0.4 shard_map.67
  46.3 0.8 %collective-permute-start.10 = (f32[256,128]{1,0:T(8,128)S(1)}, f32[256,128]{1,0:T(8,128)S(1)}, u32[]{:S(2)}, u32[]{:S(2)}) collective-permute-start(f32[256,128]{1,0:T(8,128)S(1)} %shard_map.67), channel_id=1, source_target_pairs={{0,16},{16,0},{1,17},{17,1},{2,18},{18,2},{3,19},{19,3},{4,20},{20... | collective-permute-start | bytes 393224 | tf_op jit(solution)/shard_map/ppermute | solution.py:383
  47.1 3.2 %shard_map.65 = (f32[256,512]{1,0:T(8,128)}, f32[256,512]{1,0:T(8,128)}, f32[256,256]{1,0:T(8,128)S(1)}) custom-call(f32[512,512]{1,0:T(8,128)S(1)} %shard_map.64.g_ref, bf16[512,512]{1,0:T(8,128)(2,1)S(1)} %get-tuple-element.40.p_ref, f32[256,1024]{1,0:T(8,128)S(1)} %bitcast.11, f32[256,256]{1,0:T(8,128)S(1)} %collective-permute-done.3.mine_ref, ...), custom_call_target="tpu_custom_call" | custom-call | flops 1000000 | bytes 1048576 | tf_op jit(solution)/shard_map/pallas_call | solution.py:447
  50.3 1.0 %collective-permute-done.10.second_part = f32[256,128]{1,0:T(8,128)S(1)} collective-permute-done((f32[256,128]{1,0:T(8,128)S(1)}, f32[256,128]{1,0:T(8,128)S(1)}, u32[]{:S(2)}, u32[]{:S(2)}) %collective-permute-start.10) | collective-permute-done | bytes 131104 | tf_op jit(solution)/shard_map/ppermute | solution.py:383
  51.3 0.8 %shard_map.68 = f32[256,512]{1,0:T(8,128)} custom-call(f32[256,256]{1,0:T(8,128)S(1)} %get-tuple-element.49.keep_ref, f32[256,128]{1,0:T(8,128)S(1)} %collective-permute-done.9.first_part, f32[256,128]{1,0:T(8,128)S(1)} %collective-permute-done.10.second_part, s32[1]{0:T(128)} %bitcast.1.first_ref), custom_call_target="tpu_custom_call" | custom-call | flops 100000000 | bytes 1048576 | tf_op jit(solution)/shard_map/pallas_call | solution.py:454
  (17 shorter events, 0.4 us)
Async XLA Ops:
  0.6 1.2 %copy-start = (f32[1,256,1024]{2,1,0:T(8,128)S(1)}, f32[1,256,1024]{2,1,0:T(8,128)}, u32[]{:S(2)}) copy-start(f32[1,256,1024]{2,1,0:T(8,128)} %param.3) | copy-start | bytes 3145732
  1.9 4.1 %copy-start.3 = (s32[1,512]{1,0:T(1,128)S(1)}, s32[1,512]{1,0:T(1,128)}, u32[]{:S(2)}) copy-start(s32[1,512]{1,0:T(1,128)} %map_ref.1) | copy-start | bytes 6148
  1.9 15.5 %collective-permute-start.1 = (f32[320,128]{1,0:T(8,128)S(1)}, f32[320,128]{1,0:T(8,128)S(1)}, u32[]{:S(2)}, u32[]{:S(2)}) collective-permute-start(f32[320,128]{1,0:T(8,128)S(1)} %shard_map.58), channel_id=1, source_target_pairs={{0,8},{1,9},{2,10},{3,11},{4,12},{5,13},{6,14},{7,15},{8,0},{9,1},... | collective-permute-start | bytes 491528 | tf_op jit(solution)/shard_map/ppermute | solution.py:379
  6.2 14.9 %collective-permute-start.3 = (f32[256,256]{1,0:T(8,128)S(1)}, f32[256,256]{1,0:T(8,128)S(1)}, u32[]{:S(2)}, u32[]{:S(2)}) collective-permute-start(f32[256,256]{1,0:T(8,128)S(1)} %get-tuple-element.32), channel_id=1, source_target_pairs={{0,16},{16,0},{1,17},{17,1},{2,18},{18,2},{3,19},{19,3},{4,20},{20... | collective-permute-start | bytes 786440 | tf_op jit(solution)/shard_map/ppermute | solution.py:383
  7.8 11.7 %collective-permute-start.2 = (f32[264,128]{1,0:T(8,128)S(1)}, f32[264,128]{1,0:T(8,128)S(1)}, u32[]{:S(2)}, u32[]{:S(2)}) collective-permute-start(f32[264,128]{1,0:T(8,128)S(1)} %get-tuple-element.28), channel_id=1, source_target_pairs={{0,8},{1,9},{2,10},{3,11},{4,12},{5,13},{6,14},{7,15},{8,0},{9,1},... | collective-permute-start | bytes 405512 | tf_op jit(solution)/shard_map/ppermute | solution.py:379
  8.3 15.8 %collective-permute-start = (f32[320,128]{1,0:T(8,128)S(1)}, f32[320,128]{1,0:T(8,128)S(1)}, u32[]{:S(2)}, u32[]{:S(2)}) collective-permute-start(f32[320,128]{1,0:T(8,128)S(1)} %shard_map.58), channel_id=1, source_target_pairs={{0,16},{16,0},{1,17},{17,1},{2,18},{18,2},{3,19},{19,3},{4,20},{20... | collective-permute-start | bytes 491528 | tf_op jit(solution)/shard_map/ppermute | solution.py:383
  17.4 8.4 %collective-permute-start.4 = (f32[320,128]{1,0:T(8,128)S(1)}, f32[320,128]{1,0:T(8,128)S(1)}, u32[]{:S(2)}, u32[]{:S(2)}) collective-permute-start(f32[320,128]{1,0:T(8,128)S(1)} %collective-permute-done.1.near_ref), channel_id=1, source_target_pairs={{0,16},{16,0},{1,17},{17,1},{2,18},{18,2},{3,19},{19,3},{4,20},{20... | collective-permute-start | bytes 491528 | tf_op jit(solution)/shard_map/ppermute | solution.py:383
  19.5 6.3 %collective-permute-start.5 = (f32[264,128]{1,0:T(8,128)S(1)}, f32[264,128]{1,0:T(8,128)S(1)}, u32[]{:S(2)}, u32[]{:S(2)}) collective-permute-start(f32[264,128]{1,0:T(8,128)S(1)} %collective-permute-done.2.side_ref), channel_id=1, source_target_pairs={{0,16},{16,0},{1,17},{17,1},{2,18},{18,2},{3,19},{19,3},{4,20},{20... | collective-permute-start | bytes 405512 | tf_op jit(solution)/shard_map/ppermute | solution.py:383
  21.1 21.2 %collective-permute-start.7 = (f32[512,128]{1,0:T(8,128)S(1)}, f32[512,128]{1,0:T(8,128)S(1)}, u32[]{:S(2)}, u32[]{:S(2)}) collective-permute-start(f32[512,128]{1,0:T(8,128)S(1)} %get-tuple-element.35), channel_id=1, source_target_pairs={{0,8},{1,9},{2,10},{3,11},{4,12},{5,13},{6,14},{7,15},{8,0},{9,1},... | collective-permute-start | bytes 786440 | tf_op jit(solution)/shard_map/ppermute | solution.py:379
  21.2 24.7 %collective-permute-start.8 = (f32[512,128]{1,0:T(8,128)S(1)}, f32[512,128]{1,0:T(8,128)S(1)}, u32[]{:S(2)}, u32[]{:S(2)}) collective-permute-start(f32[512,128]{1,0:T(8,128)S(1)} %get-tuple-element.36), channel_id=1, source_target_pairs={{0,8},{1,9},{2,10},{3,11},{4,12},{5,13},{6,14},{7,15},{8,0},{9,1},... | collective-permute-start | bytes 786440 | tf_op jit(solution)/shard_map/ppermute | solution.py:379
  24.6 9.4 %collective-permute-start.6 = (f32[256,256]{1,0:T(8,128)S(1)}, f32[256,256]{1,0:T(8,128)S(1)}, u32[]{:S(2)}, u32[]{:S(2)}) collective-permute-start(f32[256,256]{1,0:T(8,128)S(1)} %get-tuple-element.43), channel_id=1, source_target_pairs={{0,16},{16,0},{1,17},{17,1},{2,18},{18,2},{3,19},{19,3},{4,20},{20... | collective-permute-start | bytes 786440 | tf_op jit(solution)/shard_map/ppermute | solution.py:383
  25.8 8.2 %copy-start.1 = (f32[1,256,1024]{2,1,0:T(8,128)S(1)}, f32[1,256,1024]{2,1,0:T(8,128)}, u32[]{:S(2)}) copy-start(f32[1,256,1024]{2,1,0:T(8,128)} %param.3) | copy-start | bytes 3145732
  43.6 6.8 %collective-permute-start.9 = (f32[256,128]{1,0:T(8,128)S(1)}, f32[256,128]{1,0:T(8,128)S(1)}, u32[]{:S(2)}, u32[]{:S(2)}) collective-permute-start(f32[256,128]{1,0:T(8,128)S(1)} %get-tuple-element.50), channel_id=1, source_target_pairs={{0,16},{16,0},{1,17},{17,1},{2,18},{18,2},{3,19},{19,3},{4,20},{20... | collective-permute-start | bytes 393224 | tf_op jit(solution)/shard_map/ppermute | solution.py:383
  45.8 1.3 %copy-start.2 = (f32[1,256,512]{2,1,0:T(8,128)S(1)}, f32[1,256,512]{2,1,0:T(8,128)}, u32[]{:S(2)}) copy-start(f32[1,256,512]{2,1,0:T(8,128)} %param.4) | copy-start | bytes 1572868
  46.3 5.0 %collective-permute-start.10 = (f32[256,128]{1,0:T(8,128)S(1)}, f32[256,128]{1,0:T(8,128)S(1)}, u32[]{:S(2)}, u32[]{:S(2)}) collective-permute-start(f32[256,128]{1,0:T(8,128)S(1)} %shard_map.67), channel_id=1, source_target_pairs={{0,16},{16,0},{1,17},{17,1},{2,18},{18,2},{3,19},{19,3},{4,20},{20... | collective-permute-start | bytes 393224 | tf_op jit(solution)/shard_map/ppermute | solution.py:383

commit v13 on v12

--- a/solution.py
+++ b/solution.py
@@ -36,19 +36,24 @@
 
 
 def three_pass(left, right, dims):
+    (left_dim,), (right_dim,) = dims
     lh, rh = left.astype(BF16), right.astype(BF16)
     ll, rl = (left - lh.astype(F32)).astype(BF16), (right - rh.astype(F32)).astype(BF16)
-    return contract(lh, rh, dims) + (contract(lh, rl, dims) + contract(ll, rh, dims))
+    return contract(
+        jnp.concatenate([lh, lh, ll], axis=left_dim), jnp.concatenate([rh, rl, rh], axis=right_dim), dims
+    )
 
 
 def pick_left(onehot, x, dims):
-    high, middle, low = (part.astype(BF16) for part in split3(x))
-    return contract(onehot, high, dims) + (contract(onehot, middle, dims) + contract(onehot, low, dims))
+    (left_dim,), (right_dim,) = dims
+    parts = [part.astype(BF16) for part in split3(x)]
+    return contract(jnp.concatenate([onehot] * 3, axis=left_dim), jnp.concatenate(parts, axis=right_dim), dims)
 
 
 def pick_right(x, onehot, dims):
-    high, middle, low = (part.astype(BF16) for part in split3(x))
-    return contract(high, onehot, dims) + (contract(middle, onehot, dims) + contract(low, onehot, dims))
+    (left_dim,), (right_dim,) = dims
+    parts = [part.astype(BF16) for part in split3(x)]
+    return contract(jnp.concatenate(parts, axis=left_dim), jnp.concatenate([onehot] * 3, axis=right_dim), dims)
 
 
 def over_lanes(x, lane):
@@ -418,8 +423,6 @@
     near, near_side = lax.optimization_barrier((near, near_side))
     far_side = across(near_side)
     chunks = kernel(pack_outer_body, [f(n, q)] * 2, [vmem, vmem, smem])(t_int, outer_mine, first)
-    *chunks, _ = lax.optimization_barrier((*chunks, near_side))
-    near_r = [sibling(chunk) for chunk in chunks]
     first_late, *_ = lax.optimization_barrier((first, *chunks))
     a, m, onehot, outer = kernel(
         functools.partial(prepare_body, half),
@@ -427,6 +430,9 @@
         [vmem] * 5 + [smem],
     )(t_int, diag_other, near, near_side, column, first_late)
     outer_others = across(outer)
+    chunk_a, _ = lax.optimization_barrier((chunks[0], near_side))
+    chunk_b, onehot = lax.optimization_barrier((chunks[1], onehot))
+    near_r = [sibling(chunk_a), sibling(chunk_b)]
     top = (tiles - 2) * TILE
     a, b, scale = kernel(
         functools.partial(first_body, range(tiles - 2)),

time: 52.3 us -> 52.3 us (level)
  transfers between devices with their start and end apart: 11 -> 11, of which waited for: 6 -> 5; matrix products, arithmetic and copies ran while one was open for 0% -> 0% of each run, Pallas kernels for 42% -> 42%
where the time goes in v13:
time: 52.3 us; the launch traced here: 52.1 us
  Pallas kernels  22.8 us (44%)
  starting transfers between devices  16.8 us (32%)
  waiting for transfers between devices  10.6 us (20%)
  local copies, waits for them, and re-layouts  1.23 us (2%)
  between operations  0.74 us (1%)
    ppermute x7, starting transfers between devices, across(): return lax.ppermute(x, 'sib', [(0, 1), (1, 0)])  9.09 us
    ppermute x4, waiting for transfers between devices, sibling(): return lax.ppermute(x, 'leaf', [(i, i ^ size // 2) for i in range(size)])  9.07 us
    pallas_call x1, Pallas kernels, two_shards(): kernel(functools.partial(first_body, range(tiles - 2)), (f(n, n), f(top,...  8.15 us
    ppermute x4, starting transfers between devices, sibling(): return lax.ppermute(x, 'leaf', [(i, i ^ size // 2) for i in range(size)])  7.7 us
    pallas_call x1, Pallas kernels, two_shards(): kernel(functools.partial(middle_body, tiles - 2), (f(n, n), f(n, width)),...  4.52 us
    pallas_call x1, Pallas kernels, two_shards(): kernel(functools.partial(last_body, tiles - 1), f(n, width), [vmem] * 2,...  3.52 us
    pallas_call x1, Pallas kernels, two_shards(): kernel(functools.partial(output_body, half), (f(half, width), f(half, wid...  3.22 us
    ppermute x7, waiting for transfers between devices, across(): return lax.ppermute(x, 'sib', [(0, 1), (1, 0)])  1.56 us
  transfers between devices with their start and end apart: 11, of which 5 were waited for; matrix products, arithmetic and copies ran while one was open for 0% of the time, Pallas kernels for 42%

profile of v13, /device:TPU:0, one launch (start us, length us, event | category | flops | bytes accessed | tf_op | source)
XLA Modules:
  0.0 52.1 jit_solution(6261093163558913084)
XLA Ops:
  0.6 1.2 %copy-done = f32[1,256,1024]{2,1,0:T(8,128)S(1)} copy-done((f32[1,256,1024]{2,1,0:T(8,128)S(1)}, f32[1,256,1024]{2,1,0:T(8,128)}, u32[]{:S(2)}) %copy-start) | copy-done | bytes 1048600
  1.9 4.1 %collective-permute-start.1 = (f32[320,128]{1,0:T(8,128)S(1)}, f32[320,128]{1,0:T(8,128)S(1)}, u32[]{:S(2)}, u32[]{:S(2)}) collective-permute-start(f32[320,128]{1,0:T(8,128)S(1)} %shard_map.58), channel_id=1, source_target_pairs={{0,8},{1,9},{2,10},{3,11},{4,12},{5,13},{6,14},{7,15},{8,0},{9,1},... | collective-permute-start | bytes 491528 | tf_op jit(solution)/shard_map/ppermute | solution.py:384
  6.2 1.6 %collective-permute-start.3 = (f32[256,256]{1,0:T(8,128)S(1)}, f32[256,256]{1,0:T(8,128)S(1)}, u32[]{:S(2)}, u32[]{:S(2)}) collective-permute-start(f32[256,256]{1,0:T(8,128)S(1)} %get-tuple-element.33), channel_id=1, source_target_pairs={{0,16},{16,0},{1,17},{17,1},{2,18},{18,2},{3,19},{19,3},{4,20},{20... | collective-permute-start | bytes 786440 | tf_op jit(solution)/shard_map/ppermute | solution.py:388
  7.8 0.6 %collective-permute-start.2 = (f32[264,128]{1,0:T(8,128)S(1)}, f32[264,128]{1,0:T(8,128)S(1)}, u32[]{:S(2)}, u32[]{:S(2)}) collective-permute-start(f32[264,128]{1,0:T(8,128)S(1)} %get-tuple-element.29), channel_id=1, source_target_pairs={{0,8},{1,9},{2,10},{3,11},{4,12},{5,13},{6,14},{7,15},{8,0},{9,1},... | collective-permute-start | bytes 405512 | tf_op jit(solution)/shard_map/ppermute | solution.py:384
  8.3 0.5 %collective-permute-start = (f32[320,128]{1,0:T(8,128)S(1)}, f32[320,128]{1,0:T(8,128)S(1)}, u32[]{:S(2)}, u32[]{:S(2)}) collective-permute-start(f32[320,128]{1,0:T(8,128)S(1)} %shard_map.58), channel_id=1, source_target_pairs={{0,16},{16,0},{1,17},{17,1},{2,18},{18,2},{3,19},{19,3},{4,20},{20... | collective-permute-start | bytes 491528 | tf_op jit(solution)/shard_map/ppermute | solution.py:388
  8.8 8.6 %collective-permute-done.1.near_ref = f32[320,128]{1,0:T(8,128)S(1)} collective-permute-done((f32[320,128]{1,0:T(8,128)S(1)}, f32[320,128]{1,0:T(8,128)S(1)}, u32[]{:S(2)}, u32[]{:S(2)}) %collective-permute-start.1) | collective-permute-done | bytes 163872 | tf_op jit(solution)/shard_map/ppermute | solution.py:384
  17.4 1.8 %collective-permute-start.4 = (f32[320,128]{1,0:T(8,128)S(1)}, f32[320,128]{1,0:T(8,128)S(1)}, u32[]{:S(2)}, u32[]{:S(2)}) collective-permute-start(f32[320,128]{1,0:T(8,128)S(1)} %collective-permute-done.1.near_ref), channel_id=1, source_target_pairs={{0,16},{16,0},{1,17},{17,1},{2,18},{18,2},{3,19},{19,3},{4,20},{20... | collective-permute-start | bytes 491528 | tf_op jit(solution)/shard_map/ppermute | solution.py:388
  19.3 0.2 collective-permute-done.2.side_ref
  19.5 1.5 %collective-permute-start.5 = (f32[264,128]{1,0:T(8,128)S(1)}, f32[264,128]{1,0:T(8,128)S(1)}, u32[]{:S(2)}, u32[]{:S(2)}) collective-permute-start(f32[264,128]{1,0:T(8,128)S(1)} %collective-permute-done.2.side_ref), channel_id=1, source_target_pairs={{0,16},{16,0},{1,17},{17,1},{2,18},{18,2},{3,19},{19,3},{4,20},{20... | collective-permute-start | bytes 405512 | tf_op jit(solution)/shard_map/ppermute | solution.py:388
  21.2 0.5 %shard_map.61 = (f32[512,512]{1,0:T(8,128)S(1)}, f32[512,512]{1,0:T(8,128)S(1)}, bf16[512,512]{1,0:T(8,128)(2,1)S(1)}, f32[256,256]{1,0:T(8,128)S(1)}) custom-call(f32[256,1024]{1,0:T(8,128)S(1)} %bitcast.9, f32[320,128]{1,0:T(8,128)S(1)} %collective-permute-done.early_ref, f32[320,128]{1,0:T(8,128)S(1)} %collective-permute-done.1.near_ref, ...), custom_call_target="tpu_custom_call" | custom-call | flops 100000000 | bytes 1048576 | tf_op jit(solution)/shard_map/pallas_call | solution.py:427
  21.7 3.0 %collective-permute-start.8 = (f32[512,128]{1,0:T(8,128)S(1)}, f32[512,128]{1,0:T(8,128)S(1)}, u32[]{:S(2)}, u32[]{:S(2)}) collective-permute-start(f32[512,128]{1,0:T(8,128)S(1)} %get-tuple-element.49), channel_id=1, source_target_pairs={{0,8},{1,9},{2,10},{3,11},{4,12},{5,13},{6,14},{7,15},{8,0},{9,1},... | collective-permute-start | bytes 786440 | tf_op jit(solution)/shard_map/ppermute | solution.py:384
  24.7 0.5 %collective-permute-start.6 = (f32[256,256]{1,0:T(8,128)S(1)}, f32[256,256]{1,0:T(8,128)S(1)}, u32[]{:S(2)}, u32[]{:S(2)}) collective-permute-start(f32[256,256]{1,0:T(8,128)S(1)} %get-tuple-element.43), channel_id=1, source_target_pairs={{0,16},{16,0},{1,17},{17,1},{2,18},{18,2},{3,19},{19,3},{4,20},{20... | collective-permute-start | bytes 786440 | tf_op jit(solution)/shard_map/ppermute | solution.py:388
  25.2 0.6 %collective-permute-done.5.side_ref = f32[264,128]{1,0:T(8,128)S(1)} collective-permute-done((f32[264,128]{1,0:T(8,128)S(1)}, f32[264,128]{1,0:T(8,128)S(1)}, u32[]{:S(2)}, u32[]{:S(2)}) %collective-permute-start.5) | collective-permute-done | bytes 135200 | tf_op jit(solution)/shard_map/ppermute | solution.py:388
  25.8 8.2 %shard_map.62 = (f32[512,512]{1,0:T(8,128)S(1)}, f32[256,256]{1,0:T(8,128)S(1)}, f32[8,128]{1,0:T(8,128)S(1)}) custom-call(f32[512,512]{1,0:T(8,128)S(1)} %get-tuple-element.37.a_in, f32[512,512]{1,0:T(8,128)S(1)} %get-tuple-element.38.m_in, bf16[512,512]{1,0:T(8,128)(2,1)S(1)} %get-tuple-element.40.p_ref, f32[320,128]{1,0:T(8,128)S(1)} %collective-permute-done.4.far_ref, ...), custom_call_target="tpu_custom_call" | custom-call | flops 10000000000 | bytes 1048576 | tf_op jit(solution)/shard_map/pallas_call | solution.py:437
  34.0 4.5 %shard_map.63 = (f32[512,512]{1,0:T(8,128)S(1)}, f32[512,512]{1,0:T(8,128)S(1)}) custom-call(f32[512,512]{1,0:T(8,128)S(1)} %get-tuple-element.41.a_ref, f32[256,256]{1,0:T(8,128)S(1)} %get-tuple-element.42.b_ref, f32[256,1024]{1,0:T(8,128)S(1)} %bitcast.10, f32[256,256]{1,0:T(8,128)S(1)} %collective-permute-done.3.mine_ref, ...), custom_call_target="tpu_custom_call" | custom-call | flops 5000000000 | bytes 1048576 | tf_op jit(solution)/shard_map/pallas_call | solution.py:444
  38.5 3.5 %shard_map.64.g_ref = f32[512,512]{1,0:T(8,128)S(1)} custom-call(f32[512,512]{1,0:T(8,128)S(1)} %get-tuple-element.45.a_ref, f32[512,512]{1,0:T(8,128)S(1)} %get-tuple-element.46.g_ref), custom_call_target="tpu_custom_call" | custom-call | flops 5000000000 | bytes 1048576 | tf_op jit(solution)/shard_map/pallas_call | solution.py:447
  42.0 0.2 collective-permute-done.7.chunk_a.chunk_ref
  42.3 1.3 %shard_map.66 = (f32[512,256]{1,0:T(8,128)S(1)}, f32[256,128]{1,0:T(8,128)S(1)}) custom-call(f32[512,512]{1,0:T(8,128)S(1)} %shard_map.64.g_ref, bf16[512,512]{1,0:T(8,128)(2,1)S(1)} %get-tuple-element.40.p_ref, f32[512,128]{1,0:T(8,128)S(1)} %collective-permute-done.7.chunk_a.chunk_ref, s32[1]{0:T(128)} %bitcast.1.first_ref), custom_call_target="tpu_custom_call" | custom-call | flops 1000000000 | bytes 1048576 | tf_op jit(solution)/shard_map/pallas_call | solution.py:448
  43.6 2.2 %collective-permute-start.9 = (f32[256,128]{1,0:T(8,128)S(1)}, f32[256,128]{1,0:T(8,128)S(1)}, u32[]{:S(2)}, u32[]{:S(2)}) collective-permute-start(f32[256,128]{1,0:T(8,128)S(1)} %get-tuple-element.52), channel_id=1, source_target_pairs={{0,16},{16,0},{1,17},{17,1},{2,18},{18,2},{3,19},{19,3},{4,20},{20... | collective-permute-start | bytes 393224 | tf_op jit(solution)/shard_map/ppermute | solution.py:388
  45.8 0.4 shard_map.67
  46.3 0.8 %collective-permute-start.10 = (f32[256,128]{1,0:T(8,128)S(1)}, f32[256,128]{1,0:T(8,128)S(1)}, u32[]{:S(2)}, u32[]{:S(2)}) collective-permute-start(f32[256,128]{1,0:T(8,128)S(1)} %shard_map.67), channel_id=1, source_target_pairs={{0,16},{16,0},{1,17},{17,1},{2,18},{18,2},{3,19},{19,3},{4,20},{20... | collective-permute-start | bytes 393224 | tf_op jit(solution)/shard_map/ppermute | solution.py:388
  47.1 3.2 %shard_map.65 = (f32[256,512]{1,0:T(8,128)}, f32[256,512]{1,0:T(8,128)}, f32[256,256]{1,0:T(8,128)S(1)}) custom-call(f32[512,512]{1,0:T(8,128)S(1)} %shard_map.64.g_ref, bf16[512,512]{1,0:T(8,128)(2,1)S(1)} %get-tuple-element.40.p_ref, f32[256,1024]{1,0:T(8,128)S(1)} %bitcast.11, f32[256,256]{1,0:T(8,128)S(1)} %collective-permute-done.3.mine_ref, ...), custom_call_target="tpu_custom_call" | custom-call | flops 1000000 | bytes 1048576 | tf_op jit(solution)/shard_map/pallas_call | solution.py:453
  50.3 1.0 %collective-permute-done.10.second_part = f32[256,128]{1,0:T(8,128)S(1)} collective-permute-done((f32[256,128]{1,0:T(8,128)S(1)}, f32[256,128]{1,0:T(8,128)S(1)}, u32[]{:S(2)}, u32[]{:S(2)}) %collective-permute-start.10) | collective-permute-done | bytes 131104 | tf_op jit(solution)/shard_map/ppermute | solution.py:388
  51.3 0.8 %shard_map.68 = f32[256,512]{1,0:T(8,128)} custom-call(f32[256,256]{1,0:T(8,128)S(1)} %get-tuple-element.51.keep_ref, f32[256,128]{1,0:T(8,128)S(1)} %collective-permute-done.9.first_part, f32[256,128]{1,0:T(8,128)S(1)} %collective-permute-done.10.second_part, s32[1]{0:T(128)} %bitcast.1.first_ref), custom_call_target="tpu_custom_call" | custom-call | flops 100000000 | bytes 1048576 | tf_op jit(solution)/shard_map/pallas_call | solution.py:460
  (17 shorter events, 0.4 us)
Async XLA Ops:
  0.6 1.2 %copy-start = (f32[1,256,1024]{2,1,0:T(8,128)S(1)}, f32[1,256,1024]{2,1,0:T(8,128)}, u32[]{:S(2)}) copy-start(f32[1,256,1024]{2,1,0:T(8,128)} %param.3) | copy-start | bytes 3145732
  1.9 4.1 %copy-start.3 = (s32[1,512]{1,0:T(1,128)S(1)}, s32[1,512]{1,0:T(1,128)}, u32[]{:S(2)}) copy-start(s32[1,512]{1,0:T(1,128)} %map_ref.1) | copy-start | bytes 6148
  1.9 15.5 %collective-permute-start.1 = (f32[320,128]{1,0:T(8,128)S(1)}, f32[320,128]{1,0:T(8,128)S(1)}, u32[]{:S(2)}, u32[]{:S(2)}) collective-permute-start(f32[320,128]{1,0:T(8,128)S(1)} %shard_map.58), channel_id=1, source_target_pairs={{0,8},{1,9},{2,10},{3,11},{4,12},{5,13},{6,14},{7,15},{8,0},{9,1},... | collective-permute-start | bytes 491528 | tf_op jit(solution)/shard_map/ppermute | solution.py:384
  6.2 14.9 %collective-permute-start.3 = (f32[256,256]{1,0:T(8,128)S(1)}, f32[256,256]{1,0:T(8,128)S(1)}, u32[]{:S(2)}, u32[]{:S(2)}) collective-permute-start(f32[256,256]{1,0:T(8,128)S(1)} %get-tuple-element.33), channel_id=1, source_target_pairs={{0,16},{16,0},{1,17},{17,1},{2,18},{18,2},{3,19},{19,3},{4,20},{20... | collective-permute-start | bytes 786440 | tf_op jit(solution)/shard_map/ppermute | solution.py:388
  7.8 11.7 %collective-permute-start.2 = (f32[264,128]{1,0:T(8,128)S(1)}, f32[264,128]{1,0:T(8,128)S(1)}, u32[]{:S(2)}, u32[]{:S(2)}) collective-permute-start(f32[264,128]{1,0:T(8,128)S(1)} %get-tuple-element.29), channel_id=1, source_target_pairs={{0,8},{1,9},{2,10},{3,11},{4,12},{5,13},{6,14},{7,15},{8,0},{9,1},... | collective-permute-start | bytes 405512 | tf_op jit(solution)/shard_map/ppermute | solution.py:384
  8.3 12.9 %collective-permute-start = (f32[320,128]{1,0:T(8,128)S(1)}, f32[320,128]{1,0:T(8,128)S(1)}, u32[]{:S(2)}, u32[]{:S(2)}) collective-permute-start(f32[320,128]{1,0:T(8,128)S(1)} %shard_map.58), channel_id=1, source_target_pairs={{0,16},{16,0},{1,17},{17,1},{2,18},{18,2},{3,19},{19,3},{4,20},{20... | collective-permute-start | bytes 491528 | tf_op jit(solution)/shard_map/ppermute | solution.py:388
  17.4 8.4 %collective-permute-start.4 = (f32[320,128]{1,0:T(8,128)S(1)}, f32[320,128]{1,0:T(8,128)S(1)}, u32[]{:S(2)}, u32[]{:S(2)}) collective-permute-start(f32[320,128]{1,0:T(8,128)S(1)} %collective-permute-done.1.near_ref), channel_id=1, source_target_pairs={{0,16},{16,0},{1,17},{17,1},{2,18},{18,2},{3,19},{19,3},{4,20},{20... | collective-permute-start | bytes 491528 | tf_op jit(solution)/shard_map/ppermute | solution.py:388
  19.5 6.3 %collective-permute-start.5 = (f32[264,128]{1,0:T(8,128)S(1)}, f32[264,128]{1,0:T(8,128)S(1)}, u32[]{:S(2)}, u32[]{:S(2)}) collective-permute-start(f32[264,128]{1,0:T(8,128)S(1)} %collective-permute-done.2.side_ref), channel_id=1, source_target_pairs={{0,16},{16,0},{1,17},{17,1},{2,18},{18,2},{3,19},{19,3},{4,20},{20... | collective-permute-start | bytes 405512 | tf_op jit(solution)/shard_map/ppermute | solution.py:388
  21.1 21.2 %collective-permute-start.7 = (f32[512,128]{1,0:T(8,128)S(1)}, f32[512,128]{1,0:T(8,128)S(1)}, u32[]{:S(2)}, u32[]{:S(2)}) collective-permute-start(f32[512,128]{1,0:T(8,128)S(1)} %get-tuple-element.48), channel_id=1, source_target_pairs={{0,8},{1,9},{2,10},{3,11},{4,12},{5,13},{6,14},{7,15},{8,0},{9,1},... | collective-permute-start | bytes 786440 | tf_op jit(solution)/shard_map/ppermute | solution.py:384
  21.7 24.1 %collective-permute-start.8 = (f32[512,128]{1,0:T(8,128)S(1)}, f32[512,128]{1,0:T(8,128)S(1)}, u32[]{:S(2)}, u32[]{:S(2)}) collective-permute-start(f32[512,128]{1,0:T(8,128)S(1)} %get-tuple-element.49), channel_id=1, source_target_pairs={{0,8},{1,9},{2,10},{3,11},{4,12},{5,13},{6,14},{7,15},{8,0},{9,1},... | collective-permute-start | bytes 786440 | tf_op jit(solution)/shard_map/ppermute | solution.py:384
  24.7 9.3 %collective-permute-start.6 = (f32[256,256]{1,0:T(8,128)S(1)}, f32[256,256]{1,0:T(8,128)S(1)}, u32[]{:S(2)}, u32[]{:S(2)}) collective-permute-start(f32[256,256]{1,0:T(8,128)S(1)} %get-tuple-element.43), channel_id=1, source_target_pairs={{0,16},{16,0},{1,17},{17,1},{2,18},{18,2},{3,19},{19,3},{4,20},{20... | collective-permute-start | bytes 786440 | tf_op jit(solution)/shard_map/ppermute | solution.py:388
  25.8 8.2 %copy-start.1 = (f32[1,256,1024]{2,1,0:T(8,128)S(1)}, f32[1,256,1024]{2,1,0:T(8,128)}, u32[]{:S(2)}) copy-start(f32[1,256,1024]{2,1,0:T(8,128)} %param.3) | copy-start | bytes 3145732
  43.6 6.8 %collective-permute-start.9 = (f32[256,128]{1,0:T(8,128)S(1)}, f32[256,128]{1,0:T(8,128)S(1)}, u32[]{:S(2)}, u32[]{:S(2)}) collective-permute-start(f32[256,128]{1,0:T(8,128)S(1)} %get-tuple-element.52), channel_id=1, source_target_pairs={{0,16},{16,0},{1,17},{17,1},{2,18},{18,2},{3,19},{19,3},{4,20},{20... | collective-permute-start | bytes 393224 | tf_op jit(solution)/shard_map/ppermute | solution.py:388
  45.8 1.3 %copy-start.2 = (f32[1,256,512]{2,1,0:T(8,128)S(1)}, f32[1,256,512]{2,1,0:T(8,128)}, u32[]{:S(2)}) copy-start(f32[1,256,512]{2,1,0:T(8,128)} %param.4) | copy-start | bytes 1572868
  46.3 5.0 %collective-permute-start.10 = (f32[256,128]{1,0:T(8,128)S(1)}, f32[256,128]{1,0:T(8,128)S(1)}, u32[]{:S(2)}, u32[]{:S(2)}) collective-permute-start(f32[256,128]{1,0:T(8,128)S(1)} %shard_map.67), channel_id=1, source_target_pairs={{0,16},{16,0},{1,17},{17,1},{2,18},{18,2},{3,19},{19,3},{4,20},{20... | collective-permute-start | bytes 393224 | tf_op jit(solution)/shard_map/ppermute | solution.py:388

commit v14 on v13

--- a/solution.py
+++ b/solution.py
@@ -164,6 +164,34 @@
             g_ref[rows, :] = g_ref[rows, :] - full(factor, right)
 
 
+def eliminate_two(a_ref, b_ref):
+    size = a_ref.shape[0]
+    first, second = slice(0, TILE), slice(TILE, 2 * TILE)
+
+    def update(at, old, panel):
+        for i in range(at, size // TILE):
+            rows, offset = slice(i * TILE, (i + 1) * TILE), (i - at) * TILE
+            factor = old[:, offset : offset + TILE]
+            a_ref[rows, i * TILE :] = a_ref[rows, i * TILE :] - full(factor, panel[:, offset:], ((0,), (0,)))
+
+    top = invert_tile(a_ref[first, first])
+    old = a_ref[first, TILE:]
+    panel = full(top, old)
+    update(1, old, panel)
+    cross, beyond = panel[:, :TILE], panel[:, TILE:]
+    bottom = invert_tile(a_ref[second, second])
+    old = a_ref[second, 2 * TILE :]
+    panel = full(bottom, old)
+    update(2, old, panel)
+    a_ref[second, 2 * TILE :] = panel
+    a_ref[first, 2 * TILE :] = beyond - full(cross, panel)
+    side = full(cross, bottom)
+    b_ref[first, first] = top + full(side, cross, ((1,), (1,)))
+    b_ref[first, second] = -side
+    b_ref[second, first] = -side.T
+    b_ref[second, second] = bottom
+
+
 def call(body, outs, scratch=(), **cost):
     return pl.pallas_call(
         body,
@@ -251,7 +279,7 @@
     outer_out[...] = t_ref[:, column_blocks(half, mine)[0]]
 
 
-def first_body(steps, a_in, m_in, p_ref, far_ref, side_ref, first_ref, a_out, b_out, scale_out, m_work):
+def first_body(a_in, m_in, p_ref, far_ref, side_ref, first_ref, a_out, b_out, scale_out, m_work):
     n = a_in.shape[0]
     m_work[...] = m_in[...]
     put_sibling(m_work, far_ref, side_ref, 2, first_ref[0])
@@ -264,10 +292,7 @@
         later = slice(i * TILE, n)
         both = a_in[rows, later] + pick_left(p_ref[rows, :], moved[:, later], ((1,), (0,)))
         a_out[rows, later] = both * scale
-    top = b_out.shape[0]
-    on_diagonal = [lax.broadcasted_iota(jnp.int32, (top, top), axis) for axis in (0, 1)]
-    b_out[...] = jnp.where(on_diagonal[0] == on_diagonal[1], 1.0, 0.0).astype(F32)
-    eliminate(a_out, b_out, steps)
+    eliminate_two(a_out, b_out)
 
 
 def middle_body(k, a_ref, b_ref, t_ref, mine_ref, others_ref, scale_ref, first_ref, a_out, g_out):
@@ -433,9 +458,9 @@
     chunk_a, _ = lax.optimization_barrier((chunks[0], near_side))
     chunk_b, onehot = lax.optimization_barrier((chunks[1], onehot))
     near_r = [sibling(chunk_a), sibling(chunk_b)]
-    top = (tiles - 2) * TILE
+    top = 2 * TILE
     a, b, scale = kernel(
-        functools.partial(first_body, range(tiles - 2)),
+        first_body,
         (f(n, n), f(top, top), f(8, TILE)),
         [vmem] * 5 + [smem],
         [pltpu.VMEM((n, n), F32)],

time: 52.3 us -> 52.3 us (level)
  no operation moved by 1% of the time
where the time goes in v14:
time: 52.3 us; the launch traced here: 52.1 us
  Pallas kernels  22.8 us (44%)
  starting transfers between devices  16.8 us (32%)
  waiting for transfers between devices  10.6 us (20%)
  local copies, waits for them, and re-layouts  1.23 us (2%)
  between operations  0.74 us (1%)
    ppermute x7, starting transfers between devices, across(): return lax.ppermute(x, 'sib', [(0, 1), (1, 0)])  9.12 us
    ppermute x4, waiting for transfers between devices, sibling(): return lax.ppermute(x, 'leaf', [(i, i ^ size // 2) for i in range(size)])  8.98 us
    pallas_call x1, Pallas kernels, two_shards(): kernel(first_body, (f(n, n), f(top, top), f(8, TILE)), [vmem] * 5 + [smem...  8.2 us
    ppermute x4, starting transfers between devices, sibling(): return lax.ppermute(x, 'leaf', [(i, i ^ size // 2) for i in range(size)])  7.7 us
    pallas_call x1, Pallas kernels, two_shards(): kernel(functools.partial(middle_body, tiles - 2), (f(n, n), f(n, width)),...  4.53 us
    pallas_call x1, Pallas kernels, two_shards(): kernel(functools.partial(last_body, tiles - 1), f(n, width), [vmem] * 2,...  3.52 us
    pallas_call x1, Pallas kernels, two_shards(): kernel(functools.partial(output_body, half), (f(half, width), f(half, wid...  3.22 us
    ppermute x7, waiting for transfers between devices, across(): return lax.ppermute(x, 'sib', [(0, 1), (1, 0)])  1.57 us
  transfers between devices with their start and end apart: 11, of which 5 were waited for; matrix products, arithmetic and copies ran while one was open for 0% of the time, Pallas kernels for 42%

profile of v14, /device:TPU:0, one launch (start us, length us, event | category | flops | bytes accessed | tf_op | source)
XLA Modules:
  0.0 52.1 jit_solution(499401801021935397)
XLA Ops:
  0.6 1.2 %copy-done = f32[1,256,1024]{2,1,0:T(8,128)S(1)} copy-done((f32[1,256,1024]{2,1,0:T(8,128)S(1)}, f32[1,256,1024]{2,1,0:T(8,128)}, u32[]{:S(2)}) %copy-start) | copy-done | bytes 1048600
  1.9 4.1 %collective-permute-start.1 = (f32[320,128]{1,0:T(8,128)S(1)}, f32[320,128]{1,0:T(8,128)S(1)}, u32[]{:S(2)}, u32[]{:S(2)}) collective-permute-start(f32[320,128]{1,0:T(8,128)S(1)} %shard_map.58), channel_id=1, source_target_pairs={{0,8},{1,9},{2,10},{3,11},{4,12},{5,13},{6,14},{7,15},{8,0},{9,1},... | collective-permute-start | bytes 491528 | tf_op jit(solution)/shard_map/ppermute | solution.py:409
  6.0 0.2 shard_map.59
  6.2 1.6 %collective-permute-start.3 = (f32[256,256]{1,0:T(8,128)S(1)}, f32[256,256]{1,0:T(8,128)S(1)}, u32[]{:S(2)}, u32[]{:S(2)}) collective-permute-start(f32[256,256]{1,0:T(8,128)S(1)} %get-tuple-element.33), channel_id=1, source_target_pairs={{0,16},{16,0},{1,17},{17,1},{2,18},{18,2},{3,19},{19,3},{4,20},{20... | collective-permute-start | bytes 786440 | tf_op jit(solution)/shard_map/ppermute | solution.py:413
  7.8 0.6 %collective-permute-start.2 = (f32[264,128]{1,0:T(8,128)S(1)}, f32[264,128]{1,0:T(8,128)S(1)}, u32[]{:S(2)}, u32[]{:S(2)}) collective-permute-start(f32[264,128]{1,0:T(8,128)S(1)} %get-tuple-element.29), channel_id=1, source_target_pairs={{0,8},{1,9},{2,10},{3,11},{4,12},{5,13},{6,14},{7,15},{8,0},{9,1},... | collective-permute-start | bytes 405512 | tf_op jit(solution)/shard_map/ppermute | solution.py:409
  8.3 0.5 %collective-permute-start = (f32[320,128]{1,0:T(8,128)S(1)}, f32[320,128]{1,0:T(8,128)S(1)}, u32[]{:S(2)}, u32[]{:S(2)}) collective-permute-start(f32[320,128]{1,0:T(8,128)S(1)} %shard_map.58), channel_id=1, source_target_pairs={{0,16},{16,0},{1,17},{17,1},{2,18},{18,2},{3,19},{19,3},{4,20},{20... | collective-permute-start | bytes 491528 | tf_op jit(solution)/shard_map/ppermute | solution.py:413
  8.8 8.6 %collective-permute-done.1.near_ref = f32[320,128]{1,0:T(8,128)S(1)} collective-permute-done((f32[320,128]{1,0:T(8,128)S(1)}, f32[320,128]{1,0:T(8,128)S(1)}, u32[]{:S(2)}, u32[]{:S(2)}) %collective-permute-start.1) | collective-permute-done | bytes 163872 | tf_op jit(solution)/shard_map/ppermute | solution.py:409
  17.4 1.8 %collective-permute-start.4 = (f32[320,128]{1,0:T(8,128)S(1)}, f32[320,128]{1,0:T(8,128)S(1)}, u32[]{:S(2)}, u32[]{:S(2)}) collective-permute-start(f32[320,128]{1,0:T(8,128)S(1)} %collective-permute-done.1.near_ref), channel_id=1, source_target_pairs={{0,16},{16,0},{1,17},{17,1},{2,18},{18,2},{3,19},{19,3},{4,20},{20... | collective-permute-start | bytes 491528 | tf_op jit(solution)/shard_map/ppermute | solution.py:413
  19.3 0.2 collective-permute-done.2.side_ref
  19.5 1.5 %collective-permute-start.5 = (f32[264,128]{1,0:T(8,128)S(1)}, f32[264,128]{1,0:T(8,128)S(1)}, u32[]{:S(2)}, u32[]{:S(2)}) collective-permute-start(f32[264,128]{1,0:T(8,128)S(1)} %collective-permute-done.2.side_ref), channel_id=1, source_target_pairs={{0,16},{16,0},{1,17},{17,1},{2,18},{18,2},{3,19},{19,3},{4,20},{20... | collective-permute-start | bytes 405512 | tf_op jit(solution)/shard_map/ppermute | solution.py:413
  21.2 0.5 %shard_map.61 = (f32[512,512]{1,0:T(8,128)S(1)}, f32[512,512]{1,0:T(8,128)S(1)}, bf16[512,512]{1,0:T(8,128)(2,1)S(1)}, f32[256,256]{1,0:T(8,128)S(1)}) custom-call(f32[256,1024]{1,0:T(8,128)S(1)} %bitcast.9, f32[320,128]{1,0:T(8,128)S(1)} %collective-permute-done.early_ref, f32[320,128]{1,0:T(8,128)S(1)} %collective-permute-done.1.near_ref, ...), custom_call_target="tpu_custom_call" | custom-call | flops 100000000 | bytes 1048576 | tf_op jit(solution)/shard_map/pallas_call | solution.py:452
  21.7 3.0 %collective-permute-start.8 = (f32[512,128]{1,0:T(8,128)S(1)}, f32[512,128]{1,0:T(8,128)S(1)}, u32[]{:S(2)}, u32[]{:S(2)}) collective-permute-start(f32[512,128]{1,0:T(8,128)S(1)} %get-tuple-element.49), channel_id=1, source_target_pairs={{0,8},{1,9},{2,10},{3,11},{4,12},{5,13},{6,14},{7,15},{8,0},{9,1},... | collective-permute-start | bytes 786440 | tf_op jit(solution)/shard_map/ppermute | solution.py:409
  24.7 0.5 %collective-permute-start.6 = (f32[256,256]{1,0:T(8,128)S(1)}, f32[256,256]{1,0:T(8,128)S(1)}, u32[]{:S(2)}, u32[]{:S(2)}) collective-permute-start(f32[256,256]{1,0:T(8,128)S(1)} %get-tuple-element.43), channel_id=1, source_target_pairs={{0,16},{16,0},{1,17},{17,1},{2,18},{18,2},{3,19},{19,3},{4,20},{20... | collective-permute-start | bytes 786440 | tf_op jit(solution)/shard_map/ppermute | solution.py:413
  25.2 0.6 %collective-permute-done.5.side_ref = f32[264,128]{1,0:T(8,128)S(1)} collective-permute-done((f32[264,128]{1,0:T(8,128)S(1)}, f32[264,128]{1,0:T(8,128)S(1)}, u32[]{:S(2)}, u32[]{:S(2)}) %collective-permute-start.5) | collective-permute-done | bytes 135200 | tf_op jit(solution)/shard_map/ppermute | solution.py:413
  25.8 8.2 %shard_map.62 = (f32[512,512]{1,0:T(8,128)S(1)}, f32[256,256]{1,0:T(8,128)S(1)}, f32[8,128]{1,0:T(8,128)S(1)}) custom-call(f32[512,512]{1,0:T(8,128)S(1)} %get-tuple-element.37.a_in, f32[512,512]{1,0:T(8,128)S(1)} %get-tuple-element.38.m_in, bf16[512,512]{1,0:T(8,128)(2,1)S(1)} %get-tuple-element.40.p_ref, f32[320,128]{1,0:T(8,128)S(1)} %collective-permute-done.4.far_ref, ...), custom_call_target="tpu_custom_call" | custom-call | flops 10000000000 | bytes 1048576 | tf_op jit(solution)/shard_map/pallas_call | solution.py:462
  34.0 4.5 %shard_map.63 = (f32[512,512]{1,0:T(8,128)S(1)}, f32[512,512]{1,0:T(8,128)S(1)}) custom-call(f32[512,512]{1,0:T(8,128)S(1)} %get-tuple-element.41.a_ref, f32[256,256]{1,0:T(8,128)S(1)} %get-tuple-element.42.b_ref, f32[256,1024]{1,0:T(8,128)S(1)} %bitcast.10, f32[256,256]{1,0:T(8,128)S(1)} %collective-permute-done.3.mine_ref, ...), custom_call_target="tpu_custom_call" | custom-call | flops 5000000000 | bytes 1048576 | tf_op jit(solution)/shard_map/pallas_call | solution.py:469
  38.6 3.5 %shard_map.64.g_ref = f32[512,512]{1,0:T(8,128)S(1)} custom-call(f32[512,512]{1,0:T(8,128)S(1)} %get-tuple-element.45.a_ref, f32[512,512]{1,0:T(8,128)S(1)} %get-tuple-element.46.g_ref), custom_call_target="tpu_custom_call" | custom-call | flops 5000000000 | bytes 1048576 | tf_op jit(solution)/shard_map/pallas_call | solution.py:472
  42.3 1.3 %shard_map.66 = (f32[512,256]{1,0:T(8,128)S(1)}, f32[256,128]{1,0:T(8,128)S(1)}) custom-call(f32[512,512]{1,0:T(8,128)S(1)} %shard_map.64.g_ref, bf16[512,512]{1,0:T(8,128)(2,1)S(1)} %get-tuple-element.40.p_ref, f32[512,128]{1,0:T(8,128)S(1)} %collective-permute-done.7.chunk_a.chunk_ref, s32[1]{0:T(128)} %bitcast.1.first_ref), custom_call_target="tpu_custom_call" | custom-call | flops 1000000000 | bytes 1048576 | tf_op jit(solution)/shard_map/pallas_call | solution.py:473
  43.6 2.3 %collective-permute-start.9 = (f32[256,128]{1,0:T(8,128)S(1)}, f32[256,128]{1,0:T(8,128)S(1)}, u32[]{:S(2)}, u32[]{:S(2)}) collective-permute-start(f32[256,128]{1,0:T(8,128)S(1)} %get-tuple-element.52), channel_id=1, source_target_pairs={{0,16},{16,0},{1,17},{17,1},{2,18},{18,2},{3,19},{19,3},{4,20},{20... | collective-permute-start | bytes 393224 | tf_op jit(solution)/shard_map/ppermute | solution.py:413
  45.8 0.4 shard_map.67
  46.3 0.8 %collective-permute-start.10 = (f32[256,128]{1,0:T(8,128)S(1)}, f32[256,128]{1,0:T(8,128)S(1)}, u32[]{:S(2)}, u32[]{:S(2)}) collective-permute-start(f32[256,128]{1,0:T(8,128)S(1)} %shard_map.67), channel_id=1, source_target_pairs={{0,16},{16,0},{1,17},{17,1},{2,18},{18,2},{3,19},{19,3},{4,20},{20... | collective-permute-start | bytes 393224 | tf_op jit(solution)/shard_map/ppermute | solution.py:413
  47.1 3.2 %shard_map.65 = (f32[256,512]{1,0:T(8,128)}, f32[256,512]{1,0:T(8,128)}, f32[256,256]{1,0:T(8,128)S(1)}) custom-call(f32[512,512]{1,0:T(8,128)S(1)} %shard_map.64.g_ref, bf16[512,512]{1,0:T(8,128)(2,1)S(1)} %get-tuple-element.40.p_ref, f32[256,1024]{1,0:T(8,128)S(1)} %bitcast.11, f32[256,256]{1,0:T(8,128)S(1)} %collective-permute-done.3.mine_ref, ...), custom_call_target="tpu_custom_call" | custom-call | flops 1000000 | bytes 1048576 | tf_op jit(solution)/shard_map/pallas_call | solution.py:478
  50.3 1.0 %collective-permute-done.10.second_part = f32[256,128]{1,0:T(8,128)S(1)} collective-permute-done((f32[256,128]{1,0:T(8,128)S(1)}, f32[256,128]{1,0:T(8,128)S(1)}, u32[]{:S(2)}, u32[]{:S(2)}) %collective-permute-start.10) | collective-permute-done | bytes 131104 | tf_op jit(solution)/shard_map/ppermute | solution.py:413
  51.3 0.8 %shard_map.68 = f32[256,512]{1,0:T(8,128)} custom-call(f32[256,256]{1,0:T(8,128)S(1)} %get-tuple-element.51.keep_ref, f32[256,128]{1,0:T(8,128)S(1)} %collective-permute-done.9.first_part, f32[256,128]{1,0:T(8,128)S(1)} %collective-permute-done.10.second_part, s32[1]{0:T(128)} %bitcast.1.first_ref), custom_call_target="tpu_custom_call" | custom-call | flops 100000000 | bytes 1048576 | tf_op jit(solution)/shard_map/pallas_call | solution.py:485
  (17 shorter events, 0.3 us)
Async XLA Ops:
  0.6 1.2 %copy-start = (f32[1,256,1024]{2,1,0:T(8,128)S(1)}, f32[1,256,1024]{2,1,0:T(8,128)}, u32[]{:S(2)}) copy-start(f32[1,256,1024]{2,1,0:T(8,128)} %param.3) | copy-start | bytes 3145732
  1.9 4.1 %copy-start.3 = (s32[1,512]{1,0:T(1,128)S(1)}, s32[1,512]{1,0:T(1,128)}, u32[]{:S(2)}) copy-start(s32[1,512]{1,0:T(1,128)} %map_ref.1) | copy-start | bytes 6148
  1.9 15.5 %collective-permute-start.1 = (f32[320,128]{1,0:T(8,128)S(1)}, f32[320,128]{1,0:T(8,128)S(1)}, u32[]{:S(2)}, u32[]{:S(2)}) collective-permute-start(f32[320,128]{1,0:T(8,128)S(1)} %shard_map.58), channel_id=1, source_target_pairs={{0,8},{1,9},{2,10},{3,11},{4,12},{5,13},{6,14},{7,15},{8,0},{9,1},... | collective-permute-start | bytes 491528 | tf_op jit(solution)/shard_map/ppermute | solution.py:409
  6.2 14.9 %collective-permute-start.3 = (f32[256,256]{1,0:T(8,128)S(1)}, f32[256,256]{1,0:T(8,128)S(1)}, u32[]{:S(2)}, u32[]{:S(2)}) collective-permute-start(f32[256,256]{1,0:T(8,128)S(1)} %get-tuple-element.33), channel_id=1, source_target_pairs={{0,16},{16,0},{1,17},{17,1},{2,18},{18,2},{3,19},{19,3},{4,20},{20... | collective-permute-start | bytes 786440 | tf_op jit(solution)/shard_map/ppermute | solution.py:413
  7.8 11.7 %collective-permute-start.2 = (f32[264,128]{1,0:T(8,128)S(1)}, f32[264,128]{1,0:T(8,128)S(1)}, u32[]{:S(2)}, u32[]{:S(2)}) collective-permute-start(f32[264,128]{1,0:T(8,128)S(1)} %get-tuple-element.29), channel_id=1, source_target_pairs={{0,8},{1,9},{2,10},{3,11},{4,12},{5,13},{6,14},{7,15},{8,0},{9,1},... | collective-permute-start | bytes 405512 | tf_op jit(solution)/shard_map/ppermute | solution.py:409
  8.3 12.9 %collective-permute-start = (f32[320,128]{1,0:T(8,128)S(1)}, f32[320,128]{1,0:T(8,128)S(1)}, u32[]{:S(2)}, u32[]{:S(2)}) collective-permute-start(f32[320,128]{1,0:T(8,128)S(1)} %shard_map.58), channel_id=1, source_target_pairs={{0,16},{16,0},{1,17},{17,1},{2,18},{18,2},{3,19},{19,3},{4,20},{20... | collective-permute-start | bytes 491528 | tf_op jit(solution)/shard_map/ppermute | solution.py:413
  17.4 8.4 %collective-permute-start.4 = (f32[320,128]{1,0:T(8,128)S(1)}, f32[320,128]{1,0:T(8,128)S(1)}, u32[]{:S(2)}, u32[]{:S(2)}) collective-permute-start(f32[320,128]{1,0:T(8,128)S(1)} %collective-permute-done.1.near_ref), channel_id=1, source_target_pairs={{0,16},{16,0},{1,17},{17,1},{2,18},{18,2},{3,19},{19,3},{4,20},{20... | collective-permute-start | bytes 491528 | tf_op jit(solution)/shard_map/ppermute | solution.py:413
  19.5 6.3 %collective-permute-start.5 = (f32[264,128]{1,0:T(8,128)S(1)}, f32[264,128]{1,0:T(8,128)S(1)}, u32[]{:S(2)}, u32[]{:S(2)}) collective-permute-start(f32[264,128]{1,0:T(8,128)S(1)} %collective-permute-done.2.side_ref), channel_id=1, source_target_pairs={{0,16},{16,0},{1,17},{17,1},{2,18},{18,2},{3,19},{19,3},{4,20},{20... | collective-permute-start | bytes 405512 | tf_op jit(solution)/shard_map/ppermute | solution.py:413
  21.1 21.2 %collective-permute-start.7 = (f32[512,128]{1,0:T(8,128)S(1)}, f32[512,128]{1,0:T(8,128)S(1)}, u32[]{:S(2)}, u32[]{:S(2)}) collective-permute-start(f32[512,128]{1,0:T(8,128)S(1)} %get-tuple-element.48), channel_id=1, source_target_pairs={{0,8},{1,9},{2,10},{3,11},{4,12},{5,13},{6,14},{7,15},{8,0},{9,1},... | collective-permute-start | bytes 786440 | tf_op jit(solution)/shard_map/ppermute | solution.py:409
  21.7 24.1 %collective-permute-start.8 = (f32[512,128]{1,0:T(8,128)S(1)}, f32[512,128]{1,0:T(8,128)S(1)}, u32[]{:S(2)}, u32[]{:S(2)}) collective-permute-start(f32[512,128]{1,0:T(8,128)S(1)} %get-tuple-element.49), channel_id=1, source_target_pairs={{0,8},{1,9},{2,10},{3,11},{4,12},{5,13},{6,14},{7,15},{8,0},{9,1},... | collective-permute-start | bytes 786440 | tf_op jit(solution)/shard_map/ppermute | solution.py:409
  24.7 9.3 %collective-permute-start.6 = (f32[256,256]{1,0:T(8,128)S(1)}, f32[256,256]{1,0:T(8,128)S(1)}, u32[]{:S(2)}, u32[]{:S(2)}) collective-permute-start(f32[256,256]{1,0:T(8,128)S(1)} %get-tuple-element.43), channel_id=1, source_target_pairs={{0,16},{16,0},{1,17},{17,1},{2,18},{18,2},{3,19},{19,3},{4,20},{20... | collective-permute-start | bytes 786440 | tf_op jit(solution)/shard_map/ppermute | solution.py:413
  25.8 8.2 %copy-start.1 = (f32[1,256,1024]{2,1,0:T(8,128)S(1)}, f32[1,256,1024]{2,1,0:T(8,128)}, u32[]{:S(2)}) copy-start(f32[1,256,1024]{2,1,0:T(8,128)} %param.3) | copy-start | bytes 3145732
  43.6 6.8 %collective-permute-start.9 = (f32[256,128]{1,0:T(8,128)S(1)}, f32[256,128]{1,0:T(8,128)S(1)}, u32[]{:S(2)}, u32[]{:S(2)}) collective-permute-start(f32[256,128]{1,0:T(8,128)S(1)} %get-tuple-element.52), channel_id=1, source_target_pairs={{0,16},{16,0},{1,17},{17,1},{2,18},{18,2},{3,19},{19,3},{4,20},{20... | collective-permute-start | bytes 393224 | tf_op jit(solution)/shard_map/ppermute | solution.py:413
  45.8 1.3 %copy-start.2 = (f32[1,256,512]{2,1,0:T(8,128)S(1)}, f32[1,256,512]{2,1,0:T(8,128)}, u32[]{:S(2)}) copy-start(f32[1,256,512]{2,1,0:T(8,128)} %param.4) | copy-start | bytes 1572868
  46.3 5.0 %collective-permute-start.10 = (f32[256,128]{1,0:T(8,128)S(1)}, f32[256,128]{1,0:T(8,128)S(1)}, u32[]{:S(2)}, u32[]{:S(2)}) collective-permute-start(f32[256,128]{1,0:T(8,128)S(1)} %shard_map.67), channel_id=1, source_target_pairs={{0,16},{16,0},{1,17},{17,1},{2,18},{18,2},{3,19},{19,3},{4,20},{20... | collective-permute-start | bytes 393224 | tf_op jit(solution)/shard_map/ppermute | solution.py:413

commit v15 on v13

--- a/solution.py
+++ b/solution.py
@@ -298,11 +298,13 @@
     return [pl.ds(pl.multiple_of(x * half, half), half) for x in (mine, 1 - mine)]
 
 
-def last_body(k, a_ref, g_ref, g_out):
+def last_body(k, half, a_ref, g_ref, p_ref, first_ref, g_out, h_out):
     own, before = slice(k * TILE, (k + 1) * TILE), slice(0, k * TILE)
     right = full(invert_tile(a_ref[own, own]), g_ref[own, :])
     g_out[own, :] = right
     g_out[before, :] = g_ref[before, :] - full(a_ref[before, own], right)
+    _, there = column_blocks(half, first_ref[0])
+    h_out[...] = pick_left(p_ref[...], g_out[:, there], ((0,), (0,)))
 
 
 def send_body(half, g_ref, p_ref, chunk_ref, first_ref, h_out, send_out):
@@ -444,11 +446,10 @@
     a, g = kernel(
         functools.partial(middle_body, tiles - 2), (f(n, n), f(n, width)), [vmem] * 6 + [smem], (), 5e9
     )(a, b, t_int, outer_mine, outer_others, scale, first)
-    g = kernel(functools.partial(last_body, tiles - 1), f(n, width), [vmem] * 2, (), 5e9)(a, g)
-    h, send = kernel(
-        functools.partial(send_body, half), (f(n, half), f(half, q)), [vmem] * 3 + [smem], (), 1e9
-    )(g, onehot, near_r[0], first)
-    cross_a = across(send)
+    g, h = kernel(
+        functools.partial(last_body, tiles - 1, half), (f(n, width), f(n, half)), [vmem] * 3 + [smem], (), 5e9
+    )(a, g, onehot, first)
+    cross_a = across(kernel(send_more_body, f(half, q), [vmem] * 2, (), 1e9)(h, near_r[0]))
     cross_b = across(kernel(send_more_body, f(half, q), [vmem] * 2, (), 5e9)(h, near_r[1]))
     own_map, solution_op, keep = kernel(
         functools.partial(output_body, half),

time: 52.3 us -> 52.3 us (level)
  transfers between devices with their start and end apart: 11 -> 11, of which waited for: 5 -> 5; matrix products, arithmetic and copies ran while one was open for 0% -> 0% of each run, Pallas kernels for 42% -> 41%
where the time goes in v15:
time: 52.3 us; the launch traced here: 52.1 us
  Pallas kernels  22.5 us (43%)
  starting transfers between devices  17 us (33%)
  waiting for transfers between devices  10.7 us (20%)
  local copies, waits for them, and re-layouts  1.23 us (2%)
  between operations  0.75 us (1%)
    ppermute x7, starting transfers between devices, across(): return lax.ppermute(x, 'sib', [(0, 1), (1, 0)])  9.3 us
    ppermute x4, waiting for transfers between devices, sibling(): return lax.ppermute(x, 'leaf', [(i, i ^ size // 2) for i in range(size)])  9.1 us
    pallas_call x1, Pallas kernels, two_shards(): kernel(functools.partial(first_body, range(tiles - 2)), (f(n, n), f(top,...  8.15 us
    ppermute x4, starting transfers between devices, sibling(): return lax.ppermute(x, 'leaf', [(i, i ^ size // 2) for i in range(size)])  7.7 us
    pallas_call x1, Pallas kernels, two_shards(): kernel(functools.partial(middle_body, tiles - 2), (f(n, n), f(n, width)),...  4.51 us
    pallas_call x1, Pallas kernels, two_shards(): kernel(functools.partial(last_body, tiles - 1, half), (f(n, width), f(n,...  4.16 us
    pallas_call x1, Pallas kernels, two_shards(): kernel(functools.partial(output_body, half), (f(half, width), f(half, wid...  3.22 us
    ppermute x7, waiting for transfers between devices, across(): return lax.ppermute(x, 'sib', [(0, 1), (1, 0)])  1.56 us
  transfers between devices with their start and end apart: 11, of which 5 were waited for; matrix products, arithmetic and copies ran while one was open for 0% of the time, Pallas kernels for 41%

profile of v15, /device:TPU:0, one launch (start us, length us, event | category | flops | bytes accessed | tf_op | source)
XLA Modules:
  0.0 52.1 jit_solution(381994641196363108)
XLA Ops:
  0.6 1.2 %copy-done = f32[1,256,1024]{2,1,0:T(8,128)S(1)} copy-done((f32[1,256,1024]{2,1,0:T(8,128)S(1)}, f32[1,256,1024]{2,1,0:T(8,128)}, u32[]{:S(2)}) %copy-start) | copy-done | bytes 1048600
  1.9 4.1 %collective-permute-start.1 = (f32[320,128]{1,0:T(8,128)S(1)}, f32[320,128]{1,0:T(8,128)S(1)}, u32[]{:S(2)}, u32[]{:S(2)}) collective-permute-start(f32[320,128]{1,0:T(8,128)S(1)} %shard_map.58), channel_id=1, source_target_pairs={{0,8},{1,9},{2,10},{3,11},{4,12},{5,13},{6,14},{7,15},{8,0},{9,1},... | collective-permute-start | bytes 491528 | tf_op jit(solution)/shard_map/ppermute | solution.py:386
  6.2 1.6 %collective-permute-start.3 = (f32[256,256]{1,0:T(8,128)S(1)}, f32[256,256]{1,0:T(8,128)S(1)}, u32[]{:S(2)}, u32[]{:S(2)}) collective-permute-start(f32[256,256]{1,0:T(8,128)S(1)} %get-tuple-element.33), channel_id=1, source_target_pairs={{0,16},{16,0},{1,17},{17,1},{2,18},{18,2},{3,19},{19,3},{4,20},{20... | collective-permute-start | bytes 786440 | tf_op jit(solution)/shard_map/ppermute | solution.py:390
  7.8 0.6 %collective-permute-start.2 = (f32[264,128]{1,0:T(8,128)S(1)}, f32[264,128]{1,0:T(8,128)S(1)}, u32[]{:S(2)}, u32[]{:S(2)}) collective-permute-start(f32[264,128]{1,0:T(8,128)S(1)} %get-tuple-element.29), channel_id=1, source_target_pairs={{0,8},{1,9},{2,10},{3,11},{4,12},{5,13},{6,14},{7,15},{8,0},{9,1},... | collective-permute-start | bytes 405512 | tf_op jit(solution)/shard_map/ppermute | solution.py:386
  8.3 0.5 %collective-permute-start = (f32[320,128]{1,0:T(8,128)S(1)}, f32[320,128]{1,0:T(8,128)S(1)}, u32[]{:S(2)}, u32[]{:S(2)}) collective-permute-start(f32[320,128]{1,0:T(8,128)S(1)} %shard_map.58), channel_id=1, source_target_pairs={{0,16},{16,0},{1,17},{17,1},{2,18},{18,2},{3,19},{19,3},{4,20},{20... | collective-permute-start | bytes 491528 | tf_op jit(solution)/shard_map/ppermute | solution.py:390
  8.8 8.6 %collective-permute-done.1.near_ref = f32[320,128]{1,0:T(8,128)S(1)} collective-permute-done((f32[320,128]{1,0:T(8,128)S(1)}, f32[320,128]{1,0:T(8,128)S(1)}, u32[]{:S(2)}, u32[]{:S(2)}) %collective-permute-start.1) | collective-permute-done | bytes 163872 | tf_op jit(solution)/shard_map/ppermute | solution.py:386
  17.4 1.8 %collective-permute-start.4 = (f32[320,128]{1,0:T(8,128)S(1)}, f32[320,128]{1,0:T(8,128)S(1)}, u32[]{:S(2)}, u32[]{:S(2)}) collective-permute-start(f32[320,128]{1,0:T(8,128)S(1)} %collective-permute-done.1.near_ref), channel_id=1, source_target_pairs={{0,16},{16,0},{1,17},{17,1},{2,18},{18,2},{3,19},{19,3},{4,20},{20... | collective-permute-start | bytes 491528 | tf_op jit(solution)/shard_map/ppermute | solution.py:390
  19.3 0.2 collective-permute-done.2.side_ref
  19.5 1.5 %collective-permute-start.5 = (f32[264,128]{1,0:T(8,128)S(1)}, f32[264,128]{1,0:T(8,128)S(1)}, u32[]{:S(2)}, u32[]{:S(2)}) collective-permute-start(f32[264,128]{1,0:T(8,128)S(1)} %collective-permute-done.2.side_ref), channel_id=1, source_target_pairs={{0,16},{16,0},{1,17},{17,1},{2,18},{18,2},{3,19},{19,3},{4,20},{20... | collective-permute-start | bytes 405512 | tf_op jit(solution)/shard_map/ppermute | solution.py:390
  21.2 0.5 %shard_map.61 = (f32[512,512]{1,0:T(8,128)S(1)}, f32[512,512]{1,0:T(8,128)S(1)}, bf16[512,512]{1,0:T(8,128)(2,1)S(1)}, f32[256,256]{1,0:T(8,128)S(1)}) custom-call(f32[256,1024]{1,0:T(8,128)S(1)} %bitcast.9, f32[320,128]{1,0:T(8,128)S(1)} %collective-permute-done.early_ref, f32[320,128]{1,0:T(8,128)S(1)} %collective-permute-done.1.near_ref, ...), custom_call_target="tpu_custom_call" | custom-call | flops 100000000 | bytes 1048576 | tf_op jit(solution)/shard_map/pallas_call | solution.py:429
  21.7 3.0 %collective-permute-start.8 = (f32[512,128]{1,0:T(8,128)S(1)}, f32[512,128]{1,0:T(8,128)S(1)}, u32[]{:S(2)}, u32[]{:S(2)}) collective-permute-start(f32[512,128]{1,0:T(8,128)S(1)} %get-tuple-element.50), channel_id=1, source_target_pairs={{0,8},{1,9},{2,10},{3,11},{4,12},{5,13},{6,14},{7,15},{8,0},{9,1},... | collective-permute-start | bytes 786440 | tf_op jit(solution)/shard_map/ppermute | solution.py:386
  24.7 0.5 %collective-permute-start.6 = (f32[256,256]{1,0:T(8,128)S(1)}, f32[256,256]{1,0:T(8,128)S(1)}, u32[]{:S(2)}, u32[]{:S(2)}) collective-permute-start(f32[256,256]{1,0:T(8,128)S(1)} %get-tuple-element.43), channel_id=1, source_target_pairs={{0,16},{16,0},{1,17},{17,1},{2,18},{18,2},{3,19},{19,3},{4,20},{20... | collective-permute-start | bytes 786440 | tf_op jit(solution)/shard_map/ppermute | solution.py:390
  25.2 0.6 %collective-permute-done.5.side_ref = f32[264,128]{1,0:T(8,128)S(1)} collective-permute-done((f32[264,128]{1,0:T(8,128)S(1)}, f32[264,128]{1,0:T(8,128)S(1)}, u32[]{:S(2)}, u32[]{:S(2)}) %collective-permute-start.5) | collective-permute-done | bytes 135200 | tf_op jit(solution)/shard_map/ppermute | solution.py:390
  25.8 8.2 %shard_map.62 = (f32[512,512]{1,0:T(8,128)S(1)}, f32[256,256]{1,0:T(8,128)S(1)}, f32[8,128]{1,0:T(8,128)S(1)}) custom-call(f32[512,512]{1,0:T(8,128)S(1)} %get-tuple-element.37.a_in, f32[512,512]{1,0:T(8,128)S(1)} %get-tuple-element.38.m_in, bf16[512,512]{1,0:T(8,128)(2,1)S(1)} %get-tuple-element.40.p_ref, f32[320,128]{1,0:T(8,128)S(1)} %collective-permute-done.4.far_ref, ...), custom_call_target="tpu_custom_call" | custom-call | flops 10000000000 | bytes 1048576 | tf_op jit(solution)/shard_map/pallas_call | solution.py:439
  34.0 4.5 %shard_map.63 = (f32[512,512]{1,0:T(8,128)S(1)}, f32[512,512]{1,0:T(8,128)S(1)}) custom-call(f32[512,512]{1,0:T(8,128)S(1)} %get-tuple-element.41.a_ref, f32[256,256]{1,0:T(8,128)S(1)} %get-tuple-element.42.b_ref, f32[256,1024]{1,0:T(8,128)S(1)} %bitcast.10, f32[256,256]{1,0:T(8,128)S(1)} %collective-permute-done.3.mine_ref, ...), custom_call_target="tpu_custom_call" | custom-call | flops 5000000000 | bytes 1048576 | tf_op jit(solution)/shard_map/pallas_call | solution.py:446
  38.5 4.2 %shard_map.64 = (f32[512,512]{1,0:T(8,128)S(1)}, f32[512,256]{1,0:T(8,128)S(1)}) custom-call(f32[512,512]{1,0:T(8,128)S(1)} %get-tuple-element.45.a_ref, f32[512,512]{1,0:T(8,128)S(1)} %get-tuple-element.46.g_ref, bf16[512,512]{1,0:T(8,128)(2,1)S(1)} %get-tuple-element.40.p_ref, s32[1]{0:T(128)} %bitcast.1.first_ref), custom_call_target="tpu_custom_call" | custom-call | flops 5000000000 | bytes 1048576 | tf_op jit(solution)/shard_map/pallas_call | solution.py:449
  42.7 0.4 shard_map.66
  43.1 2.4 %collective-permute-start.9 = (f32[256,128]{1,0:T(8,128)S(1)}, f32[256,128]{1,0:T(8,128)S(1)}, u32[]{:S(2)}, u32[]{:S(2)}) collective-permute-start(f32[256,128]{1,0:T(8,128)S(1)} %shard_map.66), channel_id=1, source_target_pairs={{0,16},{16,0},{1,17},{17,1},{2,18},{18,2},{3,19},{19,3},{4,20},{20... | collective-permute-start | bytes 393224 | tf_op jit(solution)/shard_map/ppermute | solution.py:390
  45.6 0.3 collective-permute-done.8.chunk_b.chunk_ref
  45.8 0.4 shard_map.67
  46.3 0.8 %collective-permute-start.10 = (f32[256,128]{1,0:T(8,128)S(1)}, f32[256,128]{1,0:T(8,128)S(1)}, u32[]{:S(2)}, u32[]{:S(2)}) collective-permute-start(f32[256,128]{1,0:T(8,128)S(1)} %shard_map.67), channel_id=1, source_target_pairs={{0,16},{16,0},{1,17},{17,1},{2,18},{18,2},{3,19},{19,3},{4,20},{20... | collective-permute-start | bytes 393224 | tf_op jit(solution)/shard_map/ppermute | solution.py:390
  47.1 3.2 %shard_map.65 = (f32[256,512]{1,0:T(8,128)}, f32[256,512]{1,0:T(8,128)}, f32[256,256]{1,0:T(8,128)S(1)}) custom-call(f32[512,512]{1,0:T(8,128)S(1)} %get-tuple-element.47.g_ref, bf16[512,512]{1,0:T(8,128)(2,1)S(1)} %get-tuple-element.40.p_ref, f32[256,1024]{1,0:T(8,128)S(1)} %bitcast.11, f32[256,256]{1,0:T(8,128)S(1)} %collective-permute-done.3.mine_ref, ...), custom_call_target="tpu_custom_call" | custom-call | flops 1000000 | bytes 1048576 | tf_op jit(solution)/shard_map/pallas_call | solution.py:454
  50.3 1.0 %collective-permute-done.10.second_part = f32[256,128]{1,0:T(8,128)S(1)} collective-permute-done((f32[256,128]{1,0:T(8,128)S(1)}, f32[256,128]{1,0:T(8,128)S(1)}, u32[]{:S(2)}, u32[]{:S(2)}) %collective-permute-start.10) | collective-permute-done | bytes 131104 | tf_op jit(solution)/shard_map/ppermute | solution.py:390
  51.3 0.8 %shard_map.68 = f32[256,512]{1,0:T(8,128)} custom-call(f32[256,256]{1,0:T(8,128)S(1)} %get-tuple-element.52.keep_ref, f32[256,128]{1,0:T(8,128)S(1)} %collective-permute-done.9.first_part, f32[256,128]{1,0:T(8,128)S(1)} %collective-permute-done.10.second_part, s32[1]{0:T(128)} %bitcast.1.first_ref), custom_call_target="tpu_custom_call" | custom-call | flops 100000000 | bytes 1048576 | tf_op jit(solution)/shard_map/pallas_call | solution.py:461
  (17 shorter events, 0.4 us)
Async XLA Ops:
  0.6 1.2 %copy-start = (f32[1,256,1024]{2,1,0:T(8,128)S(1)}, f32[1,256,1024]{2,1,0:T(8,128)}, u32[]{:S(2)}) copy-start(f32[1,256,1024]{2,1,0:T(8,128)} %param.3) | copy-start | bytes 3145732
  1.9 4.1 %copy-start.3 = (s32[1,512]{1,0:T(1,128)S(1)}, s32[1,512]{1,0:T(1,128)}, u32[]{:S(2)}) copy-start(s32[1,512]{1,0:T(1,128)} %map_ref.1) | copy-start | bytes 6148
  1.9 15.5 %collective-permute-start.1 = (f32[320,128]{1,0:T(8,128)S(1)}, f32[320,128]{1,0:T(8,128)S(1)}, u32[]{:S(2)}, u32[]{:S(2)}) collective-permute-start(f32[320,128]{1,0:T(8,128)S(1)} %shard_map.58), channel_id=1, source_target_pairs={{0,8},{1,9},{2,10},{3,11},{4,12},{5,13},{6,14},{7,15},{8,0},{9,1},... | collective-permute-start | bytes 491528 | tf_op jit(solution)/shard_map/ppermute | solution.py:386
  6.2 14.9 %collective-permute-start.3 = (f32[256,256]{1,0:T(8,128)S(1)}, f32[256,256]{1,0:T(8,128)S(1)}, u32[]{:S(2)}, u32[]{:S(2)}) collective-permute-start(f32[256,256]{1,0:T(8,128)S(1)} %get-tuple-element.33), channel_id=1, source_target_pairs={{0,16},{16,0},{1,17},{17,1},{2,18},{18,2},{3,19},{19,3},{4,20},{20... | collective-permute-start | bytes 786440 | tf_op jit(solution)/shard_map/ppermute | solution.py:390
  7.8 11.7 %collective-permute-start.2 = (f32[264,128]{1,0:T(8,128)S(1)}, f32[264,128]{1,0:T(8,128)S(1)}, u32[]{:S(2)}, u32[]{:S(2)}) collective-permute-start(f32[264,128]{1,0:T(8,128)S(1)} %get-tuple-element.29), channel_id=1, source_target_pairs={{0,8},{1,9},{2,10},{3,11},{4,12},{5,13},{6,14},{7,15},{8,0},{9,1},... | collective-permute-start | bytes 405512 | tf_op jit(solution)/shard_map/ppermute | solution.py:386
  8.3 12.9 %collective-permute-start = (f32[320,128]{1,0:T(8,128)S(1)}, f32[320,128]{1,0:T(8,128)S(1)}, u32[]{:S(2)}, u32[]{:S(2)}) collective-permute-start(f32[320,128]{1,0:T(8,128)S(1)} %shard_map.58), channel_id=1, source_target_pairs={{0,16},{16,0},{1,17},{17,1},{2,18},{18,2},{3,19},{19,3},{4,20},{20... | collective-permute-start | bytes 491528 | tf_op jit(solution)/shard_map/ppermute | solution.py:390
  17.4 8.4 %collective-permute-start.4 = (f32[320,128]{1,0:T(8,128)S(1)}, f32[320,128]{1,0:T(8,128)S(1)}, u32[]{:S(2)}, u32[]{:S(2)}) collective-permute-start(f32[320,128]{1,0:T(8,128)S(1)} %collective-permute-done.1.near_ref), channel_id=1, source_target_pairs={{0,16},{16,0},{1,17},{17,1},{2,18},{18,2},{3,19},{19,3},{4,20},{20... | collective-permute-start | bytes 491528 | tf_op jit(solution)/shard_map/ppermute | solution.py:390
  19.5 6.3 %collective-permute-start.5 = (f32[264,128]{1,0:T(8,128)S(1)}, f32[264,128]{1,0:T(8,128)S(1)}, u32[]{:S(2)}, u32[]{:S(2)}) collective-permute-start(f32[264,128]{1,0:T(8,128)S(1)} %collective-permute-done.2.side_ref), channel_id=1, source_target_pairs={{0,16},{16,0},{1,17},{17,1},{2,18},{18,2},{3,19},{19,3},{4,20},{20... | collective-permute-start | bytes 405512 | tf_op jit(solution)/shard_map/ppermute | solution.py:390
  21.1 21.6 %collective-permute-start.7 = (f32[512,128]{1,0:T(8,128)S(1)}, f32[512,128]{1,0:T(8,128)S(1)}, u32[]{:S(2)}, u32[]{:S(2)}) collective-permute-start(f32[512,128]{1,0:T(8,128)S(1)} %get-tuple-element.49), channel_id=1, source_target_pairs={{0,8},{1,9},{2,10},{3,11},{4,12},{5,13},{6,14},{7,15},{8,0},{9,1},... | collective-permute-start | bytes 786440 | tf_op jit(solution)/shard_map/ppermute | solution.py:386
  21.7 24.1 %collective-permute-start.8 = (f32[512,128]{1,0:T(8,128)S(1)}, f32[512,128]{1,0:T(8,128)S(1)}, u32[]{:S(2)}, u32[]{:S(2)}) collective-permute-start(f32[512,128]{1,0:T(8,128)S(1)} %get-tuple-element.50), channel_id=1, source_target_pairs={{0,8},{1,9},{2,10},{3,11},{4,12},{5,13},{6,14},{7,15},{8,0},{9,1},... | collective-permute-start | bytes 786440 | tf_op jit(solution)/shard_map/ppermute | solution.py:386
  24.7 9.3 %collective-permute-start.6 = (f32[256,256]{1,0:T(8,128)S(1)}, f32[256,256]{1,0:T(8,128)S(1)}, u32[]{:S(2)}, u32[]{:S(2)}) collective-permute-start(f32[256,256]{1,0:T(8,128)S(1)} %get-tuple-element.43), channel_id=1, source_target_pairs={{0,16},{16,0},{1,17},{17,1},{2,18},{18,2},{3,19},{19,3},{4,20},{20... | collective-permute-start | bytes 786440 | tf_op jit(solution)/shard_map/ppermute | solution.py:390
  25.8 8.2 %copy-start.1 = (f32[1,256,1024]{2,1,0:T(8,128)S(1)}, f32[1,256,1024]{2,1,0:T(8,128)}, u32[]{:S(2)}) copy-start(f32[1,256,1024]{2,1,0:T(8,128)} %param.3) | copy-start | bytes 3145732
  43.1 4.0 %copy-start.2 = (f32[1,256,512]{2,1,0:T(8,128)S(1)}, f32[1,256,512]{2,1,0:T(8,128)}, u32[]{:S(2)}) copy-start(f32[1,256,512]{2,1,0:T(8,128)} %param.4) | copy-start | bytes 1572868
  43.1 7.2 %collective-permute-start.9 = (f32[256,128]{1,0:T(8,128)S(1)}, f32[256,128]{1,0:T(8,128)S(1)}, u32[]{:S(2)}, u32[]{:S(2)}) collective-permute-start(f32[256,128]{1,0:T(8,128)S(1)} %shard_map.66), channel_id=1, source_target_pairs={{0,16},{16,0},{1,17},{17,1},{2,18},{18,2},{3,19},{19,3},{4,20},{20... | collective-permute-start | bytes 393224 | tf_op jit(solution)/shard_map/ppermute | solution.py:390
  46.3 5.0 %collective-permute-start.10 = (f32[256,128]{1,0:T(8,128)S(1)}, f32[256,128]{1,0:T(8,128)S(1)}, u32[]{:S(2)}, u32[]{:S(2)}) collective-permute-start(f32[256,128]{1,0:T(8,128)S(1)} %shard_map.67), channel_id=1, source_target_pairs={{0,16},{16,0},{1,17},{17,1},{2,18},{18,2},{3,19},{19,3},{4,20},{20... | collective-permute-start | bytes 393224 | tf_op jit(solution)/shard_map/ppermute | solution.py:390
